TPU v7x, 32 devices: a whole 2x2x4 slice. The times are simulated.
32 devices in a mesh: pipe: 2 (over y), tensor: 4 (over x, core), dp: 4 (over z).
Axes of the slice: x: 2, y: 2, z: 4, core: 2. Of those that a mesh axis runs over, the one named last changes fastest.
Arguments:
- boundary: bfloat16 [2, 2, 4, 1280, 1024], P('pipe', None, 'dp', 'tensor'), may hold values from -6 to 6
- lengths: int32 [2, 4, 3], P(None, 'dp'), may hold values from 1 to 1024, 1280 in all within a row
- gains: bfloat16 [2, 2, 1024], P('pipe', None, ('tensor', 'dp')), may hold values from 0.5 to 1.5
- biases: bfloat16 [2, 4, 1024], P('pipe', None, ('tensor', 'dp')), may hold values from -1 to 1
- qkv_weight: bfloat16 [2, 1024, 3, 1024], P('pipe', 'dp', None, 'tensor'), may hold values from -0.1875 to 0.1875
- qkv_bias: bfloat16 [2, 3, 1024], P('pipe', None, ('tensor', 'dp')), may hold values from -1.5 to 1.5
- out_weight: bfloat16 [2, 1024, 1024], P('pipe', 'tensor', 'dp'), may hold values from -0.75 to 0.75
- up_weight: bfloat16 [2, 1024, 4096], P('pipe', 'dp', 'tensor'), may hold values from -0.1875 to 0.1875
- up_bias: bfloat16 [2, 4096], P('pipe', ('tensor', 'dp')), may hold values from -1.5 to 1.5
- down_weight: bfloat16 [2, 4096, 1024], P('pipe', 'tensor', 'dp'), may hold values from -0.09375 to 0.09375
Outputs:
- ends: float32 [2, 2, 4, 1280, 1024], P('pipe', None, 'dp', 'tensor')
- grad_gains: float32 [2, 2, 1024], P('pipe', None, ('tensor', 'dp'))
- grad_biases: float32 [2, 4, 1024], P('pipe', None, ('tensor', 'dp'))
- grad_qkv_weight: float32 [2, 1024, 3, 1024], P('pipe', 'dp', None, 'tensor')
- grad_qkv_bias: float32 [2, 3, 1024], P('pipe', None, ('tensor', 'dp'))
- grad_out_weight: float32 [2, 1024, 1024], P('pipe', 'tensor', 'dp')
- grad_up_weight: float32 [2, 1024, 4096], P('pipe', 'dp', 'tensor')
- grad_up_bias: float32 [2, 4096], P('pipe', ('tensor', 'dp'))
- grad_down_weight: float32 [2, 4096, 1024], P('pipe', 'tensor', 'dp')
Inputs may be any that keep to these rules, and one draw needn't show every extreme that they name: Each row lengths[m, g] sums to 1280 and its largest entry is exactly 1024.
All inputs are finite; a program needn't handle non-finite values.
Results may differ from a plain program's by a relative error of at most 0.008.
Values may be sent and summed in bfloat16 or wider, within the bound.
No kernel may reach another device: no remote copies, remote signals or barrier semaphores. Data moves between devices by JAX's collectives and lax.ppermute only.
A program may use at most 192 MiB of HBM per device.

v0:
```python
import jax
import jax.numpy as jnp
from jax import lax
from jax.sharding import PartitionSpec as P

D = 1024
H = 16
HD = 64
ROT = 16
MB = 2
TOK_MB = 1280


epsilon = 1e-05


def from_behind(value, axis, by):
    count = lax.axis_size(axis)
    pairs = [(i, i + by) for i in range(count) if 0 <= i + by < count]
    return lax.ppermute(value, axis, pairs)


def norm_rows(inputs, gain, bias):
    middle_value = jnp.mean(inputs, axis=-1, keepdims=True)
    centered = inputs - middle_value
    variance = jnp.mean(centered * centered, axis=-1, keepdims=True)
    return centered * lax.rsqrt(variance + epsilon) * gain + bias


def gelu_exact(values):
    return jax.nn.gelu(values, approximate=False)


def angles_for(lengths_row):
    finish = jnp.cumsum(lengths_row)
    places = jnp.arange(TOK_MB, dtype=jnp.int32)
    after = (places[:, None] >= finish[None, :]).astype(jnp.int32)
    segment = jnp.sum(after, axis=1)
    starts = jnp.sum(after * lengths_row[None, :], axis=1)
    position = (places - starts).astype(jnp.float32)
    inverse_freq = 10000.0 ** (-jnp.arange(ROT // 2, dtype=jnp.float32) * 2.0 / ROT)
    phase = position[:, None] * inverse_freq[None, :]
    return (segment, jnp.cos(phase), jnp.sin(phase))


def rotate(values, cosine, sine):
    rot_half = ROT // 2
    first = values[..., :rot_half]
    second = values[..., rot_half:ROT]
    remain = values[..., ROT:]
    return jnp.concatenate(
        [first * cosine - second * sine, second * cosine + first * sine, remain], axis=-1
    )


def unrotate(grads, cosine, sine):
    rot_half = ROT // 2
    first = grads[..., :rot_half]
    second = grads[..., rot_half:ROT]
    remain = grads[..., ROT:]
    return jnp.concatenate(
        [first * cosine + second * sine, second * cosine - first * sine, remain], axis=-1
    )


def inner_rows(left, right):
    return lax.dot_general(
        left, right, (((0,), (0,)), ((), ())), preferred_element_type=jnp.float32
    )


def times_transposed(left, right):
    return lax.dot_general(
        left, right, (((1,), (1,)), ((), ())), preferred_element_type=jnp.float32
    )


def block_scores(q_rows, keys, seg_rows, place_rows, segment, places):
    scores = jnp.einsum("qhd,khd->hqk", q_rows, keys, preferred_element_type=jnp.float32) * HD ** (
        -0.5
    )
    allowed = (seg_rows[:, None] == segment[None, :]) & (place_rows[:, None] >= places[None, :])
    return jnp.where(allowed[None], scores, -1e30)


def project(first_full, second_full, weights, cosine, sine, heads_local):
    qkv_w, qkv_b, out_w, up_w, up_b, down_w = weights
    total_rows = first_full.shape[0]
    raw = jnp.einsum("td,dcf->tcf", first_full, qkv_w, preferred_element_type=jnp.float32) + qkv_b
    split = raw.reshape(total_rows, 3, heads_local, HD)
    queries = rotate(split[:, 0], cosine[:, None], sine[:, None]).astype(jnp.bfloat16)
    keys = rotate(split[:, 1], cosine[:, None], sine[:, None]).astype(jnp.bfloat16)
    values = split[:, 2].astype(jnp.bfloat16)
    pre_act = jnp.dot(second_full, up_w, preferred_element_type=jnp.float32) + up_b
    hidden = gelu_exact(pre_act).astype(jnp.bfloat16)
    return (queries, keys, values, pre_act, hidden)


def attend(queries, keys, values, segment):
    total_rows = queries.shape[0]
    block = total_rows // 2
    places = jnp.arange(total_rows, dtype=jnp.int32)
    pieces = []
    tops = []
    totals = []
    for index in range(2):
        begin = index * block
        scores = block_scores(
            queries[begin : begin + block],
            keys,
            segment[begin : begin + block],
            places[begin : begin + block],
            segment,
            places,
        )
        top_score = jnp.max(scores, axis=-1, keepdims=True)
        expd = jnp.exp(scores - top_score)
        row_total = jnp.sum(expd, axis=-1, keepdims=True)
        probs = (expd / row_total).astype(jnp.bfloat16)
        pieces.append(jnp.einsum("hqk,khd->qhd", probs, values, preferred_element_type=jnp.float32))
        tops.append(top_score)
        totals.append(row_total)
    return (jnp.concatenate(pieces, axis=0), tops, totals)


def attend_back(queries, keys, values, segment, grad_context, tops, totals):
    total_rows = queries.shape[0]
    block = total_rows // 2
    places = jnp.arange(total_rows, dtype=jnp.int32)
    scale = HD ** (-0.5)
    grad_keys = jnp.zeros(keys.shape, jnp.float32)
    grad_values = jnp.zeros(values.shape, jnp.float32)
    query_grads = []
    for index in range(2):
        begin = index * block
        q_rows = queries[begin : begin + block]
        grad_rows = grad_context[begin : begin + block]
        scores = block_scores(
            q_rows,
            keys,
            segment[begin : begin + block],
            places[begin : begin + block],
            segment,
            places,
        )
        probs = jnp.exp(scores - tops[index]) / totals[index]
        grad_probs = jnp.einsum(
            "qhd,khd->hqk", grad_rows, values, preferred_element_type=jnp.float32
        )
        weighted = jnp.sum(grad_probs * probs, axis=-1, keepdims=True)
        grad_scores = (probs * (grad_probs - weighted)).astype(jnp.bfloat16)
        query_grads.append(
            jnp.einsum("hqk,khd->qhd", grad_scores, keys, preferred_element_type=jnp.float32)
            * scale
        )
        grad_keys = (
            grad_keys
            + jnp.einsum("hqk,qhd->khd", grad_scores, q_rows, preferred_element_type=jnp.float32)
            * scale
        )
        grad_values = grad_values + jnp.einsum(
            "hqk,qhd->khd",
            probs.astype(jnp.bfloat16),
            grad_rows,
            preferred_element_type=jnp.float32,
        )
    return (jnp.concatenate(query_grads, axis=0), grad_keys, grad_values)


def forward_tick(x_rows, weights, gain_all, bias_all, segment, cosine, sine, heads_local):
    first = norm_rows(x_rows, gain_all[0], bias_all[0]).astype(jnp.bfloat16)
    second = norm_rows(x_rows, gain_all[1], bias_all[1]).astype(jnp.bfloat16)
    first_full, second_full = (
        lax.all_gather(first, "tensor", axis=0, tiled=True),
        lax.all_gather(second, "tensor", axis=0, tiled=True),
    )
    queries, keys, values, pre_act, hidden = project(
        first_full, second_full, weights, cosine, sine, heads_local
    )
    context, tops, totals = attend(queries, keys, values, segment)
    context_low = context.reshape(context.shape[0], -1).astype(jnp.bfloat16)
    out_w = weights[2]
    down_w = weights[5]
    context_rows = lax.slice_in_dim(
        context_low, 0, lax.axis_size("tensor") * x_rows.shape[0], axis=0
    )
    summed = lax.psum_scatter(
        jnp.dot(context_rows, out_w, preferred_element_type=jnp.float32)
        + jnp.dot(hidden, down_w, preferred_element_type=jnp.float32),
        "tensor",
        scatter_dimension=0,
        tiled=True,
    )
    return x_rows + summed + bias_all[2] + bias_all[3]


def backward_tick(
    x_rows, cot_rows, weights, gain_all, bias_all, segment, cosine, sine, heads_local
):
    qkv_w, qkv_b, out_w, up_w, up_b, down_w = weights
    first = norm_rows(x_rows, gain_all[0], bias_all[0]).astype(jnp.bfloat16)
    second = norm_rows(x_rows, gain_all[1], bias_all[1]).astype(jnp.bfloat16)
    first_full, second_full = (
        lax.all_gather(first, "tensor", axis=0, tiled=True),
        lax.all_gather(second, "tensor", axis=0, tiled=True),
    )
    queries, keys, values, pre_act, hidden = project(
        first_full, second_full, weights, cosine, sine, heads_local
    )
    context, tops, totals = attend(queries, keys, values, segment)
    total_rows = context.shape[0]
    context_low = context.reshape(total_rows, -1).astype(jnp.bfloat16)
    cot_full = lax.all_gather(cot_rows, "tensor", axis=0, tiled=True)
    grad_out_w = inner_rows(context_low, cot_full)
    grad_down_w = inner_rows(hidden, cot_full)
    grad_context = times_transposed(cot_full, out_w).astype(jnp.bfloat16)
    grad_hidden = times_transposed(cot_full, down_w)
    activated, gelu_pull = jax.vjp(gelu_exact, pre_act)
    grad_pre = gelu_pull(grad_hidden)[0].astype(jnp.bfloat16)
    grad_up_w = inner_rows(second_full, grad_pre)
    grad_up_b = jnp.sum(grad_pre, axis=0, dtype=jnp.float32)
    grad_second = times_transposed(grad_pre, up_w)
    grad_context = grad_context.reshape(total_rows, heads_local, HD)
    grad_q, grad_k, grad_v = attend_back(queries, keys, values, segment, grad_context, tops, totals)
    grad_q = unrotate(grad_q, cosine[:, None], sine[:, None])
    grad_k = unrotate(grad_k, cosine[:, None], sine[:, None])
    grad_raw = (
        jnp.stack([grad_q, grad_k, grad_v], axis=1)
        .reshape(total_rows, 3, heads_local * HD)
        .astype(jnp.bfloat16)
    )
    grad_qkv_w = jnp.einsum("td,tcf->dcf", first_full, grad_raw, preferred_element_type=jnp.float32)
    grad_qkv_b = jnp.sum(grad_raw, axis=0, dtype=jnp.float32)
    grad_first = jnp.einsum("tcf,dcf->td", grad_raw, qkv_w, preferred_element_type=jnp.float32)
    cot_float = cot_rows.astype(jnp.float32)
    bias_out = jnp.sum(cot_float, axis=0)
    grad_first_rows, grad_second_rows = (
        lax.psum_scatter(grad_first, "tensor", scatter_dimension=0, tiled=True),
        lax.psum_scatter(grad_second, "tensor", scatter_dimension=0, tiled=True),
    )
    normed_first, pull_first = jax.vjp(norm_rows, x_rows, gain_all[0], bias_all[0])
    normed_second, pull_second = jax.vjp(norm_rows, x_rows, gain_all[1], bias_all[1])
    input_first, gain_first, bias_first = pull_first(grad_first_rows)
    input_second, gain_second, bias_second = pull_second(grad_second_rows)
    grad_inputs = cot_float + input_first + input_second
    vector_terms = (
        jnp.stack([gain_first, gain_second]),
        jnp.stack([bias_first, bias_second, bias_out, bias_out]),
    )
    weight_terms = (grad_qkv_w, grad_qkv_b, grad_out_w, grad_up_w, grad_up_b, grad_down_w)
    return (grad_inputs, weight_terms, vector_terms)


def masked(values, flag):
    return jax.tree.map(lambda item: jnp.where(flag, item, jnp.zeros_like(item)), values)


def body(
    boundary,
    lengths,
    gains,
    biases,
    qkv_weight,
    qkv_bias,
    out_weight,
    up_weight,
    up_bias,
    down_weight,
):
    section = lax.axis_index("pipe")
    is_first = section == 0
    tiles = boundary[0, :, 0]
    rows_local = tiles.shape[1]
    heads_local = H // lax.axis_size("tensor")
    width_local = qkv_weight.shape[3]
    hidden_local = up_weight.shape[2]
    gain_all, bias_all = (
        lax.all_gather(gains[0], ("tensor", "dp"), axis=1, tiled=True),
        lax.all_gather(biases[0], ("tensor", "dp"), axis=1, tiled=True),
    )
    gain_all = gain_all.astype(jnp.float32)
    bias_all = bias_all.astype(jnp.float32)
    full_shapes = (
        (D, 3, width_local),
        (3, width_local),
        (width_local, D),
        (D, hidden_local),
        (hidden_local,),
        (hidden_local, D),
    )
    grad_init = tuple((jnp.zeros(shape_item, jnp.float32) for shape_item in full_shapes))
    vector_init = (jnp.zeros((2, D), jnp.float32), jnp.zeros((4, D), jnp.float32))
    empty_rows = jnp.zeros((rows_local, D), jnp.bfloat16)
    ends_init = jnp.zeros((MB, rows_local, D), jnp.float32)

    def tick(step, carry):
        recv_fwd, recv_bwd, ends_out, grad_accum, vector_accum = carry
        weights_now = (
            lax.all_gather(qkv_weight[0], "dp", axis=0, tiled=True),
            lax.all_gather(qkv_bias[0], "dp", axis=1, tiled=True),
            lax.all_gather(out_weight[0], "dp", axis=1, tiled=True),
            lax.all_gather(up_weight[0], "dp", axis=0, tiled=True),
            lax.all_gather(up_bias[0], "dp", axis=0, tiled=True),
            lax.all_gather(down_weight[0], "dp", axis=1, tiled=True),
        )
        fwd_index = step - section
        fwd_valid = (fwd_index >= 0) & (fwd_index < MB)
        fwd_clip = jnp.clip(fwd_index, 0, MB - 1)
        own_fwd = lax.dynamic_index_in_dim(tiles, fwd_clip, 0, keepdims=False)
        fwd_in = jnp.where(is_first, own_fwd, recv_fwd).astype(jnp.float32)
        segment, cosine, sine = angles_for(
            lax.dynamic_index_in_dim(lengths, fwd_clip, 0, keepdims=False)[0]
        )
        produced = forward_tick(
            fwd_in, weights_now, gain_all, bias_all, segment, cosine, sine, heads_local
        )
        weights_back = (
            lax.all_gather(qkv_weight[0], "dp", axis=0, tiled=True),
            lax.all_gather(qkv_bias[0], "dp", axis=1, tiled=True),
            lax.all_gather(out_weight[0], "dp", axis=1, tiled=True),
            lax.all_gather(up_weight[0], "dp", axis=0, tiled=True),
            lax.all_gather(up_bias[0], "dp", axis=0, tiled=True),
            lax.all_gather(down_weight[0], "dp", axis=1, tiled=True),
        )
        back_index = step - 2 + section
        back_valid = (back_index >= 0) & (back_index < MB)
        back_clip = jnp.clip(back_index, 0, MB - 1)
        own_back = lax.dynamic_index_in_dim(tiles, back_clip, 0, keepdims=False)
        back_in = jnp.where(is_first, own_back, recv_fwd).astype(jnp.float32)
        cot_rows = jnp.where(is_first, recv_bwd, own_back)
        segment_back, cosine_back, sine_back = angles_for(
            lax.dynamic_index_in_dim(lengths, back_clip, 0, keepdims=False)[0]
        )
        grad_inputs, weight_terms, vector_terms = backward_tick(
            back_in,
            cot_rows,
            weights_back,
            gain_all,
            bias_all,
            segment_back,
            cosine_back,
            sine_back,
            heads_local,
        )
        write_index = jnp.where(is_first, back_clip, fwd_clip)
        write_valid = jnp.where(is_first, back_valid, fwd_valid)
        written = jnp.where(is_first, grad_inputs, produced)
        previous = lax.dynamic_index_in_dim(ends_out, write_index, 0, keepdims=False)
        ends_out = lax.dynamic_update_index_in_dim(
            ends_out, jnp.where(write_valid, written, previous), write_index, 0
        )
        weight_terms = masked(weight_terms, back_valid)
        vector_terms = masked(vector_terms, back_valid)
        grad_accum = jax.tree.map(
            lambda total_item, term_item: total_item + term_item, grad_accum, weight_terms
        )
        vector_accum = jax.tree.map(
            lambda total_item, term_item: total_item + term_item, vector_accum, vector_terms
        )
        next_fwd = from_behind(produced.astype(jnp.bfloat16), "pipe", 1)
        next_bwd = from_behind(grad_inputs.astype(jnp.bfloat16), "pipe", -1)
        return (next_fwd, next_bwd, ends_out, grad_accum, vector_accum)

    recv_fwd, recv_bwd, ends_out, grad_accum, vector_accum = lax.fori_loop(
        0, MB + 2, tick, (empty_rows, empty_rows, ends_init, grad_init, vector_init)
    )
    grad_accum = (
        lax.psum_scatter(grad_accum[0], "dp", scatter_dimension=0, tiled=True),
        lax.psum_scatter(grad_accum[1], "dp", scatter_dimension=1, tiled=True),
        lax.psum_scatter(grad_accum[2], "dp", scatter_dimension=1, tiled=True),
        lax.psum_scatter(grad_accum[3], "dp", scatter_dimension=0, tiled=True),
        lax.psum_scatter(grad_accum[4], "dp", scatter_dimension=0, tiled=True),
        lax.psum_scatter(grad_accum[5], "dp", scatter_dimension=1, tiled=True),
    )
    grad_gain_part, grad_bias_part = (
        lax.psum_scatter(vector_accum[0], ("tensor", "dp"), scatter_dimension=1, tiled=True),
        lax.psum_scatter(vector_accum[1], ("tensor", "dp"), scatter_dimension=1, tiled=True),
    )
    ends = ends_out[None, :, None]
    return (
        ends,
        grad_gain_part[None],
        grad_bias_part[None],
        grad_accum[0][None],
        grad_accum[1][None],
        grad_accum[2][None],
        grad_accum[3][None],
        grad_accum[4][None],
        grad_accum[5][None],
    )


def solution(mesh):
    placed = (
        P("pipe", None, "dp", "tensor", None),
        P(None, "dp", None),
        P("pipe", None, ("tensor", "dp")),
        P("pipe", None, ("tensor", "dp")),
        P("pipe", "dp", None, "tensor"),
        P("pipe", None, ("tensor", "dp")),
        P("pipe", "tensor", "dp"),
        P("pipe", "dp", "tensor"),
        P("pipe", ("tensor", "dp")),
        P("pipe", "tensor", "dp"),
    )
    return jax.shard_map(
        body,
        mesh=mesh,
        in_specs=placed,
        out_specs=(
            P("pipe", None, "dp", "tensor", None),
            P("pipe", None, ("tensor", "dp")),
            P("pipe", None, ("tensor", "dp")),
            P("pipe", "dp", None, "tensor"),
            P("pipe", None, ("tensor", "dp")),
            P("pipe", "tensor", "dp"),
            P("pipe", "dp", "tensor"),
            P("pipe", ("tensor", "dp")),
            P("pipe", "tensor", "dp"),
        ),
        check_vma=False,
    )
```

profile of v0, /device:TPU:0, one launch (start us, length us, event | category | flops | bytes accessed | tf_op | source)
XLA Modules:
  0.0 2314.4 jit_solution(16440110803425094757)
XLA Ops:
  13.0 38.8 %all-gather.7 = bf16[1,4,1024]{1,0,2:T(2,128)(2,1)S(1)} all-gather(bf16[1,4,64]{1,0,2:T(2,128)(2,1)S(1)} %copy.42), channel_id=9, replica_groups=mesh['pipe'=2,'tensor'=4,'dp'=4] {'tensor','dp'}, dimensions={2}, use_global_device_ids=true | all-gather | bytes 8704 | tf_op jit(solution)/shard_map/all_gather | solution.py:279
  53.1 33.0 %all-gather.6 = bf16[1,2,1024]{1,0,2:T(2,128)(2,1)S(1)} all-gather(bf16[1,2,64]{1,0,2:T(2,128)(2,1)S(1)} %copy.41), channel_id=8, replica_groups=mesh['pipe'=2,'tensor'=4,'dp'=4] {'tensor','dp'}, dimensions={2}, use_global_device_ids=true | all-gather | bytes 4352 | tf_op jit(solution)/shard_map/all_gather | solution.py:278
  90.3 1828.8 %while.36 = (s32[]{:T(128)}, bf16[320,1024]{1,0:T(8,128)(2,1)}, bf16[320,1024]{1,0:T(8,128)(2,1)S(1)}, f32[2,320,1024]{2,1,0:T(8,128)}, f32[1024,3,256]{2,0,1:T(...) while((s32[]{:T(128)}, bf16[320,1024]{1,0:T(8,128)(2,1)}, ...), condition=%wide.region_35.36_spmd.clone, body=%wide.region_0.35_spmd.clone.sunk | while | flops 38580609024 | bytes 903876608 | solution.py:364
  130.0 15.7 all-gather.25
  189.4 17.3 all-gather.35.cloned.1.call-done
  206.6 45.6 %all-gather.39.cloned.1.call-done = bf16[1,1024,1024]{2,1,0:T(8,128)(2,1)} async-done(((bf16[1,256,1024]{2,1,0:T(8,128)(2,1)}), bf16[1,1024,1024]{2,1,0:T(8,128)(2,1)}) %all-gather.39.cloned.1.call-update) | async-done | bytes 2097168 | tf_op jit(solution)/shard_map/while/body/eval_jaxpr/all_gather | solution.py:302
  252.3 25.7 %all-gather.37.cloned.1.call-done = bf16[1280,1024]{1,0:T(8,128)(2,1)} async-done(((bf16[320,1024]{1,0:T(8,128)(2,1)}), bf16[1280,1024]{1,0:T(8,128)(2,1)}) %all-gather.37.cloned.1.call-update) | async-done | bytes 2621456 | tf_op jit(solution)/shard_map/while/body/eval_jaxpr/all_gather | solution.py:175
  278.0 20.3 fusion.445
  312.2 20.5 all-gather.45.cloned.1.call-done
  370.1 16.2 fusion.466
  493.6 28.2 %reduce-scatter.33.cloned.1.call-done = f32[320,1024]{1,0:T(8,128)} async-done(((f32[1280,1024]{1,0:T(8,128)}), f32[320,1024]{1,0:T(8,128)}) %reduce-scatter.33.cloned.1.call-update) | async-done | bytes 1310736 | tf_op jit(solution)/shard_map/while/body/eval_jaxpr/reduce_scatter | solution.py:238
  529.5 16.9 collective-permute-done.1
  572.6 17.6 all-gather.23
  590.5 15.1 all-gather.25
  646.3 17.1 all-gather.35.cloned.1.call-done
  663.4 45.6 %all-gather.39.cloned.1.call-done = bf16[1,1024,1024]{2,1,0:T(8,128)(2,1)} async-done(((bf16[1,256,1024]{2,1,0:T(8,128)(2,1)}), bf16[1,1024,1024]{2,1,0:T(8,128)(2,1)}) %all-gather.39.cloned.1.call-update) | async-done | bytes 2097168 | tf_op jit(solution)/shard_map/while/body/eval_jaxpr/all_gather | solution.py:302
  709.0 25.7 %all-gather.37.cloned.1.call-done = bf16[1280,1024]{1,0:T(8,128)(2,1)} async-done(((bf16[320,1024]{1,0:T(8,128)(2,1)}), bf16[1280,1024]{1,0:T(8,128)(2,1)}) %all-gather.37.cloned.1.call-update) | async-done | bytes 2621456 | tf_op jit(solution)/shard_map/while/body/eval_jaxpr/all_gather | solution.py:175
  734.7 20.3 fusion.445
  769.0 20.3 all-gather.45.cloned.1.call-done
  826.7 16.1 fusion.466
  952.4 26.0 %reduce-scatter.33.cloned.1.call-done = f32[320,1024]{1,0:T(8,128)} async-done(((f32[1280,1024]{1,0:T(8,128)}), f32[320,1024]{1,0:T(8,128)}) %reduce-scatter.33.cloned.1.call-update) | async-done | bytes 1310736 | tf_op jit(solution)/shard_map/while/body/eval_jaxpr/reduce_scatter | solution.py:238
  986.1 16.9 collective-permute-done.1
  1029.7 15.6 all-gather.23
  1045.5 15.4 all-gather.25
  1103.1 17.3 all-gather.35.cloned.1.call-done
  1120.4 45.6 %all-gather.39.cloned.1.call-done = bf16[1,1024,1024]{2,1,0:T(8,128)(2,1)} async-done(((bf16[1,256,1024]{2,1,0:T(8,128)(2,1)}), bf16[1,1024,1024]{2,1,0:T(8,128)(2,1)}) %all-gather.39.cloned.1.call-update) | async-done | bytes 2097168 | tf_op jit(solution)/shard_map/while/body/eval_jaxpr/all_gather | solution.py:302
  1166.0 25.7 %all-gather.37.cloned.1.call-done = bf16[1280,1024]{1,0:T(8,128)(2,1)} async-done(((bf16[320,1024]{1,0:T(8,128)(2,1)}), bf16[1280,1024]{1,0:T(8,128)(2,1)}) %all-gather.37.cloned.1.call-update) | async-done | bytes 2621456 | tf_op jit(solution)/shard_map/while/body/eval_jaxpr/all_gather | solution.py:175
  1191.7 20.3 fusion.445
  1226.0 20.6 all-gather.45.cloned.1.call-done
  1284.0 16.1 fusion.466
  1409.9 25.6 %reduce-scatter.33.cloned.1.call-done = f32[320,1024]{1,0:T(8,128)} async-done(((f32[1280,1024]{1,0:T(8,128)}), f32[320,1024]{1,0:T(8,128)}) %reduce-scatter.33.cloned.1.call-update) | async-done | bytes 1310736 | tf_op jit(solution)/shard_map/while/body/eval_jaxpr/reduce_scatter | solution.py:238
  1443.2 16.9 collective-permute-done.1
  1486.9 15.5 all-gather.23
  1502.6 15.6 all-gather.25
  1560.3 17.1 all-gather.35.cloned.1.call-done
  1577.4 45.6 %all-gather.39.cloned.1.call-done = bf16[1,1024,1024]{2,1,0:T(8,128)(2,1)} async-done(((bf16[1,256,1024]{2,1,0:T(8,128)(2,1)}), bf16[1,1024,1024]{2,1,0:T(8,128)(2,1)}) %all-gather.39.cloned.1.call-update) | async-done | bytes 2097168 | tf_op jit(solution)/shard_map/while/body/eval_jaxpr/all_gather | solution.py:302
  1623.0 25.9 %all-gather.37.cloned.1.call-done = bf16[1280,1024]{1,0:T(8,128)(2,1)} async-done(((bf16[320,1024]{1,0:T(8,128)(2,1)}), bf16[1280,1024]{1,0:T(8,128)(2,1)}) %all-gather.37.cloned.1.call-update) | async-done | bytes 2621456 | tf_op jit(solution)/shard_map/while/body/eval_jaxpr/all_gather | solution.py:175
  1648.9 20.3 fusion.445
  1683.1 20.5 all-gather.45.cloned.1.call-done
  1741.0 16.1 fusion.466
  1866.9 25.8 %reduce-scatter.33.cloned.1.call-done = f32[320,1024]{1,0:T(8,128)} async-done(((f32[1280,1024]{1,0:T(8,128)}), f32[320,1024]{1,0:T(8,128)}) %reduce-scatter.33.cloned.1.call-update) | async-done | bytes 1310736 | tf_op jit(solution)/shard_map/while/body/eval_jaxpr/reduce_scatter | solution.py:238
  1900.4 16.9 collective-permute-done.1
  1942.1 56.0 %reduce-scatter.25.cloned.1.call-done = f32[64,2]{1,0:T(8,128)} async-done(((f32[1024,2]{1,0:T(8,128)}), f32[64,2]{1,0:T(8,128)}) %reduce-scatter.25.cloned.1.call-update) | async-done | bytes 528
  1999.5 56.9 %reduce-scatter.27.cloned.1.call-done = f32[64,4]{1,0:T(8,128)} async-done(((f32[1024,4]{1,0:T(8,128)}), f32[64,4]{1,0:T(8,128)}) %reduce-scatter.27.cloned.1.call-update) | async-done | bytes 1040
  2057.8 27.7 %reduce-scatter.19.cloned.1.call-done = f32[256,256]{1,0:T(8,128)} async-done(((f32[256,1024]{1,0:T(8,128)}), f32[256,256]{1,0:T(8,128)}) %reduce-scatter.19.cloned.1.call-update) | async-done | bytes 262160 | tf_op jit(solution)/shard_map/reduce_scatter | solution.py:370
  2085.5 61.8 %reduce-scatter.17.cloned.1.call-done = f32[256,3,256]{2,0,1:T(8,128)} async-done(((f32[1024,3,256]{2,0,1:T(8,128)}), f32[256,3,256]{2,0,1:T(8,128)}) %reduce-scatter.17.cloned.1.call-update) | async-done | bytes 786448 | tf_op jit(solution)/shard_map/reduce_scatter | solution.py:368
  2147.3 79.6 %reduce-scatter.23.cloned.1.call-done = f32[1024,256]{1,0:T(8,128)} async-done(((f32[1024,1024]{1,0:T(8,128)}), f32[1024,256]{1,0:T(8,128)}) %reduce-scatter.23.cloned.1.call-update) | async-done | bytes 1048592 | tf_op jit(solution)/shard_map/reduce_scatter | solution.py:373
  2226.9 80.1 %reduce-scatter.21.cloned.1.call-done = f32[256,1024]{1,0:T(8,128)} async-done(((f32[1024,1024]{1,0:T(8,128)}), f32[256,1024]{1,0:T(8,128)}) %reduce-scatter.21.cloned.1.call-update) | async-done | bytes 1048592 | tf_op jit(solution)/shard_map/reduce_scatter | solution.py:371
  (1117 shorter events, 990.3 us)
Async XLA Ops:
  91.0 67.8 %all-gather.41.cloned.1.call-start = ((), (), s32[]{:S(2)}) async-start(), calls=%async_computation.20 | async-start | bytes 3276800 | tf_op jit(solution)/shard_map/while/body/eval_jaxpr/all_gather | solution.py:174
  99.5 107.1 %all-gather.35.cloned.1.call-start = ((), (), s32[]{:S(2)}) async-start(), calls=%async_computation.17 | async-start | bytes 2621440 | tf_op jit(solution)/shard_map/while/body/eval_jaxpr/all_gather | solution.py:304
  100.2 152.0 %all-gather.39.cloned.1.call-start = ((), (), s32[]{:S(2)}) async-start(), calls=%async_computation.19 | async-start | bytes 2621440 | tf_op jit(solution)/shard_map/while/body/eval_jaxpr/all_gather | solution.py:302
  100.8 177.2 %all-gather.37.cloned.1.call-start = ((), (), s32[]{:S(2)}) async-start(), calls=%async_computation.18 | async-start | bytes 3276800 | tf_op jit(solution)/shard_map/while/body/eval_jaxpr/all_gather | solution.py:175
  101.4 203.6 %all-gather.47.cloned.1.call-start = ((), (), s32[]{:S(2)}) async-start(), calls=%async_computation.24 | async-start | bytes 3276800 | tf_op jit(solution)/shard_map/while/body/eval_jaxpr/all_gather | solution.py:204
  102.0 230.7 %all-gather.45.cloned.1.call-start = ((), (), s32[]{:S(2)}) async-start(), calls=%async_computation.23 | async-start | bytes 3276800 | tf_op jit(solution)/shard_map/while/body/eval_jaxpr/all_gather | solution.py:213
  102.7 267.4 %all-gather.49.cloned.1.call-start = ((), (), s32[]{:S(2)}) async-start(), calls=%async_computation.26 | async-start | bytes 3276800 | tf_op jit(solution)/shard_map/while/body/eval_jaxpr/all_gather | solution.py:205
  103.5 383.5 %reduce-scatter.31.cloned.1.call-start = ((), (), s32[]{:S(2)}) async-start(), calls=%async_computation.22 | async-start | bytes 6553600 | tf_op jit(solution)/shard_map/while/body/eval_jaxpr/reduce_scatter | solution.py:187
  304.0 189.6 %reduce-scatter.35.cloned.1.call-start = ((), (), s32[]{:S(2)}) async-start(), calls=%async_computation.27 | async-start | bytes 6553600 | tf_op jit(solution)/shard_map/while/body/eval_jaxpr/reduce_scatter | solution.py:239
  397.9 123.8 %reduce-scatter.33.cloned.1.call-start = ((), (), s32[]{:S(2)}) async-start(), calls=%async_computation.25 | async-start | bytes 6553600 | tf_op jit(solution)/shard_map/while/body/eval_jaxpr/reduce_scatter | solution.py:238
  546.9 62.9 %all-gather.43.cloned.1.call-start = ((), (), s32[]{:S(2)}) async-start(), calls=%async_computation.21 | async-start | bytes 1966080 | tf_op jit(solution)/shard_map/while/body/eval_jaxpr/all_gather | solution.py:299
  547.5 68.3 %all-gather.41.cloned.1.call-start = ((), (), s32[]{:S(2)}) async-start(), calls=%async_computation.20 | async-start | bytes 3276800 | tf_op jit(solution)/shard_map/while/body/eval_jaxpr/all_gather | solution.py:174
  555.9 107.5 %all-gather.35.cloned.1.call-start = ((), (), s32[]{:S(2)}) async-start(), calls=%async_computation.17 | async-start | bytes 2621440 | tf_op jit(solution)/shard_map/while/body/eval_jaxpr/all_gather | solution.py:304
  556.5 152.5 %all-gather.39.cloned.1.call-start = ((), (), s32[]{:S(2)}) async-start(), calls=%async_computation.19 | async-start | bytes 2621440 | tf_op jit(solution)/shard_map/while/body/eval_jaxpr/all_gather | solution.py:302
  557.1 177.6 %all-gather.37.cloned.1.call-start = ((), (), s32[]{:S(2)}) async-start(), calls=%async_computation.18 | async-start | bytes 3276800 | tf_op jit(solution)/shard_map/while/body/eval_jaxpr/all_gather | solution.py:175
  557.7 204.0 %all-gather.47.cloned.1.call-start = ((), (), s32[]{:S(2)}) async-start(), calls=%async_computation.24 | async-start | bytes 3276800 | tf_op jit(solution)/shard_map/while/body/eval_jaxpr/all_gather | solution.py:204
  558.3 231.0 %all-gather.45.cloned.1.call-start = ((), (), s32[]{:S(2)}) async-start(), calls=%async_computation.23 | async-start | bytes 3276800 | tf_op jit(solution)/shard_map/while/body/eval_jaxpr/all_gather | solution.py:213
  558.9 267.8 %all-gather.49.cloned.1.call-start = ((), (), s32[]{:S(2)}) async-start(), calls=%async_computation.26 | async-start | bytes 3276800 | tf_op jit(solution)/shard_map/while/body/eval_jaxpr/all_gather | solution.py:205
  559.6 386.1 %reduce-scatter.31.cloned.1.call-start = ((), (), s32[]{:S(2)}) async-start(), calls=%async_computation.22 | async-start | bytes 6553600 | tf_op jit(solution)/shard_map/while/body/eval_jaxpr/reduce_scatter | solution.py:187
  760.7 191.6 %reduce-scatter.35.cloned.1.call-start = ((), (), s32[]{:S(2)}) async-start(), calls=%async_computation.27 | async-start | bytes 6553600 | tf_op jit(solution)/shard_map/while/body/eval_jaxpr/reduce_scatter | solution.py:239
  854.5 123.9 %reduce-scatter.33.cloned.1.call-start = ((), (), s32[]{:S(2)}) async-start(), calls=%async_computation.25 | async-start | bytes 6553600 | tf_op jit(solution)/shard_map/while/body/eval_jaxpr/reduce_scatter | solution.py:238
  1004.2 68.3 %all-gather.41.cloned.1.call-start = ((), (), s32[]{:S(2)}) async-start(), calls=%async_computation.20 | async-start | bytes 3276800 | tf_op jit(solution)/shard_map/while/body/eval_jaxpr/all_gather | solution.py:174
  1012.7 107.6 %all-gather.35.cloned.1.call-start = ((), (), s32[]{:S(2)}) async-start(), calls=%async_computation.17 | async-start | bytes 2621440 | tf_op jit(solution)/shard_map/while/body/eval_jaxpr/all_gather | solution.py:304
  1013.5 152.5 %all-gather.39.cloned.1.call-start = ((), (), s32[]{:S(2)}) async-start(), calls=%async_computation.19 | async-start | bytes 2621440 | tf_op jit(solution)/shard_map/while/body/eval_jaxpr/all_gather | solution.py:302
  1014.1 177.6 %all-gather.37.cloned.1.call-start = ((), (), s32[]{:S(2)}) async-start(), calls=%async_computation.18 | async-start | bytes 3276800 | tf_op jit(solution)/shard_map/while/body/eval_jaxpr/all_gather | solution.py:175
  1014.6 204.2 %all-gather.47.cloned.1.call-start = ((), (), s32[]{:S(2)}) async-start(), calls=%async_computation.24 | async-start | bytes 3276800 | tf_op jit(solution)/shard_map/while/body/eval_jaxpr/all_gather | solution.py:204
  1015.4 231.2 %all-gather.45.cloned.1.call-start = ((), (), s32[]{:S(2)}) async-start(), calls=%async_computation.23 | async-start | bytes 3276800 | tf_op jit(solution)/shard_map/while/body/eval_jaxpr/all_gather | solution.py:213
  1016.1 267.8 %all-gather.49.cloned.1.call-start = ((), (), s32[]{:S(2)}) async-start(), calls=%async_computation.26 | async-start | bytes 3276800 | tf_op jit(solution)/shard_map/while/body/eval_jaxpr/all_gather | solution.py:205
  1016.7 386.4 %reduce-scatter.31.cloned.1.call-start = ((), (), s32[]{:S(2)}) async-start(), calls=%async_computation.22 | async-start | bytes 6553600 | tf_op jit(solution)/shard_map/while/body/eval_jaxpr/reduce_scatter | solution.py:187
  1217.7 192.3 %reduce-scatter.35.cloned.1.call-start = ((), (), s32[]{:S(2)}) async-start(), calls=%async_computation.27 | async-start | bytes 6553600 | tf_op jit(solution)/shard_map/while/body/eval_jaxpr/reduce_scatter | solution.py:239
  1311.7 123.8 %reduce-scatter.33.cloned.1.call-start = ((), (), s32[]{:S(2)}) async-start(), calls=%async_computation.25 | async-start | bytes 6553600 | tf_op jit(solution)/shard_map/while/body/eval_jaxpr/reduce_scatter | solution.py:238
  1460.6 61.8 %all-gather.43.cloned.1.call-start = ((), (), s32[]{:S(2)}) async-start(), calls=%async_computation.21 | async-start | bytes 1966080 | tf_op jit(solution)/shard_map/while/body/eval_jaxpr/all_gather | solution.py:299
  1461.4 68.3 %all-gather.41.cloned.1.call-start = ((), (), s32[]{:S(2)}) async-start(), calls=%async_computation.20 | async-start | bytes 3276800 | tf_op jit(solution)/shard_map/while/body/eval_jaxpr/all_gather | solution.py:174
  1469.9 107.5 %all-gather.35.cloned.1.call-start = ((), (), s32[]{:S(2)}) async-start(), calls=%async_computation.17 | async-start | bytes 2621440 | tf_op jit(solution)/shard_map/while/body/eval_jaxpr/all_gather | solution.py:304
  1470.5 152.6 %all-gather.39.cloned.1.call-start = ((), (), s32[]{:S(2)}) async-start(), calls=%async_computation.19 | async-start | bytes 2621440 | tf_op jit(solution)/shard_map/while/body/eval_jaxpr/all_gather | solution.py:302
  1471.0 177.8 %all-gather.37.cloned.1.call-start = ((), (), s32[]{:S(2)}) async-start(), calls=%async_computation.18 | async-start | bytes 3276800 | tf_op jit(solution)/shard_map/while/body/eval_jaxpr/all_gather | solution.py:175
  1471.8 204.1 %all-gather.47.cloned.1.call-start = ((), (), s32[]{:S(2)}) async-start(), calls=%async_computation.24 | async-start | bytes 3276800 | tf_op jit(solution)/shard_map/while/body/eval_jaxpr/all_gather | solution.py:204
  1472.4 231.3 %all-gather.45.cloned.1.call-start = ((), (), s32[]{:S(2)}) async-start(), calls=%async_computation.23 | async-start | bytes 3276800 | tf_op jit(solution)/shard_map/while/body/eval_jaxpr/all_gather | solution.py:213
  1473.1 267.9 %all-gather.49.cloned.1.call-start = ((), (), s32[]{:S(2)}) async-start(), calls=%async_computation.26 | async-start | bytes 3276800 | tf_op jit(solution)/shard_map/while/body/eval_jaxpr/all_gather | solution.py:205
  1473.9 386.3 %reduce-scatter.31.cloned.1.call-start = ((), (), s32[]{:S(2)}) async-start(), calls=%async_computation.22 | async-start | bytes 6553600 | tf_op jit(solution)/shard_map/while/body/eval_jaxpr/reduce_scatter | solution.py:187
  1674.9 192.0 %reduce-scatter.35.cloned.1.call-start = ((), (), s32[]{:S(2)}) async-start(), calls=%async_computation.27 | async-start | bytes 6553600 | tf_op jit(solution)/shard_map/while/body/eval_jaxpr/reduce_scatter | solution.py:239
  1768.8 123.9 %reduce-scatter.33.cloned.1.call-start = ((), (), s32[]{:S(2)}) async-start(), calls=%async_computation.25 | async-start | bytes 6553600 | tf_op jit(solution)/shard_map/while/body/eval_jaxpr/reduce_scatter | solution.py:238
  1920.7 77.4 %reduce-scatter.25.cloned.1.call-start = ((), (), s32[]{:S(2)}) async-start(), calls=%async_computation.14 | async-start | bytes 557056
  1922.5 133.9 %reduce-scatter.27.cloned.1.call-start = ((), (), s32[]{:S(2)}) async-start(), calls=%async_computation.15 | async-start | bytes 557056
  1924.3 161.3 %reduce-scatter.19.cloned.1.call-start = ((), (), s32[]{:S(2)}) async-start(), calls=%async_computation.11 | async-start | bytes 1310720 | tf_op jit(solution)/shard_map/reduce_scatter | solution.py:370
  1925.0 222.3 %reduce-scatter.17.cloned.1.call-start = ((), (), s32[]{:S(2)}) async-start(), calls=%async_computation.10 | async-start | bytes 3932160 | tf_op jit(solution)/shard_map/reduce_scatter | solution.py:368
  1925.8 301.1 %reduce-scatter.23.cloned.1.call-start = ((), (), s32[]{:S(2)}) async-start(), calls=%async_computation.13 | async-start | bytes 5242880 | tf_op jit(solution)/shard_map/reduce_scatter | solution.py:373
  1926.5 380.5 %reduce-scatter.21.cloned.1.call-start = ((), (), s32[]{:S(2)}) async-start(), calls=%async_computation.12 | async-start | bytes 5242880 | tf_op jit(solution)/shard_map/reduce_scatter | solution.py:371
  (301 other events, 5951.0 us)
Sparse Core Ops, SparseCore 0:
  92.7 40.7 all-gather.42
  135.0 23.7 all-gather.40
  160.4 46.2 all-gather.34
  208.1 44.1 all-gather.38
  253.7 24.2 all-gather.36
  279.4 25.5 all-gather.46
  307.1 25.5 all-gather.44
  334.3 25.5 all-gather.48
  362.4 51.3 reduce-scatter.30
  416.4 51.4 reduce-scatter.34
  470.4 51.3 reduce-scatter.32
  549.0 39.5 all-gather.42
  590.1 25.5 all-gather.40
  617.1 46.2 all-gather.34
  664.8 44.1 all-gather.38
  710.4 24.2 all-gather.36
  736.1 25.5 all-gather.46
  763.7 25.5 all-gather.44
  790.9 25.5 all-gather.48
  818.8 51.3 reduce-scatter.30
  873.0 51.4 reduce-scatter.34
  927.0 51.3 reduce-scatter.32
  1005.9 39.9 all-gather.42
  1047.3 25.2 all-gather.40
  1074.1 46.2 all-gather.34
  1121.8 44.1 all-gather.38
  1167.4 24.2 all-gather.36
  1193.2 25.5 all-gather.46
  1221.0 25.5 all-gather.44
  1248.0 25.5 all-gather.48
  1276.1 51.3 reduce-scatter.30
  1330.3 51.4 reduce-scatter.34
  1384.1 51.3 reduce-scatter.32
  1463.0 39.8 all-gather.42
  1504.5 25.1 all-gather.40
  1531.1 46.2 all-gather.34
  1578.8 44.1 all-gather.38
  1624.6 24.2 all-gather.36
  1650.3 25.5 all-gather.46
  1678.0 25.5 all-gather.44
  1705.2 25.5 all-gather.48
  1733.3 51.3 reduce-scatter.30
  1787.3 51.4 reduce-scatter.34
  1841.3 51.3 reduce-scatter.32
Sparse Core Ops, SparseCore 1:
  1921.8 18.2 reduce-scatter.28
  1943.9 54.1 reduce-scatter.24
  2001.5 54.9 reduce-scatter.26
  2059.4 26.1 reduce-scatter.18
  2088.4 58.8 reduce-scatter.16
  2150.2 76.7 reduce-scatter.22
  2229.8 77.2 reduce-scatter.20
where the time goes:
time: 2320 us; the launch traced here: 2310 us
  waiting for transfers between devices  1020 us (44%)
  matrix products  724 us (31%)
  blocking collectives  252 us (11%)
  other arithmetic  161 us (7%)
  local copies, waits for them, and re-layouts  105 us (5%)
    all_gather x4, waiting for transfers between devices, tick(): lax.all_gather(up_weight[0], 'dp', axis=0, tiled=True)  183 us
    unnamed x10, waiting for transfers between devices  116 us
    dot_general x16, matrix products, attend(): jnp.einsum('hqk,khd->qhd', probs, values, preferred_element_type=jnp.floa...  113 us
    reduce_scatter x4, waiting for transfers between devices, backward_tick(): lax.psum_scatter(grad_first, 'tensor', scatter_dimension=0, tiled=True)  106 us
    all_gather x4, waiting for transfers between devices, forward_tick(): lax.all_gather(second, 'tensor', axis=0, tiled=True)  103 us
    all_gather x4, waiting for transfers between devices, backward_tick(): cot_full = lax.all_gather(cot_rows, 'tensor', axis=0, tiled=True)  81.9 us
    dot_general x4, matrix products, forward_tick(): jnp.dot(hidden, down_w, preferred_element_type=jnp.float32)  81.1 us
    reduce_scatter x1, waiting for transfers between devices, body(): lax.psum_scatter(grad_accum[3], 'dp', scatter_dimension=0, tiled=True)  80.1 us
  transfers between devices with their start and end apart: 59, of which 38 were waited for; matrix products, arithmetic and copies ran while one was open for 41% of the time, Pallas kernels for 0%

commit v1 on v0

v1 whole, which is shorter than its diff:
```python
import functools

import jax
import jax.numpy as jnp
from jax import lax
from jax.experimental import pallas as pl
from jax.experimental.pallas import tpu as pltpu
from jax.sharding import PartitionSpec as P

D = 1024
H = 16
HD = 64
ROT = 16
MB = 2
TOK_MB = 1280
EPS = 1e-05
CHUNK = 256
CHUNKS = TOK_MB // CHUNK
BF = jnp.bfloat16
F32 = jnp.float32
ANY = pl.BlockSpec(memory_space=pl.ANY)
VMEM = pl.BlockSpec(memory_space=pltpu.VMEM)
SMEM = pl.BlockSpec(memory_space=pltpu.SMEM)
LIMIT = 58 * 1024 * 1024


def dot(left, right, left_dim, right_dim):
    return lax.dot_general(
        left, right, (((left_dim,), (right_dim,)), ((), ())), preferred_element_type=F32
    )


def shape(dims, dtype):
    return jax.ShapeDtypeStruct(dims, dtype)


def swap(value, axis, bit):
    count = lax.axis_size(axis)
    return lax.ppermute(value, axis, [(i, i ^ (1 << bit)) for i in range(count)])


def bits_of(axis):
    return lax.axis_size(axis).bit_length() - 1


def pick(value, index, axis):
    return lax.dynamic_index_in_dim(value, index, axis, keepdims=False)


def gather_blocks(value):
    blocks = {0: value}
    for bit in reversed(range(bits_of("tensor"))):
        for s in list(blocks):
            blocks[s | (1 << bit)] = swap(blocks[s], "tensor", bit)
    return [blocks[s] for s in range(len(blocks))]


def gather_tensor(value):
    index = lax.axis_index("tensor")
    value = value[None]
    for bit in reversed(range(bits_of("tensor"))):
        other = swap(value, "tensor", bit)
        mine = ((index >> bit) & 1) == 0
        low = jnp.where(mine, value, other)
        high = jnp.where(mine, other, value)
        value = jnp.stack([low, high], axis=1).reshape((-1,) + value.shape[1:])
    return value


def scatter_tensor(keep, send):
    index = lax.axis_index("tensor")
    value = keep.astype(F32) + swap(send, "tensor", 0).astype(F32)
    for bit in range(1, bits_of("tensor")):
        own = (index >> bit) & 1
        pairs = value.reshape((value.shape[0] // 2, 2) + value.shape[1:])
        other = swap(pick(pairs, 1 - own, 1).astype(BF), "tensor", bit)
        value = pick(pairs, own, 1) + other.astype(F32)
    return value[0]


def sum_pipe(value):
    low = value.astype(BF)
    return low, swap(low, "pipe", 0)


def scatter_line(value, axis, low):
    count = lax.axis_size(axis)
    index = lax.axis_index(axis)
    from_left = from_right = None
    for step in range(1, count):
        reach = count - step
        right_term = pick(value, jnp.minimum(index + reach, count - 1), 0).astype(F32)
        left_term = pick(value, jnp.maximum(index - reach, 0), 0).astype(F32)
        if from_left is not None:
            right_term = right_term + from_left.astype(F32)
            left_term = left_term + from_right.astype(F32)
        from_left = lax.ppermute(
            right_term.astype(low), axis, [(j, j + 1) for j in range(step)]
        )
        from_right = lax.ppermute(
            left_term.astype(low), axis, [(j + 1, j) for j in range(count - 1 - step, count - 1)]
        )
    own = pick(value, index, 0).astype(F32)
    if from_left is None:
        return own
    return own + from_left.astype(F32) + from_right.astype(F32)


def copies_of_blocks(index, blocks, target, sems):
    copies = []
    for s, block in enumerate(blocks):
        rows = block.shape[0]
        where = pl.multiple_of((index ^ s) * rows, rows)
        copies.append(pltpu.make_async_copy(block, target.at[pl.ds(where, rows)], sems.at[s]))
    return copies


def copies_to_halves(index, source, keep, send, sems, rows):
    copies = []
    own = index & 1
    for block in range(source.shape[0] // rows):
        part = source.at[pl.ds(block * rows, rows)]
        copies.append(
            (
                own == block & 1,
                pltpu.make_async_copy(part, keep.at[block >> 1], sems.at[block]),
                pltpu.make_async_copy(part, send.at[block >> 1], sems.at[block]),
            )
        )
    return copies


def start_half(copy):
    is_kept, to_keep, to_send = copy

    @pl.when(is_kept)
    def _():
        to_keep.start()

    @pl.when(jnp.logical_not(is_kept))
    def _():
        to_send.start()


def normalize(rows):
    rows = rows.astype(F32)
    centered = rows - jnp.mean(rows, axis=-1, keepdims=True)
    scale = lax.rsqrt(jnp.mean(centered * centered, axis=-1, keepdims=True) + EPS)
    return centered * scale, scale


def gelu_pair(values):
    share = 0.5 * (1.0 + lax.erf(values * 0.7071067811865476))
    density = jnp.exp(-0.5 * values * values) * 0.3989422804014327
    return values * share, share + values * density


def rotate(values, table_cos, table_sin, sign):
    width = values.shape[1]
    half = ROT // 2
    lanes = lax.broadcasted_iota(jnp.int32, values.shape, 1) % HD
    partner = jnp.where(
        lanes < half, pltpu.roll(values, width - half, 1), pltpu.roll(values, half, 1)
    )
    return values * table_cos + partner * (table_sin * sign)


def project_kernel(blocks, w, *refs):
    index_ref = refs[0]
    x_refs = refs[1 : 1 + blocks]
    (qkv_ref, up_ref, norms_ref, qkv_bias_ref, up_bias_ref, cos_ref, sin_ref) = refs[
        1 + blocks : 8 + blocks
    ]
    (first_ref, second_ref, q_ref, k_ref, v_ref, hidden_ref, slope_ref) = refs[
        8 + blocks : 15 + blocks
    ]
    x_all, sems = refs[15 + blocks :]
    step = pl.program_id(0)

    @pl.when(step == 0)
    def _():
        copies = copies_of_blocks(index_ref[0], x_refs, x_all, sems)
        for copy in copies:
            copy.start()
        for copy in copies:
            copy.wait()

    rows = x_all[pl.ds(pl.multiple_of(step * CHUNK, CHUNK), CHUNK)]
    hat, _ = normalize(rows)
    first = (hat * norms_ref[0:1] + norms_ref[2:3]).astype(BF)
    second = (hat * norms_ref[1:2] + norms_ref[3:4]).astype(BF)
    first_ref[...] = first
    second_ref[...] = second
    raw = dot(first, qkv_ref[...], 1, 0) + qkv_bias_ref[...]
    table_cos, table_sin = cos_ref[...], sin_ref[...]
    q_ref[...] = rotate(raw[:, :w], table_cos, table_sin, 1.0).astype(BF)
    k_ref[...] = rotate(raw[:, w : 2 * w], table_cos, table_sin, 1.0).astype(BF)
    v_ref[...] = raw[:, 2 * w :].astype(BF)
    hidden, slope = gelu_pair(dot(second, up_ref[...], 1, 0) + up_bias_ref[...])
    hidden_ref[...] = hidden.astype(BF)
    slope_ref[...] = slope.astype(BF)


def project(index, x_blocks, weights, angles):
    _, table_cos, table_sin = angles
    blocks = len(x_blocks)
    w = weights["w"]
    hidden = weights["up"].shape[1]

    def rows(width):
        return pl.BlockSpec((CHUNK, width), lambda i: (i, 0))

    def whole(value):
        return pl.BlockSpec(value.shape, lambda i: (0,) * value.ndim)

    fixed = [weights[name] for name in ("qkv", "up", "norms", "qkv_bias", "up_bias")]
    widths = [D, D, w, w, w, hidden, hidden]
    flops = 2 * TOK_MB * D * (3 * w + hidden)
    return pl.pallas_call(
        functools.partial(project_kernel, blocks, w),
        grid=(CHUNKS,),
        in_specs=[SMEM] + [ANY] * blocks + [whole(v) for v in fixed] + [rows(w)] * 2,
        out_specs=[rows(width) for width in widths],
        out_shape=[shape((TOK_MB, width), BF) for width in widths],
        scratch_shapes=[
            pltpu.VMEM((TOK_MB, D), BF),
            pltpu.SemaphoreType.DMA((blocks,)),
        ],
        compiler_params=pltpu.CompilerParams(vmem_limit_bytes=LIMIT),
        cost_estimate=pl.CostEstimate(flops=3 * flops, bytes_accessed=14 << 20, transcendentals=0),
        name="project",
    )(index, *x_blocks, *fixed, table_cos, table_sin)


def allowed_in(starts, q_block, k_block):
    key = lax.broadcasted_iota(jnp.int32, (CHUNK, CHUNK), 0) + k_block * CHUNK
    query = lax.broadcasted_iota(jnp.int32, (CHUNK, CHUNK), 1) + q_block * CHUNK
    return (key <= query) & (key >= starts)


def head_only(values, head):
    lanes = lax.broadcasted_iota(jnp.int32, values.shape, 1)
    inside = (lanes >= head * HD) & (lanes < (head + 1) * HD)
    return jnp.where(inside, values, jnp.zeros_like(values))


def chunk_of(block):
    return pl.ds(pl.multiple_of(block * CHUNK, CHUNK), CHUNK)


def attend_kernel(heads, w, *refs):
    (index_ref, first_key_ref, starts_ref, q_ref, k_ref, v_ref, hidden_ref, low_ref) = refs[:8]
    (keep_ref, send_ref, context_ref, logs_ref) = refs[8:12]
    (low_all, partial, v_turned, scores, low_sems, out_sems) = refs[12:]
    dp, share = low_ref.shape[0], low_ref.shape[2]
    rows = keep_ref.shape[1]
    loads = [
        pltpu.make_async_copy(low_ref.at[j], low_all.at[:, pl.ds(j * share, share)], low_sems.at[j])
        for j in range(dp)
    ]
    for load in loads:
        load.start()
    outs = copies_to_halves(index_ref[0], partial, keep_ref, send_ref, out_sems, rows)
    v_turned[...] = v_ref[...].T
    logs_ref[...] = jnp.zeros_like(logs_ref)
    for load in loads:
        load.wait()

    @pl.loop(0, CHUNKS)
    def _(block):
        at = chunk_of(block)
        starts = starts_ref[:, at]
        queries = q_ref[at] * BF(HD**-0.5)
        turned = []
        for head in range(heads):
            mine = head_only(queries, head)

            def score(key_block, top, mine=mine):
                s = dot(k_ref[chunk_of(key_block)], mine, 1, 1)
                s = jnp.where(allowed_in(starts, block, key_block), s, -1e30)
                scores[chunk_of(key_block)] = s
                return jnp.maximum(top, jnp.max(s, axis=0, keepdims=True))

            top = lax.fori_loop(
                first_key_ref[block], block + 1, score, jnp.full((1, CHUNK), -1e30, F32)
            )

            def weigh(key_block, carry, head=head, top=top):
                total, sums = carry
                e = jnp.exp(scores[chunk_of(key_block)] - top)
                total = total + jnp.sum(e, axis=0, keepdims=True)
                part = v_turned[head * HD : (head + 1) * HD, chunk_of(key_block)]
                return total, sums + dot(part, e.astype(BF), 1, 0)

            total, sums = lax.fori_loop(
                first_key_ref[block],
                block + 1,
                weigh,
                (jnp.zeros((1, CHUNK), F32), jnp.zeros((HD, CHUNK), F32)),
            )
            turned.append(sums / total)
            logs_ref[head : head + 1, at] = top + jnp.log(total)
        if heads * HD < w:
            turned.append(jnp.zeros((w - heads * HD, CHUNK), F32))
        context = jnp.concatenate(turned, axis=0).T.astype(BF)
        context_ref[at] = context
        total = dot(context, low_all[:w], 1, 0) + dot(hidden_ref[at], low_all[w:], 1, 0)
        partial[at] = total.astype(BF)

    for out in outs:
        start_half(out)
    for out in outs:
        out[1].wait()


def attend(index, kept, weights, angles):
    queries, keys, values, hidden = kept[2:6]
    starts, _, _ = angles
    first_key = starts[::CHUNK] // CHUNK
    w, heads, low = weights["w"], weights["heads"], weights["low"]
    dp = low.shape[0]
    tensor = lax.axis_size("tensor")
    rows = TOK_MB // tensor
    wide = w + hidden.shape[1]
    flops = 2 * TOK_MB * D * wide
    return pl.pallas_call(
        functools.partial(attend_kernel, heads, w),
        in_specs=[SMEM, SMEM, VMEM, VMEM, VMEM, VMEM, VMEM, ANY],
        out_specs=[ANY, ANY, VMEM, VMEM],
        out_shape=[
            shape((tensor // 2, rows, D), BF),
            shape((tensor // 2, rows, D), BF),
            shape((TOK_MB, w), BF),
            shape((8, TOK_MB), F32),
        ],
        scratch_shapes=[
            pltpu.VMEM((wide, D), BF),
            pltpu.VMEM((TOK_MB, D), BF),
            pltpu.VMEM((w, TOK_MB), BF),
            pltpu.VMEM((TOK_MB, CHUNK), F32),
            pltpu.SemaphoreType.DMA((dp,)),
            pltpu.SemaphoreType.DMA((tensor,)),
        ],
        compiler_params=pltpu.CompilerParams(vmem_limit_bytes=LIMIT),
        cost_estimate=pl.CostEstimate(flops=4 * flops, bytes_accessed=8 << 20, transcendentals=0),
        name="attend",
    )(index, first_key, starts[None], queries, keys, values, hidden, low)


def backward_kernel(blocks, heads, w, *refs):
    index_ref, first_key_ref = refs[:2]
    c_refs = refs[2 : 2 + blocks]
    x_refs = refs[2 + blocks : 2 + 2 * blocks]
    (starts_ref, q_ref, k_ref, v_ref, context_ref, logs_ref, slope_ref) = refs[
        2 + 2 * blocks : 9 + 2 * blocks
    ]
    (qkv_ref, up_ref, low_ref, norms_ref, cos_ref, sin_ref) = refs[
        9 + 2 * blocks : 15 + 2 * blocks
    ]
    (keep_ref, send_ref, raw_ref, pre_ref, vectors_ref, raw_sum_ref, pre_sum_ref) = refs[
        15 + 2 * blocks : 22 + 2 * blocks
    ]
    (
        c_all,
        x_all,
        low_all,
        partial,
        grad_context,
        k_turned,
        weighted,
        grad_q,
        grad_k,
        grad_v,
        c_sems,
        x_sems,
        low_sems,
        out_sems,
    ) = refs[22 + 2 * blocks :]
    index = index_ref[0]
    dp, share = low_ref.shape[0], low_ref.shape[2]
    rows = keep_ref.shape[1]
    loads = [
        pltpu.make_async_copy(low_ref.at[j], low_all.at[:, pl.ds(j * share, share)], low_sems.at[j])
        for j in range(dp)
    ]
    loads += copies_of_blocks(index, c_refs, c_all, c_sems)
    x_loads = copies_of_blocks(index, x_refs, x_all, x_sems)
    for load in loads + x_loads:
        load.start()
    outs = copies_to_halves(index, partial, keep_ref, send_ref, out_sems, rows)
    k_turned[...] = (k_ref[...] * BF(HD**-0.5)).T
    grad_k[...] = jnp.zeros_like(grad_k)
    grad_v[...] = jnp.zeros_like(grad_v)
    weighted[...] = jnp.zeros_like(weighted)
    vectors_ref[...] = jnp.zeros_like(vectors_ref)
    raw_sum_ref[...] = jnp.zeros_like(raw_sum_ref)
    pre_sum_ref[...] = jnp.zeros_like(pre_sum_ref)
    for load in loads:
        load.wait()

    @pl.loop(0, CHUNKS)
    def _(block):
        at = chunk_of(block)
        both = dot(c_all[at], low_all[...], 1, 1)
        context_part = both[:, :w].astype(BF)
        grad_context[at] = context_part
        products = (context_part.astype(F32) * context_ref[at].astype(F32)).T
        for head in range(heads):
            weighted[head : head + 1, at] = jnp.sum(
                products[head * HD : (head + 1) * HD], axis=0, keepdims=True
            )
        grad_pre = (both[:, w:] * slope_ref[at].astype(F32)).astype(BF)
        pre_ref[at] = grad_pre
        pre_sum_ref[...] += jnp.sum(grad_pre.astype(F32), axis=0, keepdims=True)

    @pl.loop(0, CHUNKS)
    def _(block):
        at = chunk_of(block)
        starts = starts_ref[:, at]
        queries = q_ref[at] * BF(HD**-0.5)
        grads = grad_context[at]
        queries_of = [head_only(queries, head) for head in range(heads)]
        grads_of = [head_only(grads, head) for head in range(heads)]

        def pair(key_block, sums):
            keys_at = chunk_of(key_block)
            allowed = allowed_in(starts, block, key_block)
            new_sums = []
            to_k = jnp.zeros((CHUNK, w), F32)
            to_v = jnp.zeros((CHUNK, w), F32)
            for head in range(heads):
                s = dot(k_ref[keys_at], queries_of[head], 1, 1)
                p = jnp.exp(jnp.where(allowed, s, -1e30) - logs_ref[head : head + 1, at])
                grad_p = dot(v_ref[keys_at], grads_of[head], 1, 1)
                grad_s = (p * (grad_p - weighted[head : head + 1, at])).astype(BF)
                to_k = to_k + dot(grad_s, queries_of[head], 1, 0)
                to_v = to_v + dot(p.astype(BF), grads_of[head], 1, 0)
                part = k_turned[head * HD : (head + 1) * HD, keys_at]
                new_sums.append(sums[head] + dot(part, grad_s, 1, 0))
            grad_k[keys_at] += to_k
            grad_v[keys_at] += to_v
            return tuple(new_sums)

        sums = lax.fori_loop(
            first_key_ref[block],
            block + 1,
            pair,
            tuple(jnp.zeros((HD, CHUNK), F32) for _ in range(heads)),
        )
        if heads * HD < w:
            sums = sums + (jnp.zeros((w - heads * HD, CHUNK), F32),)
        grad_q[at] = jnp.concatenate(sums, axis=0).T

    for load in x_loads:
        load.wait()

    @pl.loop(0, CHUNKS)
    def _(block):
        at = chunk_of(block)
        table_cos, table_sin = cos_ref[at], sin_ref[at]
        grad_raw = jnp.concatenate(
            [
                rotate(grad_q[at], table_cos, table_sin, -1.0),
                rotate(grad_k[at], table_cos, table_sin, -1.0),
                grad_v[at],
            ],
            axis=1,
        ).astype(BF)
        raw_ref[at] = grad_raw
        raw_sum_ref[...] += jnp.sum(grad_raw.astype(F32), axis=0, keepdims=True)
        grad_first = dot(grad_raw, qkv_ref[...], 1, 1)
        grad_second = dot(pre_ref[at], up_ref[...], 1, 1)
        hat, _ = normalize(x_all[at])
        vectors_ref[0:1] += jnp.sum(grad_first * hat, axis=0, keepdims=True)
        vectors_ref[1:2] += jnp.sum(grad_second * hat, axis=0, keepdims=True)
        vectors_ref[2:3] += jnp.sum(grad_first, axis=0, keepdims=True)
        vectors_ref[3:4] += jnp.sum(grad_second, axis=0, keepdims=True)
        partial[at] = (grad_first * norms_ref[0:1] + grad_second * norms_ref[1:2]).astype(BF)

    for out in outs:
        start_half(out)
    for out in outs:
        out[1].wait()


def backward(index, c_blocks, x_blocks, kept, weights, angles):
    _, _, queries, keys, values, hidden, slope, context, logs = kept
    starts, table_cos, table_sin = angles
    first_key = starts[::CHUNK] // CHUNK
    blocks = len(c_blocks)
    w, heads, low = weights["w"], weights["heads"], weights["low"]
    dp = low.shape[0]
    rows = TOK_MB // blocks
    ff = hidden.shape[1]
    flops = 2 * TOK_MB * D * (4 * w + 2 * ff)
    return pl.pallas_call(
        functools.partial(backward_kernel, blocks, heads, w),
        in_specs=[SMEM] * 2 + [ANY] * (2 * blocks) + [VMEM] * 9 + [ANY] + [VMEM] * 3,
        out_specs=[ANY, ANY] + [VMEM] * 5,
        out_shape=[
            shape((blocks // 2, rows, D), BF),
            shape((blocks // 2, rows, D), BF),
            shape((TOK_MB, 3 * w), BF),
            shape((TOK_MB, ff), BF),
            shape((8, D), F32),
            shape((1, 3 * w), F32),
            shape((1, ff), F32),
        ],
        scratch_shapes=[
            pltpu.VMEM((TOK_MB, D), BF),
            pltpu.VMEM((TOK_MB, D), BF),
            pltpu.VMEM((w + ff, D), BF),
            pltpu.VMEM((TOK_MB, D), BF),
            pltpu.VMEM((TOK_MB, w), BF),
            pltpu.VMEM((w, TOK_MB), BF),
            pltpu.VMEM((8, TOK_MB), F32),
            pltpu.VMEM((TOK_MB, w), F32),
            pltpu.VMEM((TOK_MB, w), F32),
            pltpu.VMEM((TOK_MB, w), F32),
            pltpu.SemaphoreType.DMA((blocks,)),
            pltpu.SemaphoreType.DMA((blocks,)),
            pltpu.SemaphoreType.DMA((dp,)),
            pltpu.SemaphoreType.DMA((blocks,)),
        ],
        compiler_params=pltpu.CompilerParams(vmem_limit_bytes=LIMIT),
        cost_estimate=pl.CostEstimate(flops=3 * flops, bytes_accessed=16 << 20, transcendentals=0),
        name="backward",
    )(
        index,
        first_key,
        *c_blocks,
        *x_blocks,
        starts[None],
        queries,
        keys,
        values,
        context,
        logs,
        slope,
        weights["qkv"],
        weights["up"],
        low,
        weights["norms"],
        table_cos,
        table_sin,
    )


def weights_kernel(blocks, *refs):
    index_ref = refs[0]
    c_refs = [refs[1 + unit * blocks : 1 + (unit + 1) * blocks] for unit in range(MB)]
    inner = refs[1 + MB * blocks : 1 + MB * (blocks + 6)]
    main_ref, low_ref = refs[1 + MB * (blocks + 6) : 3 + MB * (blocks + 6)]
    c_all, sems = refs[3 + MB * (blocks + 6) :]
    copies = []
    for unit in range(MB):
        copies += copies_of_blocks(index_ref[0], c_refs[unit], c_all.at[unit], sems.at[unit])
    for copy in copies:
        copy.start()
    dp, share = main_ref.shape[0], main_ref.shape[2]
    w3, ff = inner[0].shape[1], inner[1].shape[1]
    w = inner[2].shape[1]

    def fill(target, begin, size, left, right):
        for j in range(dp):
            cols = slice(j * share, (j + 1) * share)
            total = sum(
                dot(left(unit)[...], right(unit)[:, cols], 0, 0) for unit in range(MB)
            )
            target[j, begin : begin + size] = total.astype(BF)

    fill(main_ref, 0, w3, lambda u: inner[6 * u], lambda u: inner[6 * u + 4])
    fill(main_ref, w3, ff, lambda u: inner[6 * u + 1], lambda u: inner[6 * u + 5])
    for copy in copies:
        copy.wait()
    fill(low_ref, 0, w, lambda u: inner[6 * u + 2], lambda u: c_all.at[u])
    fill(low_ref, w, ff, lambda u: inner[6 * u + 3], lambda u: c_all.at[u])


def weight_grads(index, c_blocks, inner, dp):
    blocks = len(c_blocks[0])
    w3, ff, w = (inner[0][i].shape[1] for i in range(3))
    flops = 2 * MB * TOK_MB * D * (w3 + 2 * ff + w)
    return pl.pallas_call(
        functools.partial(weights_kernel, blocks),
        in_specs=[SMEM] + [ANY] * (MB * blocks) + [VMEM] * (MB * 6),
        out_specs=[VMEM, VMEM],
        out_shape=[
            shape((dp, w3 + ff, D // dp), BF),
            shape((dp, w + ff, D // dp), BF),
        ],
        scratch_shapes=[
            pltpu.VMEM((MB, TOK_MB, D), BF),
            pltpu.SemaphoreType.DMA((MB, blocks)),
        ],
        compiler_params=pltpu.CompilerParams(vmem_limit_bytes=LIMIT),
        cost_estimate=pl.CostEstimate(flops=2 * flops, bytes_accessed=24 << 20, transcendentals=0),
        name="weight_grads",
    )(index, *[b for unit in c_blocks for b in unit], *[v for unit in inner for v in unit])


def norm_back_kernel(x_ref, own_ref, other_ref, cot_ref, out_ref):
    grad_hat = own_ref[...].astype(F32) + other_ref[...].astype(F32)
    hat, scale = normalize(x_ref[...])
    mean = jnp.mean(grad_hat, axis=-1, keepdims=True)
    along = jnp.mean(grad_hat * hat, axis=-1, keepdims=True)
    grad = cot_ref[...].astype(F32) + (grad_hat - mean - hat * along) * scale
    out_ref[...] = grad.astype(out_ref.dtype)


def norm_back(x_rows, own, other, cot_rows, dtype):
    return pl.pallas_call(
        norm_back_kernel,
        in_specs=[VMEM] * 4,
        out_specs=VMEM,
        out_shape=shape(x_rows.shape, dtype),
        compiler_params=pltpu.CompilerParams(vmem_limit_bytes=LIMIT),
        cost_estimate=pl.CostEstimate(
            flops=20 * x_rows.size, bytes_accessed=4 << 20, transcendentals=0
        ),
        name="norm_back",
    )(x_rows, own, other, cot_rows)


def angles_for(lengths_row, w):
    finish = jnp.cumsum(lengths_row)
    places = jnp.arange(TOK_MB, dtype=jnp.int32)
    after = (places[:, None] >= finish[None, :]).astype(jnp.int32)
    starts = jnp.sum(after * lengths_row[None, :], axis=1)
    position = (places - starts).astype(F32)
    inverse_freq = 10000.0 ** (-jnp.arange(ROT // 2, dtype=F32) * 2.0 / ROT)
    phase = position[:, None] * inverse_freq[None, :]
    cosine, sine = jnp.cos(phase), jnp.sin(phase)
    rest = HD - ROT
    table_cos = jnp.concatenate([cosine, cosine, jnp.ones((TOK_MB, rest), F32)], axis=1)
    table_sin = jnp.concatenate([-sine, sine, jnp.zeros((TOK_MB, rest), F32)], axis=1)
    return starts, jnp.tile(table_cos, (1, w // HD)), jnp.tile(table_sin, (1, w // HD))


def body(
    boundary,
    lengths,
    gains,
    biases,
    qkv_weight,
    qkv_bias,
    out_weight,
    up_weight,
    up_bias,
    down_weight,
):
    stage = lax.axis_index("pipe")
    at_first = stage == 0
    dp = lax.axis_size("dp")
    tensor = lax.axis_size("tensor")
    index = lax.axis_index("tensor").astype(jnp.int32)[None]
    share = D // dp
    width = qkv_weight.shape[3] // 2
    ff = up_weight.shape[2] // 2
    heads = width // HD
    w = max(width, 128)

    def split(mine, other):
        return jnp.where(at_first, mine, other), jnp.where(at_first, other, mine)

    def half(value, which, axis):
        size = value.shape[axis] // 2
        return lax.dynamic_slice_in_dim(value, which * size, size, axis)

    def padded(value, axis):
        if w == width:
            return value
        pads = [(0, 0)] * value.ndim
        pads[axis] = (0, w - width)
        return jnp.pad(value, pads)

    def packs(which):
        qkv = padded(half(qkv_weight[0], which, 2), 2).reshape(share, 3 * w)
        main = jnp.concatenate([qkv, half(up_weight[0], which, 1)], axis=1)
        low = jnp.concatenate(
            [padded(half(out_weight[0], which, 0), 0), half(down_weight[0], which, 0)], axis=0
        )
        return main, low

    main_mine, low_mine = packs(stage)
    main_sent, low_sent = packs(1 - stage)
    mains = split(main_mine, swap(main_sent, "pipe", 0))
    lows = split(low_mine, swap(low_sent, "pipe", 0))

    piece = gains.shape[2]
    small = jnp.concatenate([gains[0].reshape(-1), biases[0].reshape(-1)])
    small = gather_tensor(small).reshape(-1)
    small = jnp.concatenate([small, qkv_bias[0].reshape(-1), up_bias[0]])
    small = jnp.stack(split(small, swap(small, "pipe", 0)))
    small = lax.all_gather(small, "dp", axis=0)
    small = jnp.moveaxis(small, 0, 1).astype(F32)
    norms = small[:, :, : tensor * 6 * piece].reshape(2, dp, tensor, 6, piece)
    norms = norms.transpose(0, 3, 2, 1, 4).reshape(2, 6, D)
    rest = small[:, :, tensor * 6 * piece :]
    qkv_biases = rest[:, :, : 3 * piece].reshape(2, dp, 3, piece)
    qkv_biases = qkv_biases.transpose(0, 2, 1, 3).reshape(2, 3, 2 * width)
    qkv_biases = padded(half(qkv_biases, stage, 2), 2).reshape(2, 1, 3 * w)
    up_biases = half(rest[:, :, 3 * piece :].reshape(2, 1, 2 * ff), stage, 2)

    layers = []
    for layer in range(2):
        main = lax.all_gather(mains[layer], "dp", axis=0, tiled=True)
        low = lax.all_gather(lows[layer], "dp", axis=0)
        layers.append(
            dict(
                w=w,
                heads=heads,
                qkv=main[:, : 3 * w],
                up=main[:, 3 * w :],
                low=low,
                norms=norms[layer],
                qkv_bias=qkv_biases[layer],
                up_bias=up_biases[layer],
            )
        )

    tiles = boundary[0, :, 0]
    angles = [angles_for(lengths[unit, 0], w) for unit in range(MB)]
    x_rows, cot_rows = [], []
    for unit in range(MB):
        x_own, cot_own = split(tiles[unit], swap(tiles[unit], "pipe", 0))
        x_rows.append(x_own)
        cot_rows.append(cot_own)
    x_blocks = [gather_blocks(rows) for rows in x_rows]
    c_blocks = [gather_blocks(rows) for rows in cot_rows]

    def forward(blocks, layer, unit):
        kept = project(index, blocks, layers[layer], angles[unit])
        keep, send, context, logs = attend(index, kept, layers[layer], angles[unit])
        return scatter_tensor(keep, send), [*kept, context, logs]

    def finish(rows, value, layer):
        own, other = sum_pipe(value)
        bias = layers[layer]["norms"]
        return rows.astype(F32) + own.astype(F32) + other.astype(F32) + (bias[4] + bias[5])

    kept = [[None] * MB, [None] * MB]
    middle_rows, middle_blocks, outputs = [], [None] * MB, []
    for unit in range(MB):
        value, kept[0][unit] = forward(x_blocks[unit], 0, unit)
        middle_rows.append(finish(x_rows[unit], value, 0).astype(BF))
    back = [[None] * MB, [None] * MB]
    cot0_rows, ends = [], []
    for unit in range(MB):
        middle_blocks[unit] = gather_blocks(middle_rows[unit])
        value, kept[1][unit] = forward(middle_blocks[unit], 1, unit)
        outputs.append(finish(middle_rows[unit], value, 1))
        keep, send, *back[1][unit] = backward(
            index, c_blocks[unit], middle_blocks[unit], kept[1][unit], layers[1], angles[unit]
        )
        own, other = sum_pipe(scatter_tensor(keep, send))
        cot0_rows.append(norm_back(middle_rows[unit], own, other, cot_rows[unit], BF))

    def grads_of(layer, blocks):
        inner = []
        for unit in range(MB):
            grad_raw, grad_pre = back[layer][unit][:2]
            first, second = kept[layer][unit][:2]
            hidden, context = kept[layer][unit][5], kept[layer][unit][7]
            inner.append([grad_raw, grad_pre, context, hidden, first, second])
        main, low = weight_grads(index, blocks, inner, dp)
        main = lax.psum_scatter(main, "dp", scatter_dimension=0)
        low = lax.psum_scatter(low, "dp", scatter_dimension=0)
        return main, low

    reduced = [None, grads_of(1, c_blocks)]
    cot0_blocks = []
    for unit in range(MB):
        cot0_blocks.append(gather_blocks(cot0_rows[unit]))
        keep, send, *back[0][unit] = backward(
            index, cot0_blocks[unit], x_blocks[unit], kept[0][unit], layers[0], angles[unit]
        )
        own, other = sum_pipe(scatter_tensor(keep, send))
        ends.append(norm_back(x_rows[unit], own, other, cot0_rows[unit], F32))
    reduced[0] = grads_of(0, cot0_blocks)
    ends = jnp.stack([jnp.where(at_first, ends[unit], outputs[unit]) for unit in range(MB)])

    def join(parts, axis):
        keep = jnp.where(at_first, parts[0], parts[1])
        other = swap(jnp.where(at_first, parts[1], parts[0]), "pipe", 0)
        return jnp.concatenate(split(keep, other), axis=axis)

    main = join([reduced[layer][0][None] for layer in range(2)], 0)
    low = join([reduced[layer][1][None] for layer in range(2)], 0)
    grad_qkv = main[:, : 3 * w].reshape(2, 3, w, share)[:, :, :width]
    grad_qkv = grad_qkv.transpose(3, 1, 0, 2).reshape(share, 3, 2 * width).astype(F32)
    grad_up = main[:, 3 * w :].reshape(2 * ff, share).T.astype(F32)
    grad_out = low[:, :width].reshape(2 * width, share).astype(F32)
    grad_down = low[:, w:].reshape(2 * ff, share).astype(F32)

    own_rows = [
        jnp.sum(jnp.stack([row.astype(F32) for row in rows]), axis=(0, 1))
        for rows in (cot0_rows, cot_rows)
    ]
    once = jnp.where(at_first, 1.0, 0.0)
    tails, raw_sums, pre_sums = [], [], []
    for layer in range(2):
        sums = [sum(back[layer][unit][i] for unit in range(MB)) for i in range(2, 5)]
        tails.append(jnp.concatenate([sums[0][:4], own_rows[layer][None] * once]))
        raw_sums.append(sums[1].reshape(3, w)[:, :width])
        pre_sums.append(sums[2][0])
    mine = jnp.where(at_first, tails[0], tails[1])
    mine = mine + swap(jnp.where(at_first, tails[1], tails[0]), "pipe", 0)
    mine = mine.reshape(5, tensor, D // tensor).transpose(1, 0, 2)
    place = lax.axis_index("tensor")
    for bit in range(bits_of("tensor")):
        own = (place >> bit) & 1
        pairs = mine.reshape((mine.shape[0] // 2, 2) + mine.shape[1:])
        mine = pick(pairs, own, 1) + swap(pick(pairs, 1 - own, 1), "tensor", bit)
    mine = mine[0].reshape(5, dp, piece).transpose(1, 0, 2).reshape(dp, 5 * piece)
    flat_qkv = join(raw_sums, 1)
    flat_qkv = flat_qkv.reshape(3, dp, piece).transpose(1, 0, 2).reshape(dp, 3 * piece)
    flat_up = join(pre_sums, 0).reshape(dp, -1)
    vector = scatter_line(jnp.concatenate([mine, flat_qkv, flat_up], axis=1), "dp", F32)
    norm_grads = vector[: 5 * piece].reshape(5, piece)
    grad_gains = norm_grads[:2]
    grad_biases = jnp.concatenate([norm_grads[2:5], norm_grads[4:5]])
    grad_qkv_bias = vector[5 * piece : 8 * piece].reshape(3, piece)
    grad_up_bias = vector[8 * piece :]
    return (
        ends[None, :, None],
        grad_gains[None],
        grad_biases[None],
        grad_qkv[None],
        grad_qkv_bias[None],
        grad_out[None],
        grad_up[None],
        grad_up_bias[None],
        grad_down[None],
    )


def solution(mesh):
    placed = (
        P("pipe", None, "dp", "tensor", None),
        P(None, "dp", None),
        P("pipe", None, ("tensor", "dp")),
        P("pipe", None, ("tensor", "dp")),
        P("pipe", "dp", None, "tensor"),
        P("pipe", None, ("tensor", "dp")),
        P("pipe", "tensor", "dp"),
        P("pipe", "dp", "tensor"),
        P("pipe", ("tensor", "dp")),
        P("pipe", "tensor", "dp"),
    )
    return jax.shard_map(
        body,
        mesh=mesh,
        in_specs=placed,
        out_specs=(placed[0],) + placed[2:],
        check_vma=False,
    )
```

time: 2320 us -> 673 us (0.29)
  waiting for transfers between devices: 1020 us -> 223 us
  matrix products: 724 us -> 0 us
  Pallas kernels: 0 us -> 255 us
  blocking collectives: 252 us -> 13.6 us
  other arithmetic: 161 us -> 43.7 us
  local copies, waits for them, and re-layouts: 105 us -> 44.8 us
  starting transfers between devices: 22.9 us -> 72.7 us
    dot_general x100 -> x0, matrix products: 614 us -> none  [the longest x16 113 us: attend(): jnp.einsum('hqk,khd->qhd', probs, values, preferred_element_type=jnp.floa...]
    all_gather x32 -> x4, waiting for transfers between devices: 470 us -> 15.8 us  [the longest x2 15.8 us: body(): low = lax.all_gather(lows[layer], 'dp', axis=0)]
    reduce_scatter x16 -> x4, waiting for transfers between devices: 355 us -> 3.02 us  [the longest x2 3.02 us: grads_of(): main = lax.psum_scatter(main, 'dp', scatter_dimension=0)]
    pallas_call x0 -> x18, Pallas kernels: none -> 255 us  [the longest x4 100 us: backward(): pl.pallas_call(functools.partial(backward_kernel, blocks, heads, w), in_s...]
    all_gather x14 -> x1, blocking collectives: 240 us -> 13.6 us  [body(): small = lax.all_gather(small, 'dp', axis=0)]
    ppermute x8 -> x68, waiting for transfers between devices: 67.6 us -> 204 us  [the longest x62 204 us: swap(): return lax.ppermute(value, axis, [(i, i ^ 1 << bit) for i in range(count)])]
    unnamed x10 -> x8, waiting for transfers between devices: 116 us -> 0.15 us
    sub x16 -> x0, matrix products: 110 us -> none  [the longest x8 67.9 us: attend_back(): probs = jnp.exp(scores - tops[index]) / totals[index]]
  transfers between devices with their start and end apart: 59 -> 76, of which waited for: 38 -> 27; matrix products, arithmetic and copies ran while one was open for 41% -> 10% of each run, Pallas kernels for 0% -> 38%
where the time goes in v1:
time: 673 us; the launch traced here: 669 us
  Pallas kernels  255 us (38%)
  waiting for transfers between devices  223 us (33%)
  starting transfers between devices  72.7 us (11%)
  local copies, waits for them, and re-layouts  44.8 us (7%)
  other arithmetic  43.7 us (6%)
  between operations  15.9 us (2%)
  blocking collectives  13.6 us (2%)
    ppermute x62, waiting for transfers between devices, swap(): return lax.ppermute(value, axis, [(i, i ^ 1 << bit) for i in range(count)])  204 us
    pallas_call x4, Pallas kernels, backward(): pl.pallas_call(functools.partial(backward_kernel, blocks, heads, w), in_s...  100 us
    pallas_call x4, Pallas kernels, attend(): pl.pallas_call(functools.partial(attend_kernel, heads, w), in_specs=[SMEM...  66.9 us
    ppermute x62, starting transfers between devices, swap(): return lax.ppermute(value, axis, [(i, i ^ 1 << bit) for i in range(count)])  45.1 us
    pallas_call x4, Pallas kernels, project(): pl.pallas_call(functools.partial(project_kernel, blocks, w), grid=(CHUNKS...  41.4 us
    pallas_call x2, Pallas kernels, weight_grads(): pl.pallas_call(functools.partial(weights_kernel, blocks), in_specs=[SMEM]...  32.6 us
    ppermute x3, starting transfers between devices, scatter_line(): lax.ppermute(right_term.astype(low), axis, [(j, j + 1) for j in range(ste...  24.3 us
    all_gather x2, waiting for transfers between devices, body(): low = lax.all_gather(lows[layer], 'dp', axis=0)  15.8 us
  transfers between devices with their start and end apart: 76, of which 27 were waited for; matrix products, arithmetic and copies ran while one was open for 10% of the time, Pallas kernels for 38%

profile of v1, /device:TPU:0, one launch (start us, length us, event | category | flops | bytes accessed | tf_op | source)
XLA Modules:
  0.0 669.3 jit_solution(7178501911432251689)
XLA Ops:
  9.7 3.0 collective-permute-start
  19.9 32.4 %collective-permute-done.4 = bf16[256,896]{1,0:T(8,128)(2,1)S(1)} collective-permute-done((bf16[256,896]{1,0:T(8,128)(2,1)S(1)}, bf16[256,896]{1,0:T(8,128)(2,1)S(1)}, u32[]{:S(2)}, u32[]{:S(2)}) %collective-permute-start.4) | collective-permute-done | bytes 458784 | tf_op jit(solution)/shard_map/ppermute | solution.py:39
  69.1 13.6 %all-gather.3 = bf16[4,2,1984]{2,1,0:T(2,128)(2,1)S(1)} all-gather(bf16[1,2,1984]{2,1,0:T(2,128)(2,1)S(1)} %maximum_bitcast_fusion.1), channel_id=2, replica_groups=mesh['pipe'=2,'tensor'=4,'dp'=4] {'dp'}, dimensions={0}, use_global_device_ids=true | all-gather | bytes 39680 | tf_op jit(solution)/shard_map/all_gather | solution.py:695
  86.3 13.7 %collective-permute-done.32.refs_3_.refs_8_ = bf16[320,1024]{1,0:T(8,128)(2,1)} collective-permute-done((bf16[320,1024]{1,0:T(8,128)(2,1)S(1)}, bf16[320,1024]{1,0:T(8,128)(2,1)}, u32[]{:S(2)}, u32[]{:S(2)}) %collective-permute-start.32) | collective-permute-done | bytes 655392 | tf_op jit(solution)/shard_map/ppermute | solution.py:39
  104.3 10.4 %project.4 = (bf16[1280,1024]{1,0:T(8,128)(2,1)}, bf16[1280,1024]{1,0:T(8,128)(2,1)}, bf16[1280,128]{1,0:T(8,128)(2,1)}, bf16[1280,128]{1,0:T(8,128)(2,1)}, bf16...) custom-call(s32[1]{0:T(128)} %bitcast.1.refs_0_, bf16[320,1024]{1,0:T(8,128)(2,1)} %copy-done.11, ...), custom_call_target="tpu_custom_call" | custom-call | flops 7046430720 | bytes 14680064 | tf_op jit(solution)/shard_map/project/pallas_call | solution.py:219
  114.7 15.8 %all-gather.13.cloned.1.call-done = bf16[2560,256]{1,0:T(8,128)(2,1)} async-done(((bf16[640,256]{1,0:T(8,128)(2,1)}), bf16[2560,256]{1,0:T(8,128)(2,1)}) %all-gather.13.cloned.1.call-update) | async-done | bytes 1310736 | tf_op jit(solution)/shard_map/all_gather | solution.py:708
  130.5 16.7 %attend.4 = (bf16[2,320,1024]{2,1,0:T(8,128)(2,1)}, bf16[2,320,1024]{2,1,0:T(8,128)(2,1)}, bf16[1280,128]{1,0:T(8,128)(2,1)}, f32[8,1280]{1,0:T(8,128)}) custom-call(s32[1]{0:T(128)} %bitcast.1.refs_0_, s32[5]{0:T(128)} %and_select_fusion.1.refs_1_, s32[1,1280]{1,0:T(1,128)} %broadcast_in_dim.20.refs_2_.refs_10_, ...), custom_call_target="tpu_custom_call" | custom-call | flops 6710886400 | bytes 8388608 | tf_op jit(solution)/shard_map/attend/pallas_call | solution.py:326
  148.1 10.3 %project.6 = (bf16[1280,1024]{1,0:T(8,128)(2,1)}, bf16[1280,1024]{1,0:T(8,128)(2,1)}, bf16[1280,128]{1,0:T(8,128)(2,1)}, bf16[1280,128]{1,0:T(8,128)(2,1)}, bf16...) custom-call(s32[1]{0:T(128)} %bitcast.1.refs_0_, bf16[320,1024]{1,0:T(8,128)(2,1)} %copy-done.9, ...), custom_call_target="tpu_custom_call" | custom-call | flops 7046430720 | bytes 14680064 | tf_op jit(solution)/shard_map/project/pallas_call | solution.py:219
  158.4 16.8 %attend.6 = (bf16[2,320,1024]{2,1,0:T(8,128)(2,1)}, bf16[2,320,1024]{2,1,0:T(8,128)(2,1)}, bf16[1280,128]{1,0:T(8,128)(2,1)}, f32[8,1280]{1,0:T(8,128)}) custom-call(s32[1]{0:T(128)} %bitcast.1.refs_0_, s32[5]{0:T(128)} %and_select_fusion.refs_1_, s32[1,1280]{1,0:T(1,128)} %broadcast_in_dim.22.refs_2_.refs_10_, ...), custom_call_target="tpu_custom_call" | custom-call | flops 6710886400 | bytes 8388608 | tf_op jit(solution)/shard_map/attend/pallas_call | solution.py:326
  185.0 10.7 %collective-permute-done.10 = bf16[1,320,1024]{2,1,0:T(8,128)(2,1)S(1)} collective-permute-done((bf16[1,320,1024]{2,1,0:T(8,128)(2,1)S(1)}, bf16[1,320,1024]{2,1,0:T(8,128)(2,1)S(1)}, u32[]{:S(2)}, u32[]{:S(2)}) %collective-permute-start.10) | collective-permute-done | bytes 655392 | tf_op jit(solution)/shard_map/ppermute | solution.py:39
  198.8 10.1 %collective-permute-done.35 = bf16[1,320,1024]{2,1,0:T(8,128)(2,1)} collective-permute-done((bf16[1,320,1024]{2,1,0:T(8,128)(2,1)S(1)}, bf16[1,320,1024]{2,1,0:T(8,128)(2,1)}, u32[]{:S(2)}, u32[]{:S(2)}) %collective-permute-start.35) | collective-permute-done | bytes 655392 | tf_op jit(solution)/shard_map/ppermute | solution.py:39
  212.5 13.9 %collective-permute-done.36 = bf16[320,1024]{1,0:T(8,128)(2,1)} collective-permute-done((bf16[320,1024]{1,0:T(8,128)(2,1)S(1)}, bf16[320,1024]{1,0:T(8,128)(2,1)}, u32[]{:S(2)}, u32[]{:S(2)}) %collective-permute-start.36) | collective-permute-done | bytes 655392 | tf_op jit(solution)/shard_map/ppermute | solution.py:39
  226.4 2.7 add_convert_fusion.8
  230.8 2.7 convert_reduce_fusion.1
  235.5 11.5 %collective-permute-done.16.refs_3_.refs_8_ = bf16[320,1024]{1,0:T(8,128)(2,1)} collective-permute-done((bf16[320,1024]{1,0:T(8,128)(2,1)S(1)}, bf16[320,1024]{1,0:T(8,128)(2,1)}, u32[]{:S(2)}, u32[]{:S(2)}) %collective-permute-start.16) | collective-permute-done | bytes 655392 | tf_op jit(solution)/shard_map/ppermute | solution.py:39
  252.7 8.3 %collective-permute-done.13.refs_4_.refs_3_ = bf16[320,1024]{1,0:T(8,128)(2,1)S(1)} collective-permute-done((bf16[320,1024]{1,0:T(8,128)(2,1)S(1)}, bf16[320,1024]{1,0:T(8,128)(2,1)S(1)}, u32[]{:S(2)}, u32[]{:S(2)}) %collective-permute-start.13) | collective-permute-done | bytes 655392 | tf_op jit(solution)/shard_map/ppermute | solution.py:39
  261.0 11.4 %collective-permute-done.38.refs_4_.refs_7_ = bf16[320,1024]{1,0:T(8,128)(2,1)S(1)} collective-permute-done((bf16[320,1024]{1,0:T(8,128)(2,1)}, bf16[320,1024]{1,0:T(8,128)(2,1)S(1)}, u32[]{:S(2)}, u32[]{:S(2)}) %collective-permute-start.38) | collective-permute-done | bytes 655392 | tf_op jit(solution)/shard_map/ppermute | solution.py:39
  274.4 10.3 %project.5 = (bf16[1280,1024]{1,0:T(8,128)(2,1)}, bf16[1280,1024]{1,0:T(8,128)(2,1)}, bf16[1280,128]{1,0:T(8,128)(2,1)}, bf16[1280,128]{1,0:T(8,128)(2,1)}, bf16...) custom-call(s32[1]{0:T(128)} %bitcast.1.refs_0_, bf16[320,1024]{1,0:T(8,128)(2,1)} %copy-done.5, ...), custom_call_target="tpu_custom_call" | custom-call | flops 7046430720 | bytes 14680064 | tf_op jit(solution)/shard_map/project/pallas_call | solution.py:219
  284.8 16.7 %attend.5 = (bf16[2,320,1024]{2,1,0:T(8,128)(2,1)}, bf16[2,320,1024]{2,1,0:T(8,128)(2,1)}, bf16[1280,128]{1,0:T(8,128)(2,1)}, f32[8,1280]{1,0:T(8,128)}) custom-call(s32[1]{0:T(128)} %bitcast.1.refs_0_, s32[5]{0:T(128)} %and_select_fusion.1.refs_1_, s32[1,1280]{1,0:T(1,128)} %broadcast_in_dim.20.refs_2_.refs_10_, ...), custom_call_target="tpu_custom_call" | custom-call | flops 6710886400 | bytes 8388608 | tf_op jit(solution)/shard_map/attend/pallas_call | solution.py:326
  302.2 24.9 %backward.4 = (bf16[2,320,1024]{2,1,0:T(8,128)(2,1)}, bf16[2,320,1024]{2,1,0:T(8,128)(2,1)}, bf16[1280,384]{1,0:T(8,128)(2,1)}, bf16[1280,512]{1,0:T(8,128)(2,1)...) custom-call(s32[1]{0:T(128)} %bitcast.1.refs_0_, s32[5]{0:T(128)} %and_select_fusion.1.refs_1_, ...), custom_call_target="tpu_custom_call" | custom-call | flops 12079595520 | bytes 16777216 | tf_op jit(solution)/shard_map/backward/pallas_call | solution.py:496
  328.9 10.3 %project.7 = (bf16[1280,1024]{1,0:T(8,128)(2,1)}, bf16[1280,1024]{1,0:T(8,128)(2,1)}, bf16[1280,128]{1,0:T(8,128)(2,1)}, bf16[1280,128]{1,0:T(8,128)(2,1)}, bf16...) custom-call(s32[1]{0:T(128)} %bitcast.1.refs_0_, bf16[320,1024]{1,0:T(8,128)(2,1)} %copy-done.7, ...), custom_call_target="tpu_custom_call" | custom-call | flops 7046430720 | bytes 14680064 | tf_op jit(solution)/shard_map/project/pallas_call | solution.py:219
  339.2 16.7 %attend.7 = (bf16[2,320,1024]{2,1,0:T(8,128)(2,1)}, bf16[2,320,1024]{2,1,0:T(8,128)(2,1)}, bf16[1280,128]{1,0:T(8,128)(2,1)}, f32[8,1280]{1,0:T(8,128)}) custom-call(s32[1]{0:T(128)} %bitcast.1.refs_0_, s32[5]{0:T(128)} %and_select_fusion.refs_1_, s32[1,1280]{1,0:T(1,128)} %broadcast_in_dim.22.refs_2_.refs_10_, ...), custom_call_target="tpu_custom_call" | custom-call | flops 6710886400 | bytes 8388608 | tf_op jit(solution)/shard_map/attend/pallas_call | solution.py:326
  356.8 25.4 %backward.6 = (bf16[2,320,1024]{2,1,0:T(8,128)(2,1)}, bf16[2,320,1024]{2,1,0:T(8,128)(2,1)}, bf16[1280,384]{1,0:T(8,128)(2,1)}, bf16[1280,512]{1,0:T(8,128)(2,1)...) custom-call(s32[1]{0:T(128)} %bitcast.1.refs_0_, s32[5]{0:T(128)} %and_select_fusion.refs_1_, ...), custom_call_target="tpu_custom_call" | custom-call | flops 12079595520 | bytes 16777216 | tf_op jit(solution)/shard_map/backward/pallas_call | solution.py:496
  386.8 14.2 %collective-permute-done.19 = bf16[1,320,1024]{2,1,0:T(8,128)(2,1)S(1)} collective-permute-done((bf16[1,320,1024]{2,1,0:T(8,128)(2,1)S(1)}, bf16[1,320,1024]{2,1,0:T(8,128)(2,1)S(1)}, u32[]{:S(2)}, u32[]{:S(2)}) %collective-permute-start.19) | collective-permute-done | bytes 655392 | tf_op jit(solution)/shard_map/ppermute | solution.py:39
  402.8 11.4 %collective-permute-done.44 = bf16[1,320,1024]{2,1,0:T(8,128)(2,1)S(1)} collective-permute-done((bf16[1,320,1024]{2,1,0:T(8,128)(2,1)S(1)}, bf16[1,320,1024]{2,1,0:T(8,128)(2,1)S(1)}, u32[]{:S(2)}, u32[]{:S(2)}) %collective-permute-start.44) | collective-permute-done | bytes 655392 | tf_op jit(solution)/shard_map/ppermute | solution.py:39
  417.2 3.5 norm_back.4.refs_2_.cot_ref.refs_1_
  421.2 9.2 %collective-permute-done.45.other_ref = bf16[320,1024]{1,0:T(8,128)(2,1)S(1)} collective-permute-done((bf16[320,1024]{1,0:T(8,128)(2,1)S(1)}, bf16[320,1024]{1,0:T(8,128)(2,1)S(1)}, u32[]{:S(2)}, u32[]{:S(2)}) %collective-permute-start.45) | collective-permute-done | bytes 655392 | tf_op jit(solution)/shard_map/ppermute | solution.py:39
  431.3 3.5 norm_back.6.refs_2_.cot_ref.refs_5_
  436.3 16.5 %weight_grads.3 = (bf16[4,896,256]{2,1,0:T(8,128)(2,1)}, bf16[4,640,256]{2,1,0:T(8,128)(2,1)}) custom-call(s32[1]{0:T(128)} %bitcast.1.refs_0_, bf16[320,1024]{1,0:T(8,128)(2,1)} %copy-done.19, bf16[320,1024]{1,0:T(8,128)(2,1)} %collective-permute-done.12.refs_3_.refs_2_, bf16[320,1024]{1,0:T(8,128)(2,1)} %copy-done.60, ...), custom_call_target="tpu_custom_call" | custom-call | flops 16106127360 | bytes 25165824 | tf_op jit(solution)/shard_map/weight_grads/pallas_call | solution.py:584
  455.5 24.9 %backward.5 = (bf16[2,320,1024]{2,1,0:T(8,128)(2,1)}, bf16[2,320,1024]{2,1,0:T(8,128)(2,1)}, bf16[1280,384]{1,0:T(8,128)(2,1)}, bf16[1280,512]{1,0:T(8,128)(2,1)...) custom-call(s32[1]{0:T(128)} %bitcast.1.refs_0_, s32[5]{0:T(128)} %and_select_fusion.1.refs_1_, ...), custom_call_target="tpu_custom_call" | custom-call | flops 12079595520 | bytes 16777216 | tf_op jit(solution)/shard_map/backward/pallas_call | solution.py:496
  481.5 24.9 %backward.7 = (bf16[2,320,1024]{2,1,0:T(8,128)(2,1)}, bf16[2,320,1024]{2,1,0:T(8,128)(2,1)}, bf16[1280,384]{1,0:T(8,128)(2,1)}, bf16[1280,512]{1,0:T(8,128)(2,1)...) custom-call(s32[1]{0:T(128)} %bitcast.1.refs_0_, s32[5]{0:T(128)} %and_select_fusion.refs_1_, ...), custom_call_target="tpu_custom_call" | custom-call | flops 12079595520 | bytes 16777216 | tf_op jit(solution)/shard_map/backward/pallas_call | solution.py:496
  506.5 16.1 %weight_grads.2 = (bf16[4,896,256]{2,1,0:T(8,128)(2,1)}, bf16[4,640,256]{2,1,0:T(8,128)(2,1)}) custom-call(s32[1]{0:T(128)} %bitcast.1.refs_0_, bf16[320,1024]{1,0:T(8,128)(2,1)} %norm_back.4.refs_2_.cot_ref.refs_1_, bf16[320,1024]{1,0:T(8,128)(2,1)} %copy-done.64, bf16[320,1024]{1,0:T(8,128)(2,1)} %copy-done.63, bf16[320,1024]{1,0:T(8,128)(2,1)} %copy-done.66, ...), custom_call_target="tpu_custom_call" | custom-call | flops 16106127360 | bytes 25165824 | tf_op jit(solution)/shard_map/weight_grads/pallas_call | solution.py:584
  523.5 2.7 collective-permute-done.27
  535.7 2.9 collective-permute-done.58
  539.2 3.2 collective-permute-done.55
  544.4 3.1 collective-permute-done.57
  548.5 2.8 collective-permute-start.60
  553.7 4.9 collective-permute-start.61
  562.4 16.6 %collective-permute-start.62 = (f32[768]{0:T(1024)S(1)}, f32[768]{0:T(1024)S(1)}, u32[]{:S(2)}, u32[]{:S(2)}) collective-permute-start(f32[768]{0:T(1024)S(1)} %add.315), channel_id=1, source_target_pairs={{0,1},{1,2},{2,3},{4,5},{5,6},{6,7},{8,9},{9,10},{10,11},{12,13},{... | collective-permute-start | bytes 9224 | tf_op jit(solution)/shard_map/ppermute | solution.py:97
  588.9 10.3 %collective-permute-done.25 = bf16[1,320,1024]{2,1,0:T(8,128)(2,1)S(1)} collective-permute-done((bf16[1,320,1024]{2,1,0:T(8,128)(2,1)S(1)}, bf16[1,320,1024]{2,1,0:T(8,128)(2,1)S(1)}, u32[]{:S(2)}, u32[]{:S(2)}) %collective-permute-start.25) | collective-permute-done | bytes 655392 | tf_op jit(solution)/shard_map/ppermute | solution.py:39
  600.1 9.3 %collective-permute-done.50 = bf16[1,320,1024]{2,1,0:T(8,128)(2,1)S(1)} collective-permute-done((bf16[1,320,1024]{2,1,0:T(8,128)(2,1)S(1)}, bf16[1,320,1024]{2,1,0:T(8,128)(2,1)S(1)}, u32[]{:S(2)}, u32[]{:S(2)}) %collective-permute-start.50) | collective-permute-done | bytes 655392 | tf_op jit(solution)/shard_map/ppermute | solution.py:39
  616.1 3.5 collective-permute-done.26.other_ref
  620.4 3.7 norm_back.5
  624.1 8.8 %collective-permute-done.51.other_ref = bf16[320,1024]{1,0:T(8,128)(2,1)} collective-permute-done((bf16[320,1024]{1,0:T(8,128)(2,1)S(1)}, bf16[320,1024]{1,0:T(8,128)(2,1)}, u32[]{:S(2)}, u32[]{:S(2)}) %collective-permute-start.51) | collective-permute-done | bytes 655392 | tf_op jit(solution)/shard_map/ppermute | solution.py:39
  632.9 3.7 norm_back.7
  636.6 2.7 select_bitcast_fusion.1
  642.3 3.0 reduce-scatter.5.cloned.1.call-done
  649.6 8.9 %collective-permute-done.66 = bf16[1,896,256]{2,1,0:T(8,128)(2,1)S(1)} collective-permute-done((bf16[1,896,256]{2,1,0:T(8,128)(2,1)S(1)}, bf16[1,896,256]{2,1,0:T(8,128)(2,1)S(1)}, u32[]{:S(2)}, u32[]{:S(2)}) %collective-permute-start.66) | collective-permute-done | bytes 458784 | tf_op jit(solution)/shard_map/ppermute | solution.py:39
  (450 shorter events, 130.9 us)
Async XLA Ops:
  7.2 92.8 %all-gather.9.cloned.1.call-start = ((), (), s32[]{:S(2)}) async-start(), calls=%async_computation.4 | async-start | bytes 2293760 | tf_op jit(solution)/shard_map/all_gather | solution.py:707
  9.7 55.0 %collective-permute-start = (bf16[320,1024]{1,0:T(8,128)(2,1)}, bf16[320,1024]{1,0:T(8,128)(2,1)S(1)}, u32[]{:S(2)}, u32[]{:S(2)}) collective-permute-start(bf16[320,1024]{1,0:T(8,128)(2,1)} %get-tuple-element.225), channel_id=1, source_target_pairs={{0,16},{16,0},{1,17},{17,1},{2,18},{18,2},{3,19},{19,3},{4,20},{20... | collective-permute-start | bytes 1966088 | tf_op jit(solution)/shard_map/ppermute | solution.py:39
  12.7 52.0 %collective-permute-start.30 = (bf16[320,1024]{1,0:T(8,128)(2,1)}, bf16[320,1024]{1,0:T(8,128)(2,1)}, u32[]{:S(2)}, u32[]{:S(2)}) collective-permute-start(bf16[320,1024]{1,0:T(8,128)(2,1)} %get-tuple-element.226), channel_id=1, source_target_pairs={{0,16},{16,0},{1,17},{17,1},{2,18},{18,2},{3,19},{19,3},{4,20},{20... | collective-permute-start | bytes 1966088 | tf_op jit(solution)/shard_map/ppermute | solution.py:39
  13.3 39.0 %collective-permute-start.4 = (bf16[256,896]{1,0:T(8,128)(2,1)S(1)}, bf16[256,896]{1,0:T(8,128)(2,1)S(1)}, u32[]{:S(2)}, u32[]{:S(2)}) collective-permute-start(bf16[256,896]{1,0:T(8,128)(2,1)S(1)} %pad_maximum_fusion.3), channel_id=1, source_target_pairs={{0,16},{16,0},{1,17},{17,1},{2,18},{18,2},{3,19},{19,3},{4,20},{20... | collective-permute-start | bytes 1376264 | tf_op jit(solution)/shard_map/ppermute | solution.py:39
  15.5 39.4 %collective-permute-start.5 = (bf16[1,384]{1,0:T(2,128)(2,1)S(1)}, bf16[1,384]{1,0:T(2,128)(2,1)}, u32[]{:S(2)}, u32[]{:S(2)}) collective-permute-start(bf16[1,384]{1,0:T(2,128)(2,1)S(1)} %broadcast_in_dim.21), channel_id=1, source_target_pairs={{0,8},{4,12},{8,0},{12,4},{1,9},{5,13},{9,1},{13,5},{2,10},{6,14},... | collective-permute-start | bytes 2312 | tf_op jit(solution)/shard_map/ppermute | solution.py:39
  18.5 48.5 %collective-permute-start.8 = (bf16[640,256]{1,0:T(8,128)(2,1)}, bf16[640,256]{1,0:T(8,128)(2,1)}, u32[]{:S(2)}, u32[]{:S(2)}) collective-permute-start(bf16[640,256]{1,0:T(8,128)(2,1)} %pad_maximum_fusion.6), channel_id=1, source_target_pairs={{0,16},{16,0},{1,17},{17,1},{2,18},{18,2},{3,19},{19,3},{4,20},{20... | collective-permute-start | bytes 983048 | tf_op jit(solution)/shard_map/ppermute | solution.py:39
  53.4 77.1 %all-gather.13.cloned.1.call-start = ((), (), s32[]{:S(2)}) async-start(), calls=%async_computation.10 | async-start | bytes 1638400 | tf_op jit(solution)/shard_map/all_gather | solution.py:708
  69.0 179.3 %all-gather.11.cloned.1.call-start = ((), (), s32[]{:S(2)}) async-start(), calls=%async_computation.5 | async-start | bytes 2293760 | tf_op jit(solution)/shard_map/all_gather | solution.py:707
  82.7 21.6 %collective-permute-start.1 = (bf16[320,1024]{1,0:T(8,128)(2,1)S(1)}, bf16[320,1024]{1,0:T(8,128)(2,1)}, u32[]{:S(2)}, u32[]{:S(2)}) collective-permute-start(bf16[320,1024]{1,0:T(8,128)(2,1)S(1)} %get-tuple-element.223.refs_1_.refs_6_.x_ref), channel_id=1, source_target_pairs={{0,4},{4,0},{8,12},{12,8},{1,5},{5,1},{9,13},{13,9},{2,6},{6,2},{1... | collective-permute-start | bytes 1966088 | tf_op jit(solution)/shard_map/ppermute | solution.py:39
  83.2 21.1 %collective-permute-start.3 = (bf16[320,1024]{1,0:T(8,128)(2,1)}, bf16[320,1024]{1,0:T(8,128)(2,1)}, u32[]{:S(2)}, u32[]{:S(2)}) collective-permute-start(bf16[320,1024]{1,0:T(8,128)(2,1)} %collective-permute-done.2.refs_3_.refs_8_), channel_id=1, source_target_pairs={{0,4},{4,0},{8,12},{12,8},{1,5},{5,1},{9,13},{13,9},{2,6},{6,2},{1... | collective-permute-start | bytes 1966088 | tf_op jit(solution)/shard_map/ppermute | solution.py:39
  86.0 61.3 %collective-permute-start.31 = (bf16[320,1024]{1,0:T(8,128)(2,1)S(1)}, bf16[320,1024]{1,0:T(8,128)(2,1)S(1)}, u32[]{:S(2)}, u32[]{:S(2)}) collective-permute-start(bf16[320,1024]{1,0:T(8,128)(2,1)S(1)} %get-tuple-element.224.refs_1_.refs_6_.x_ref), channel_id=1, source_target_pairs={{0,4},{4,0},{8,12},{12,8},{1,5},{5,1},{9,13},{13,9},{2,6},{6,2},{1... | collective-permute-start | bytes 1966088 | tf_op jit(solution)/shard_map/ppermute | solution.py:39
  100.0 47.3 %collective-permute-start.33 = (bf16[320,1024]{1,0:T(8,128)(2,1)}, bf16[320,1024]{1,0:T(8,128)(2,1)}, u32[]{:S(2)}, u32[]{:S(2)}) collective-permute-start(bf16[320,1024]{1,0:T(8,128)(2,1)} %collective-permute-done.32.refs_3_.refs_8_), channel_id=1, source_target_pairs={{0,4},{4,0},{8,12},{12,8},{1,5},{5,1},{9,13},{13,9},{2,6},{6,2},{1... | collective-permute-start | bytes 1966088 | tf_op jit(solution)/shard_map/ppermute | solution.py:39
  147.2 28.9 %collective-permute-start.9 = (bf16[2,320,1024]{2,1,0:T(8,128)(2,1)}, bf16[2,320,1024]{2,1,0:T(8,128)(2,1)}, u32[]{:S(2)}, u32[]{:S(2)}) collective-permute-start(bf16[2,320,1024]{2,1,0:T(8,128)(2,1)} %get-tuple-element.90), channel_id=1, source_target_pairs={{0,4},{4,0},{8,12},{12,8},{1,5},{5,1},{9,13},{13,9},{2,6},{6,2},{1... | collective-permute-start | bytes 3932168 | tf_op jit(solution)/shard_map/ppermute | solution.py:39
  175.8 109.0 %all-gather.15.cloned.1.call-start = ((), (), s32[]{:S(2)}) async-start(), calls=%async_computation.11 | async-start | bytes 1638400 | tf_op jit(solution)/shard_map/all_gather | solution.py:708
  183.5 25.4 %collective-permute-start.35 = (bf16[1,320,1024]{2,1,0:T(8,128)(2,1)S(1)}, bf16[1,320,1024]{2,1,0:T(8,128)(2,1)}, u32[]{:S(2)}, u32[]{:S(2)}) collective-permute-start(bf16[1,320,1024]{2,1,0:T(8,128)(2,1)S(1)} %dynamic-slice_convert_fusion.3), channel_id=1, source_target_pairs={{0,8},{4,12},{8,0},{12,4},{1,9},{5,13},{9,1},{13,5},{2,10},{6,14},... | collective-permute-start | bytes 1966088 | tf_op jit(solution)/shard_map/ppermute | solution.py:39
  230.8 382.1 %reduce-scatter.11.cloned.1.call-start = ((), (), s32[]{:S(2)}) async-start(), calls=%async_computation.9 | async-start | bytes 1638400 | tf_op jit(solution)/shard_map/reduce_scatter | solution.py:768
  233.5 27.5 %collective-permute-start.13 = (bf16[320,1024]{1,0:T(8,128)(2,1)S(1)}, bf16[320,1024]{1,0:T(8,128)(2,1)S(1)}, u32[]{:S(2)}, u32[]{:S(2)}) collective-permute-start(bf16[320,1024]{1,0:T(8,128)(2,1)S(1)} %get-tuple-element.218.refs_2_.cot_ref.refs_1_), channel_id=1, source_target_pairs={{0,8},{4,12},{8,0},{12,4},{1,9},{5,13},{9,1},{13,5},{2,10},{6,14},... | collective-permute-start | bytes 1966088 | tf_op jit(solution)/shard_map/ppermute | solution.py:39
  234.1 38.4 %collective-permute-start.38 = (bf16[320,1024]{1,0:T(8,128)(2,1)}, bf16[320,1024]{1,0:T(8,128)(2,1)S(1)}, u32[]{:S(2)}, u32[]{:S(2)}) collective-permute-start(bf16[320,1024]{1,0:T(8,128)(2,1)} %get-tuple-element.222.refs_2_.cot_ref.refs_5_), channel_id=1, source_target_pairs={{0,8},{4,12},{8,0},{12,4},{1,9},{5,13},{9,1},{13,5},{2,10},{6,14},... | collective-permute-start | bytes 1966088 | tf_op jit(solution)/shard_map/ppermute | solution.py:39
  235.5 36.9 %collective-permute-start.15 = (bf16[320,1024]{1,0:T(8,128)(2,1)S(1)}, bf16[320,1024]{1,0:T(8,128)(2,1)}, u32[]{:S(2)}, u32[]{:S(2)}) collective-permute-start(bf16[320,1024]{1,0:T(8,128)(2,1)S(1)} %get-tuple-element.269.refs_1_.refs_6_.x_ref), channel_id=1, source_target_pairs={{0,4},{4,0},{8,12},{12,8},{1,5},{5,1},{9,13},{13,9},{2,6},{6,2},{1... | collective-permute-start | bytes 1966088 | tf_op jit(solution)/shard_map/ppermute | solution.py:39
  247.0 25.9 %collective-permute-start.17 = (bf16[320,1024]{1,0:T(8,128)(2,1)}, bf16[320,1024]{1,0:T(8,128)(2,1)}, u32[]{:S(2)}, u32[]{:S(2)}) collective-permute-start(bf16[320,1024]{1,0:T(8,128)(2,1)} %collective-permute-done.16.refs_3_.refs_8_), channel_id=1, source_target_pairs={{0,4},{4,0},{8,12},{12,8},{1,5},{5,1},{9,13},{13,9},{2,6},{6,2},{1... | collective-permute-start | bytes 1966088 | tf_op jit(solution)/shard_map/ppermute | solution.py:39
  247.8 53.8 %collective-permute-start.12 = (bf16[320,1024]{1,0:T(8,128)(2,1)S(1)}, bf16[320,1024]{1,0:T(8,128)(2,1)}, u32[]{:S(2)}, u32[]{:S(2)}) collective-permute-start(bf16[320,1024]{1,0:T(8,128)(2,1)S(1)} %get-tuple-element.218.refs_2_.cot_ref.refs_1_), channel_id=1, source_target_pairs={{0,4},{4,0},{8,12},{12,8},{1,5},{5,1},{9,13},{13,9},{2,6},{6,2},{1... | collective-permute-start | bytes 1966088 | tf_op jit(solution)/shard_map/ppermute | solution.py:39
  261.0 95.0 %collective-permute-start.37 = (bf16[320,1024]{1,0:T(8,128)(2,1)}, bf16[320,1024]{1,0:T(8,128)(2,1)}, u32[]{:S(2)}, u32[]{:S(2)}) collective-permute-start(bf16[320,1024]{1,0:T(8,128)(2,1)} %get-tuple-element.222.refs_2_.cot_ref.refs_5_), channel_id=1, source_target_pairs={{0,4},{4,0},{8,12},{12,8},{1,5},{5,1},{9,13},{13,9},{2,6},{6,2},{1... | collective-permute-start | bytes 1966088 | tf_op jit(solution)/shard_map/ppermute | solution.py:39
  272.4 29.7 %collective-permute-start.14 = (bf16[320,1024]{1,0:T(8,128)(2,1)S(1)}, bf16[320,1024]{1,0:T(8,128)(2,1)}, u32[]{:S(2)}, u32[]{:S(2)}) collective-permute-start(bf16[320,1024]{1,0:T(8,128)(2,1)S(1)} %collective-permute-done.13.refs_4_.refs_3_), channel_id=1, source_target_pairs={{0,4},{4,0},{8,12},{12,8},{1,5},{5,1},{9,13},{13,9},{2,6},{6,2},{1... | collective-permute-start | bytes 1966088 | tf_op jit(solution)/shard_map/ppermute | solution.py:39
  272.4 83.6 %collective-permute-start.39 = (bf16[320,1024]{1,0:T(8,128)(2,1)S(1)}, bf16[320,1024]{1,0:T(8,128)(2,1)S(1)}, u32[]{:S(2)}, u32[]{:S(2)}) collective-permute-start(bf16[320,1024]{1,0:T(8,128)(2,1)S(1)} %collective-permute-done.38.refs_4_.refs_7_), channel_id=1, source_target_pairs={{0,4},{4,0},{8,12},{12,8},{1,5},{5,1},{9,13},{13,9},{2,6},{6,2},{1... | collective-permute-start | bytes 1966088 | tf_op jit(solution)/shard_map/ppermute | solution.py:39
  272.9 28.7 %collective-permute-start.41 = (bf16[320,1024]{1,0:T(8,128)(2,1)S(1)}, bf16[320,1024]{1,0:T(8,128)(2,1)}, u32[]{:S(2)}, u32[]{:S(2)}) collective-permute-start(bf16[320,1024]{1,0:T(8,128)(2,1)S(1)} %get-tuple-element.270.refs_1_.refs_6_.x_ref), channel_id=1, source_target_pairs={{0,8},{4,12},{8,0},{12,4},{1,9},{5,13},{9,1},{13,5},{2,10},{6,14},... | collective-permute-start | bytes 1966088 | tf_op jit(solution)/shard_map/ppermute | solution.py:39
  301.6 25.6 %collective-permute-start.40 = (bf16[320,1024]{1,0:T(8,128)(2,1)S(1)}, bf16[320,1024]{1,0:T(8,128)(2,1)S(1)}, u32[]{:S(2)}, u32[]{:S(2)}) collective-permute-start(bf16[320,1024]{1,0:T(8,128)(2,1)S(1)} %get-tuple-element.270.refs_1_.refs_6_.x_ref), channel_id=1, source_target_pairs={{0,4},{4,0},{8,12},{12,8},{1,5},{5,1},{9,13},{13,9},{2,6},{6,2},{1... | collective-permute-start | bytes 1966088 | tf_op jit(solution)/shard_map/ppermute | solution.py:39
  301.7 25.5 %collective-permute-start.42 = (bf16[320,1024]{1,0:T(8,128)(2,1)}, bf16[320,1024]{1,0:T(8,128)(2,1)S(1)}, u32[]{:S(2)}, u32[]{:S(2)}) collective-permute-start(bf16[320,1024]{1,0:T(8,128)(2,1)} %collective-permute-done.41.refs_3_.refs_8_), channel_id=1, source_target_pairs={{0,4},{4,0},{8,12},{12,8},{1,5},{5,1},{9,13},{13,9},{2,6},{6,2},{1... | collective-permute-start | bytes 1966088 | tf_op jit(solution)/shard_map/ppermute | solution.py:39
  327.0 55.7 %collective-permute-start.18 = (bf16[2,320,1024]{2,1,0:T(8,128)(2,1)}, bf16[2,320,1024]{2,1,0:T(8,128)(2,1)S(1)}, u32[]{:S(2)}, u32[]{:S(2)}) collective-permute-start(bf16[2,320,1024]{2,1,0:T(8,128)(2,1)} %get-tuple-element.99), channel_id=1, source_target_pairs={{0,4},{4,0},{8,12},{12,8},{1,5},{5,1},{9,13},{13,9},{2,6},{6,2},{1... | collective-permute-start | bytes 3932168 | tf_op jit(solution)/shard_map/ppermute | solution.py:39
  386.2 28.0 %collective-permute-start.44 = (bf16[1,320,1024]{2,1,0:T(8,128)(2,1)S(1)}, bf16[1,320,1024]{2,1,0:T(8,128)(2,1)S(1)}, u32[]{:S(2)}, u32[]{:S(2)}) collective-permute-start(bf16[1,320,1024]{2,1,0:T(8,128)(2,1)S(1)} %dynamic-slice_convert_fusion.2), channel_id=1, source_target_pairs={{0,8},{4,12},{8,0},{12,4},{1,9},{5,13},{9,1},{13,5},{2,10},{6,14},... | collective-permute-start | bytes 1966088 | tf_op jit(solution)/shard_map/ppermute | solution.py:39
  421.2 33.2 %collective-permute-start.21 = (bf16[320,1024]{1,0:T(8,128)(2,1)}, bf16[320,1024]{1,0:T(8,128)(2,1)S(1)}, u32[]{:S(2)}, u32[]{:S(2)}) collective-permute-start(bf16[320,1024]{1,0:T(8,128)(2,1)} %norm_back.4.refs_2_.cot_ref.refs_1_), channel_id=1, source_target_pairs={{0,4},{4,0},{8,12},{12,8},{1,5},{5,1},{9,13},{13,9},{2,6},{6,2},{1... | collective-permute-start | bytes 1966088 | tf_op jit(solution)/shard_map/ppermute | solution.py:39
  434.7 19.5 %collective-permute-start.47 = (bf16[320,1024]{1,0:T(8,128)(2,1)}, bf16[320,1024]{1,0:T(8,128)(2,1)S(1)}, u32[]{:S(2)}, u32[]{:S(2)}) collective-permute-start(bf16[320,1024]{1,0:T(8,128)(2,1)} %norm_back.6.refs_2_.cot_ref.refs_5_), channel_id=1, source_target_pairs={{0,8},{4,12},{8,0},{12,4},{1,9},{5,13},{9,1},{13,5},{2,10},{6,14},... | collective-permute-start | bytes 1966088 | tf_op jit(solution)/shard_map/ppermute | solution.py:39
  452.8 160.0 %reduce-scatter.9.cloned.1.call-start = ((), (), s32[]{:S(2)}) async-start(), calls=%async_computation.8 | async-start | bytes 1638400 | tf_op jit(solution)/shard_map/reduce_scatter | solution.py:768
  453.9 26.5 %collective-permute-start.46 = (bf16[320,1024]{1,0:T(8,128)(2,1)S(1)}, bf16[320,1024]{1,0:T(8,128)(2,1)S(1)}, u32[]{:S(2)}, u32[]{:S(2)}) collective-permute-start(bf16[320,1024]{1,0:T(8,128)(2,1)S(1)} %copy-done.13), channel_id=1, source_target_pairs={{0,4},{4,0},{8,12},{12,8},{1,5},{5,1},{9,13},{13,9},{2,6},{6,2},{1... | collective-permute-start | bytes 1966088 | tf_op jit(solution)/shard_map/ppermute | solution.py:39
  454.2 26.3 %collective-permute-start.48 = (bf16[320,1024]{1,0:T(8,128)(2,1)S(1)}, bf16[320,1024]{1,0:T(8,128)(2,1)S(1)}, u32[]{:S(2)}, u32[]{:S(2)}) collective-permute-start(bf16[320,1024]{1,0:T(8,128)(2,1)S(1)} %collective-permute-done.47.refs_4_.refs_7_), channel_id=1, source_target_pairs={{0,4},{4,0},{8,12},{12,8},{1,5},{5,1},{9,13},{13,9},{2,6},{6,2},{1... | collective-permute-start | bytes 1966088 | tf_op jit(solution)/shard_map/ppermute | solution.py:39
  522.6 119.6 %reduce-scatter.7.cloned.1.call-start = ((), (), s32[]{:S(2)}) async-start(), calls=%async_computation.7 | async-start | bytes 2293760 | tf_op jit(solution)/shard_map/reduce_scatter | solution.py:767
  523.4 121.9 %reduce-scatter.5.cloned.1.call-start = ((), (), s32[]{:S(2)}) async-start(), calls=%async_computation.6 | async-start | bytes 2293760 | tf_op jit(solution)/shard_map/reduce_scatter | solution.py:767
  528.9 24.8 %collective-permute-start.28 = (bf16[1,320,1024]{2,1,0:T(8,128)(2,1)}, bf16[1,320,1024]{2,1,0:T(8,128)(2,1)}, u32[]{:S(2)}, u32[]{:S(2)}) collective-permute-start(bf16[1,320,1024]{2,1,0:T(8,128)(2,1)} %dynamic-slice_convert_fusion.4), channel_id=1, source_target_pairs={{0,8},{4,12},{8,0},{12,4},{1,9},{5,13},{9,1},{13,5},{2,10},{6,14},... | collective-permute-start | bytes 1966088 | tf_op jit(solution)/shard_map/ppermute | solution.py:39
  532.8 29.6 %collective-permute-start.24 = (bf16[2,320,1024]{2,1,0:T(8,128)(2,1)}, bf16[2,320,1024]{2,1,0:T(8,128)(2,1)}, u32[]{:S(2)}, u32[]{:S(2)}) collective-permute-start(bf16[2,320,1024]{2,1,0:T(8,128)(2,1)} %get-tuple-element.104), channel_id=1, source_target_pairs={{0,4},{4,0},{8,12},{12,8},{1,5},{5,1},{9,13},{13,9},{2,6},{6,2},{1... | collective-permute-start | bytes 3932168 | tf_op jit(solution)/shard_map/ppermute | solution.py:39
  532.9 48.5 %collective-permute-start.49 = (bf16[2,320,1024]{2,1,0:T(8,128)(2,1)}, bf16[2,320,1024]{2,1,0:T(8,128)(2,1)}, u32[]{:S(2)}, u32[]{:S(2)}) collective-permute-start(bf16[2,320,1024]{2,1,0:T(8,128)(2,1)} %get-tuple-element.126), channel_id=1, source_target_pairs={{0,4},{4,0},{8,12},{12,8},{1,5},{5,1},{9,13},{13,9},{2,6},{6,2},{1... | collective-permute-start | bytes 3932168 | tf_op jit(solution)/shard_map/ppermute | solution.py:39
  552.2 32.3 %collective-permute-start.53 = (bf16[1,320,1024]{2,1,0:T(8,128)(2,1)}, bf16[1,320,1024]{2,1,0:T(8,128)(2,1)}, u32[]{:S(2)}, u32[]{:S(2)}) collective-permute-start(bf16[1,320,1024]{2,1,0:T(8,128)(2,1)} %dynamic-slice_convert_fusion), channel_id=1, source_target_pairs={{0,8},{4,12},{8,0},{12,4},{1,9},{5,13},{9,1},{13,5},{2,10},{6,14},... | collective-permute-start | bytes 1966088 | tf_op jit(solution)/shard_map/ppermute | solution.py:39
  560.3 76.3 %collective-permute-start.29 = (bf16[320,1024]{1,0:T(8,128)(2,1)S(1)}, bf16[320,1024]{1,0:T(8,128)(2,1)}, u32[]{:S(2)}, u32[]{:S(2)}) collective-permute-start(bf16[320,1024]{1,0:T(8,128)(2,1)S(1)} %fusion.3), channel_id=1, source_target_pairs={{0,16},{16,0},{1,17},{17,1},{2,18},{18,2},{3,19},{19,3},{4,20},{20... | collective-permute-start | bytes 1966088 | tf_op jit(solution)/shard_map/ppermute | solution.py:39
  561.1 26.6 %collective-permute-start.65 = (f32[768]{0:T(1024)S(1)}, f32[768]{0:T(1024)S(1)}, u32[]{:S(2)}, u32[]{:S(2)}) collective-permute-start(f32[768]{0:T(1024)S(1)} %add.318), channel_id=1, source_target_pairs={{1,0},{2,1},{3,2},{5,4},{6,5},{7,6},{9,8},{10,9},{11,10},{13,12},{... | collective-permute-start | bytes 9224 | tf_op jit(solution)/shard_map/ppermute | solution.py:100
  562.4 26.4 %collective-permute-start.62 = (f32[768]{0:T(1024)S(1)}, f32[768]{0:T(1024)S(1)}, u32[]{:S(2)}, u32[]{:S(2)}) collective-permute-start(f32[768]{0:T(1024)S(1)} %add.315), channel_id=1, source_target_pairs={{0,1},{1,2},{2,3},{4,5},{5,6},{6,7},{8,9},{9,10},{10,11},{12,13},{... | collective-permute-start | bytes 9224 | tf_op jit(solution)/shard_map/ppermute | solution.py:97
  584.5 24.9 %collective-permute-start.50 = (bf16[1,320,1024]{2,1,0:T(8,128)(2,1)S(1)}, bf16[1,320,1024]{2,1,0:T(8,128)(2,1)S(1)}, u32[]{:S(2)}, u32[]{:S(2)}) collective-permute-start(bf16[1,320,1024]{2,1,0:T(8,128)(2,1)S(1)} %dynamic-slice_convert_fusion.1), channel_id=1, source_target_pairs={{0,8},{4,12},{8,0},{12,4},{1,9},{5,13},{9,1},{13,5},{2,10},{6,14},... | collective-permute-start | bytes 1966088 | tf_op jit(solution)/shard_map/ppermute | solution.py:39
  587.7 48.9 %collective-permute-start.54 = (bf16[320,1024]{1,0:T(8,128)(2,1)}, bf16[320,1024]{1,0:T(8,128)(2,1)S(1)}, u32[]{:S(2)}, u32[]{:S(2)}) collective-permute-start(bf16[320,1024]{1,0:T(8,128)(2,1)} %fusion.7), channel_id=1, source_target_pairs={{0,16},{16,0},{1,17},{17,1},{2,18},{18,2},{3,19},{19,3},{4,20},{20... | collective-permute-start | bytes 1966088 | tf_op jit(solution)/shard_map/ppermute | solution.py:39
  599.4 20.2 %collective-permute-start.26 = (bf16[320,1024]{1,0:T(8,128)(2,1)S(1)}, bf16[320,1024]{1,0:T(8,128)(2,1)S(1)}, u32[]{:S(2)}, u32[]{:S(2)}) collective-permute-start(bf16[320,1024]{1,0:T(8,128)(2,1)S(1)} %fusion.2.own_ref), channel_id=1, source_target_pairs={{0,16},{16,0},{1,17},{17,1},{2,18},{18,2},{3,19},{19,3},{4,20},{20... | collective-permute-start | bytes 1966088 | tf_op jit(solution)/shard_map/ppermute | solution.py:39
  609.6 23.3 %collective-permute-start.51 = (bf16[320,1024]{1,0:T(8,128)(2,1)S(1)}, bf16[320,1024]{1,0:T(8,128)(2,1)}, u32[]{:S(2)}, u32[]{:S(2)}) collective-permute-start(bf16[320,1024]{1,0:T(8,128)(2,1)S(1)} %fusion.6.own_ref), channel_id=1, source_target_pairs={{0,16},{16,0},{1,17},{17,1},{2,18},{18,2},{3,19},{19,3},{4,20},{20... | collective-permute-start | bytes 1966088 | tf_op jit(solution)/shard_map/ppermute | solution.py:39
  614.6 26.6 %collective-permute-start.67 = (bf16[1,640,256]{2,1,0:T(8,128)(2,1)}, bf16[1,640,256]{2,1,0:T(8,128)(2,1)}, u32[]{:S(2)}, u32[]{:S(2)}) collective-permute-start(bf16[1,640,256]{2,1,0:T(8,128)(2,1)} %broadcast_select_fusion.12), channel_id=1, source_target_pairs={{0,16},{16,0},{1,17},{17,1},{2,18},{18,2},{3,19},{19,3},{4,20},{20... | collective-permute-start | bytes 983048 | tf_op jit(solution)/shard_map/ppermute | solution.py:39
  (102 other events, 831.5 us)
Sparse Core Ops, SparseCore 0:
  53.5 43.7 all-gather.8
  98.9 31.5 all-gather.12
  175.9 43.3 all-gather.10
  230.9 33.7 all-gather.14
  453.0 37.9 reduce-scatter.10
  522.7 40.8 reduce-scatter.8
  566.0 38.3 reduce-scatter.6
  606.7 38.5 reduce-scatter.4

commit v2 on v0

v2 whole, which is shorter than its diff:
```python
import functools

import jax
import jax.numpy as jnp
from jax import lax
from jax.experimental import pallas as pl
from jax.experimental.pallas import tpu as pltpu
from jax.sharding import PartitionSpec as P

D = 1024
H = 16
HD = 64
ROT = 16
MB = 2
TOK_MB = 1280
EPS = 1e-05
CHUNK = 256
FLOPS = 10**11
BF = jnp.bfloat16
F32 = jnp.float32
ANY = pl.BlockSpec(memory_space=pl.ANY)
VMEM = pl.BlockSpec(memory_space=pltpu.VMEM)
SMEM = pl.BlockSpec(memory_space=pltpu.SMEM)


def dot(left, right, left_dim, right_dim):
    return lax.dot_general(
        left, right, (((left_dim,), (right_dim,)), ((), ())), preferred_element_type=F32
    )


def shape(dims, dtype):
    return jax.ShapeDtypeStruct(dims, dtype)


def swap(value, axis, bit):
    count = lax.axis_size(axis)
    return lax.ppermute(value, axis, [(i, i ^ (1 << bit)) for i in range(count)])


def bits_of(axis):
    return lax.axis_size(axis).bit_length() - 1


def pick(value, index, axis):
    return lax.dynamic_index_in_dim(value, index, axis, keepdims=False)


def gather_blocks(value):
    blocks = {0: value}
    for bit in reversed(range(bits_of("tensor"))):
        for s in list(blocks):
            blocks[s | (1 << bit)] = swap(blocks[s], "tensor", bit)
    return [blocks[s] for s in range(len(blocks))]


def gather_tensor(value):
    index = lax.axis_index("tensor")
    value = value[None]
    for bit in reversed(range(bits_of("tensor"))):
        other = swap(value, "tensor", bit)
        mine = ((index >> bit) & 1) == 0
        low = jnp.where(mine, value, other)
        high = jnp.where(mine, other, value)
        value = jnp.stack([low, high], axis=1).reshape((-1,) + value.shape[1:])
    return value


def after(value, *others):
    return lax.optimization_barrier((value, *others))[0]


def line_parts(value, axis):
    count = lax.axis_size(axis)
    left, right = [value], [value]
    for hop in range(1, count):
        left.append(lax.ppermute(left[-1], axis, [(j, j + 1) for j in range(hop - 1, count - 1)]))
        right.append(lax.ppermute(right[-1], axis, [(j + 1, j) for j in range(count - hop)]))
    return left + right[1:]


def gather_direct(value, axis):
    count = lax.axis_size(axis)
    index = lax.axis_index(axis)
    found = [value]
    for hop in range(1, count):
        found.append(lax.ppermute(value, axis, [(j, (j + hop) % count) for j in range(count)]))
    turned = jnp.stack(found[::-1] * 2)
    return lax.dynamic_slice_in_dim(turned, count - 1 - index, count, 0)


def scatter_direct(value, axis):
    count = lax.axis_size(axis)
    index = lax.axis_index(axis)
    total = pick(value, index, 0)
    for hop in range(1, count):
        sent = pick(value, (index + hop) % count, 0)
        total = total + lax.ppermute(sent, axis, [(j, (j + hop) % count) for j in range(count)])
    return total


def copies_of_blocks(index, blocks, target, sems):
    copies = []
    for s, block in enumerate(blocks):
        rows = block.shape[0]
        where = pl.multiple_of((index ^ s) * rows, rows)
        copies.append(pltpu.make_async_copy(block, target.at[pl.ds(where, rows)], sems.at[s]))
    return copies


def copies_to_halves(index, source, keep, send, sems, rows):
    copies = []
    own = index & 1
    for block in range(source.shape[0] // rows):
        part = source.at[pl.ds(block * rows, rows)]
        copies.append(
            (
                own == block & 1,
                pltpu.make_async_copy(part, keep.at[block >> 1], sems.at[block]),
                pltpu.make_async_copy(part, send.at[block >> 1], sems.at[block]),
            )
        )
    return copies


def start_half(copy):
    is_kept, to_keep, to_send = copy

    @pl.when(is_kept)
    def _():
        to_keep.start()

    @pl.when(jnp.logical_not(is_kept))
    def _():
        to_send.start()


def normalize(rows):
    rows = rows.astype(F32)
    centered = rows - jnp.mean(rows, axis=-1, keepdims=True)
    scale = lax.rsqrt(jnp.mean(centered * centered, axis=-1, keepdims=True) + EPS)
    return centered * scale, scale


def gelu_pair(values):
    share = 0.5 * (1.0 + lax.erf(values * 0.7071067811865476))
    density = jnp.exp(-0.5 * values * values) * 0.3989422804014327
    return values * share, share + values * density


def rotate(values, table_cos, table_sin, sign):
    width = values.shape[1]
    half = ROT // 2
    lanes = lax.broadcasted_iota(jnp.int32, values.shape, 1) % HD
    partner = jnp.where(
        lanes < half, pltpu.roll(values, width - half, 1), pltpu.roll(values, half, 1)
    )
    return values * table_cos + partner * (table_sin * sign)


def unpack_table(packed, sign):
    width = packed.shape[1]
    lanes = lax.broadcasted_iota(jnp.int32, packed.shape, 1) % HD
    table_cos = jnp.where(lanes < ROT, packed, 1.0)
    table_sin = jnp.where(lanes < ROT, pltpu.roll(packed, width - ROT, 1) * sign, 0.0)
    return table_cos, table_sin


def rotate(values, table_cos, table_sin):
    width = values.shape[1]
    half = ROT // 2
    lanes = lax.broadcasted_iota(jnp.int32, values.shape, 1) % HD
    partner = jnp.where(
        lanes < half, pltpu.roll(values, width - half, 1), pltpu.roll(values, half, 1)
    )
    return values * table_cos + partner * table_sin


def chunks():
    return [slice(begin, begin + CHUNK) for begin in range(0, TOK_MB, CHUNK)]


class Order:
    def __init__(self):
        self.last = []

    def hold(self, *values):
        self.last = [*self.last, *values]

    def call(self, kernel, name, vmem, in_specs, out_specs, out_shape, scratch, args, **more):
        count = len(args)
        deps = self.last

        def outer(*refs):
            kernel(*refs[:count], *refs[count + len(deps) :])

        results = pl.pallas_call(
            outer,
            in_specs=in_specs + [ANY] * len(deps),
            out_specs=out_specs,
            out_shape=out_shape,
            scratch_shapes=scratch,
            compiler_params=pltpu.CompilerParams(vmem_limit_bytes=vmem << 20),
            cost_estimate=pl.CostEstimate(
                flops=FLOPS, bytes_accessed=1024, transcendentals=0
            ),
            name=name,
            **more,
        )(*args, *deps)
        self.last = [min(results, key=lambda result: result.size)]
        return results

    def pause(self):
        def nothing(out_ref):
            out_ref[...] = jnp.zeros_like(out_ref)

        self.call(nothing, "pause", 2, [], [VMEM], [shape((8, 128), F32)], [], [])


def loads_of_weights(source, row, target, sems, first=0):
    dp, _, share = source.shape
    rows = target.shape[0]
    return [
        pltpu.make_async_copy(
            source.at[j, pl.ds(row, rows)],
            target.at[:, pl.ds(j * share, share)],
            sems.at[first + j],
        )
        for j in range(dp)
    ]


def start_all(copies):
    for copy in copies:
        copy.start()


def wait_all(copies):
    for copy in copies:
        copy.wait()


class Leaving:
    def __init__(self, index, source, keep, send, sems):
        self.rows = keep.shape[1]
        self.copies = copies_to_halves(index, source, keep, send, sems, self.rows)
        self.done = 0

    def reached(self, end):
        while self.done < len(self.copies) and (self.done + 1) * self.rows <= end:
            start_half(self.copies[self.done])
            self.done += 1

    def wait(self):
        for copy in self.copies:
            copy[1].wait()


def masked(scores, starts, begin):
    key = lax.broadcasted_iota(jnp.int32, scores.shape, 0)
    query = lax.broadcasted_iota(jnp.int32, scores.shape, 1) + begin
    return jnp.where((key <= query) & (key >= starts), scores, -1e30)


def head_only(values, head):
    lanes = lax.broadcasted_iota(jnp.int32, values.shape, 1)
    inside = (lanes >= head * HD) & (lanes < (head + 1) * HD)
    return jnp.where(inside, values, jnp.zeros_like(values))


def turned_back(parts, w):
    rest = w - len(parts) * HD
    if rest:
        parts = parts + [jnp.zeros((rest, parts[0].shape[1]), F32)]
    return jnp.concatenate(parts, axis=0).T


def do_project(w, x_all, main, norms_ref, bias_ref, table_ref, q_ref, k_ref, v_ref, hidden_ref, slope_ref):
    for at in chunks():
        hat, _ = normalize(x_all[at])
        first = (hat * norms_ref[0:1] + norms_ref[2:3]).astype(BF)
        second = (hat * norms_ref[1:2] + norms_ref[3:4]).astype(BF)
        raw = dot(first, main[: 3 * w], 1, 1) + bias_ref[:, : 3 * w]
        table_cos, table_sin = unpack_table(table_ref[at], 1.0)
        q_ref[at] = rotate(raw[:, :w], table_cos, table_sin).astype(BF)
        k_ref[at] = rotate(raw[:, w : 2 * w], table_cos, table_sin).astype(BF)
        v_ref[at] = raw[:, 2 * w :].astype(BF)
        hidden, slope = gelu_pair(dot(second, main[3 * w :], 1, 1) + bias_ref[:, 3 * w :])
        hidden_ref[at] = hidden.astype(BF)
        slope_ref[at] = slope.astype(BF)


def do_attend(heads, w, starts_ref, q_ref, k_ref, v_ref, hidden_ref, low, loads, context_ref, logs_ref, v_turned, partial, leaving):
    v_turned[...] = v_ref[...].T
    logs_ref[...] = jnp.zeros_like(logs_ref)
    for at in chunks():
        starts = starts_ref[:, at]
        queries = q_ref[at] * BF(HD**-0.5)
        turned = []
        for head in range(heads):
            s = dot(k_ref[: at.stop], head_only(queries, head), 1, 1)
            s = masked(s, starts, at.start)
            top = jnp.max(s, axis=0, keepdims=True)
            e = jnp.exp(s - top)
            total = jnp.sum(e, axis=0, keepdims=True)
            part = v_turned[head * HD : (head + 1) * HD, : at.stop]
            turned.append(dot(part, e.astype(BF), 1, 0) / total)
            logs_ref[head : head + 1, at] = top + jnp.log(total)
        context = turned_back(turned, w).astype(BF)
        context_ref[at] = context
        if at.start == 0:
            wait_all(loads)
        total = dot(context, low[:w], 1, 0) + dot(hidden_ref[at], low[w:], 1, 0)
        partial[at] = total.astype(BF)
        leaving.reached(at.stop)


def do_enter(w, c_all, low, slope_ref, grad_context, pre_ref, sum_ref):
    total = jnp.zeros(sum_ref.shape, F32)
    for at in chunks():
        both = dot(c_all[at], low[...], 1, 1)
        grad_context[at] = both[:, :w].astype(BF)
        grad_pre = (both[:, w:] * slope_ref[at].astype(F32)).astype(BF)
        pre_ref[at] = grad_pre
        total = total + jnp.sum(grad_pre.astype(F32), axis=0, keepdims=True)
    sum_ref[...] = total


def do_backward(
    heads,
    w,
    starts_ref,
    q_ref,
    k_ref,
    v_ref,
    context_ref,
    logs_ref,
    grad_context,
    pre_ref,
    x_loads,
    x_all,
    main,
    norms_ref,
    table_ref,
    raw_ref,
    vectors_ref,
    sum_ref,
    k_turned,
    grad_q,
    grad_k,
    grad_v,
    partial,
    leaving,
):
    k_turned[...] = (k_ref[...] * BF(HD**-0.5)).T
    grad_k[...] = jnp.zeros_like(grad_k)
    grad_v[...] = jnp.zeros_like(grad_v)
    for at in chunks():
        starts = starts_ref[:, at]
        queries = q_ref[at] * BF(HD**-0.5)
        grads = grad_context[at]
        products = (grads.astype(F32) * context_ref[at].astype(F32)).T
        to_k = to_v = 0.0
        turned = []
        for head in range(heads):
            lanes = slice(head * HD, (head + 1) * HD)
            q, g = head_only(queries, head), head_only(grads, head)
            weighted = jnp.sum(products[lanes], axis=0, keepdims=True)
            s = masked(dot(k_ref[: at.stop], q, 1, 1), starts, at.start)
            p = jnp.exp(s - logs_ref[head : head + 1, at])
            grad_p = dot(v_ref[: at.stop], g, 1, 1)
            grad_s = (p * (grad_p - weighted)).astype(BF)
            to_k = to_k + dot(grad_s, q, 1, 0)
            to_v = to_v + dot(p.astype(BF), g, 1, 0)
            turned.append(dot(k_turned[lanes, : at.stop], grad_s, 1, 0))
        grad_k[: at.stop] += to_k
        grad_v[: at.stop] += to_v
        grad_q[at] = turned_back(turned, w)
    wait_all(x_loads)
    sums = [jnp.zeros((1, D), F32) for _ in range(4)]
    raw_sum = jnp.zeros(sum_ref.shape, F32)
    for at in chunks():
        table_cos, table_sin = unpack_table(table_ref[at], -1.0)
        grad_raw = jnp.concatenate(
            [
                rotate(grad_q[at], table_cos, table_sin),
                rotate(grad_k[at], table_cos, table_sin),
                grad_v[at],
            ],
            axis=1,
        ).astype(BF)
        raw_ref[at] = grad_raw
        raw_sum = raw_sum + jnp.sum(grad_raw.astype(F32), axis=0, keepdims=True)
        grad_first = dot(grad_raw, main[: 3 * w], 1, 0)
        grad_second = dot(pre_ref[at], main[3 * w :], 1, 0)
        hat, _ = normalize(x_all[at])
        for i, term in enumerate(
            (grad_first * hat, grad_second * hat, grad_first, grad_second)
        ):
            sums[i] = sums[i] + jnp.sum(term, axis=0, keepdims=True)
        partial[at] = (grad_first * norms_ref[0:1] + grad_second * norms_ref[1:2]).astype(BF)
        leaving.reached(at.stop)
    vectors_ref[...] = jnp.concatenate(sums + [jnp.zeros((4, D), F32)], axis=0)
    sum_ref[...] = raw_sum


def rows_of(*widths):
    return [shape((TOK_MB, width), BF) for width in widths]


def halves_of(blocks):
    return [shape((blocks // 2, TOK_MB // blocks, D), BF)] * 2


def held(*widths):
    return [pltpu.VMEM((TOK_MB, width), BF) for width in widths]


def dma(*counts):
    return [pltpu.SemaphoreType.DMA((count,)) for count in counts]


def project_kernel(blocks, w, row, *refs):
    index_ref = refs[0]
    x_refs = refs[1 : 1 + blocks]
    main_ref, norms_ref, bias_ref, table_ref = refs[1 + blocks : 5 + blocks]
    outs = refs[5 + blocks : 10 + blocks]
    x_all, main, x_sems, main_sems = refs[10 + blocks :]
    loads = copies_of_blocks(index_ref[0], x_refs, x_all, x_sems)
    loads += loads_of_weights(main_ref, row, main, main_sems)
    start_all(loads)
    wait_all(loads)
    do_project(w, x_all, main, norms_ref, bias_ref, table_ref, *outs)


def project(order, index, x_blocks, weights, angles):
    blocks = len(x_blocks)
    w, ff = weights["w"], weights["ff"]
    main, row = weights["main"]
    return order.call(
        functools.partial(project_kernel, blocks, w, row),
        "project",
        24,
        [SMEM] + [ANY] * (blocks + 1) + [VMEM] * 3,
        [VMEM] * 5,
        rows_of(w, w, w, ff, ff),
        held(D) + [pltpu.VMEM((3 * w + ff, D), BF)] + dma(blocks, main.shape[0]),
        [index, *x_blocks, main, weights["norms"], weights["bias"], angles[1]],
    )


def attend_kernel(heads, w, row, *refs):
    index_ref, starts_ref, q_ref, k_ref, v_ref, hidden_ref, low_ref = refs[:7]
    keep_ref, send_ref, context_ref, logs_ref = refs[7:11]
    low, partial, v_turned, low_sems, out_sems = refs[11:]
    loads = loads_of_weights(low_ref, row, low, low_sems)
    start_all(loads)
    leaving = Leaving(index_ref[0], partial, keep_ref, send_ref, out_sems)
    do_attend(
        heads,
        w,
        starts_ref,
        q_ref,
        k_ref,
        v_ref,
        hidden_ref,
        low,
        loads,
        context_ref,
        logs_ref,
        v_turned,
        partial,
        leaving,
    )
    leaving.wait()


def attend(order, index, blocks, kept, weights, angles):
    w, heads, ff = weights["w"], weights["heads"], weights["ff"]
    low, row = weights["low"]
    return order.call(
        functools.partial(attend_kernel, heads, w, row),
        "attend",
        28,
        [SMEM] + [VMEM] * 5 + [ANY],
        [ANY, ANY, VMEM, VMEM],
        halves_of(blocks) + rows_of(w) + [shape((8, TOK_MB), F32)],
        [pltpu.VMEM((w + ff, D), BF)]
        + held(D)
        + [pltpu.VMEM((w, TOK_MB), BF)]
        + dma(low.shape[0], blocks),
        [index, angles[0], *kept[:4], low],
    )


def enter_kernel(blocks, w, row, *refs):
    index_ref = refs[0]
    c_refs = refs[1 : 1 + blocks]
    low_ref, slope_ref = refs[1 + blocks : 3 + blocks]
    context_ref, pre_ref, sum_ref = refs[3 + blocks : 6 + blocks]
    c_all, low, c_sems, low_sems = refs[6 + blocks :]
    loads = loads_of_weights(low_ref, row, low, low_sems)
    loads += copies_of_blocks(index_ref[0], c_refs, c_all, c_sems)
    start_all(loads)
    wait_all(loads)
    do_enter(w, c_all, low, slope_ref, context_ref, pre_ref, sum_ref)


def enter(order, index, c_blocks, kept, weights):
    w, ff = weights["w"], weights["ff"]
    low, row = weights["low"]
    blocks = len(c_blocks)
    return order.call(
        functools.partial(enter_kernel, blocks, w, row),
        "enter",
        20,
        [SMEM] + [ANY] * (blocks + 1) + [VMEM],
        [VMEM] * 3,
        rows_of(w, ff) + [shape((1, ff), F32)],
        held(D) + [pltpu.VMEM((w + ff, D), BF)] + dma(blocks, low.shape[0]),
        [index, *c_blocks, low, kept[4]],
    )


def scratch_of_backward(w):
    return [pltpu.VMEM((w, TOK_MB), BF)] + [pltpu.VMEM((TOK_MB, w), F32)] * 3


def backward_kernel(blocks, heads, w, row, *refs):
    index_ref = refs[0]
    x_refs = refs[1 : 1 + blocks]
    inner = refs[1 + blocks : 9 + blocks]
    main_ref, norms_ref, table_ref = refs[9 + blocks : 12 + blocks]
    keep_ref, send_ref, *outs = refs[12 + blocks : 17 + blocks]
    x_all, main, partial, *scratch, x_sems, main_sems, out_sems = refs[17 + blocks :]
    loads = copies_of_blocks(index_ref[0], x_refs, x_all, x_sems)
    loads += loads_of_weights(main_ref, row, main, main_sems)
    start_all(loads)
    leaving = Leaving(index_ref[0], partial, keep_ref, send_ref, out_sems)
    do_backward(
        heads, w, *inner, loads, x_all, main, norms_ref, table_ref, *outs, *scratch, partial, leaving
    )
    leaving.wait()


def backward(order, index, x_blocks, kept, entered, weights, angles):
    queries, keys, values, _, _, context, logs = kept
    blocks = len(x_blocks)
    w, heads, ff = weights["w"], weights["heads"], weights["ff"]
    main, row = weights["main"]
    return order.call(
        functools.partial(backward_kernel, blocks, heads, w, row),
        "backward",
        36,
        [SMEM] + [ANY] * blocks + [VMEM] * 8 + [ANY] + [VMEM] * 2,
        [ANY, ANY] + [VMEM] * 3,
        halves_of(blocks) + rows_of(3 * w) + [shape((8, D), F32), shape((1, 3 * w), F32)],
        held(D)
        + [pltpu.VMEM((3 * w + ff, D), BF)]
        + held(D)
        + scratch_of_backward(w)
        + dma(blocks, main.shape[0], blocks),
        [
            index,
            *x_blocks,
            angles[0],
            queries,
            keys,
            values,
            context,
            logs,
            entered[0],
            entered[1],
            main,
            weights["norms"],
            angles[1],
        ],
    )


def whole_backward_kernel(blocks, heads, w, main_row, low_row, *refs):
    index_ref = refs[0]
    c_refs = refs[1 : 1 + blocks]
    x_refs = refs[1 + blocks : 1 + 2 * blocks]
    starts_ref, q_ref, k_ref, v_ref, context_ref, logs_ref, slope_ref = refs[
        1 + 2 * blocks : 8 + 2 * blocks
    ]
    main_ref, low_ref, norms_ref, table_ref = refs[8 + 2 * blocks : 12 + 2 * blocks]
    keep_ref, send_ref, pre_ref, pre_sum_ref, *outs = refs[12 + 2 * blocks : 19 + 2 * blocks]
    c_all, x_all, main, low, partial, grad_context, *scratch = refs[19 + 2 * blocks : 29 + 2 * blocks]
    c_sems, x_sems, main_sems, low_sems, out_sems = refs[29 + 2 * blocks :]
    loads = loads_of_weights(low_ref, low_row, low, low_sems)
    loads += copies_of_blocks(index_ref[0], c_refs, c_all, c_sems)
    later = copies_of_blocks(index_ref[0], x_refs, x_all, x_sems)
    later += loads_of_weights(main_ref, main_row, main, main_sems)
    start_all(loads + later)
    leaving = Leaving(index_ref[0], partial, keep_ref, send_ref, out_sems)
    wait_all(loads)
    do_enter(w, c_all, low, slope_ref, grad_context, pre_ref, pre_sum_ref)
    do_backward(
        heads,
        w,
        starts_ref,
        q_ref,
        k_ref,
        v_ref,
        context_ref,
        logs_ref,
        grad_context,
        pre_ref,
        later,
        x_all,
        main,
        norms_ref,
        table_ref,
        *outs,
        *scratch,
        partial,
        leaving,
    )
    leaving.wait()


def whole_backward(order, index, c_blocks, x_blocks, kept, weights, angles):
    queries, keys, values, _, slope, context, logs = kept
    blocks = len(x_blocks)
    w, heads, ff = weights["w"], weights["heads"], weights["ff"]
    main, main_row = weights["main"]
    low, low_row = weights["low"]
    dp = main.shape[0]
    return order.call(
        functools.partial(whole_backward_kernel, blocks, heads, w, main_row, low_row),
        "whole_backward",
        42,
        [SMEM] + [ANY] * (2 * blocks) + [VMEM] * 7 + [ANY] * 2 + [VMEM] * 2,
        [ANY, ANY] + [VMEM] * 5,
        halves_of(blocks)
        + rows_of(ff)
        + [shape((1, ff), F32)]
        + rows_of(3 * w)
        + [shape((8, D), F32), shape((1, 3 * w), F32)],
        held(D, D)
        + [pltpu.VMEM((3 * w + ff, D), BF), pltpu.VMEM((w + ff, D), BF)]
        + held(D, w)
        + scratch_of_backward(w)
        + dma(blocks, blocks, dp, dp, blocks),
        [
            index,
            *c_blocks,
            *x_blocks,
            angles[0],
            queries,
            keys,
            values,
            context,
            logs,
            slope,
            main,
            low,
            weights["norms"],
            angles[1],
        ],
    )


def layer_kernel(blocks, heads, w, main_row, low_row, *refs):
    index_ref = refs[0]
    c_refs = refs[1 : 1 + blocks]
    x_refs = refs[1 + blocks : 1 + 2 * blocks]
    starts_ref, main_ref, low_ref, norms_ref, bias_ref, table_ref = refs[
        1 + 2 * blocks : 7 + 2 * blocks
    ]
    (y_keep, y_send, u_keep, u_send, hidden_ref, context_ref, pre_ref, pre_sum_ref, *outs) = refs[
        7 + 2 * blocks : 18 + 2 * blocks
    ]
    (c_all, x_all, main, low, y_all, u_all, q_ref, k_ref, v_ref, slope_ref, grad_context) = refs[
        18 + 2 * blocks : 29 + 2 * blocks
    ]
    logs_ref, v_turned, *scratch = refs[29 + 2 * blocks : 35 + 2 * blocks]
    c_sems, x_sems, main_sems, low_sems, y_sems, u_sems = refs[35 + 2 * blocks :]
    index = index_ref[0]
    loads = copies_of_blocks(index, x_refs, x_all, x_sems)
    loads += loads_of_weights(main_ref, main_row, main, main_sems)
    low_loads = loads_of_weights(low_ref, low_row, low, low_sems)
    c_loads = copies_of_blocks(index, c_refs, c_all, c_sems)
    start_all(loads + low_loads + c_loads)
    y_leaving = Leaving(index, y_all, y_keep, y_send, y_sems)
    u_leaving = Leaving(index, u_all, u_keep, u_send, u_sems)
    wait_all(loads)
    do_project(
        w, x_all, main, norms_ref, bias_ref, table_ref, q_ref, k_ref, v_ref, hidden_ref, slope_ref
    )
    do_attend(
        heads,
        w,
        starts_ref,
        q_ref,
        k_ref,
        v_ref,
        hidden_ref,
        low,
        low_loads,
        context_ref,
        logs_ref,
        v_turned,
        y_all,
        y_leaving,
    )
    wait_all(c_loads)
    do_enter(w, c_all, low, slope_ref, grad_context, pre_ref, pre_sum_ref)
    do_backward(
        heads,
        w,
        starts_ref,
        q_ref,
        k_ref,
        v_ref,
        context_ref,
        logs_ref,
        grad_context,
        pre_ref,
        [],
        x_all,
        main,
        norms_ref,
        table_ref,
        *outs,
        *scratch,
        u_all,
        u_leaving,
    )
    y_leaving.wait()
    u_leaving.wait()


def whole_layer(order, index, c_blocks, x_blocks, weights, angles):
    blocks = len(x_blocks)
    w, heads, ff = weights["w"], weights["heads"], weights["ff"]
    main, main_row = weights["main"]
    low, low_row = weights["low"]
    dp = main.shape[0]
    return order.call(
        functools.partial(layer_kernel, blocks, heads, w, main_row, low_row),
        "whole_layer",
        60,
        [SMEM] + [ANY] * (2 * blocks) + [VMEM] + [ANY] * 2 + [VMEM] * 3,
        [ANY] * 4 + [VMEM] * 7,
        halves_of(blocks)
        + halves_of(blocks)
        + rows_of(ff, w, ff)
        + [shape((1, ff), F32)]
        + rows_of(3 * w)
        + [shape((8, D), F32), shape((1, 3 * w), F32)],
        held(D, D)
        + [pltpu.VMEM((3 * w + ff, D), BF), pltpu.VMEM((w + ff, D), BF)]
        + held(D, D, w, w, w, ff, w)
        + [pltpu.VMEM((8, TOK_MB), F32), pltpu.VMEM((w, TOK_MB), BF)]
        + scratch_of_backward(w)
        + dma(blocks, blocks, dp, dp, blocks, blocks),
        [
            index,
            *c_blocks,
            *x_blocks,
            angles[0],
            main,
            low,
            weights["norms"],
            weights["bias"],
            angles[1],
        ],
    )


def fill(target, begin, lefts, rights):
    dp, _, share = target.shape
    size = lefts[0].shape[1]
    for j in range(dp):
        cols = slice(j * share, (j + 1) * share)
        total = sum(dot(left[...], right[:, cols], 0, 0) for left, right in zip(lefts, rights))
        target[j, begin : begin + size] = total.astype(BF)


def grads_kernel(blocks, plan, *refs):
    index_ref, norms_ref = refs[:2]
    with_cot = None in plan
    normed = sorted({which for which in plan if which is not None})
    sets = with_cot + bool(normed)
    count = MB * blocks
    c_refs = refs[2 : 2 + count * with_cot]
    x_refs = refs[2 + count * with_cot : 2 + count * sets]
    lefts = refs[2 + count * sets : 2 + count * sets + MB * len(plan)]
    out_ref, *scratch = refs[2 + count * sets + MB * len(plan) :]
    sems = scratch.pop()
    index = index_ref[0]

    def loads(source, target, which):
        copies = []
        for unit in range(MB):
            part = source[unit * blocks : (unit + 1) * blocks]
            copies += copies_of_blocks(index, part, target.at[unit], sems.at[which, unit])
        return copies

    rights = {}
    c_loads, x_loads = [], []
    if with_cot:
        rights[None] = scratch[0]
        c_loads = loads(c_refs, scratch[0], 0)
    if normed:
        x_loads = loads(x_refs, scratch[with_cot], 1)
    start_all(c_loads + x_loads)
    for i, which in enumerate(normed):
        rights[which] = scratch[with_cot + i]
    begin = 0
    wait_all(c_loads)
    for i, which in enumerate(plan):
        if which is not None and x_loads:
            wait_all(x_loads)
            x_loads = []
            raw = scratch[with_cot]
            for unit in range(MB):
                for at in chunks():
                    hat, _ = normalize(raw[unit, at])
                    for norm in normed:
                        row = hat * norms_ref[norm : norm + 1] + norms_ref[2 + norm : 3 + norm]
                        rights[norm][unit, at] = row.astype(BF)
        part = lefts[i * MB : (i + 1) * MB]
        fill(out_ref, begin, part, [rights[which].at[unit] for unit in range(MB)])
        begin += part[0].shape[1]


def weight_grads(order, index, c_blocks, x_blocks, pieces, norms, dp):
    plan = [which for _, which in pieces]
    blocks = len(x_blocks[0])
    rows = []
    if None in plan:
        rows += [block for unit in c_blocks for block in unit]
    if any(which is not None for which in plan):
        rows += [block for unit in x_blocks for block in unit]
    lefts = [left for part, _ in pieces for left in part]
    size = sum(part[0].shape[1] for part, _ in pieces)
    buffers = len(set(plan))
    return order.call(
        functools.partial(grads_kernel, blocks, plan),
        "weight_grads",
        60,
        [SMEM, VMEM] + [ANY] * len(rows) + [VMEM] * len(lefts),
        [VMEM],
        [shape((dp, size, D // dp), BF)],
        [pltpu.VMEM((MB, TOK_MB, D), BF)] * buffers
        + [pltpu.SemaphoreType.DMA((2, MB, blocks))],
        [index, norms, *rows, *lefts],
    )[0]


def pack_kernel(width, w, stage_ref, qkv_ref, up_ref, out_ref, down_ref, *refs):
    at_first = stage_ref[0] == 0
    ff = down_ref.shape[0] // 2
    mains, lows = refs[:2], refs[2:]

    def put(target, begin, size, low, high):
        target[0][begin : begin + size] = jnp.where(at_first, low, high)
        target[1][begin : begin + size] = jnp.where(at_first, high, low)

    if w != width:
        for ref in refs:
            ref[...] = jnp.zeros_like(ref)
    for i in range(3):
        turned = qkv_ref[i].T
        put(mains, i * w, width, turned[:width], turned[width:])
    turned = up_ref[...].T
    put(mains, 3 * w, ff, turned[:ff], turned[ff:])
    put(lows, 0, width, out_ref[:width], out_ref[width:])
    put(lows, w, ff, down_ref[:ff], down_ref[ff:])


def pack(order, stage, qkv, up, out, down, w):
    width = out.shape[0] // 2
    ff = down.shape[0] // 2
    share = out.shape[1]
    return order.call(
        functools.partial(pack_kernel, width, w),
        "pack",
        24,
        [SMEM] + [VMEM] * 4,
        [VMEM] * 4,
        [shape((3 * w + ff, share), BF)] * 2 + [shape((w + ff, share), BF)] * 2,
        [],
        [stage, qkv, up, out, down],
    )


def assemble_kernel(count, index_ref, *refs):
    parts, out_ref, sems = refs[: 2 * count - 1], refs[-2], refs[-1]
    index = index_ref[0]
    copies = [(index >= 0, pltpu.make_async_copy(parts[0], out_ref.at[index], sems.at[0]))]
    for hop in range(1, count):
        for sign, number in ((-1, hop), (1, count - 1 + hop)):
            place = index + sign * hop
            inside = (place >= 0) & (place < count)
            target = out_ref.at[jnp.clip(place, 0, count - 1)]
            copies.append(
                (inside, pltpu.make_async_copy(parts[number], target, sems.at[number]))
            )
    for inside, copy in copies:
        pl.when(inside)(copy.start)
    for inside, copy in copies:
        pl.when(inside)(copy.wait)


def assemble(order, index, parts):
    count = (len(parts) + 1) // 2
    return order.call(
        functools.partial(assemble_kernel, count),
        "assemble",
        4,
        [SMEM] + [ANY] * len(parts),
        [ANY],
        [shape((count, *parts[0].shape), BF)],
        dma(len(parts)),
        [index, *parts],
    )[0]


def by_stage_kernel(stage_ref, mine_ref, other_ref, *refs):
    at_first = stage_ref[0] == 0
    mine, other = mine_ref[...], other_ref[...]
    refs[-2][...] = jnp.where(at_first, mine, other)
    second = jnp.where(at_first, other, mine)
    if len(refs) > 2:
        rows = refs[0].shape[0]
        refs[-1][:rows] = refs[0][...]
        refs[-1][rows:] = second
    else:
        refs[-1][...] = second


def by_stage(order, stage, mine, other, above=()):
    rows = mine.shape[0] + sum(value.shape[0] for value in above)
    return order.call(
        by_stage_kernel,
        "by_stage",
        16,
        [SMEM] + [VMEM] * (2 + len(above)),
        [VMEM] * 2,
        [shape(mine.shape, BF), shape((rows, mine.shape[1]), BF)],
        [],
        [stage, mine, other, *above],
    )


def unpack_outer_kernel(width, w, ff, *refs):
    stage_ref, mine0, mine1, from0, from1, up_ref, out_ref, down_ref = refs
    at_first = stage_ref[0] == 0

    def halves(begin, size):
        rows = slice(begin, begin + size)
        low = jnp.where(at_first, mine0[rows], from1[rows])
        high = jnp.where(at_first, from0[rows], mine1[rows])
        return low.astype(F32), high.astype(F32)

    out_ref[:width], out_ref[width:] = halves(0, width)
    down_ref[:ff], down_ref[ff:] = halves(w, ff)
    low, high = halves(w + ff, ff)
    up_ref[:, :ff] = low.T
    up_ref[:, ff:] = high.T


def unpack_inner_kernel(width, w, stage_ref, mine0, mine1, from0, from1, qkv_ref):
    at_first = stage_ref[0] == 0
    for i in range(3):
        rows = slice(i * w, i * w + width)
        low = jnp.where(at_first, mine0[rows], from1[rows]).astype(F32)
        high = jnp.where(at_first, from0[rows], mine1[rows]).astype(F32)
        qkv_ref[i] = jnp.concatenate([low, high], axis=0).T


def unpack(kernel, order, stage, parts, out_shape):
    return order.call(
        kernel,
        "unpack",
        24,
        [SMEM] + [VMEM] * 4,
        [VMEM] * len(out_shape),
        out_shape,
        [],
        [stage, *parts],
    )


def picked_kernel(bit, flip, pairs, plains, *refs):
    index_ref = refs[0]
    out_ref, held, sems = refs[1 + pairs + plains :]
    want = (index_ref[0] >> bit) & 1
    if flip:
        want = 1 - want
    copies = []
    for i in range(pairs + plains):
        for j in range(out_ref.shape[0]):
            source = refs[1 + i].at[j, want] if i < pairs else refs[1 + i].at[j]
            copies.append(pltpu.make_async_copy(source, held.at[i, j], sems.at[i, j]))
    for copy in copies:
        copy.start()
    for copy in copies:
        copy.wait()
    total = held[0].astype(F32)
    for i in range(1, pairs + plains):
        total = total + held[i].astype(F32)
    out_ref[...] = total.astype(BF)


def picked_sum(order, where, bit, flip, pairs, plains=()):
    dims = (pairs[0].shape[0],) + pairs[0].shape[2:]
    terms = [*pairs, *plains]
    return order.call(
        functools.partial(picked_kernel, bit, flip, len(pairs), len(plains)),
        "picked_sum",
        20,
        [SMEM] + [ANY] * len(terms),
        [VMEM],
        [shape(dims, BF)],
        [
            pltpu.VMEM((len(terms), *dims), BF),
            pltpu.SemaphoreType.DMA((len(terms), dims[0])),
        ],
        [where, *terms],
    )[0]


class Sum:
    def __init__(self, where, keep, send):
        self.where = where
        self.terms = [keep, swap(send, "tensor", 0)]

    def send(self, order):
        place = lax.axis_index("tensor")
        last = bits_of("tensor") - 1
        for bit in range(1, last + 1):
            pairs = [
                term.reshape((term.shape[0] // 2, 2) + term.shape[1:]) for term in self.terms
            ]
            sent = picked_sum(order, self.where, bit, True, pairs)
            self.received = swap(sent, "tensor", bit)
            if bit < last:
                own = (place >> bit) & 1
                self.terms = [pick(pair, own, 1) for pair in pairs] + [self.received]
        self.pairs = pairs
        return self

    def cross(self, order):
        last = bits_of("tensor") - 1
        self.own = picked_sum(order, self.where, last, False, self.pairs, [self.received])[0]
        self.other = swap(self.own, "pipe", 0)
        return self


def add_rows_kernel(x_ref, own_ref, other_ref, norms_ref, out_ref):
    bias = norms_ref[4:5] + norms_ref[5:6]
    total = x_ref[...].astype(F32) + own_ref[...].astype(F32) + other_ref[...].astype(F32)
    out_ref[...] = (total + bias).astype(out_ref.dtype)


def add_rows(order, x_rows, summed, weights):
    return order.call(
        add_rows_kernel,
        "add_rows",
        12,
        [VMEM] * 4,
        [VMEM],
        [shape(x_rows.shape, BF)],
        [],
        [x_rows, summed.own, summed.other, weights["norms"]],
    )[0]


def norm_back_rows(x_ref, own_ref, other_ref, cot_ref):
    grad_hat = own_ref[...].astype(F32) + other_ref[...].astype(F32)
    hat, scale = normalize(x_ref[...])
    mean = jnp.mean(grad_hat, axis=-1, keepdims=True)
    along = jnp.mean(grad_hat * hat, axis=-1, keepdims=True)
    return cot_ref[...].astype(F32) + (grad_hat - mean - hat * along) * scale


def norm_back_kernel(x_ref, own_ref, other_ref, cot_ref, out_ref):
    out_ref[...] = norm_back_rows(x_ref, own_ref, other_ref, cot_ref).astype(BF)


def norm_back(order, x_rows, summed, cot_rows):
    return order.call(
        norm_back_kernel,
        "norm_back",
        16,
        [VMEM] * 4,
        [VMEM],
        [shape(x_rows.shape, BF)],
        [],
        [x_rows, summed.own, summed.other, cot_rows],
    )[0]


def ends_kernel(unit, stage_ref, x_ref, own_ref, other_ref, cot_ref, *refs):
    middle_ref, y_own_ref, y_other_ref, norms_ref = refs[:4]
    ends_ref, token_ref, held, sem = refs[-4:]
    token_ref[...] = jnp.zeros_like(token_ref)

    @pl.when(stage_ref[0] == 0)
    def _():
        held[...] = norm_back_rows(x_ref, own_ref, other_ref, cot_ref)

    @pl.when(stage_ref[0] != 0)
    def _():
        add_rows_kernel(middle_ref, y_own_ref, y_other_ref, norms_ref, held)

    copy = pltpu.make_async_copy(held, ends_ref.at[unit], sem)
    copy.start()
    copy.wait()


def write_ends(order, unit, stage, ends, x_rows, summed, cot_rows, middle_rows, y_sum, weights):
    args = [
        stage,
        x_rows,
        summed.own,
        summed.other,
        cot_rows,
        middle_rows,
        y_sum.own,
        y_sum.other,
        weights["norms"],
    ]
    more = {}
    if ends is not None:
        more = dict(input_output_aliases={len(args): 0})
        args.append(ends)
    return order.call(
        functools.partial(ends_kernel, unit),
        "ends",
        20,
        [SMEM] + [VMEM] * 8 + [ANY] * len(more),
        [ANY, VMEM],
        [shape((MB, *x_rows.shape), F32), shape((8, 128), F32)],
        [pltpu.VMEM(x_rows.shape, F32), pltpu.SemaphoreType.DMA],
        args,
        **more,
    )[0]


def angles_for(lengths_row, w):
    finish = jnp.cumsum(lengths_row)
    places = jnp.arange(TOK_MB, dtype=jnp.int32)
    after = (places[:, None] >= finish[None, :]).astype(jnp.int32)
    starts = jnp.sum(after * lengths_row[None, :], axis=1)
    position = (places - starts).astype(F32)
    inverse_freq = 10000.0 ** (-jnp.arange(ROT // 2, dtype=F32) * 2.0 / ROT)
    phase = position[:, None] * inverse_freq[None, :]
    cosine, sine = jnp.cos(phase), jnp.sin(phase)
    rest = jnp.zeros((TOK_MB, HD - 2 * ROT), F32)
    table = jnp.concatenate([cosine, cosine, -sine, sine, rest], axis=1)
    return starts[None], jnp.tile(table, (1, w // HD))


def body(
    boundary,
    lengths,
    gains,
    biases,
    qkv_weight,
    qkv_bias,
    out_weight,
    up_weight,
    up_bias,
    down_weight,
):
    stage = lax.axis_index("pipe")
    at_first = stage == 0
    dp = lax.axis_size("dp")
    tensor = lax.axis_size("tensor")
    index = lax.axis_index("tensor").astype(jnp.int32)[None]
    stage_word = stage.astype(jnp.int32)[None]
    order = Order()
    share = D // dp
    width = qkv_weight.shape[3] // 2
    ff = up_weight.shape[2] // 2
    heads = width // HD
    w = max(width, 128)
    cut = 3 * w + ff

    def split(mine, other):
        return jnp.where(at_first, mine, other), jnp.where(at_first, other, mine)

    def half(value, which, axis):
        size = value.shape[axis] // 2
        return lax.dynamic_slice_in_dim(value, which * size, size, axis)

    def padded(value, axis):
        if w == width:
            return value
        pads = [(0, 0)] * value.ndim
        pads[axis] = (0, w - width)
        return jnp.pad(value, pads)

    tiles = boundary[0, :, 0]
    angles = [angles_for(lengths[unit, 0], w) for unit in range(MB)]
    main_mine, main_sent, low_mine, low_sent = pack(
        order,
        stage_word,
        jnp.moveaxis(qkv_weight[0], 1, 0),
        up_weight[0],
        out_weight[0],
        down_weight[0],
        w,
    )
    main_other = swap(main_sent, "pipe", 0)
    low_other = swap(after(low_sent, main_other), "pipe", 0)
    tile_other = swap(after(tiles[0], low_other), "pipe", 0)
    order.pause()
    main_0, main_1 = by_stage(order, stage_word, main_mine, main_other)
    order.pause()
    low_0, both_1 = by_stage(order, stage_word, low_mine, low_other, [main_1])
    low_parts = line_parts(low_0, "dp")

    piece = gains.shape[2]
    small = jnp.concatenate([gains[0].reshape(-1), biases[0].reshape(-1)])
    small = gather_tensor(after(small, main_0)).reshape(-1)
    small = jnp.concatenate([small, qkv_bias[0].reshape(-1), up_bias[0]])
    small = jnp.stack(split(small, swap(small, "pipe", 0)))
    small = gather_direct(small, "dp")
    small = jnp.moveaxis(small, 0, 1).astype(F32)
    norms = small[:, :, : tensor * 6 * piece].reshape(2, dp, tensor, 6, piece)
    norms = norms.transpose(0, 3, 2, 1, 4).reshape(2, 6, D)
    rest = small[:, :, tensor * 6 * piece :]
    qkv_biases = rest[:, :, : 3 * piece].reshape(2, dp, 3, piece)
    qkv_biases = qkv_biases.transpose(0, 2, 1, 3).reshape(2, 3, 2 * width)
    qkv_biases = padded(half(qkv_biases, stage, 2), 2).reshape(2, 1, 3 * w)
    up_biases = half(rest[:, :, 3 * piece :].reshape(2, 1, 2 * ff), stage, 2)
    main_biases = jnp.concatenate([qkv_biases, up_biases], axis=2)

    layers = [
        dict(w=w, ff=ff, heads=heads, norms=norms[layer], bias=main_biases[layer])
        for layer in range(2)
    ]
    main_0 = lax.all_gather(main_0, "dp", axis=0)
    both_1 = lax.all_gather(after(both_1, main_0, *low_parts[1:]), "dp", axis=0)
    layers[0].update(main=(main_0, 0))
    layers[1].update(main=(both_1, 0), low=(both_1, cut))
    x_rows, cot_rows, x_blocks, c_blocks = [], [], [], []

    def take_tile(other):
        rows, cot = by_stage(order, stage_word, tiles[len(x_rows)], other)
        x_rows.append(rows)
        cot_rows.append(cot)
        x_blocks.append(gather_blocks(rows))

    order.hold(*[value for pair in angles for value in pair])
    order.pause()
    take_tile(tile_other)
    tile_other = swap(after(tiles[1], tile_other), "pipe", 0)
    order.hold(norms, main_biases)
    order.pause()
    take_tile(tile_other)
    order.pause()
    c_blocks.append(gather_blocks(after(cot_rows[0], x_blocks[1][tensor // 2])))

    units = range(MB)
    kept = [[None] * MB, [None] * MB]
    entered = [[None] * MB, [None] * MB]
    back = [[None] * MB, [None] * MB]

    def across(value, source):
        return lax.ppermute(value, "pipe", [(source, 1 - source)])

    class VectorSums:
        def __init__(self, cot_a, cot_b):
            own = [
                sum(jnp.sum(rows.astype(F32), axis=0) for rows in pair)
                for pair in ((cot_a, cot_b), cot_rows)
            ]
            once = jnp.where(at_first, 1.0, 0.0)
            packs = []
            for layer in range(2):
                rows = sum(back[layer][unit][1] for unit in units)[:4]
                raw = sum(back[layer][unit][2] for unit in units).reshape(3, w)[:, :width]
                pre = sum(entered[layer][unit][2] for unit in units)
                flat = [rows.reshape(-1), own[layer] * once, raw.reshape(-1), pre[0]]
                packs.append(jnp.concatenate(flat))
            self.mine = jnp.where(at_first, packs[0], packs[1])
            self.other = jnp.where(at_first, packs[1], packs[0])

        def across(self):
            self.received = swap(self.other, "pipe", 0)
            return self.received

        def along_tensor(self):
            rows = 5 * D
            norm = (self.mine[:rows] + self.received[:rows]).reshape(5, tensor, D // tensor)
            norm = norm.transpose(1, 0, 2)
            place = lax.axis_index("tensor")
            for bit in range(bits_of("tensor")):
                own = (place >> bit) & 1
                pairs = norm.reshape((norm.shape[0] // 2, 2) + norm.shape[1:])
                norm = pick(pairs, own, 1) + swap(pick(pairs, 1 - own, 1), "tensor", bit)
            norm = norm[0].reshape(5, dp, piece).transpose(1, 0, 2).reshape(dp, 5 * piece)
            low, high = split(self.mine[rows:], self.received[rows:])
            raw = jnp.stack([low[: 3 * width], high[: 3 * width]]).reshape(2, 3, width)
            raw = raw.transpose(1, 0, 2).reshape(3, dp, piece).transpose(1, 0, 2)
            pre = jnp.concatenate([low[3 * width :], high[3 * width :]]).reshape(dp, -1)
            self.parts = jnp.concatenate([norm, raw.reshape(dp, 3 * piece), pre], axis=1)
            return self.parts

        def along_dp(self):
            self.total = scatter_direct(self.parts, "dp")
            return self.total

        def results(self):
            norm = self.total[: 5 * piece].reshape(5, piece)
            raw = self.total[5 * piece : 8 * piece].reshape(3, piece)
            return norm, raw, self.total[8 * piece :]

    def run_project(layer, unit, blocks):
        kept[layer][unit] = project(order, index, blocks, layers[layer], angles[unit])

    def run_attend(layer, unit):
        keep, send, *rest = attend(
            order, index, tensor, kept[layer][unit], layers[layer], angles[unit]
        )
        kept[layer][unit] = [*kept[layer][unit], *rest]
        return Sum(index, keep, send)

    def run_backward(layer, unit, cots, blocks):
        keep, send, pre, pre_sum, *back[layer][unit] = whole_backward(
            order, index, cots, blocks, kept[layer][unit], layers[layer], angles[unit]
        )
        entered[layer][unit] = [None, pre, pre_sum]
        return Sum(index, keep, send)

    def run_layer(unit, blocks):
        y_keep, y_send, u_keep, u_send, hidden, context, pre, pre_sum, *rest = whole_layer(
            order, index, c_blocks[unit], blocks, layers[1], angles[unit]
        )
        kept[1][unit] = [None, None, None, hidden, None, context, None]
        entered[1][unit] = [None, pre, pre_sum]
        back[1][unit] = rest
        return Sum(index, y_keep, y_send), Sum(index, u_keep, u_send)

    def reduced(layer, names, cots, rows):
        lefts = dict(
            out=([kept[layer][unit][5] for unit in units], None),
            down=([kept[layer][unit][3] for unit in units], None),
            up=([entered[layer][unit][1] for unit in units], 1),
            qkv=([back[layer][unit] and back[layer][unit][0] for unit in units], 0),
        )
        pieces = [lefts[name] for name in names]
        value = weight_grads(order, index, cots, rows, pieces, layers[layer]["norms"], dp)
        return lax.psum_scatter(value, "dp", scatter_dimension=0)

    run_project(0, 0, x_blocks[0])
    dp_index = lax.axis_index("dp").astype(jnp.int32)[None]
    layers[0].update(low=(assemble(order, dp_index, low_parts), 0))
    sum_a = run_attend(0, 0)
    run_project(0, 1, x_blocks[1])
    order.hold(*c_blocks[0])
    sum_a.send(order)
    sum_b = run_attend(0, 1)
    sum_a.cross(order)
    sum_b.send(order)
    middle_a = add_rows(order, x_rows[0], sum_a, layers[0])
    blocks_a = gather_blocks(after(middle_a, sum_b.received))
    sum_b.cross(order)
    order.pause()
    middle_b = add_rows(order, x_rows[1], sum_b, layers[0])
    blocks_b = gather_blocks(after(middle_b, blocks_a[-1]))
    c_blocks.append(gather_blocks(after(cot_rows[1], blocks_b[tensor // 2])))
    middle_blocks = [blocks_a, blocks_b]

    y_a, sum_a = run_layer(0, blocks_a)
    order.pause()
    sum_a.send(order)
    run_project(1, 1, blocks_b)
    y_b = run_attend(1, 1)
    sum_a.cross(order)
    order.hold(*c_blocks[1])
    y_a.send(order)
    sum_b = run_backward(1, 1, c_blocks[1], blocks_b)
    cot_a = norm_back(order, middle_a, sum_a, cot_rows[0])
    sum_b.send(order)
    y_a.cross(order)
    grads_1 = reduced(1, ("out", "down", "up", "qkv"), c_blocks, middle_blocks)
    sum_b.cross(order)
    cot_blocks = [gather_blocks(after(cot_a, sum_b.own))]
    order.hold(y_a.other)
    order.pause()
    cot_b = norm_back(order, middle_b, sum_b, cot_rows[1])
    cot_blocks.append(gather_blocks(after(cot_b, cot_blocks[0][-1])))

    sum_a = run_backward(0, 0, cot_blocks[0], x_blocks[0])
    order.pause()
    entered[0][1] = enter(order, index, cot_blocks[1], kept[0][1], layers[0])
    sum_a.send(order)
    order.hold(grads_1)
    outer_0 = reduced(0, ("out", "down", "up"), cot_blocks, x_blocks)
    sum_a.cross(order)
    y_b.send(order)
    from_1 = across(grads_1, 0)
    keep, send, *back[0][1] = backward(
        order, index, x_blocks[1], kept[0][1], entered[0][1], layers[0], angles[1]
    )
    sum_b = Sum(index, keep, send)
    order.hold(from_1)
    y_b.cross(order)
    sum_b.send(order)
    vectors = VectorSums(cot_a, cot_b)
    order.pause()
    inner_0 = reduced(0, ("qkv",), cot_blocks, x_blocks)
    order.hold(vectors.across())
    ends = write_ends(
        order, 0, stage_word, None, x_rows[0], sum_a, cot_a, middle_a, y_a, layers[1]
    )
    order.hold(vectors.along_tensor())
    sum_b.cross(order)
    from_outer = across(outer_0, 1)
    order.hold(vectors.along_dp())
    order.pause()
    ends = write_ends(
        order, 1, stage_word, ends, x_rows[1], sum_b, cot_b, middle_b, y_b, layers[1]
    )

    inner_1, outer_1 = grads_1[w + 2 * ff :], grads_1[: w + 2 * ff]
    grad_up, grad_out, grad_down = unpack(
        functools.partial(unpack_outer_kernel, width, w, ff),
        order,
        stage_word,
        [outer_0, outer_1, from_outer, from_1[: w + 2 * ff]],
        [
            shape((share, 2 * ff), F32),
            shape((2 * width, share), F32),
            shape((2 * ff, share), F32),
        ],
    )
    grad_qkv = unpack(
        functools.partial(unpack_inner_kernel, width, w),
        order,
        stage_word,
        [inner_0, inner_1, across(inner_0, 1), from_1[w + 2 * ff :]],
        [shape((3, share, 2 * width), F32)],
    )[0]
    grad_qkv = jnp.moveaxis(grad_qkv, 0, 1)

    norm_grads, grad_qkv_bias, grad_up_bias = vectors.results()
    grad_gains = norm_grads[:2]
    grad_biases = jnp.concatenate([norm_grads[2:5], norm_grads[4:5]])
    return (
        ends[None, :, None],
        grad_gains[None],
        grad_biases[None],
        grad_qkv[None],
        grad_qkv_bias[None],
        grad_out[None],
        grad_up[None],
        grad_up_bias[None],
        grad_down[None],
    )


def solution(mesh):
    placed = (
        P("pipe", None, "dp", "tensor", None),
        P(None, "dp", None),
        P("pipe", None, ("tensor", "dp")),
        P("pipe", None, ("tensor", "dp")),
        P("pipe", "dp", None, "tensor"),
        P("pipe", None, ("tensor", "dp")),
        P("pipe", "tensor", "dp"),
        P("pipe", "dp", "tensor"),
        P("pipe", ("tensor", "dp")),
        P("pipe", "tensor", "dp"),
    )
    return jax.shard_map(
        body,
        mesh=mesh,
        in_specs=placed,
        out_specs=(placed[0],) + placed[2:],
        check_vma=False,
    )
```

time: 2320 us -> 546 us (0.24)
  waiting for transfers between devices: 1020 us -> 165 us
  matrix products: 724 us -> 0 us
  blocking collectives: 252 us -> 0 us
  Pallas kernels: 0 us -> 242 us
  other arithmetic: 161 us -> 12.6 us
  local copies, waits for them, and re-layouts: 105 us -> 37.1 us
  starting transfers between devices: 22.9 us -> 63.6 us
    dot_general x100 -> x0, matrix products: 614 us -> none  [the longest x16 113 us: attend(): jnp.einsum('hqk,khd->qhd', probs, values, preferred_element_type=jnp.floa...]
    all_gather x32 -> x2, waiting for transfers between devices: 470 us -> 0.02 us  [the longest x1 0.02 us: body(): both_1 = lax.all_gather(after(both_1, main_0, *low_parts[1:]), 'dp', axis=0)]
    reduce_scatter x16 -> x3, waiting for transfers between devices: 355 us -> 4.05 us  [reduced(): return lax.psum_scatter(value, 'dp', scatter_dimension=0)]
    pallas_call x0 -> x55, Pallas kernels: none -> 242 us  [call(): pl.pallas_call(outer, in_specs=in_specs + [ANY] * len(deps), out_specs=ou...]
    all_gather x14 -> x0, blocking collectives: 240 us -> none  [the longest x4 63 us: tick(): lax.all_gather(qkv_bias[0], 'dp', axis=1, tiled=True)]
    unnamed x10 -> x5, waiting for transfers between devices: 116 us -> 0.08 us
    sub x16 -> x0, matrix products: 110 us -> none  [the longest x8 67.9 us: attend_back(): probs = jnp.exp(scores - tops[index]) / totals[index]]
    ppermute x8 -> x73, waiting for transfers between devices: 67.6 us -> 161 us  [the longest x58 115 us: swap(): return lax.ppermute(value, axis, [(i, i ^ 1 << bit) for i in range(count)])]
  transfers between devices with their start and end apart: 59 -> 78, of which waited for: 38 -> 25; matrix products, arithmetic and copies ran while one was open for 41% -> 4% of each run, Pallas kernels for 0% -> 45%
where the time goes in v2:
time: 546 us; the launch traced here: 536 us
  Pallas kernels  242 us (44%)
  waiting for transfers between devices  165 us (30%)
  starting transfers between devices  63.6 us (12%)
  local copies, waits for them, and re-layouts  37.1 us (7%)
  between operations  16.5 us (3%)
  other arithmetic  12.6 us (2%)
    pallas_call x55, Pallas kernels, call(): pl.pallas_call(outer, in_specs=in_specs + [ANY] * len(deps), out_specs=ou...  242 us
    ppermute x58, waiting for transfers between devices, swap(): return lax.ppermute(value, axis, [(i, i ^ 1 << bit) for i in range(count)])  115 us
    ppermute x58, starting transfers between devices, swap(): return lax.ppermute(value, axis, [(i, i ^ 1 << bit) for i in range(count)])  37.9 us
    unnamed x303, local copies, waits for them, and re-layouts  28.9 us
    ppermute x3, waiting for transfers between devices, line_parts(): lax.ppermute(right[-1], axis, [(j + 1, j) for j in range(count - hop)])  19.3 us
    ppermute x3, waiting for transfers between devices, line_parts(): lax.ppermute(left[-1], axis, [(j, j + 1) for j in range(hop - 1, count -...  11.3 us
  transfers between devices with their start and end apart: 78, of which 25 were waited for; matrix products, arithmetic and copies ran while one was open for 4% of the time, Pallas kernels for 45%

profile of v2, /device:TPU:0, one launch (start us, length us, event | category | flops | bytes accessed | tf_op | source)
XLA Modules:
  0.0 536.3 jit_solution(14525013984235344386)
XLA Ops:
  11.5 3.0 collective-permute-start
  18.8 6.3 %collective-permute-done.refs_2_ = bf16[896,256]{1,0:T(8,128)(2,1)S(1)} collective-permute-done((bf16[896,256]{1,0:T(8,128)(2,1)S(1)}, bf16[896,256]{1,0:T(8,128)(2,1)S(1)}, u32[]{:S(2)}, u32[]{:S(2)}) %collective-permute-start) | collective-permute-done | bytes 458784 | tf_op jit(solution)/shard_map/ppermute | solution.py:38
  34.6 3.9 collective-permute-start.7
  41.1 3.5 collective-permute-done.8
  52.8 11.3 %collective-permute-done.16.refs_2_ = bf16[640,256]{1,0:T(8,128)(2,1)} collective-permute-done((bf16[640,256]{1,0:T(8,128)(2,1)S(1)}, bf16[640,256]{1,0:T(8,128)(2,1)}, u32[]{:S(2)}, u32[]{:S(2)}) %collective-permute-start.16) | collective-permute-done | bytes 327712 | tf_op jit(solution)/shard_map/ppermute | solution.py:77
  65.5 11.4 %collective-permute-done.19.refs_5_ = bf16[640,256]{1,0:T(8,128)(2,1)} collective-permute-done((bf16[640,256]{1,0:T(8,128)(2,1)S(1)}, bf16[640,256]{1,0:T(8,128)(2,1)}, u32[]{:S(2)}, u32[]{:S(2)}) %collective-permute-start.19) | collective-permute-done | bytes 327712 | tf_op jit(solution)/shard_map/ppermute | solution.py:78
  82.9 7.9 %collective-permute-done.20.refs_6_ = bf16[640,256]{1,0:T(8,128)(2,1)} collective-permute-done((bf16[640,256]{1,0:T(8,128)(2,1)}, bf16[640,256]{1,0:T(8,128)(2,1)}, u32[]{:S(2)}, u32[]{:S(2)}) %collective-permute-start.20) | collective-permute-done | bytes 327712 | tf_op jit(solution)/shard_map/ppermute | solution.py:78
  93.9 3.8 collective-permute-done.3.refs_2_
  101.2 14.1 %collective-permute-done.11.refs_3_.refs_16_.refs_8_ = bf16[320,1024]{1,0:T(8,128)(2,1)} collective-permute-done((bf16[320,1024]{1,0:T(8,128)(2,1)}, bf16[320,1024]{1,0:T(8,128)(2,1)}, u32[]{:S(2)}, u32[]{:S(2)}) %collective-permute-start.11) | collective-permute-done | bytes 655392 | tf_op jit(solution)/shard_map/ppermute | solution.py:38
  117.9 6.5 %project.3 = (bf16[1280,128]{1,0:T(8,128)(2,1)S(1)}, bf16[1280,128]{1,0:T(8,128)(2,1)S(1)}, bf16[1280,128]{1,0:T(8,128)(2,1)S(1)}, bf16[1280,512]{1,0:T(8,128)(2,1)S(1)}, bf16[1280,512]{1,0:T(8,128)(2,1)S(1)}) custom-call(s32[1]{0:T(128)} %bitcast.29.refs_0_, bf16[320,1024]{1,0:T(8,128)(2,1)} %get-tuple-element.109.refs_0_.refs_1_.refs_5_.refs_10_.refs_2_, ...), custom_call_target="tpu_custom_call" | custom-call | flops 99999997952 | bytes 1024 | tf_op jit(solution)/shard_map/project/pallas_call | solution.py:197
  127.6 10.2 %attend.3 = (bf16[2,320,1024]{2,1,0:T(8,128)(2,1)S(1)}, bf16[2,320,1024]{2,1,0:T(8,128)(2,1)}, bf16[1280,128]{1,0:T(8,128)(2,1)S(1)}, f32[8,1280]{1,0:T(8,128)S(1)}) custom-call(s32[1]{0:T(128)} %bitcast.29.refs_0_, s32[1,1280]{1,0:T(1,128)S(1)} %broadcast_in_dim.49.refs_1_.refs_9_, bf16[1280,128]{1,0:T(8,128)(2,1)S(1)} %get-tuple-element.112.refs_8_.refs_2_.refs_10_, ...), custom_call_target="tpu_custom_call" | custom-call | flops 99999997952 | bytes 1024 | tf_op jit(solution)/shard_map/attend/pallas_call | solution.py:197
  140.5 6.8 %project.4 = (bf16[1280,128]{1,0:T(8,128)(2,1)S(1)}, bf16[1280,128]{1,0:T(8,128)(2,1)S(1)}, bf16[1280,128]{1,0:T(8,128)(2,1)S(1)}, bf16[1280,512]{1,0:T(8,128)(2,1)S(1)}, bf16[1280,512]{1,0:T(8,128)(2,1)S(1)}) custom-call(s32[1]{0:T(128)} %bitcast.29.refs_0_, bf16[320,1024]{1,0:T(8,128)(2,1)} %get-tuple-element.111.refs_0_.refs_1_.refs_14_.refs_6_, ...), custom_call_target="tpu_custom_call" | custom-call | flops 99999997952 | bytes 1024 | tf_op jit(solution)/shard_map/project/pallas_call | solution.py:197
  147.4 3.0 picked_sum.16.refs_7_
  151.9 9.7 %attend.4 = (bf16[2,320,1024]{2,1,0:T(8,128)(2,1)S(1)}, bf16[2,320,1024]{2,1,0:T(8,128)(2,1)S(1)}, bf16[1280,128]{1,0:T(8,128)(2,1)S(1)}, f32[8,1280]{1,0:T(8,128)S(1)}) custom-call(s32[1]{0:T(128)} %bitcast.29.refs_0_, s32[1,1280]{1,0:T(1,128)S(1)} %broadcast_in_dim.50.refs_3_.refs_1_.refs_9_.refs_5_, ...), custom_call_target="tpu_custom_call" | custom-call | flops 99999997952 | bytes 1024 | tf_op jit(solution)/shard_map/attend/pallas_call | solution.py:197
  161.8 5.3 collective-permute-done.27.refs_3_
  171.4 13.3 %collective-permute-done.29.refs_2_ = bf16[320,1024]{1,0:T(8,128)(2,1)S(1)} collective-permute-done((bf16[320,1024]{1,0:T(8,128)(2,1)S(1)}, bf16[320,1024]{1,0:T(8,128)(2,1)S(1)}, u32[]{:S(2)}, u32[]{:S(2)}) %collective-permute-start.29) | collective-permute-done | bytes 655392 | tf_op jit(solution)/shard_map/ppermute | solution.py:38
  190.0 13.0 %collective-permute-done.31.refs_7_.refs_12_ = bf16[320,1024]{1,0:T(8,128)(2,1)S(1)} collective-permute-done((bf16[320,1024]{1,0:T(8,128)(2,1)S(1)}, bf16[320,1024]{1,0:T(8,128)(2,1)S(1)}, u32[]{:S(2)}, u32[]{:S(2)}) %collective-permute-start.31) | collective-permute-done | bytes 655392 | tf_op jit(solution)/shard_map/ppermute | solution.py:38
  203.0 2.4 add_rows.3.refs_15_.refs_1_.refs_5_.refs_14_.refs_0_
  207.8 33.1 %whole_layer.1 = (bf16[2,320,1024]{2,1,0:T(8,128)(2,1)}, bf16[2,320,1024]{2,1,0:T(8,128)(2,1)}, bf16[2,320,1024]{2,1,0:T(8,128)(2,1)}, bf16[2,320,1024]{2,1,0:T(...) custom-call(s32[1]{0:T(128)} %bitcast.29.refs_0_, ...), custom_call_target="tpu_custom_call" | custom-call | flops 99999997952 | bytes 1024 | tf_op jit(solution)/shard_map/whole_layer/pallas_call | solution.py:197
  243.2 15.3 %collective-permute-done.35.refs_6_.refs_3_.refs_8_ = bf16[320,1024]{1,0:T(8,128)(2,1)} collective-permute-done((bf16[320,1024]{1,0:T(8,128)(2,1)}, bf16[320,1024]{1,0:T(8,128)(2,1)}, u32[]{:S(2)}, u32[]{:S(2)}) %collective-permute-start.35) | collective-permute-done | bytes 655392 | tf_op jit(solution)/shard_map/ppermute | solution.py:38
  261.2 6.5 %project.5 = (bf16[1280,128]{1,0:T(8,128)(2,1)S(1)}, bf16[1280,128]{1,0:T(8,128)(2,1)S(1)}, bf16[1280,128]{1,0:T(8,128)(2,1)S(1)}, bf16[1280,512]{1,0:T(8,128)(2,1)S(1)}, bf16[1280,512]{1,0:T(8,128)(2,1)S(1)}) custom-call(s32[1]{0:T(128)} %bitcast.29.refs_0_, bf16[320,1024]{1,0:T(8,128)(2,1)} %add_rows.3.refs_15_.refs_1_.refs_5_.refs_14_.refs_0_, ...), custom_call_target="tpu_custom_call" | custom-call | flops 99999997952 | bytes 1024 | tf_op jit(solution)/shard_map/project/pallas_call | solution.py:197
  268.8 10.4 %attend.5 = (bf16[2,320,1024]{2,1,0:T(8,128)(2,1)S(1)}, bf16[2,320,1024]{2,1,0:T(8,128)(2,1)}, bf16[1280,128]{1,0:T(8,128)(2,1)S(1)}, f32[8,1280]{1,0:T(8,128)S(1)}) custom-call(s32[1]{0:T(128)} %bitcast.29.refs_0_, s32[1,1280]{1,0:T(1,128)S(1)} %broadcast_in_dim.50.refs_3_.refs_1_.refs_9_.refs_5_, ...), custom_call_target="tpu_custom_call" | custom-call | flops 99999997952 | bytes 1024 | tf_op jit(solution)/shard_map/attend/pallas_call | solution.py:197
  279.4 3.0 picked_sum.21.refs_3_
  283.9 2.5 picked_sum.22.refs_20_
  288.0 19.5 %whole_backward.2 = (bf16[2,320,1024]{2,1,0:T(8,128)(2,1)S(1)}, bf16[2,320,1024]{2,1,0:T(8,128)(2,1)S(1)}, bf16[1280,512]{1,0:T(8,128)(2,1)}, f32[1,512]{1,0:T(1...) custom-call(s32[1]{0:T(128)} %bitcast.29.refs_0_, ...), custom_call_target="tpu_custom_call" | custom-call | flops 99999997952 | bytes 1024 | tf_op jit(solution)/shard_map/whole_backward/pallas_call | solution.py:197
  309.6 3.3 norm_back.2.refs_3_.refs_1_.refs_2_.refs_4_
  316.8 2.6 picked_sum.24.refs_26_
  320.2 18.7 %weight_grads.3.refs_4_ = bf16[4,1536,256]{2,1,0:T(8,128)(2,1)} custom-call(s32[1]{0:T(128)} %bitcast.29.refs_0_, f32[6,1024]{1,0:T(8,128)} %squeeze.106.refs_12_.refs_6_.refs_18_.refs_1_.refs_8_, bf16[320,1024]{1,0:T(8,128)(2,1)} %get-tuple-element.124.refs_4_.refs_1_.refs_3_.refs_2_, bf16[320,1024]{1,0:T(8,128)(2,1)} %collective-permute-done.23.refs_5_.refs_2_.refs_3_, ...), custom_call_target="tpu_custom_call" | custom-call | flops 99999997952 | bytes 1024 | tf_op jit(solution)/shard_map/weight_grads/pallas_call | solution.py:197
  348.1 15.0 %collective-permute-done.49.refs_3_.refs_4_ = bf16[320,1024]{1,0:T(8,128)(2,1)S(1)} collective-permute-done((bf16[320,1024]{1,0:T(8,128)(2,1)}, bf16[320,1024]{1,0:T(8,128)(2,1)S(1)}, u32[]{:S(2)}, u32[]{:S(2)}) %collective-permute-start.49) | collective-permute-done | bytes 655392 | tf_op jit(solution)/shard_map/ppermute | solution.py:38
  363.1 3.3 norm_back.3.refs_20_.refs_1_.refs_6_.refs_4_
  369.8 18.8 %whole_backward.3 = (bf16[2,320,1024]{2,1,0:T(8,128)(2,1)S(1)}, bf16[2,320,1024]{2,1,0:T(8,128)(2,1)S(1)}, bf16[1280,512]{1,0:T(8,128)(2,1)}, f32[1,512]{1,0:T(1...) custom-call(s32[1]{0:T(128)} %bitcast.29.refs_0_, ...), custom_call_target="tpu_custom_call" | custom-call | flops 99999997952 | bytes 1024 | tf_op jit(solution)/shard_map/whole_backward/pallas_call | solution.py:197
  391.5 3.9 enter.1
  398.7 4.0 reduce-scatter.4.cloned.1.call-done
  402.7 4.3 collective-permute-start.60
  407.0 15.7 %weight_grads.4.refs_4_ = bf16[4,1152,256]{2,1,0:T(8,128)(2,1)} custom-call(s32[1]{0:T(128)} %bitcast.29.refs_0_, f32[6,1024]{1,0:T(8,128)} %copy-done.14, bf16[320,1024]{1,0:T(8,128)(2,1)} %norm_back.2.refs_3_.refs_1_.refs_2_.refs_4_, bf16[320,1024]{1,0:T(8,128)(2,1)} %collective-permute-done.54.refs_2_.refs_3_, bf16[320,1024]{1,0:T(8,128)(2,1)} %copy-done.52, ...), custom_call_target="tpu_custom_call" | custom-call | flops 99999997952 | bytes 1024 | tf_op jit(solution)/shard_map/weight_grads/pallas_call | solution.py:197
  428.9 2.5 picked_sum.28.refs_16_
  433.1 12.7 %backward.1 = (bf16[2,320,1024]{2,1,0:T(8,128)(2,1)S(1)}, bf16[2,320,1024]{2,1,0:T(8,128)(2,1)S(1)}, bf16[1280,384]{1,0:T(8,128)(2,1)S(1)}, f32[8,1024]{1,0:T(8,128)S(1)}, f32[1,384]{1,0:T(1,128)S(1)}) custom-call(s32[1]{0:T(128)} %bitcast.29.refs_0_, bf16[320,1024]{1,0:T(8,128)(2,1)} %get-tuple-element.111.refs_0_.refs_1_.refs_14_.refs_6_, ...), custom_call_target="tpu_custom_call" | custom-call | flops 99999997952 | bytes 1024 | tf_op jit(solution)/shard_map/backward/pallas_call | solution.py:197
  448.1 3.8 collective-permute-done.63.refs_10_
  454.1 2.8 collective-permute-done.65
  457.3 2.6 collective-permute-start.70
  462.5 3.4 collective-permute-done.69
  469.9 2.4 picked_sum.29.refs_3_
  478.7 9.8 %weight_grads.5.refs_9_ = bf16[4,384,256]{2,1,0:T(8,128)(2,1)} custom-call(s32[1]{0:T(128)} %bitcast.29.refs_0_, f32[6,1024]{1,0:T(8,128)} %copy-done.14, bf16[320,1024]{1,0:T(8,128)(2,1)} %get-tuple-element.109.refs_0_.refs_1_.refs_5_.refs_10_.refs_2_, bf16[320,1024]{1,0:T(8,128)(2,1)} %collective-permute-done.13.refs_2_.refs_6_.refs_11_.refs_3_, ...), custom_call_target="tpu_custom_call" | custom-call | flops 99999997952 | bytes 1024 | tf_op jit(solution)/shard_map/weight_grads/pallas_call | solution.py:197
  489.7 4.2 ends.2
  497.2 16.3 %collective-permute-done.66.refs_3_ = bf16[320,1024]{1,0:T(8,128)(2,1)S(1)} collective-permute-done((bf16[320,1024]{1,0:T(8,128)(2,1)S(1)}, bf16[320,1024]{1,0:T(8,128)(2,1)S(1)}, u32[]{:S(2)}, u32[]{:S(2)}) %collective-permute-start.66) | collective-permute-done | bytes 655392 | tf_op jit(solution)/shard_map/ppermute | solution.py:38
  513.5 3.9 ends.3
  518.7 6.1 %collective-permute-done.72.refs_3_ = bf16[1152,256]{1,0:T(8,128)(2,1)} collective-permute-done((bf16[1152,256]{1,0:T(8,128)(2,1)}, bf16[1152,256]{1,0:T(8,128)(2,1)}, u32[]{:S(2)}, u32[]{:S(2)}) %collective-permute-start.72) | collective-permute-done | bytes 589856 | tf_op jit(solution)/shard_map/ppermute | solution.py:1269
  524.8 2.7 unpack.2
  (587 shorter events, 131.2 us)
Async XLA Ops:
  7.2 109.2 %all-gather.5.cloned.1.call-start = ((), (), s32[]{:S(2)}) async-start(), calls=%async_computation.6 | async-start | bytes 2293760 | tf_op jit(solution)/shard_map/all_gather | solution.py:1241
  38.5 168.5 %all-gather.7.cloned.1.call-start = ((), (), s32[]{:S(2)}) async-start(), calls=%async_computation.7 | async-start | bytes 3932160 | tf_op jit(solution)/shard_map/all_gather | solution.py:1242
  50.9 26.0 %collective-permute-start.19 = (bf16[640,256]{1,0:T(8,128)(2,1)S(1)}, bf16[640,256]{1,0:T(8,128)(2,1)}, u32[]{:S(2)}, u32[]{:S(2)}) collective-permute-start(bf16[640,256]{1,0:T(8,128)(2,1)S(1)} %get-tuple-element.108.refs_0_.refs_1_), channel_id=1, source_target_pairs={{1,0},{2,1},{3,2},{5,4},{6,5},{7,6},{9,8},{10,9},{11,10},{13,12},{... | collective-permute-start | bytes 983048 | tf_op jit(solution)/shard_map/ppermute | solution.py:78
  52.2 26.0 %collective-permute-start.2 = (bf16[320,1024]{1,0:T(8,128)(2,1)S(1)}, bf16[320,1024]{1,0:T(8,128)(2,1)S(1)}, u32[]{:S(2)}, u32[]{:S(2)}) collective-permute-start(bf16[320,1024]{1,0:T(8,128)(2,1)S(1)} %copy-done.4), channel_id=1, source_target_pairs={{0,16},{16,0},{1,17},{17,1},{2,18},{18,2},{3,19},{19,3},{4,20},{20... | collective-permute-start | bytes 1966088 | tf_op jit(solution)/shard_map/ppermute | solution.py:38
  64.1 17.4 %collective-permute-start.17 = (bf16[640,256]{1,0:T(8,128)(2,1)}, bf16[640,256]{1,0:T(8,128)(2,1)}, u32[]{:S(2)}, u32[]{:S(2)}) collective-permute-start(bf16[640,256]{1,0:T(8,128)(2,1)} %collective-permute-done.16.refs_2_), channel_id=1, source_target_pairs={{1,2},{2,3},{5,6},{6,7},{9,10},{10,11},{13,14},{14,15},{17,18},{18... | collective-permute-start | bytes 983048 | tf_op jit(solution)/shard_map/ppermute | solution.py:77
  79.4 36.0 %collective-permute-start.13 = (bf16[320,1024]{1,0:T(8,128)(2,1)}, bf16[320,1024]{1,0:T(8,128)(2,1)}, u32[]{:S(2)}, u32[]{:S(2)}) collective-permute-start(bf16[320,1024]{1,0:T(8,128)(2,1)} %get-tuple-element.109.refs_0_.refs_1_.refs_5_.refs_10_.refs_2_), channel_id=1, source_target_pairs={{0,4},{4,0},{8,12},{12,8},{1,5},{5,1},{9,13},{13,9},{2,6},{6,2},{1... | collective-permute-start | bytes 1966088 | tf_op jit(solution)/shard_map/ppermute | solution.py:38
  79.4 20.0 %collective-permute-start.14 = (bf16[320,1024]{1,0:T(8,128)(2,1)}, bf16[320,1024]{1,0:T(8,128)(2,1)}, u32[]{:S(2)}, u32[]{:S(2)}) collective-permute-start(bf16[320,1024]{1,0:T(8,128)(2,1)} %get-tuple-element.109.refs_0_.refs_1_.refs_5_.refs_10_.refs_2_), channel_id=1, source_target_pairs={{0,8},{4,12},{8,0},{12,4},{1,9},{5,13},{9,1},{13,5},{2,10},{6,14},... | collective-permute-start | bytes 1966088 | tf_op jit(solution)/shard_map/ppermute | solution.py:38
  80.9 16.9 %collective-permute-start.3 = (bf16[320,1024]{1,0:T(8,128)(2,1)S(1)}, bf16[320,1024]{1,0:T(8,128)(2,1)S(1)}, u32[]{:S(2)}, u32[]{:S(2)}) collective-permute-start(bf16[320,1024]{1,0:T(8,128)(2,1)S(1)} %copy-done.3), channel_id=1, source_target_pairs={{0,16},{16,0},{1,17},{17,1},{2,18},{18,2},{3,19},{19,3},{4,20},{20... | collective-permute-start | bytes 1966088 | tf_op jit(solution)/shard_map/ppermute | solution.py:38
  81.5 44.0 %collective-permute-start.18 = (bf16[640,256]{1,0:T(8,128)(2,1)}, bf16[640,256]{1,0:T(8,128)(2,1)}, u32[]{:S(2)}, u32[]{:S(2)}) collective-permute-start(bf16[640,256]{1,0:T(8,128)(2,1)} %collective-permute-done.17.refs_3_), channel_id=1, source_target_pairs={{2,3},{6,7},{10,11},{14,15},{18,19},{22,23},{26,27},{30,31}} | collective-permute-start | bytes 983048 | tf_op jit(solution)/shard_map/ppermute | solution.py:77
  90.8 34.8 %collective-permute-start.21 = (bf16[640,256]{1,0:T(8,128)(2,1)}, bf16[640,256]{1,0:T(8,128)(2,1)}, u32[]{:S(2)}, u32[]{:S(2)}) collective-permute-start(bf16[640,256]{1,0:T(8,128)(2,1)} %collective-permute-done.20.refs_6_), channel_id=1, source_target_pairs={{1,0},{5,4},{9,8},{13,12},{17,16},{21,20},{25,24},{29,28}} | collective-permute-start | bytes 983048 | tf_op jit(solution)/shard_map/ppermute | solution.py:78
  98.9 16.5 %collective-permute-start.11 = (bf16[320,1024]{1,0:T(8,128)(2,1)}, bf16[320,1024]{1,0:T(8,128)(2,1)}, u32[]{:S(2)}, u32[]{:S(2)}) collective-permute-start(bf16[320,1024]{1,0:T(8,128)(2,1)} %get-tuple-element.111.refs_0_.refs_1_.refs_14_.refs_6_), channel_id=1, source_target_pairs={{0,8},{4,12},{8,0},{12,4},{1,9},{5,13},{9,1},{13,5},{2,10},{6,14},... | collective-permute-start | bytes 1966088 | tf_op jit(solution)/shard_map/ppermute | solution.py:38
  99.4 16.4 %collective-permute-start.15 = (bf16[320,1024]{1,0:T(8,128)(2,1)}, bf16[320,1024]{1,0:T(8,128)(2,1)S(1)}, u32[]{:S(2)}, u32[]{:S(2)}) collective-permute-start(bf16[320,1024]{1,0:T(8,128)(2,1)} %collective-permute-done.14.refs_3_.refs_7_.refs_12_.refs_4_), channel_id=1, source_target_pairs={{0,4},{4,0},{8,12},{12,8},{1,5},{5,1},{9,13},{13,9},{2,6},{6,2},{1... | collective-permute-start | bytes 1966088 | tf_op jit(solution)/shard_map/ppermute | solution.py:38
  115.3 25.1 %collective-permute-start.10 = (bf16[320,1024]{1,0:T(8,128)(2,1)}, bf16[320,1024]{1,0:T(8,128)(2,1)}, u32[]{:S(2)}, u32[]{:S(2)}) collective-permute-start(bf16[320,1024]{1,0:T(8,128)(2,1)} %get-tuple-element.111.refs_0_.refs_1_.refs_14_.refs_6_), channel_id=1, source_target_pairs={{0,4},{4,0},{8,12},{12,8},{1,5},{5,1},{9,13},{13,9},{2,6},{6,2},{1... | collective-permute-start | bytes 1966088 | tf_op jit(solution)/shard_map/ppermute | solution.py:38
  115.4 32.0 %collective-permute-start.23 = (bf16[320,1024]{1,0:T(8,128)(2,1)}, bf16[320,1024]{1,0:T(8,128)(2,1)}, u32[]{:S(2)}, u32[]{:S(2)}) collective-permute-start(bf16[320,1024]{1,0:T(8,128)(2,1)} %get-tuple-element.124.refs_4_.refs_1_.refs_3_.refs_2_), channel_id=1, source_target_pairs={{0,4},{4,0},{8,12},{12,8},{1,5},{5,1},{9,13},{13,9},{2,6},{6,2},{1... | collective-permute-start | bytes 1966088 | tf_op jit(solution)/shard_map/ppermute | solution.py:38
  115.9 24.0 %collective-permute-start.24 = (bf16[320,1024]{1,0:T(8,128)(2,1)}, bf16[320,1024]{1,0:T(8,128)(2,1)}, u32[]{:S(2)}, u32[]{:S(2)}) collective-permute-start(bf16[320,1024]{1,0:T(8,128)(2,1)} %get-tuple-element.124.refs_4_.refs_1_.refs_3_.refs_2_), channel_id=1, source_target_pairs={{0,8},{4,12},{8,0},{12,4},{1,9},{5,13},{9,1},{13,5},{2,10},{6,14},... | collective-permute-start | bytes 1966088 | tf_op jit(solution)/shard_map/ppermute | solution.py:38
  139.6 263.1 %reduce-scatter.4.cloned.1.call-start = ((), (), s32[]{:S(2)}) async-start(), calls=%async_computation.3 | async-start | bytes 3932160 | tf_op jit(solution)/shard_map/reduce_scatter | solution.py:1353
  150.4 16.7 %collective-permute-start.27 = (bf16[1,320,1024]{2,1,0:T(8,128)(2,1)S(1)}, bf16[1,320,1024]{2,1,0:T(8,128)(2,1)S(1)}, u32[]{:S(2)}, u32[]{:S(2)}) collective-permute-start(bf16[1,320,1024]{2,1,0:T(8,128)(2,1)S(1)} %picked_sum.16.refs_7_), channel_id=1, source_target_pairs={{0,8},{4,12},{8,0},{12,4},{1,9},{5,13},{9,1},{13,5},{2,10},{6,14},... | collective-permute-start | bytes 1966088 | tf_op jit(solution)/shard_map/ppermute | solution.py:38
  168.7 16.0 %collective-permute-start.29 = (bf16[320,1024]{1,0:T(8,128)(2,1)S(1)}, bf16[320,1024]{1,0:T(8,128)(2,1)S(1)}, u32[]{:S(2)}, u32[]{:S(2)}) collective-permute-start(bf16[320,1024]{1,0:T(8,128)(2,1)S(1)} %bitcast.158), channel_id=1, source_target_pairs={{0,16},{16,0},{1,17},{17,1},{2,18},{18,2},{3,19},{19,3},{4,20},{20... | collective-permute-start | bytes 1966088 | tf_op jit(solution)/shard_map/ppermute | solution.py:38
  169.9 16.1 %collective-permute-start.28 = (bf16[1,320,1024]{2,1,0:T(8,128)(2,1)S(1)}, bf16[1,320,1024]{2,1,0:T(8,128)(2,1)S(1)}, u32[]{:S(2)}, u32[]{:S(2)}) collective-permute-start(bf16[1,320,1024]{2,1,0:T(8,128)(2,1)S(1)} %picked_sum.18.refs_4_), channel_id=1, source_target_pairs={{0,8},{4,12},{8,0},{12,4},{1,9},{5,13},{9,1},{13,5},{2,10},{6,14},... | collective-permute-start | bytes 1966088 | tf_op jit(solution)/shard_map/ppermute | solution.py:38
  190.0 17.0 %collective-permute-start.39 = (bf16[320,1024]{1,0:T(8,128)(2,1)S(1)}, bf16[320,1024]{1,0:T(8,128)(2,1)S(1)}, u32[]{:S(2)}, u32[]{:S(2)}) collective-permute-start(bf16[320,1024]{1,0:T(8,128)(2,1)S(1)} %add_rows.2.refs_4_.refs_5_.refs_0_.refs_10_), channel_id=1, source_target_pairs={{0,4},{4,0},{8,12},{12,8},{1,5},{5,1},{9,13},{13,9},{2,6},{6,2},{1... | collective-permute-start | bytes 1966088 | tf_op jit(solution)/shard_map/ppermute | solution.py:38
  205.5 36.0 %collective-permute-start.33 = (bf16[320,1024]{1,0:T(8,128)(2,1)}, bf16[320,1024]{1,0:T(8,128)(2,1)S(1)}, u32[]{:S(2)}, u32[]{:S(2)}) collective-permute-start(bf16[320,1024]{1,0:T(8,128)(2,1)} %add_rows.3.refs_15_.refs_1_.refs_5_.refs_14_.refs_0_), channel_id=1, source_target_pairs={{0,8},{4,12},{8,0},{12,4},{1,9},{5,13},{9,1},{13,5},{2,10},{6,14},... | collective-permute-start | bytes 1966088 | tf_op jit(solution)/shard_map/ppermute | solution.py:38
  207.0 53.6 %collective-permute-start.37 = (bf16[320,1024]{1,0:T(8,128)(2,1)}, bf16[320,1024]{1,0:T(8,128)(2,1)}, u32[]{:S(2)}, u32[]{:S(2)}) collective-permute-start(bf16[320,1024]{1,0:T(8,128)(2,1)} %add_rows.3.refs_15_.refs_1_.refs_5_.refs_14_.refs_0_), channel_id=1, source_target_pairs={{0,4},{4,0},{8,12},{12,8},{1,5},{5,1},{9,13},{13,9},{2,6},{6,2},{1... | collective-permute-start | bytes 1966088 | tf_op jit(solution)/shard_map/ppermute | solution.py:38
  240.9 17.6 %collective-permute-start.40 = (bf16[2,320,1024]{2,1,0:T(8,128)(2,1)}, bf16[2,320,1024]{2,1,0:T(8,128)(2,1)S(1)}, u32[]{:S(2)}, u32[]{:S(2)}) collective-permute-start(bf16[2,320,1024]{2,1,0:T(8,128)(2,1)} %get-tuple-element.136), channel_id=1, source_target_pairs={{0,4},{4,0},{8,12},{12,8},{1,5},{5,1},{9,13},{13,9},{2,6},{6,2},{1... | collective-permute-start | bytes 3932168 | tf_op jit(solution)/shard_map/ppermute | solution.py:38
  241.5 17.0 %collective-permute-start.35 = (bf16[320,1024]{1,0:T(8,128)(2,1)}, bf16[320,1024]{1,0:T(8,128)(2,1)}, u32[]{:S(2)}, u32[]{:S(2)}) collective-permute-start(bf16[320,1024]{1,0:T(8,128)(2,1)} %get-tuple-element.132.refs_4_.refs_1_.refs_6_.refs_3_), channel_id=1, source_target_pairs={{0,8},{4,12},{8,0},{12,4},{1,9},{5,13},{9,1},{13,5},{2,10},{6,14},... | collective-permute-start | bytes 1966088 | tf_op jit(solution)/shard_map/ppermute | solution.py:38
  242.7 41.1 %collective-permute-start.41 = (bf16[2,320,1024]{2,1,0:T(8,128)(2,1)}, bf16[2,320,1024]{2,1,0:T(8,128)(2,1)}, u32[]{:S(2)}, u32[]{:S(2)}) collective-permute-start(bf16[2,320,1024]{2,1,0:T(8,128)(2,1)} %get-tuple-element.146), channel_id=1, source_target_pairs={{0,4},{4,0},{8,12},{12,8},{1,5},{5,1},{9,13},{13,9},{2,6},{6,2},{1... | collective-permute-start | bytes 3932168 | tf_op jit(solution)/shard_map/ppermute | solution.py:38
  242.7 41.1 %collective-permute-start.34 = (bf16[320,1024]{1,0:T(8,128)(2,1)}, bf16[320,1024]{1,0:T(8,128)(2,1)}, u32[]{:S(2)}, u32[]{:S(2)}) collective-permute-start(bf16[320,1024]{1,0:T(8,128)(2,1)} %get-tuple-element.132.refs_4_.refs_1_.refs_6_.refs_3_), channel_id=1, source_target_pairs={{0,4},{4,0},{8,12},{12,8},{1,5},{5,1},{9,13},{13,9},{2,6},{6,2},{1... | collective-permute-start | bytes 1966088 | tf_op jit(solution)/shard_map/ppermute | solution.py:38
  258.6 25.3 %collective-permute-start.36 = (bf16[320,1024]{1,0:T(8,128)(2,1)}, bf16[320,1024]{1,0:T(8,128)(2,1)}, u32[]{:S(2)}, u32[]{:S(2)}) collective-permute-start(bf16[320,1024]{1,0:T(8,128)(2,1)} %collective-permute-done.35.refs_6_.refs_3_.refs_8_), channel_id=1, source_target_pairs={{0,4},{4,0},{8,12},{12,8},{1,5},{5,1},{9,13},{13,9},{2,6},{6,2},{1... | collective-permute-start | bytes 1966088 | tf_op jit(solution)/shard_map/ppermute | solution.py:38
  260.5 18.8 %collective-permute-start.42 = (bf16[1,320,1024]{2,1,0:T(8,128)(2,1)}, bf16[1,320,1024]{2,1,0:T(8,128)(2,1)}, u32[]{:S(2)}, u32[]{:S(2)}) collective-permute-start(bf16[1,320,1024]{2,1,0:T(8,128)(2,1)} %picked_sum.20.refs_9_), channel_id=1, source_target_pairs={{0,8},{4,12},{8,0},{12,4},{1,9},{5,13},{9,1},{13,5},{2,10},{6,14},... | collective-permute-start | bytes 1966088 | tf_op jit(solution)/shard_map/ppermute | solution.py:38
  279.3 149.5 %collective-permute-start.55 = (bf16[2,320,1024]{2,1,0:T(8,128)(2,1)}, bf16[2,320,1024]{2,1,0:T(8,128)(2,1)}, u32[]{:S(2)}, u32[]{:S(2)}) collective-permute-start(bf16[2,320,1024]{2,1,0:T(8,128)(2,1)} %get-tuple-element.165), channel_id=1, source_target_pairs={{0,4},{4,0},{8,12},{12,8},{1,5},{5,1},{9,13},{13,9},{2,6},{6,2},{1... | collective-permute-start | bytes 3932168 | tf_op jit(solution)/shard_map/ppermute | solution.py:38
  282.5 27.1 %collective-permute-start.44 = (bf16[320,1024]{1,0:T(8,128)(2,1)}, bf16[320,1024]{1,0:T(8,128)(2,1)}, u32[]{:S(2)}, u32[]{:S(2)}) collective-permute-start(bf16[320,1024]{1,0:T(8,128)(2,1)} %bitcast.47.refs_1_), channel_id=1, source_target_pairs={{0,16},{16,0},{1,17},{17,1},{2,18},{18,2},{3,19},{19,3},{4,20},{20... | collective-permute-start | bytes 1966088 | tf_op jit(solution)/shard_map/ppermute | solution.py:38
  286.4 30.4 %collective-permute-start.46 = (bf16[1,320,1024]{2,1,0:T(8,128)(2,1)}, bf16[1,320,1024]{2,1,0:T(8,128)(2,1)}, u32[]{:S(2)}, u32[]{:S(2)}) collective-permute-start(bf16[1,320,1024]{2,1,0:T(8,128)(2,1)} %picked_sum.22.refs_20_), channel_id=1, source_target_pairs={{0,8},{4,12},{8,0},{12,4},{1,9},{5,13},{9,1},{13,5},{2,10},{6,14},... | collective-permute-start | bytes 1966088 | tf_op jit(solution)/shard_map/ppermute | solution.py:38
  316.1 23.0 %collective-permute-start.45 = (bf16[1,320,1024]{2,1,0:T(8,128)(2,1)}, bf16[1,320,1024]{2,1,0:T(8,128)(2,1)}, u32[]{:S(2)}, u32[]{:S(2)}) collective-permute-start(bf16[1,320,1024]{2,1,0:T(8,128)(2,1)} %picked_sum.23.refs_4_), channel_id=1, source_target_pairs={{0,8},{4,12},{8,0},{12,4},{1,9},{5,13},{9,1},{13,5},{2,10},{6,14},... | collective-permute-start | bytes 1966088 | tf_op jit(solution)/shard_map/ppermute | solution.py:38
  319.4 28.5 %collective-permute-start.48 = (bf16[320,1024]{1,0:T(8,128)(2,1)}, bf16[320,1024]{1,0:T(8,128)(2,1)}, u32[]{:S(2)}, u32[]{:S(2)}) collective-permute-start(bf16[320,1024]{1,0:T(8,128)(2,1)} %bitcast.49.refs_6_), channel_id=1, source_target_pairs={{0,16},{16,0},{1,17},{17,1},{2,18},{18,2},{3,19},{19,3},{4,20},{20... | collective-permute-start | bytes 1966088 | tf_op jit(solution)/shard_map/ppermute | solution.py:38
  338.9 156.9 %reduce-scatter.8.cloned.1.call-start = ((), (), s32[]{:S(2)}) async-start(), calls=%async_computation.5 | async-start | bytes 2949120 | tf_op jit(solution)/shard_map/reduce_scatter | solution.py:1353
  345.2 17.9 %collective-permute-start.47 = (bf16[320,1024]{1,0:T(8,128)(2,1)S(1)}, bf16[320,1024]{1,0:T(8,128)(2,1)S(1)}, u32[]{:S(2)}, u32[]{:S(2)}) collective-permute-start(bf16[320,1024]{1,0:T(8,128)(2,1)S(1)} %bitcast.154), channel_id=1, source_target_pairs={{0,16},{16,0},{1,17},{17,1},{2,18},{18,2},{3,19},{19,3},{4,20},{20... | collective-permute-start | bytes 1966088 | tf_op jit(solution)/shard_map/ppermute | solution.py:38
  346.5 16.5 %collective-permute-start.49 = (bf16[320,1024]{1,0:T(8,128)(2,1)}, bf16[320,1024]{1,0:T(8,128)(2,1)S(1)}, u32[]{:S(2)}, u32[]{:S(2)}) collective-permute-start(bf16[320,1024]{1,0:T(8,128)(2,1)} %norm_back.2.refs_3_.refs_1_.refs_2_.refs_4_), channel_id=1, source_target_pairs={{0,8},{4,12},{8,0},{12,4},{1,9},{5,13},{9,1},{13,5},{2,10},{6,14},... | collective-permute-start | bytes 1966088 | tf_op jit(solution)/shard_map/ppermute | solution.py:38
  348.0 21.8 %collective-permute-start.54 = (bf16[320,1024]{1,0:T(8,128)(2,1)}, bf16[320,1024]{1,0:T(8,128)(2,1)}, u32[]{:S(2)}, u32[]{:S(2)}) collective-permute-start(bf16[320,1024]{1,0:T(8,128)(2,1)} %norm_back.2.refs_3_.refs_1_.refs_2_.refs_4_), channel_id=1, source_target_pairs={{0,4},{4,0},{8,12},{12,8},{1,5},{5,1},{9,13},{13,9},{2,6},{6,2},{1... | collective-permute-start | bytes 1966088 | tf_op jit(solution)/shard_map/ppermute | solution.py:38
  368.2 21.6 %collective-permute-start.51 = (bf16[320,1024]{1,0:T(8,128)(2,1)}, bf16[320,1024]{1,0:T(8,128)(2,1)}, u32[]{:S(2)}, u32[]{:S(2)}) collective-permute-start(bf16[320,1024]{1,0:T(8,128)(2,1)} %norm_back.3.refs_20_.refs_1_.refs_6_.refs_4_), channel_id=1, source_target_pairs={{0,4},{4,0},{8,12},{12,8},{1,5},{5,1},{9,13},{13,9},{2,6},{6,2},{1... | collective-permute-start | bytes 1966088 | tf_op jit(solution)/shard_map/ppermute | solution.py:38
  368.5 20.2 %collective-permute-start.52 = (bf16[320,1024]{1,0:T(8,128)(2,1)}, bf16[320,1024]{1,0:T(8,128)(2,1)S(1)}, u32[]{:S(2)}, u32[]{:S(2)}) collective-permute-start(bf16[320,1024]{1,0:T(8,128)(2,1)} %norm_back.3.refs_20_.refs_1_.refs_6_.refs_4_), channel_id=1, source_target_pairs={{0,8},{4,12},{8,0},{12,4},{1,9},{5,13},{9,1},{13,5},{2,10},{6,14},... | collective-permute-start | bytes 1966088 | tf_op jit(solution)/shard_map/ppermute | solution.py:38
  397.2 25.7 %collective-permute-start.57 = (bf16[1,320,1024]{2,1,0:T(8,128)(2,1)}, bf16[1,320,1024]{2,1,0:T(8,128)(2,1)S(1)}, u32[]{:S(2)}, u32[]{:S(2)}) collective-permute-start(bf16[1,320,1024]{2,1,0:T(8,128)(2,1)} %picked_sum.26.refs_24_), channel_id=1, source_target_pairs={{0,8},{4,12},{8,0},{12,4},{1,9},{5,13},{9,1},{13,5},{2,10},{6,14},... | collective-permute-start | bytes 1966088 | tf_op jit(solution)/shard_map/ppermute | solution.py:38
  402.7 65.9 %collective-permute-start.60 = (bf16[1536,256]{1,0:T(8,128)(2,1)}, bf16[1536,256]{1,0:T(8,128)(2,1)}, u32[]{:S(2)}, u32[]{:S(2)}) collective-permute-start(bf16[1536,256]{1,0:T(8,128)(2,1)} %bitcast.189), channel_id=1, source_target_pairs={{0,16},{1,17},{2,18},{3,19},{4,20},{5,21},{6,22},{7,23},{8,24},{9,... | collective-permute-start | bytes 2359304 | tf_op jit(solution)/shard_map/ppermute | solution.py:1269
  422.7 94.7 %reduce-scatter.6.cloned.1.call-start = ((), (), s32[]{:S(2)}) async-start(), calls=%async_computation.4 | async-start | bytes 983040 | tf_op jit(solution)/shard_map/reduce_scatter | solution.py:1353
  431.4 37.2 %collective-permute-start.59 = (bf16[1,320,1024]{2,1,0:T(8,128)(2,1)}, bf16[1,320,1024]{2,1,0:T(8,128)(2,1)S(1)}, u32[]{:S(2)}, u32[]{:S(2)}) collective-permute-start(bf16[1,320,1024]{2,1,0:T(8,128)(2,1)} %picked_sum.28.refs_16_), channel_id=1, source_target_pairs={{0,8},{4,12},{8,0},{12,4},{1,9},{5,13},{9,1},{13,5},{2,10},{6,14},... | collective-permute-start | bytes 1966088 | tf_op jit(solution)/shard_map/ppermute | solution.py:38
  465.9 22.6 %collective-permute-start.62 = (bf16[320,1024]{1,0:T(8,128)(2,1)}, bf16[320,1024]{1,0:T(8,128)(2,1)}, u32[]{:S(2)}, u32[]{:S(2)}) collective-permute-start(bf16[320,1024]{1,0:T(8,128)(2,1)} %bitcast.57.refs_2_), channel_id=1, source_target_pairs={{0,16},{16,0},{1,17},{17,1},{2,18},{18,2},{3,19},{19,3},{4,20},{20... | collective-permute-start | bytes 1966088 | tf_op jit(solution)/shard_map/ppermute | solution.py:38
  472.4 24.8 %collective-permute-start.67 = (bf16[320,1024]{1,0:T(8,128)(2,1)}, bf16[320,1024]{1,0:T(8,128)(2,1)}, u32[]{:S(2)}, u32[]{:S(2)}) collective-permute-start(bf16[320,1024]{1,0:T(8,128)(2,1)} %bitcast.65.refs_6_), channel_id=1, source_target_pairs={{0,16},{16,0},{1,17},{17,1},{2,18},{18,2},{3,19},{19,3},{4,20},{20... | collective-permute-start | bytes 1966088 | tf_op jit(solution)/shard_map/ppermute | solution.py:38
  478.0 15.9 %collective-permute-start.61 = (bf16[1,320,1024]{2,1,0:T(8,128)(2,1)}, bf16[1,320,1024]{2,1,0:T(8,128)(2,1)}, u32[]{:S(2)}, u32[]{:S(2)}) collective-permute-start(bf16[1,320,1024]{2,1,0:T(8,128)(2,1)} %picked_sum.30.refs_0_), channel_id=1, source_target_pairs={{0,8},{4,12},{8,0},{12,4},{1,9},{5,13},{9,1},{13,5},{2,10},{6,14},... | collective-permute-start | bytes 1966088 | tf_op jit(solution)/shard_map/ppermute | solution.py:38
  495.7 17.7 %collective-permute-start.66 = (bf16[320,1024]{1,0:T(8,128)(2,1)S(1)}, bf16[320,1024]{1,0:T(8,128)(2,1)S(1)}, u32[]{:S(2)}, u32[]{:S(2)}) collective-permute-start(bf16[320,1024]{1,0:T(8,128)(2,1)S(1)} %bitcast.152), channel_id=1, source_target_pairs={{0,16},{16,0},{1,17},{17,1},{2,18},{18,2},{3,19},{19,3},{4,20},{20... | collective-permute-start | bytes 1966088 | tf_op jit(solution)/shard_map/ppermute | solution.py:38
  495.9 29.0 %collective-permute-start.72 = (bf16[1152,256]{1,0:T(8,128)(2,1)}, bf16[1152,256]{1,0:T(8,128)(2,1)}, u32[]{:S(2)}, u32[]{:S(2)}) collective-permute-start(bf16[1152,256]{1,0:T(8,128)(2,1)} %bitcast.160), channel_id=1, source_target_pairs={{16,0},{17,1},{18,2},{19,3},{20,4},{21,5},{22,6},{23,7},{24,8},{25... | collective-permute-start | bytes 1769480 | tf_op jit(solution)/shard_map/ppermute | solution.py:1269
  (177 other events, 2085.3 us)
Sparse Core Ops, SparseCore 0:
  38.6 48.8 all-gather.4
  139.8 66.2 all-gather.6
  339.0 63.6 reduce-scatter.3
  422.8 47.3 reduce-scatter.7
  488.6 21.6 reduce-scatter.5

commit v3 on v2

--- a/solution.py
+++ b/solution.py
@@ -49,8 +49,10 @@
 def gather_blocks(value):
     blocks = {0: value}
     for bit in reversed(range(bits_of("tensor"))):
+        found = [blocks[s] for s in blocks if s]
         for s in list(blocks):
-            blocks[s | (1 << bit)] = swap(blocks[s], "tensor", bit)
+            sent = after(blocks[s], *found) if found and s == 0 else blocks[s]
+            blocks[s | (1 << bit)] = swap(sent, "tensor", bit)
     return [blocks[s] for s in range(len(blocks))]
 
 
@@ -68,15 +70,6 @@
 
 def after(value, *others):
     return lax.optimization_barrier((value, *others))[0]
-
-
-def line_parts(value, axis):
-    count = lax.axis_size(axis)
-    left, right = [value], [value]
-    for hop in range(1, count):
-        left.append(lax.ppermute(left[-1], axis, [(j, j + 1) for j in range(hop - 1, count - 1)]))
-        right.append(lax.ppermute(right[-1], axis, [(j + 1, j) for j in range(count - hop)]))
-    return left + right[1:]
 
 
 def gather_direct(value, axis):
@@ -513,7 +506,7 @@
     return order.call(
         functools.partial(enter_kernel, blocks, w, row),
         "enter",
-        20,
+        60,
         [SMEM] + [ANY] * (blocks + 1) + [VMEM],
         [VMEM] * 3,
         rows_of(w, ff) + [shape((1, ff), F32)],
@@ -551,7 +544,7 @@
     return order.call(
         functools.partial(backward_kernel, blocks, heads, w, row),
         "backward",
-        36,
+        60,
         [SMEM] + [ANY] * blocks + [VMEM] * 8 + [ANY] + [VMEM] * 2,
         [ANY, ANY] + [VMEM] * 3,
         halves_of(blocks) + rows_of(3 * w) + [shape((8, D), F32), shape((1, 3 * w), F32)],
@@ -631,7 +624,7 @@
     return order.call(
         functools.partial(whole_backward_kernel, blocks, heads, w, main_row, low_row),
         "whole_backward",
-        42,
+        60,
         [SMEM] + [ANY] * (2 * blocks) + [VMEM] * 7 + [ANY] * 2 + [VMEM] * 2,
         [ANY, ANY] + [VMEM] * 5,
         halves_of(blocks)
@@ -771,206 +764,172 @@
     )
 
 
-def fill(target, begin, lefts, rights):
-    dp, _, share = target.shape
-    size = lefts[0].shape[1]
-    for j in range(dp):
-        cols = slice(j * share, (j + 1) * share)
-        total = sum(dot(left[...], right[:, cols], 0, 0) for left, right in zip(lefts, rights))
-        target[j, begin : begin + size] = total.astype(BF)
-
-
-def grads_kernel(blocks, plan, *refs):
+def grads_kernel(blocks, plan, extra, *refs):
     index_ref, norms_ref = refs[:2]
     with_cot = None in plan
     normed = sorted({which for which in plan if which is not None})
-    sets = with_cot + bool(normed)
     count = MB * blocks
-    c_refs = refs[2 : 2 + count * with_cot]
-    x_refs = refs[2 + count * with_cot : 2 + count * sets]
-    lefts = refs[2 + count * sets : 2 + count * sets + MB * len(plan)]
-    out_ref, *scratch = refs[2 + count * sets + MB * len(plan) :]
-    sems = scratch.pop()
+    row_refs = refs[2 : 2 + count]
+    lefts = refs[2 + count : 2 + count + MB * len(plan)]
+    rest = refs[2 + count + MB * len(plan) :]
+    extra_ref, rest = (rest[0], rest[1:]) if extra else (None, rest)
+    out_ref, total, *scratch = rest
+    side_sems, sems = scratch.pop(), scratch.pop()
+    sides, scratch = scratch[: MB * len(plan)], scratch[MB * len(plan) :]
     index = index_ref[0]
-
-    def loads(source, target, which):
-        copies = []
-        for unit in range(MB):
-            part = source[unit * blocks : (unit + 1) * blocks]
-            copies += copies_of_blocks(index, part, target.at[unit], sems.at[which, unit])
-        return copies
-
-    rights = {}
-    c_loads, x_loads = [], []
-    if with_cot:
-        rights[None] = scratch[0]
-        c_loads = loads(c_refs, scratch[0], 0)
-    if normed:
-        x_loads = loads(x_refs, scratch[with_cot], 1)
-    start_all(c_loads + x_loads)
-    for i, which in enumerate(normed):
-        rights[which] = scratch[with_cot + i]
-    begin = 0
-    wait_all(c_loads)
-    for i, which in enumerate(plan):
-        if which is not None and x_loads:
-            wait_all(x_loads)
-            x_loads = []
-            raw = scratch[with_cot]
-            for unit in range(MB):
-                for at in chunks():
-                    hat, _ = normalize(raw[unit, at])
-                    for norm in normed:
-                        row = hat * norms_ref[norm : norm + 1] + norms_ref[2 + norm : 3 + norm]
-                        rights[norm][unit, at] = row.astype(BF)
-        part = lefts[i * MB : (i + 1) * MB]
-        fill(out_ref, begin, part, [rights[which].at[unit] for unit in range(MB)])
-        begin += part[0].shape[1]
-
-
-def weight_grads(order, index, c_blocks, x_blocks, pieces, norms, dp):
+    dp, _, share = out_ref.shape
+    loads = []
+    for unit in range(MB):
+        part = row_refs[unit * blocks : (unit + 1) * blocks]
+        loads.append(copies_of_blocks(index, part, scratch[0].at[unit], sems.at[unit]))
+        for i in range(len(plan)):
+            left = lefts[i * MB + unit]
+            loads[unit].append(
+                pltpu.make_async_copy(left, sides[i * MB + unit], side_sems.at[i * MB + unit])
+            )
+        start_all(loads[unit])
+    for unit in range(MB):
+        wait_all(loads[unit])
+        rights = {None: scratch[0]}
+        if not with_cot:
+            rights = dict(zip(normed, scratch))
+            for at in chunks():
+                hat, _ = normalize(scratch[0][unit, at])
+                for norm in normed:
+                    row = hat * norms_ref[norm : norm + 1] + norms_ref[2 + norm : 3 + norm]
+                    rights[norm][unit, at] = row.astype(BF)
+        begin = 0
+        for i, which in enumerate(plan):
+            left = sides[i * MB + unit]
+            rows = slice(begin, begin + left.shape[1])
+            part = dot(left[...], rights[which][unit], 0, 0)
+            if unit:
+                part = part + total[rows]
+            if unit + 1 < MB:
+                total[rows] = part
+            else:
+                for j in range(dp):
+                    out_ref[j, rows] = part[:, j * share : (j + 1) * share].astype(BF)
+            begin = rows.stop
+    if extra:
+        out_ref[:, begin:] = extra_ref[...]
+
+
+def weight_grads(order, index, c_blocks, x_blocks, pieces, norms, dp, extra=()):
     plan = [which for _, which in pieces]
     blocks = len(x_blocks[0])
-    rows = []
-    if None in plan:
-        rows += [block for unit in c_blocks for block in unit]
-    if any(which is not None for which in plan):
-        rows += [block for unit in x_blocks for block in unit]
+    rows = [block for unit in (c_blocks if None in plan else x_blocks) for block in unit]
     lefts = [left for part, _ in pieces for left in part]
-    size = sum(part[0].shape[1] for part, _ in pieces)
+    size = sum(part[0].shape[1] for part, _ in pieces) + sum(value.shape[1] for value in extra)
     buffers = len(set(plan))
     return order.call(
-        functools.partial(grads_kernel, blocks, plan),
+        functools.partial(grads_kernel, blocks, plan, bool(extra)),
         "weight_grads",
         60,
-        [SMEM, VMEM] + [ANY] * len(rows) + [VMEM] * len(lefts),
+        [SMEM, VMEM] + [ANY] * (len(rows) + len(lefts)) + [VMEM] * len(extra),
         [VMEM],
         [shape((dp, size, D // dp), BF)],
-        [pltpu.VMEM((MB, TOK_MB, D), BF)] * buffers
-        + [pltpu.SemaphoreType.DMA((2, MB, blocks))],
-        [index, norms, *rows, *lefts],
+        [pltpu.VMEM((size, D), F32)]
+        + [pltpu.VMEM(left.shape, BF) for left in lefts]
+        + [pltpu.VMEM((MB, TOK_MB, D), BF)] * buffers
+        + [pltpu.SemaphoreType.DMA((MB, blocks)), pltpu.SemaphoreType.DMA((len(lefts),))],
+        [index, norms, *rows, *lefts, *extra],
     )[0]
 
 
-def pack_kernel(width, w, stage_ref, qkv_ref, up_ref, out_ref, down_ref, *refs):
+SMALL = 16
+
+
+def put_halves(at_first, keep, send, begin, size, low, high):
+    keep[begin : begin + size] = jnp.where(at_first, low, high)
+    send[begin : begin + size] = jnp.where(at_first, high, low)
+
+
+def pack_kernel(width, w, stage_ref, qkv_ref, up_ref, out_ref, down_ref, keep_ref, send_ref, *held):
+    (qkv, up, out, down), sems = held[:4], held[4]
+    sources = (qkv_ref, up_ref, out_ref, down_ref)
+    loads = [
+        pltpu.make_async_copy(source, target, sems.at[i])
+        for i, (source, target) in enumerate(zip(sources, held))
+    ]
+    start_all(loads)
     at_first = stage_ref[0] == 0
-    ff = down_ref.shape[0] // 2
-    mains, lows = refs[:2], refs[2:]
-
-    def put(target, begin, size, low, high):
-        target[0][begin : begin + size] = jnp.where(at_first, low, high)
-        target[1][begin : begin + size] = jnp.where(at_first, high, low)
-
+    ff = up.shape[1] // 2
     if w != width:
-        for ref in refs:
-            ref[...] = jnp.zeros_like(ref)
+        keep_ref[...] = jnp.zeros_like(keep_ref)
+        send_ref[...] = jnp.zeros_like(send_ref)
+    wait_all(loads)
     for i in range(3):
-        turned = qkv_ref[i].T
-        put(mains, i * w, width, turned[:width], turned[width:])
-    turned = up_ref[...].T
-    put(mains, 3 * w, ff, turned[:ff], turned[ff:])
-    put(lows, 0, width, out_ref[:width], out_ref[width:])
-    put(lows, w, ff, down_ref[:ff], down_ref[ff:])
+        turned = qkv[i].T
+        put_halves(at_first, keep_ref, send_ref, i * w, width, turned[:width], turned[width:])
+    turned = up[...].T
+    put_halves(at_first, keep_ref, send_ref, 3 * w, ff, turned[:ff], turned[ff:])
+    begin = 3 * w + ff
+    put_halves(at_first, keep_ref, send_ref, begin, width, out[:width], out[width:])
+    put_halves(at_first, keep_ref, send_ref, begin + w, ff, down[:ff], down[ff:])
 
 
 def pack(order, stage, qkv, up, out, down, w):
-    width = out.shape[0] // 2
-    ff = down.shape[0] // 2
-    share = out.shape[1]
+    width, ff, share = qkv.shape[2] // 2, up.shape[1] // 2, up.shape[0]
     return order.call(
         functools.partial(pack_kernel, width, w),
         "pack",
-        24,
-        [SMEM] + [VMEM] * 4,
-        [VMEM] * 4,
-        [shape((3 * w + ff, share), BF)] * 2 + [shape((w + ff, share), BF)] * 2,
-        [],
+        60,
+        [SMEM] + [ANY] * 4,
+        [VMEM] * 2,
+        [shape((4 * w + 2 * ff, share), BF)] * 2,
+        [pltpu.VMEM(value.shape, BF) for value in (qkv, up, out, down)] + dma(4),
         [stage, qkv, up, out, down],
     )
 
 
-def assemble_kernel(count, index_ref, *refs):
-    parts, out_ref, sems = refs[: 2 * count - 1], refs[-2], refs[-1]
-    index = index_ref[0]
-    copies = [(index >= 0, pltpu.make_async_copy(parts[0], out_ref.at[index], sems.at[0]))]
-    for hop in range(1, count):
-        for sign, number in ((-1, hop), (1, count - 1 + hop)):
-            place = index + sign * hop
-            inside = (place >= 0) & (place < count)
-            target = out_ref.at[jnp.clip(place, 0, count - 1)]
-            copies.append(
-                (inside, pltpu.make_async_copy(parts[number], target, sems.at[number]))
-            )
-    for inside, copy in copies:
-        pl.when(inside)(copy.start)
-    for inside, copy in copies:
-        pl.when(inside)(copy.wait)
-
-
-def assemble(order, index, parts):
-    count = (len(parts) + 1) // 2
-    return order.call(
-        functools.partial(assemble_kernel, count),
-        "assemble",
-        4,
-        [SMEM] + [ANY] * len(parts),
-        [ANY],
-        [shape((count, *parts[0].shape), BF)],
-        dma(len(parts)),
-        [index, *parts],
-    )[0]
-
-
-def by_stage_kernel(stage_ref, mine_ref, other_ref, *refs):
+def by_stage_kernel(stage_ref, *refs):
     at_first = stage_ref[0] == 0
-    mine, other = mine_ref[...], other_ref[...]
-    refs[-2][...] = jnp.where(at_first, mine, other)
-    second = jnp.where(at_first, other, mine)
-    if len(refs) > 2:
-        rows = refs[0].shape[0]
-        refs[-1][:rows] = refs[0][...]
-        refs[-1][rows:] = second
-    else:
-        refs[-1][...] = second
-
-
-def by_stage(order, stage, mine, other, above=()):
-    rows = mine.shape[0] + sum(value.shape[0] for value in above)
+    pairs, (first_ref, second_ref) = refs[:-2], refs[-2:]
+    begin = 0
+    for mine_ref, other_ref in zip(pairs[::2], pairs[1::2]):
+        rows = slice(begin, begin + mine_ref.shape[0])
+        mine, other = mine_ref[...], other_ref[...]
+        first_ref[rows] = jnp.where(at_first, mine, other)
+        second_ref[rows] = jnp.where(at_first, other, mine)
+        begin = rows.stop
+
+
+def by_stage(order, stage, *pairs):
+    rows = sum(mine.shape[0] for mine in pairs[::2])
     return order.call(
         by_stage_kernel,
         "by_stage",
         16,
-        [SMEM] + [VMEM] * (2 + len(above)),
+        [SMEM] + [VMEM] * len(pairs),
         [VMEM] * 2,
-        [shape(mine.shape, BF), shape((rows, mine.shape[1]), BF)],
+        [shape((rows, pairs[0].shape[1]), BF)] * 2,
         [],
-        [stage, mine, other, *above],
-    )
+        [stage, *pairs],
+    )
+
+
+def both_halves(stage_ref, mine0, mine1, from0, from1, begin, size):
+    at_first = stage_ref[0] == 0
+    rows = slice(begin, begin + size)
+    low = jnp.where(at_first, mine0[rows], from1[rows])
+    high = jnp.where(at_first, from0[rows], mine1[rows])
+    return low.astype(F32), high.astype(F32)
 
 
 def unpack_outer_kernel(width, w, ff, *refs):
-    stage_ref, mine0, mine1, from0, from1, up_ref, out_ref, down_ref = refs
-    at_first = stage_ref[0] == 0
-
-    def halves(begin, size):
-        rows = slice(begin, begin + size)
-        low = jnp.where(at_first, mine0[rows], from1[rows])
-        high = jnp.where(at_first, from0[rows], mine1[rows])
-        return low.astype(F32), high.astype(F32)
-
-    out_ref[:width], out_ref[width:] = halves(0, width)
-    down_ref[:ff], down_ref[ff:] = halves(w, ff)
-    low, high = halves(w + ff, ff)
+    parts, (out_ref, down_ref) = refs[:5], refs[5:]
+    out_ref[:width], out_ref[width:] = both_halves(*parts, 0, width)
+    down_ref[:ff], down_ref[ff:] = both_halves(*parts, w, ff)
+
+
+def unpack_inner_kernel(width, w, ff, *refs):
+    parts, (up_ref, qkv_ref) = refs[:5], refs[5:]
+    low, high = both_halves(*parts, 0, ff)
     up_ref[:, :ff] = low.T
     up_ref[:, ff:] = high.T
-
-
-def unpack_inner_kernel(width, w, stage_ref, mine0, mine1, from0, from1, qkv_ref):
-    at_first = stage_ref[0] == 0
     for i in range(3):
-        rows = slice(i * w, i * w + width)
-        low = jnp.where(at_first, mine0[rows], from1[rows]).astype(F32)
-        high = jnp.where(at_first, from0[rows], mine1[rows]).astype(F32)
+        low, high = both_halves(*parts, ff + i * w, width)
         qkv_ref[i] = jnp.concatenate([low, high], axis=0).T
 
 
@@ -1031,7 +990,7 @@
         self.where = where
         self.terms = [keep, swap(send, "tensor", 0)]
 
-    def send(self, order):
+    def send(self, order, *others):
         place = lax.axis_index("tensor")
         last = bits_of("tensor") - 1
         for bit in range(1, last + 1):
@@ -1039,7 +998,8 @@
                 term.reshape((term.shape[0] // 2, 2) + term.shape[1:]) for term in self.terms
             ]
             sent = picked_sum(order, self.where, bit, True, pairs)
-            self.received = swap(sent, "tensor", bit)
+            self.sent = sent
+            self.received = swap(after(sent, *others) if others else sent, "tensor", bit)
             if bit < last:
                 own = (place >> bit) & 1
                 self.terms = [pick(pair, own, 1) for pair in pairs] + [self.received]
@@ -1200,7 +1160,23 @@
 
     tiles = boundary[0, :, 0]
     angles = [angles_for(lengths[unit, 0], w) for unit in range(MB)]
-    main_mine, main_sent, low_mine, low_sent = pack(
+    far = tensor // 2
+
+    def gather_far(value):
+        blocks = {0: value}
+        for bit in reversed(range(1, bits_of("tensor"))):
+            for s in list(blocks):
+                blocks[s | (1 << bit)] = swap(blocks[s], "tensor", bit)
+        return [blocks[s] for s in sorted(blocks)]
+
+    piece = gains.shape[2]
+    small = jnp.concatenate([gains[0], biases[0]])
+    small = jnp.moveaxis(gather_tensor(small), 0, 1).reshape(6, share)
+    flat = jnp.concatenate([qkv_bias[0].reshape(-1), up_bias[0]])
+    flat = jnp.pad(flat, (0, (SMALL - 6) * share - flat.shape[0])).reshape(-1, share)
+    small = jnp.concatenate([small, flat])
+
+    mine, sent = pack(
         order,
         stage_word,
         jnp.moveaxis(qkv_weight[0], 1, 0),
@@ -1209,111 +1185,100 @@
         down_weight[0],
         w,
     )
-    main_other = swap(main_sent, "pipe", 0)
-    low_other = swap(after(low_sent, main_other), "pipe", 0)
-    tile_other = swap(after(tiles[0], low_other), "pipe", 0)
+    other = swap(sent, "pipe", 0)
+    order.hold(small)
     order.pause()
-    main_0, main_1 = by_stage(order, stage_word, main_mine, main_other)
+    small_other = swap(small, "pipe", 0)
+    def gather_near(order, blocks):
+        found = [None] * tensor
+        for i, rows in enumerate(blocks):
+            found[2 * i] = rows
+            found[2 * i + 1] = swap(after(rows, order.last[0]), "tensor", 0)
+        return found
+
     order.pause()
-    low_0, both_1 = by_stage(order, stage_word, low_mine, low_other, [main_1])
-    low_parts = line_parts(low_0, "dp")
-
-    piece = gains.shape[2]
-    small = jnp.concatenate([gains[0].reshape(-1), biases[0].reshape(-1)])
-    small = gather_tensor(after(small, main_0)).reshape(-1)
-    small = jnp.concatenate([small, qkv_bias[0].reshape(-1), up_bias[0]])
-    small = jnp.stack(split(small, swap(small, "pipe", 0)))
-    small = gather_direct(small, "dp")
-    small = jnp.moveaxis(small, 0, 1).astype(F32)
-    norms = small[:, :, : tensor * 6 * piece].reshape(2, dp, tensor, 6, piece)
-    norms = norms.transpose(0, 3, 2, 1, 4).reshape(2, 6, D)
-    rest = small[:, :, tensor * 6 * piece :]
-    qkv_biases = rest[:, :, : 3 * piece].reshape(2, dp, 3, piece)
-    qkv_biases = qkv_biases.transpose(0, 2, 1, 3).reshape(2, 3, 2 * width)
-    qkv_biases = padded(half(qkv_biases, stage, 2), 2).reshape(2, 1, 3 * w)
-    up_biases = half(rest[:, :, 3 * piece :].reshape(2, 1, 2 * ff), stage, 2)
-    main_biases = jnp.concatenate([qkv_biases, up_biases], axis=2)
-
-    layers = [
-        dict(w=w, ff=ff, heads=heads, norms=norms[layer], bias=main_biases[layer])
-        for layer in range(2)
-    ]
-    main_0 = lax.all_gather(main_0, "dp", axis=0)
-    both_1 = lax.all_gather(after(both_1, main_0, *low_parts[1:]), "dp", axis=0)
-    layers[0].update(main=(main_0, 0))
-    layers[1].update(main=(both_1, 0), low=(both_1, cut))
+    stack_0, stack_1 = by_stage(order, stage_word, mine, other, small, small_other)
+    far_tiles = [gather_far(after(tile, order.last[0])) for tile in tiles]
+    stack_0 = lax.all_gather(stack_0, "dp", axis=0)
+
+    def vectors_of(gathered, row):
+        small = gathered[:, row : row + SMALL].astype(F32)
+        norms = small[:, :6].reshape(dp, 6, tensor, piece).transpose(1, 2, 0, 3).reshape(6, D)
+        flat = small[:, 6:].reshape(dp, -1)
+        raw = flat[:, : 3 * piece].reshape(dp, 3, piece).transpose(1, 0, 2)
+        raw = padded(half(raw.reshape(3, 2 * width), stage, 1), 1).reshape(1, 3 * w)
+        up = flat[:, 3 * piece : 3 * piece + up_bias.shape[1]].reshape(1, 2 * ff)
+        return dict(norms=norms, bias=jnp.concatenate([raw, half(up, stage, 1)], axis=1))
+
     x_rows, cot_rows, x_blocks, c_blocks = [], [], [], []
 
-    def take_tile(other):
-        rows, cot = by_stage(order, stage_word, tiles[len(x_rows)], other)
-        x_rows.append(rows)
-        cot_rows.append(cot)
-        x_blocks.append(gather_blocks(rows))
+    def take_tiles(unit):
+        others = [swap(tile, "pipe", 0) for tile in far_tiles[unit]]
+        order.pause()
+        x_far, cot_far = [], []
+        for mine, other in zip(far_tiles[unit], others):
+            rows, cot = by_stage(order, stage_word, mine, other)
+            x_far.append(rows)
+            cot_far.append(cot)
+        x_rows.append(x_far[0])
+        cot_rows.append(cot_far[0])
+        order.pause()
+        x_blocks.append(gather_near(order, x_far))
+        order.pause()
+        order.hold(*x_blocks[unit])
+        order.pause()
+        c_blocks.append(gather_near(order, cot_far))
+        order.pause()
+        order.hold(*c_blocks[unit])
 
     order.hold(*[value for pair in angles for value in pair])
     order.pause()
-    take_tile(tile_other)
-    tile_other = swap(after(tiles[1], tile_other), "pipe", 0)
-    order.hold(norms, main_biases)
+    take_tiles(0)
+    stack_1 = lax.all_gather(after(stack_1, x_rows[0]), "dp", axis=0)
+    take_tiles(1)
     order.pause()
-    take_tile(tile_other)
-    order.pause()
-    c_blocks.append(gather_blocks(after(cot_rows[0], x_blocks[1][tensor // 2])))
+    row = 4 * w + 2 * ff
+    layers = [
+        dict(w=w, ff=ff, heads=heads, main=(stack, 0), low=(stack, cut))
+        for stack in (stack_0, stack_1)
+    ]
+    layers[0].update(vectors_of(stack_0, row))
 
     units = range(MB)
     kept = [[None] * MB, [None] * MB]
     entered = [[None] * MB, [None] * MB]
     back = [[None] * MB, [None] * MB]
 
-    def across(value, source):
-        return lax.ppermute(value, "pipe", [(source, 1 - source)])
-
-    class VectorSums:
-        def __init__(self, cot_a, cot_b):
-            own = [
-                sum(jnp.sum(rows.astype(F32), axis=0) for rows in pair)
-                for pair in ((cot_a, cot_b), cot_rows)
-            ]
-            once = jnp.where(at_first, 1.0, 0.0)
-            packs = []
-            for layer in range(2):
-                rows = sum(back[layer][unit][1] for unit in units)[:4]
-                raw = sum(back[layer][unit][2] for unit in units).reshape(3, w)[:, :width]
-                pre = sum(entered[layer][unit][2] for unit in units)
-                flat = [rows.reshape(-1), own[layer] * once, raw.reshape(-1), pre[0]]
-                packs.append(jnp.concatenate(flat))
-            self.mine = jnp.where(at_first, packs[0], packs[1])
-            self.other = jnp.where(at_first, packs[1], packs[0])
-
-        def across(self):
-            self.received = swap(self.other, "pipe", 0)
-            return self.received
-
-        def along_tensor(self):
-            rows = 5 * D
-            norm = (self.mine[:rows] + self.received[:rows]).reshape(5, tensor, D // tensor)
-            norm = norm.transpose(1, 0, 2)
-            place = lax.axis_index("tensor")
-            for bit in range(bits_of("tensor")):
-                own = (place >> bit) & 1
-                pairs = norm.reshape((norm.shape[0] // 2, 2) + norm.shape[1:])
-                norm = pick(pairs, own, 1) + swap(pick(pairs, 1 - own, 1), "tensor", bit)
-            norm = norm[0].reshape(5, dp, piece).transpose(1, 0, 2).reshape(dp, 5 * piece)
-            low, high = split(self.mine[rows:], self.received[rows:])
-            raw = jnp.stack([low[: 3 * width], high[: 3 * width]]).reshape(2, 3, width)
-            raw = raw.transpose(1, 0, 2).reshape(3, dp, piece).transpose(1, 0, 2)
-            pre = jnp.concatenate([low[3 * width :], high[3 * width :]]).reshape(dp, -1)
-            self.parts = jnp.concatenate([norm, raw.reshape(dp, 3 * piece), pre], axis=1)
-            return self.parts
-
-        def along_dp(self):
-            self.total = scatter_direct(self.parts, "dp")
-            return self.total
-
-        def results(self):
-            norm = self.total[: 5 * piece].reshape(5, piece)
-            raw = self.total[5 * piece : 8 * piece].reshape(3, piece)
-            return norm, raw, self.total[8 * piece :]
+    def vector_rows(layer, cots):
+        own = sum(jnp.sum(rows.astype(F32), axis=0) for rows in cots)
+        own = own * jnp.where(at_first, 1.0, 0.0)
+        rows = sum(back[layer][unit][1] for unit in units)[:4]
+        rows = jnp.concatenate([rows, own[None]]).reshape(5, tensor, dp, piece)
+        rows = rows.transpose(2, 0, 1, 3).reshape(dp, 5, share)
+        raw = sum(back[layer][unit][2] for unit in units).reshape(3, w)[:, :width]
+        raw = raw.reshape(3, dp // 2, piece).transpose(1, 0, 2).reshape(dp // 2, 3 * piece)
+        pre = sum(entered[layer][unit][2] for unit in units).reshape(dp // 2, -1)
+        pads = [jnp.pad(item, ((0, 0), (0, share - item.shape[1]))) for item in (raw, pre)]
+        held = lax.dynamic_update_slice(
+            jnp.zeros((dp, 2, share), F32), jnp.stack(pads, axis=1), (stage * (dp // 2), 0, 0)
+        )
+        return [jnp.pad(jnp.concatenate([rows, held], axis=1), ((0, 0), (0, SMALL - 7), (0, 0))).astype(BF)]
+
+    def vectors_from(rows_0, rows_1):
+        both = jnp.stack([rows_0, rows_1]).astype(F32)
+        norm = both[:, :5].reshape(2, 5, tensor, piece).transpose(2, 0, 1, 3)
+        place = lax.axis_index("tensor")
+        total = pick(norm, place, 0)
+        for s in range(1, tensor):
+            pairs = [(i, i ^ s) for i in range(tensor)]
+            total = total + lax.ppermute(pick(norm, place ^ s, 0), "tensor", pairs)
+        flat = jnp.concatenate([total.reshape(2, -1), both[:, 5:7].reshape(2, -1)], axis=1)
+        mine = jnp.where(at_first, flat[0], flat[1])
+        total = mine + swap(jnp.where(at_first, flat[1], flat[0]), "pipe", 0)
+        norm = total[: 5 * piece].reshape(5, piece)
+        raw = total[5 * piece : 5 * piece + 3 * piece].reshape(3, piece)
+        begin = 5 * piece + share
+        return norm, raw, total[begin : begin + up_bias.shape[1]]
 
     def run_project(layer, unit, blocks):
         kept[layer][unit] = project(order, index, blocks, layers[layer], angles[unit])
@@ -1341,110 +1306,112 @@
         back[1][unit] = rest
         return Sum(index, y_keep, y_send), Sum(index, u_keep, u_send)
 
-    def reduced(layer, names, cots, rows):
-        lefts = dict(
-            out=([kept[layer][unit][5] for unit in units], None),
-            down=([kept[layer][unit][3] for unit in units], None),
-            up=([entered[layer][unit][1] for unit in units], 1),
-            qkv=([back[layer][unit] and back[layer][unit][0] for unit in units], 0),
+    def reduced(layer, names, cots, rows, extra=()):
+        sources = dict(
+            out=(kept, 5, None), down=(kept, 3, None), up=(entered, 1, 1), qkv=(back, 0, 0)
         )
-        pieces = [lefts[name] for name in names]
-        value = weight_grads(order, index, cots, rows, pieces, layers[layer]["norms"], dp)
+        pieces = []
+        for name in names:
+            held_in, place, which = sources[name]
+            pieces.append(([held_in[layer][unit][place] for unit in units], which))
+        norms = layers[layer]["norms"]
+        value = weight_grads(order, index, cots, rows, pieces, norms, dp, extra)
         return lax.psum_scatter(value, "dp", scatter_dimension=0)
 
     run_project(0, 0, x_blocks[0])
-    dp_index = lax.axis_index("dp").astype(jnp.int32)[None]
-    layers[0].update(low=(assemble(order, dp_index, low_parts), 0))
     sum_a = run_attend(0, 0)
+    order.pause()
+    sum_a.send(order)
     run_project(0, 1, x_blocks[1])
-    order.hold(*c_blocks[0])
-    sum_a.send(order)
     sum_b = run_attend(0, 1)
     sum_a.cross(order)
     sum_b.send(order)
     middle_a = add_rows(order, x_rows[0], sum_a, layers[0])
-    blocks_a = gather_blocks(after(middle_a, sum_b.received))
+    far_a = gather_far(middle_a)
     sum_b.cross(order)
     order.pause()
+    blocks_a = gather_near(order, far_a)
+    order.hold(stack_1)
     middle_b = add_rows(order, x_rows[1], sum_b, layers[0])
-    blocks_b = gather_blocks(after(middle_b, blocks_a[-1]))
-    c_blocks.append(gather_blocks(after(cot_rows[1], blocks_b[tensor // 2])))
-    middle_blocks = [blocks_a, blocks_b]
+    far_b = gather_far(middle_b)
+    layers[1].update(vectors_of(after(stack_1, middle_b), row))
 
     y_a, sum_a = run_layer(0, blocks_a)
     order.pause()
+    blocks_b = gather_near(order, far_b)
+    middle_blocks = [blocks_a, blocks_b]
+    order.hold(y_a.terms[1])
     sum_a.send(order)
     run_project(1, 1, blocks_b)
     y_b = run_attend(1, 1)
     sum_a.cross(order)
-    order.hold(*c_blocks[1])
+    order.hold(y_b.terms[1])
     y_a.send(order)
+    y_b.send(order)
     sum_b = run_backward(1, 1, c_blocks[1], blocks_b)
     cot_a = norm_back(order, middle_a, sum_a, cot_rows[0])
     sum_b.send(order)
     y_a.cross(order)
-    grads_1 = reduced(1, ("out", "down", "up", "qkv"), c_blocks, middle_blocks)
+    outer_1 = reduced(1, ("out", "down"), c_blocks, middle_blocks)
     sum_b.cross(order)
-    cot_blocks = [gather_blocks(after(cot_a, sum_b.own))]
-    order.hold(y_a.other)
+    far_a = gather_far(after(cot_a, order.last[0]))
+    inner_1 = reduced(1, ("up", "qkv"), c_blocks, middle_blocks, vector_rows(1, cot_rows))
+    cot_blocks = [gather_near(order, far_a)]
+    y_b.cross(order)
+    cot_b = norm_back(order, middle_b, sum_b, cot_rows[1])
+    far_b = gather_far(cot_b)
+
+    order.hold(outer_1, y_a.other)
     order.pause()
-    cot_b = norm_back(order, middle_b, sum_b, cot_rows[1])
-    cot_blocks.append(gather_blocks(after(cot_b, cot_blocks[0][-1])))
-
+    from_outer_1 = swap(outer_1, "pipe", 0)
     sum_a = run_backward(0, 0, cot_blocks[0], x_blocks[0])
+    cot_blocks.append(gather_near(order, far_b))
     order.pause()
+    outer_0 = reduced(0, ("out", "down"), cot_blocks, x_blocks)
+    sum_a.send(order)
+    order.hold(from_outer_1, inner_1, y_b.other)
     entered[0][1] = enter(order, index, cot_blocks[1], kept[0][1], layers[0])
-    sum_a.send(order)
-    order.hold(grads_1)
-    outer_0 = reduced(0, ("out", "down", "up"), cot_blocks, x_blocks)
-    sum_a.cross(order)
-    y_b.send(order)
-    from_1 = across(grads_1, 0)
+    from_inner_1 = swap(inner_1, "pipe", 0)
     keep, send, *back[0][1] = backward(
         order, index, x_blocks[1], kept[0][1], entered[0][1], layers[0], angles[1]
     )
     sum_b = Sum(index, keep, send)
-    order.hold(from_1)
-    y_b.cross(order)
+    order.hold(from_inner_1)
+    inner_0 = reduced(0, ("up", "qkv"), cot_blocks, x_blocks, vector_rows(0, (cot_a, cot_b)))
+    from_outer_0 = swap(after(outer_0, order.last[0]), "pipe", 0)
+    order.pause()
     sum_b.send(order)
-    vectors = VectorSums(cot_a, cot_b)
+    sum_a.cross(order)
     order.pause()
-    inner_0 = reduced(0, ("qkv",), cot_blocks, x_blocks)
-    order.hold(vectors.across())
+    sum_b.cross(order)
     ends = write_ends(
         order, 0, stage_word, None, x_rows[0], sum_a, cot_a, middle_a, y_a, layers[1]
     )
-    order.hold(vectors.along_tensor())
-    sum_b.cross(order)
-    from_outer = across(outer_0, 1)
-    order.hold(vectors.along_dp())
-    order.pause()
-    ends = write_ends(
-        order, 1, stage_word, ends, x_rows[1], sum_b, cot_b, middle_b, y_b, layers[1]
-    )
-
-    inner_1, outer_1 = grads_1[w + 2 * ff :], grads_1[: w + 2 * ff]
-    grad_up, grad_out, grad_down = unpack(
+    order.hold(from_outer_0)
+    grad_out, grad_down = unpack(
         functools.partial(unpack_outer_kernel, width, w, ff),
         order,
         stage_word,
-        [outer_0, outer_1, from_outer, from_1[: w + 2 * ff]],
-        [
-            shape((share, 2 * ff), F32),
-            shape((2 * width, share), F32),
-            shape((2 * ff, share), F32),
-        ],
-    )
-    grad_qkv = unpack(
-        functools.partial(unpack_inner_kernel, width, w),
+        [outer_0, outer_1, from_outer_0, from_outer_1],
+        [shape((2 * width, share), F32), shape((2 * ff, share), F32)],
+    )
+    order.hold(inner_0)
+    ends = write_ends(
+        order, 1, stage_word, ends, x_rows[1], sum_b, cot_b, middle_b, y_b, layers[1]
+    )
+    last = 3 * w + ff
+    from_inner_0 = swap(inner_0, "pipe", 0)
+    vectors = vectors_from(inner_0[last:], inner_1[last:])
+    order.hold(from_inner_0)
+    grad_up, grad_qkv = unpack(
+        functools.partial(unpack_inner_kernel, width, w, ff),
         order,
         stage_word,
-        [inner_0, inner_1, across(inner_0, 1), from_1[w + 2 * ff :]],
-        [shape((3, share, 2 * width), F32)],
-    )[0]
+        [inner_0, inner_1, from_inner_0, from_inner_1],
+        [shape((share, 2 * ff), F32), shape((3, share, 2 * width), F32)],
+    )
     grad_qkv = jnp.moveaxis(grad_qkv, 0, 1)
-
-    norm_grads, grad_qkv_bias, grad_up_bias = vectors.results()
+    norm_grads, grad_qkv_bias, grad_up_bias = vectors
     grad_gains = norm_grads[:2]
     grad_biases = jnp.concatenate([norm_grads[2:5], norm_grads[4:5]])
     return (

time: 546 us -> 501 us (0.918)
  waiting for transfers between devices: 165 us -> 126 us
  starting transfers between devices: 63.6 us -> 47.3 us
  Pallas kernels: 242 us -> 249 us
  local copies, waits for them, and re-layouts: 37.1 us -> 43.6 us
    ppermute x15 -> x3, waiting for transfers between devices: 45.3 us -> 0.97 us  [vectors_from(): total = total + lax.ppermute(pick(norm, place ^ s, 0), 'tensor', pairs)]
    ppermute x15 -> x3, starting transfers between devices: 24.9 us -> 1.93 us  [vectors_from(): total = total + lax.ppermute(pick(norm, place ^ s, 0), 'tensor', pairs)]
    pallas_call x55 -> x66, Pallas kernels: 242 us -> 249 us  [call(): pl.pallas_call(outer, in_specs=in_specs + [ANY] * len(deps), out_specs=ou...]
    ppermute x58 -> x59, starting transfers between devices: 37.9 us -> 45 us  [swap(): return lax.ppermute(value, axis, [(i, i ^ 1 << bit) for i in range(count)])]
    unnamed x303 -> x265, local copies, waits for them, and re-layouts: 28.9 us -> 33.8 us
    ppermute x58 -> x59, waiting for transfers between devices: 115 us -> 118 us  [swap(): return lax.ppermute(value, axis, [(i, i ^ 1 << bit) for i in range(count)])]
  transfers between devices with their start and end apart: 78 -> 68, of which waited for: 25 -> 28; matrix products, arithmetic and copies ran while one was open for 4% -> 5% of each run, Pallas kernels for 45% -> 49%
where the time goes in v3:
time: 501 us; the launch traced here: 496 us
  Pallas kernels  249 us (50%)
  waiting for transfers between devices  126 us (25%)
  starting transfers between devices  47.3 us (9%)
  local copies, waits for them, and re-layouts  43.6 us (9%)
  between operations  16.1 us (3%)
  other arithmetic  13.8 us (3%)
    pallas_call x66, Pallas kernels, call(): pl.pallas_call(outer, in_specs=in_specs + [ANY] * len(deps), out_specs=ou...  249 us
    ppermute x59, waiting for transfers between devices, swap(): return lax.ppermute(value, axis, [(i, i ^ 1 << bit) for i in range(count)])  118 us
    ppermute x59, starting transfers between devices, swap(): return lax.ppermute(value, axis, [(i, i ^ 1 << bit) for i in range(count)])  45 us
    unnamed x265, local copies, waits for them, and re-layouts  33.8 us
  transfers between devices with their start and end apart: 68, of which 28 were waited for; matrix products, arithmetic and copies ran while one was open for 5% of the time, Pallas kernels for 49%

profile of v3, /device:TPU:0, one launch (start us, length us, event | category | flops | bytes accessed | tf_op | source)
XLA Modules:
  0.0 495.7 jit_solution(12536939771217392283)
XLA Ops:
  7.3 3.0 pack.1
  10.2 3.0 collective-permute-start
  21.0 10.3 %collective-permute-done.3.refs_4_ = bf16[16,256]{1,0:T(8,128)(2,1)} collective-permute-done((bf16[16,256]{1,0:T(8,128)(2,1)}, bf16[16,256]{1,0:T(8,128)(2,1)}, u32[]{:S(2)}, u32[]{:S(2)}) %collective-permute-start.3) | collective-permute-done | bytes 8224 | tf_op jit(solution)/shard_map/ppermute | solution.py:38
  31.3 2.4 by_stage.5
  37.9 13.8 %collective-permute-done.5.refs_1_ = bf16[320,1024]{1,0:T(8,128)(2,1)} collective-permute-done((bf16[320,1024]{1,0:T(8,128)(2,1)}, bf16[320,1024]{1,0:T(8,128)(2,1)}, u32[]{:S(2)}, u32[]{:S(2)}) %collective-permute-start.5) | collective-permute-done | bytes 655392 | tf_op jit(solution)/shard_map/ppermute | solution.py:38
  55.1 8.9 %collective-permute-done.12.refs_1_ = bf16[320,1024]{1,0:T(8,128)(2,1)} collective-permute-done((bf16[320,1024]{1,0:T(8,128)(2,1)}, bf16[320,1024]{1,0:T(8,128)(2,1)}, u32[]{:S(2)}, u32[]{:S(2)}) %collective-permute-start.12) | collective-permute-done | bytes 655392 | tf_op jit(solution)/shard_map/ppermute | solution.py:38
  66.1 15.3 %collective-permute-done.6.refs_2_ = bf16[320,1024]{1,0:T(8,128)(2,1)S(1)} collective-permute-done((bf16[320,1024]{1,0:T(8,128)(2,1)}, bf16[320,1024]{1,0:T(8,128)(2,1)S(1)}, u32[]{:S(2)}, u32[]{:S(2)}) %collective-permute-start.6) | collective-permute-done | bytes 655392 | tf_op jit(solution)/shard_map/ppermute | solution.py:38
  104.8 1.9 copy-done.26
  110.0 6.1 %project.3 = (bf16[1280,128]{1,0:T(8,128)(2,1)S(1)}, bf16[1280,128]{1,0:T(8,128)(2,1)S(1)}, bf16[1280,128]{1,0:T(8,128)(2,1)S(1)}, bf16[1280,512]{1,0:T(8,128)(2,1)S(1)}, bf16[1280,512]{1,0:T(8,128)(2,1)S(1)}) custom-call(s32[1]{0:T(128)} %bitcast.26.refs_0_, bf16[320,1024]{1,0:T(8,128)(2,1)S(1)} %copy-done.48, bf16[320,1024]{1,0:T(8,128)(2,1)S(1)} %copy-done.53, ...), custom_call_target="tpu_custom_call" | custom-call | flops 99999997952 | bytes 1024 | tf_op jit(solution)/shard_map/project/pallas_call | solution.py:190
  117.2 10.1 %attend.3 = (bf16[2,320,1024]{2,1,0:T(8,128)(2,1)S(1)}, bf16[2,320,1024]{2,1,0:T(8,128)(2,1)S(1)}, bf16[1280,128]{1,0:T(8,128)(2,1)S(1)}, f32[8,1280]{1,0:T(8,128)S(1)}) custom-call(s32[1]{0:T(128)} %bitcast.26.refs_0_, s32[1,1280]{1,0:T(1,128)S(1)} %copy-done.17, bf16[1280,128]{1,0:T(8,128)(2,1)S(1)} %get-tuple-element.132.refs_2_.refs_7_.refs_10_, ...), custom_call_target="tpu_custom_call" | custom-call | flops 99999997952 | bytes 1024 | tf_op jit(solution)/shard_map/attend/pallas_call | solution.py:190
  128.1 2.4 collective-permute-done.18
  133.5 6.5 %project.4 = (bf16[1280,128]{1,0:T(8,128)(2,1)S(1)}, bf16[1280,128]{1,0:T(8,128)(2,1)S(1)}, bf16[1280,128]{1,0:T(8,128)(2,1)S(1)}, bf16[1280,512]{1,0:T(8,128)(2,1)S(1)}, bf16[1280,512]{1,0:T(8,128)(2,1)S(1)}) custom-call(s32[1]{0:T(128)} %bitcast.26.refs_0_, bf16[320,1024]{1,0:T(8,128)(2,1)S(1)} %get-tuple-element.126.refs_3_.refs_1_.refs_0_.refs_6_, ...), custom_call_target="tpu_custom_call" | custom-call | flops 99999997952 | bytes 1024 | tf_op jit(solution)/shard_map/project/pallas_call | solution.py:190
  141.2 9.8 %attend.4 = (bf16[2,320,1024]{2,1,0:T(8,128)(2,1)S(1)}, bf16[2,320,1024]{2,1,0:T(8,128)(2,1)S(1)}, bf16[1280,128]{1,0:T(8,128)(2,1)S(1)}, f32[8,1280]{1,0:T(8,128)S(1)}) custom-call(s32[1]{0:T(128)} %bitcast.26.refs_0_, s32[1,1280]{1,0:T(1,128)S(1)} %copy-done.15, bf16[1280,128]{1,0:T(8,128)(2,1)S(1)} %get-tuple-element.139.refs_2_.refs_7_.refs_6_, ...), custom_call_target="tpu_custom_call" | custom-call | flops 99999997952 | bytes 1024 | tf_op jit(solution)/shard_map/attend/pallas_call | solution.py:190
  155.8 14.4 %collective-permute-done.22.refs_2_ = bf16[320,1024]{1,0:T(8,128)(2,1)S(1)} collective-permute-done((bf16[320,1024]{1,0:T(8,128)(2,1)S(1)}, bf16[320,1024]{1,0:T(8,128)(2,1)S(1)}, u32[]{:S(2)}, u32[]{:S(2)}) %collective-permute-start.22) | collective-permute-done | bytes 655392 | tf_op jit(solution)/shard_map/ppermute | solution.py:38
  174.4 13.6 %collective-permute-done.25.refs_7_.refs_4_ = bf16[320,1024]{1,0:T(8,128)(2,1)} collective-permute-done((bf16[320,1024]{1,0:T(8,128)(2,1)}, bf16[320,1024]{1,0:T(8,128)(2,1)}, u32[]{:S(2)}, u32[]{:S(2)}) %collective-permute-start.25) | collective-permute-done | bytes 655392 | tf_op jit(solution)/shard_map/ppermute | solution.py:38
  189.1 1.9 copy-done.29
  191.0 2.2 add_rows.3.refs_15_.refs_1_.refs_5_.refs_6_.refs_0_
  197.2 33.1 %whole_layer.1 = (bf16[2,320,1024]{2,1,0:T(8,128)(2,1)}, bf16[2,320,1024]{2,1,0:T(8,128)(2,1)}, bf16[2,320,1024]{2,1,0:T(8,128)(2,1)}, bf16[2,320,1024]{2,1,0:T(...) custom-call(s32[1]{0:T(128)} %bitcast.26.refs_0_, ...), custom_call_target="tpu_custom_call" | custom-call | flops 99999997952 | bytes 1024 | tf_op jit(solution)/shard_map/whole_layer/pallas_call | solution.py:190
  233.6 1.9 collective-permute-done.31.refs_4_
  238.2 6.5 %project.5 = (bf16[1280,128]{1,0:T(8,128)(2,1)S(1)}, bf16[1280,128]{1,0:T(8,128)(2,1)S(1)}, bf16[1280,128]{1,0:T(8,128)(2,1)S(1)}, bf16[1280,512]{1,0:T(8,128)(2,1)S(1)}, bf16[1280,512]{1,0:T(8,128)(2,1)S(1)}) custom-call(s32[1]{0:T(128)} %bitcast.26.refs_0_, bf16[320,1024]{1,0:T(8,128)(2,1)} %add_rows.3.refs_15_.refs_1_.refs_5_.refs_6_.refs_0_, ...), custom_call_target="tpu_custom_call" | custom-call | flops 99999997952 | bytes 1024 | tf_op jit(solution)/shard_map/project/pallas_call | solution.py:190
  245.9 9.7 %attend.5 = (bf16[2,320,1024]{2,1,0:T(8,128)(2,1)S(1)}, bf16[2,320,1024]{2,1,0:T(8,128)(2,1)S(1)}, bf16[1280,128]{1,0:T(8,128)(2,1)S(1)}, f32[8,1280]{1,0:T(8,128)S(1)}) custom-call(s32[1]{0:T(128)} %bitcast.26.refs_0_, s32[1,1280]{1,0:T(1,128)S(1)} %copy-done.15, bf16[1280,128]{1,0:T(8,128)(2,1)S(1)} %get-tuple-element.158.refs_2_.refs_7_.refs_10_, ...), custom_call_target="tpu_custom_call" | custom-call | flops 99999997952 | bytes 1024 | tf_op jit(solution)/shard_map/attend/pallas_call | solution.py:190
  255.9 3.2 picked_sum.21.refs_3_
  263.3 1.8 picked_sum.23.refs_20_
  266.1 20.7 %whole_backward.2 = (bf16[2,320,1024]{2,1,0:T(8,128)(2,1)}, bf16[2,320,1024]{2,1,0:T(8,128)(2,1)}, bf16[1280,512]{1,0:T(8,128)(2,1)}, f32[1,512]{1,0:T(1,128)}, ...) custom-call(s32[1]{0:T(128)} %bitcast.26.refs_0_, bf16[320,1024]{1,0:T(8,128)(2,1)} %copy-done.6, ...), custom_call_target="tpu_custom_call" | custom-call | flops 99999997952 | bytes 1024 | tf_op jit(solution)/shard_map/whole_backward/pallas_call | solution.py:190
  290.8 3.4 norm_back.2.refs_3_.refs_1_.refs_2_.refs_4_
  294.2 1.8 convert_reduce_fusion.1
  298.7 2.6 picked_sum.25.refs_14_
  301.4 8.1 %weight_grads.4.refs_4_ = bf16[4,640,256]{2,1,0:T(8,128)(2,1)} custom-call(s32[1]{0:T(128)} %bitcast.26.refs_0_, f32[6,1024]{1,0:T(8,128)} %reshape.342.refs_12_.refs_6_.refs_18_.refs_1_.refs_8_, bf16[320,1024]{1,0:T(8,128)(2,1)} %copy-done.8, bf16[320,1024]{1,0:T(8,128)(2,1)} %copy-done.59, bf16[320,1024]{1,0:T(8,128)(2,1)} %copy-done.58, ...), custom_call_target="tpu_custom_call" | custom-call | flops 99999997952 | bytes 1024 | tf_op jit(solution)/shard_map/weight_grads/pallas_call | solution.py:190
  310.2 4.8 collective-permute-done.36.refs_3_
  316.3 2.6 picked_sum.26.refs_15_
  320.7 12.3 %weight_grads.5.refs_4_ = bf16[4,912,256]{2,1,0:T(8,128)(2,1)} custom-call(s32[1]{0:T(128)} %bitcast.26.refs_0_, f32[6,1024]{1,0:T(8,128)} %reshape.342.refs_12_.refs_6_.refs_18_.refs_1_.refs_8_, bf16[320,1024]{1,0:T(8,128)(2,1)} %add_rows.2.refs_4_.refs_5_.refs_0_.refs_2_, bf16[320,1024]{1,0:T(8,128)(2,1)} %copy-done.122, ...), custom_call_target="tpu_custom_call" | custom-call | flops 99999997952 | bytes 1024 | tf_op jit(solution)/shard_map/weight_grads/pallas_call | solution.py:190
  337.2 3.0 picked_sum.27.refs_4_
  341.9 3.3 norm_back.3.refs_0_.refs_6_.refs_1_.refs_4_
  348.4 20.6 %whole_backward.3 = (bf16[2,320,1024]{2,1,0:T(8,128)(2,1)}, bf16[2,320,1024]{2,1,0:T(8,128)(2,1)}, bf16[1280,512]{1,0:T(8,128)(2,1)}, f32[1,512]{1,0:T(1,128)}, ...) custom-call(s32[1]{0:T(128)} %bitcast.26.refs_0_, ...), custom_call_target="tpu_custom_call" | custom-call | flops 99999997952 | bytes 1024 | tf_op jit(solution)/shard_map/whole_backward/pallas_call | solution.py:190
  373.2 8.1 %weight_grads.6.refs_3_ = bf16[4,640,256]{2,1,0:T(8,128)(2,1)} custom-call(s32[1]{0:T(128)} %bitcast.26.refs_0_, f32[6,1024]{1,0:T(8,128)} %copy-done.13, bf16[320,1024]{1,0:T(8,128)(2,1)} %norm_back.2.refs_3_.refs_1_.refs_2_.refs_4_, bf16[320,1024]{1,0:T(8,128)(2,1)} %collective-permute-done.40.refs_2_.refs_3_, ...), custom_call_target="tpu_custom_call" | custom-call | flops 99999997952 | bytes 1024 | tf_op jit(solution)/shard_map/weight_grads/pallas_call | solution.py:190
  387.7 6.9 %enter.1 = (bf16[1280,128]{1,0:T(8,128)(2,1)}, bf16[1280,512]{1,0:T(8,128)(2,1)}, f32[1,512]{1,0:T(1,128)}) custom-call(s32[1]{0:T(128)} %bitcast.26.refs_0_, bf16[320,1024]{1,0:T(8,128)(2,1)} %norm_back.3.refs_0_.refs_6_.refs_1_.refs_4_, bf16[320,1024]{1,0:T(8,128)(2,1)} %copy-done.123, bf16[320,1024]{1,0:T(8,128)(2,1)} %collective-permute-done.45.refs_8_.refs_3_, ...), custom_call_target="tpu_custom_call" | custom-call | flops 99999997952 | bytes 1024 | tf_op jit(solution)/shard_map/enter/pallas_call | solution.py:190
  394.6 14.8 %backward.1 = (bf16[2,320,1024]{2,1,0:T(8,128)(2,1)}, bf16[2,320,1024]{2,1,0:T(8,128)(2,1)}, bf16[1280,384]{1,0:T(8,128)(2,1)}, f32[8,1024]{1,0:T(8,128)}, f32[1,384]{1,0:T(1,128)}) custom-call(s32[1]{0:T(128)} %bitcast.26.refs_0_, bf16[320,1024]{1,0:T(8,128)(2,1)} %copy-done.45, bf16[320,1024]{1,0:T(8,128)(2,1)} %collective-permute-done.14.refs_2_.refs_7_, ...), custom_call_target="tpu_custom_call" | custom-call | flops 99999997952 | bytes 1024 | tf_op jit(solution)/shard_map/backward/pallas_call | solution.py:190
  413.4 12.3 %weight_grads.7.refs_0_ = bf16[4,912,256]{2,1,0:T(8,128)(2,1)} custom-call(s32[1]{0:T(128)} %bitcast.26.refs_0_, f32[6,1024]{1,0:T(8,128)} %copy-done.13, bf16[320,1024]{1,0:T(8,128)(2,1)} %copy-done.47, bf16[320,1024]{1,0:T(8,128)(2,1)} %copy-done.52, bf16[320,1024]{1,0:T(8,128)(2,1)} %copy-done.50, bf16[320,1024]{1,0:T(8,128)(2,1)} %copy-done.54, ...), custom_call_target="tpu_custom_call" | custom-call | flops 99999997952 | bytes 1024 | tf_op jit(solution)/shard_map/weight_grads/pallas_call | solution.py:190
  428.6 2.4 picked_sum.29.refs_4_
  435.8 12.7 %collective-permute-done.52.refs_3_ = bf16[1,320,1024]{2,1,0:T(8,128)(2,1)} collective-permute-done((bf16[1,320,1024]{2,1,0:T(8,128)(2,1)}, bf16[1,320,1024]{2,1,0:T(8,128)(2,1)}, u32[]{:S(2)}, u32[]{:S(2)}) %collective-permute-start.52) | collective-permute-done | bytes 655392 | tf_op jit(solution)/shard_map/ppermute | solution.py:38
  448.5 2.6 picked_sum.31.refs_9_
  452.4 3.7 ends.2
  456.1 2.3 collective-permute-done.56.refs_3_.refs_6_
  458.4 2.3 unpack.2
  460.8 6.8 %reduce-scatter.11.cloned.1.call-done = bf16[1,912,256]{2,1,0:T(8,128)(2,1)} async-done(((bf16[4,912,256]{2,1,0:T(8,128)(2,1)}), bf16[1,912,256]{2,1,0:T(8,128)(2,1)}) %reduce-scatter.11.cloned.1.call-update) | async-done | bytes 466960 | tf_op jit(solution)/shard_map/reduce_scatter | solution.py:1319
  476.5 4.1 ends.3
  480.7 2.8 collective-permute-done.60
  486.2 2.5 unpack.3
  (546 shorter events, 130.5 us)
Async XLA Ops:
  7.2 96.3 %all-gather.5.cloned.1.call-start = ((), (), s32[]{:S(2)}) async-start(), calls=%async_computation.8 | async-start | bytes 3973120 | tf_op jit(solution)/shard_map/all_gather | solution.py:1202
  10.2 21.1 %collective-permute-start = (bf16[1536,256]{1,0:T(8,128)(2,1)}, bf16[1536,256]{1,0:T(8,128)(2,1)}, u32[]{:S(2)}, u32[]{:S(2)}) collective-permute-start(bf16[1536,256]{1,0:T(8,128)(2,1)} %get-tuple-element.112), channel_id=1, source_target_pairs={{0,16},{16,0},{1,17},{17,1},{2,18},{18,2},{3,19},{19,3},{4,20},{20... | collective-permute-start | bytes 2359304 | tf_op jit(solution)/shard_map/ppermute | solution.py:38
  20.5 10.8 %collective-permute-start.3 = (bf16[16,256]{1,0:T(8,128)(2,1)}, bf16[16,256]{1,0:T(8,128)(2,1)}, u32[]{:S(2)}, u32[]{:S(2)}) collective-permute-start(bf16[16,256]{1,0:T(8,128)(2,1)} %pad_maximum_fusion.1.refs_1_.refs_3_), channel_id=1, source_target_pairs={{0,16},{16,0},{1,17},{17,1},{2,18},{18,2},{3,19},{19,3},{4,20},{20... | collective-permute-start | bytes 24584 | tf_op jit(solution)/shard_map/ppermute | solution.py:38
  33.7 18.0 %collective-permute-start.5 = (bf16[320,1024]{1,0:T(8,128)(2,1)}, bf16[320,1024]{1,0:T(8,128)(2,1)}, u32[]{:S(2)}, u32[]{:S(2)}) collective-permute-start(bf16[320,1024]{1,0:T(8,128)(2,1)} %get-tuple-element.115.refs_1_), channel_id=1, source_target_pairs={{0,8},{4,12},{8,0},{12,4},{1,9},{5,13},{9,1},{13,5},{2,10},{6,14},... | collective-permute-start | bytes 1966088 | tf_op jit(solution)/shard_map/ppermute | solution.py:38
  35.4 18.0 %collective-permute-start.7 = (bf16[320,1024]{1,0:T(8,128)(2,1)}, bf16[320,1024]{1,0:T(8,128)(2,1)}, u32[]{:S(2)}, u32[]{:S(2)}) collective-permute-start(bf16[320,1024]{1,0:T(8,128)(2,1)} %get-tuple-element.115.refs_1_), channel_id=1, source_target_pairs={{0,16},{16,0},{1,17},{17,1},{2,18},{18,2},{3,19},{19,3},{4,20},{20... | collective-permute-start | bytes 1966088 | tf_op jit(solution)/shard_map/ppermute | solution.py:38
  36.9 53.5 %collective-permute-start.4 = (bf16[320,1024]{1,0:T(8,128)(2,1)}, bf16[320,1024]{1,0:T(8,128)(2,1)}, u32[]{:S(2)}, u32[]{:S(2)}) collective-permute-start(bf16[320,1024]{1,0:T(8,128)(2,1)} %get-tuple-element.114.refs_1_), channel_id=1, source_target_pairs={{0,16},{16,0},{1,17},{17,1},{2,18},{18,2},{3,19},{19,3},{4,20},{20... | collective-permute-start | bytes 1966088 | tf_op jit(solution)/shard_map/ppermute | solution.py:38
  37.4 26.5 %collective-permute-start.12 = (bf16[320,1024]{1,0:T(8,128)(2,1)}, bf16[320,1024]{1,0:T(8,128)(2,1)}, u32[]{:S(2)}, u32[]{:S(2)}) collective-permute-start(bf16[320,1024]{1,0:T(8,128)(2,1)} %get-tuple-element.114.refs_1_), channel_id=1, source_target_pairs={{0,8},{4,12},{8,0},{12,4},{1,9},{5,13},{9,1},{13,5},{2,10},{6,14},... | collective-permute-start | bytes 1966088 | tf_op jit(solution)/shard_map/ppermute | solution.py:38
  37.8 150.2 %all-gather.7.cloned.1.call-start = ((), (), s32[]{:S(2)}) async-start(), calls=%async_computation.9 | async-start | bytes 3973120 | tf_op jit(solution)/shard_map/all_gather | solution.py:1237
  51.7 29.7 %collective-permute-start.6 = (bf16[320,1024]{1,0:T(8,128)(2,1)}, bf16[320,1024]{1,0:T(8,128)(2,1)S(1)}, u32[]{:S(2)}, u32[]{:S(2)}) collective-permute-start(bf16[320,1024]{1,0:T(8,128)(2,1)} %collective-permute-done.5.refs_1_), channel_id=1, source_target_pairs={{0,16},{16,0},{1,17},{17,1},{2,18},{18,2},{3,19},{19,3},{4,20},{20... | collective-permute-start | bytes 1966088 | tf_op jit(solution)/shard_map/ppermute | solution.py:38
  54.9 293.0 %reduce-scatter.5.cloned.1.call-start = ((), (), s32[]{:S(2)}) async-start(), calls=%async_computation.4 | async-start | bytes 1638400 | tf_op jit(solution)/shard_map/reduce_scatter | solution.py:1319
  64.0 29.2 %collective-permute-start.13 = (bf16[320,1024]{1,0:T(8,128)(2,1)}, bf16[320,1024]{1,0:T(8,128)(2,1)}, u32[]{:S(2)}, u32[]{:S(2)}) collective-permute-start(bf16[320,1024]{1,0:T(8,128)(2,1)} %collective-permute-done.12.refs_1_), channel_id=1, source_target_pairs={{0,16},{16,0},{1,17},{17,1},{2,18},{18,2},{3,19},{19,3},{4,20},{20... | collective-permute-start | bytes 1966088 | tf_op jit(solution)/shard_map/ppermute | solution.py:38
  131.9 19.2 %collective-permute-start.20 = (bf16[1,320,1024]{2,1,0:T(8,128)(2,1)}, bf16[1,320,1024]{2,1,0:T(8,128)(2,1)}, u32[]{:S(2)}, u32[]{:S(2)}) collective-permute-start(bf16[1,320,1024]{2,1,0:T(8,128)(2,1)} %picked_sum.16.refs_9_), channel_id=1, source_target_pairs={{0,8},{4,12},{8,0},{12,4},{1,9},{5,13},{9,1},{13,5},{2,10},{6,14},... | collective-permute-start | bytes 1966088 | tf_op jit(solution)/shard_map/ppermute | solution.py:38
  153.0 17.2 %collective-permute-start.22 = (bf16[320,1024]{1,0:T(8,128)(2,1)S(1)}, bf16[320,1024]{1,0:T(8,128)(2,1)S(1)}, u32[]{:S(2)}, u32[]{:S(2)}) collective-permute-start(bf16[320,1024]{1,0:T(8,128)(2,1)S(1)} %bitcast.193), channel_id=1, source_target_pairs={{0,16},{16,0},{1,17},{17,1},{2,18},{18,2},{3,19},{19,3},{4,20},{20... | collective-permute-start | bytes 1966088 | tf_op jit(solution)/shard_map/ppermute | solution.py:38
  155.1 16.9 %collective-permute-start.21 = (bf16[1,320,1024]{2,1,0:T(8,128)(2,1)S(1)}, bf16[1,320,1024]{2,1,0:T(8,128)(2,1)S(1)}, u32[]{:S(2)}, u32[]{:S(2)}) collective-permute-start(bf16[1,320,1024]{2,1,0:T(8,128)(2,1)S(1)} %picked_sum.18.refs_4_), channel_id=1, source_target_pairs={{0,8},{4,12},{8,0},{12,4},{1,9},{5,13},{9,1},{13,5},{2,10},{6,14},... | collective-permute-start | bytes 1966088 | tf_op jit(solution)/shard_map/ppermute | solution.py:38
  171.3 16.6 %collective-permute-start.25 = (bf16[320,1024]{1,0:T(8,128)(2,1)}, bf16[320,1024]{1,0:T(8,128)(2,1)}, u32[]{:S(2)}, u32[]{:S(2)}) collective-permute-start(bf16[320,1024]{1,0:T(8,128)(2,1)} %add_rows.2.refs_4_.refs_5_.refs_0_.refs_2_), channel_id=1, source_target_pairs={{0,8},{4,12},{8,0},{12,4},{1,9},{5,13},{9,1},{13,5},{2,10},{6,14},... | collective-permute-start | bytes 1966088 | tf_op jit(solution)/shard_map/ppermute | solution.py:38
  172.9 16.2 %collective-permute-start.23 = (bf16[320,1024]{1,0:T(8,128)(2,1)S(1)}, bf16[320,1024]{1,0:T(8,128)(2,1)}, u32[]{:S(2)}, u32[]{:S(2)}) collective-permute-start(bf16[320,1024]{1,0:T(8,128)(2,1)S(1)} %bitcast.191), channel_id=1, source_target_pairs={{0,16},{16,0},{1,17},{17,1},{2,18},{18,2},{3,19},{19,3},{4,20},{20... | collective-permute-start | bytes 1966088 | tf_op jit(solution)/shard_map/ppermute | solution.py:38
  174.4 22.0 %collective-permute-start.24 = (bf16[320,1024]{1,0:T(8,128)(2,1)}, bf16[320,1024]{1,0:T(8,128)(2,1)S(1)}, u32[]{:S(2)}, u32[]{:S(2)}) collective-permute-start(bf16[320,1024]{1,0:T(8,128)(2,1)} %add_rows.2.refs_4_.refs_5_.refs_0_.refs_2_), channel_id=1, source_target_pairs={{0,4},{4,0},{8,12},{12,8},{1,5},{5,1},{9,13},{13,9},{2,6},{6,2},{1... | collective-permute-start | bytes 1966088 | tf_op jit(solution)/shard_map/ppermute | solution.py:38
  187.9 8.5 %collective-permute-start.26 = (bf16[320,1024]{1,0:T(8,128)(2,1)}, bf16[320,1024]{1,0:T(8,128)(2,1)}, u32[]{:S(2)}, u32[]{:S(2)}) collective-permute-start(bf16[320,1024]{1,0:T(8,128)(2,1)} %collective-permute-done.25.refs_7_.refs_4_), channel_id=1, source_target_pairs={{0,4},{4,0},{8,12},{12,8},{1,5},{5,1},{9,13},{13,9},{2,6},{6,2},{1... | collective-permute-start | bytes 1966088 | tf_op jit(solution)/shard_map/ppermute | solution.py:38
  193.2 38.5 %collective-permute-start.28 = (bf16[320,1024]{1,0:T(8,128)(2,1)}, bf16[320,1024]{1,0:T(8,128)(2,1)}, u32[]{:S(2)}, u32[]{:S(2)}) collective-permute-start(bf16[320,1024]{1,0:T(8,128)(2,1)} %add_rows.3.refs_15_.refs_1_.refs_5_.refs_6_.refs_0_), channel_id=1, source_target_pairs={{0,8},{4,12},{8,0},{12,4},{1,9},{5,13},{9,1},{13,5},{2,10},{6,14},... | collective-permute-start | bytes 1966088 | tf_op jit(solution)/shard_map/ppermute | solution.py:38
  231.6 6.1 %collective-permute-start.27 = (bf16[320,1024]{1,0:T(8,128)(2,1)}, bf16[320,1024]{1,0:T(8,128)(2,1)S(1)}, u32[]{:S(2)}, u32[]{:S(2)}) collective-permute-start(bf16[320,1024]{1,0:T(8,128)(2,1)} %add_rows.3.refs_15_.refs_1_.refs_5_.refs_6_.refs_0_), channel_id=1, source_target_pairs={{0,4},{4,0},{8,12},{12,8},{1,5},{5,1},{9,13},{13,9},{2,6},{6,2},{1... | collective-permute-start | bytes 1966088 | tf_op jit(solution)/shard_map/ppermute | solution.py:38
  231.7 6.1 %collective-permute-start.29 = (bf16[320,1024]{1,0:T(8,128)(2,1)}, bf16[320,1024]{1,0:T(8,128)(2,1)S(1)}, u32[]{:S(2)}, u32[]{:S(2)}) collective-permute-start(bf16[320,1024]{1,0:T(8,128)(2,1)} %collective-permute-done.28.refs_3_.refs_7_.refs_8_), channel_id=1, source_target_pairs={{0,4},{4,0},{8,12},{12,8},{1,5},{5,1},{9,13},{13,9},{2,6},{6,2},{1... | collective-permute-start | bytes 1966088 | tf_op jit(solution)/shard_map/ppermute | solution.py:38
  237.0 18.8 %collective-permute-start.33 = (bf16[1,320,1024]{2,1,0:T(8,128)(2,1)}, bf16[1,320,1024]{2,1,0:T(8,128)(2,1)}, u32[]{:S(2)}, u32[]{:S(2)}) collective-permute-start(bf16[1,320,1024]{2,1,0:T(8,128)(2,1)} %picked_sum.20.refs_9_), channel_id=1, source_target_pairs={{0,8},{4,12},{8,0},{12,4},{1,9},{5,13},{9,1},{13,5},{2,10},{6,14},... | collective-permute-start | bytes 1966088 | tf_op jit(solution)/shard_map/ppermute | solution.py:38
  259.1 31.0 %collective-permute-start.35 = (bf16[320,1024]{1,0:T(8,128)(2,1)}, bf16[320,1024]{1,0:T(8,128)(2,1)}, u32[]{:S(2)}, u32[]{:S(2)}) collective-permute-start(bf16[320,1024]{1,0:T(8,128)(2,1)} %bitcast.47.refs_1_), channel_id=1, source_target_pairs={{0,16},{16,0},{1,17},{17,1},{2,18},{18,2},{3,19},{19,3},{4,20},{20... | collective-permute-start | bytes 1966088 | tf_op jit(solution)/shard_map/ppermute | solution.py:38
  262.1 36.7 %collective-permute-start.37 = (bf16[1,320,1024]{2,1,0:T(8,128)(2,1)}, bf16[1,320,1024]{2,1,0:T(8,128)(2,1)}, u32[]{:S(2)}, u32[]{:S(2)}) collective-permute-start(bf16[1,320,1024]{2,1,0:T(8,128)(2,1)} %picked_sum.22.refs_3_), channel_id=1, source_target_pairs={{0,8},{4,12},{8,0},{12,4},{1,9},{5,13},{9,1},{13,5},{2,10},{6,14},... | collective-permute-start | bytes 1966088 | tf_op jit(solution)/shard_map/ppermute | solution.py:38
  265.2 68.1 %collective-permute-start.39 = (bf16[1,320,1024]{2,1,0:T(8,128)(2,1)}, bf16[1,320,1024]{2,1,0:T(8,128)(2,1)}, u32[]{:S(2)}, u32[]{:S(2)}) collective-permute-start(bf16[1,320,1024]{2,1,0:T(8,128)(2,1)} %picked_sum.23.refs_20_), channel_id=1, source_target_pairs={{0,8},{4,12},{8,0},{12,4},{1,9},{5,13},{9,1},{13,5},{2,10},{6,14},... | collective-permute-start | bytes 1966088 | tf_op jit(solution)/shard_map/ppermute | solution.py:38
  286.8 9.2 %collective-permute-start.34 = (bf16[2,320,1024]{2,1,0:T(8,128)(2,1)}, bf16[2,320,1024]{2,1,0:T(8,128)(2,1)S(1)}, u32[]{:S(2)}, u32[]{:S(2)}) collective-permute-start(bf16[2,320,1024]{2,1,0:T(8,128)(2,1)} %get-tuple-element.169), channel_id=1, source_target_pairs={{0,4},{4,0},{8,12},{12,8},{1,5},{5,1},{9,13},{13,9},{2,6},{6,2},{1... | collective-permute-start | bytes 3932168 | tf_op jit(solution)/shard_map/ppermute | solution.py:38
  297.5 17.5 %collective-permute-start.36 = (bf16[1,320,1024]{2,1,0:T(8,128)(2,1)}, bf16[1,320,1024]{2,1,0:T(8,128)(2,1)}, u32[]{:S(2)}, u32[]{:S(2)}) collective-permute-start(bf16[1,320,1024]{2,1,0:T(8,128)(2,1)} %picked_sum.24.refs_4_), channel_id=1, source_target_pairs={{0,8},{4,12},{8,0},{12,4},{1,9},{5,13},{9,1},{13,5},{2,10},{6,14},... | collective-permute-start | bytes 1966088 | tf_op jit(solution)/shard_map/ppermute | solution.py:38
  309.5 77.3 %reduce-scatter.7.cloned.1.call-start = ((), (), s32[]{:S(2)}) async-start(), calls=%async_computation.5 | async-start | bytes 2334720 | tf_op jit(solution)/shard_map/reduce_scatter | solution.py:1319
  309.6 38.2 %collective-permute-start.43 = (bf16[320,1024]{1,0:T(8,128)(2,1)}, bf16[320,1024]{1,0:T(8,128)(2,1)}, u32[]{:S(2)}, u32[]{:S(2)}) collective-permute-start(bf16[320,1024]{1,0:T(8,128)(2,1)} %bitcast.53.refs_6_), channel_id=1, source_target_pairs={{0,16},{16,0},{1,17},{17,1},{2,18},{18,2},{3,19},{19,3},{4,20},{20... | collective-permute-start | bytes 1966088 | tf_op jit(solution)/shard_map/ppermute | solution.py:38
  318.9 23.0 %collective-permute-start.38 = (bf16[320,1024]{1,0:T(8,128)(2,1)}, bf16[320,1024]{1,0:T(8,128)(2,1)}, u32[]{:S(2)}, u32[]{:S(2)}) collective-permute-start(bf16[320,1024]{1,0:T(8,128)(2,1)} %bitcast.48.refs_1_), channel_id=1, source_target_pairs={{0,16},{16,0},{1,17},{17,1},{2,18},{18,2},{3,19},{19,3},{4,20},{20... | collective-permute-start | bytes 1966088 | tf_op jit(solution)/shard_map/ppermute | solution.py:38
  319.6 22.3 %collective-permute-start.41 = (bf16[320,1024]{1,0:T(8,128)(2,1)}, bf16[320,1024]{1,0:T(8,128)(2,1)}, u32[]{:S(2)}, u32[]{:S(2)}) collective-permute-start(bf16[320,1024]{1,0:T(8,128)(2,1)} %norm_back.2.refs_3_.refs_1_.refs_2_.refs_4_), channel_id=1, source_target_pairs={{0,8},{4,12},{8,0},{12,4},{1,9},{5,13},{9,1},{13,5},{2,10},{6,14},... | collective-permute-start | bytes 1966088 | tf_op jit(solution)/shard_map/ppermute | solution.py:38
  333.0 15.4 %collective-permute-start.40 = (bf16[320,1024]{1,0:T(8,128)(2,1)}, bf16[320,1024]{1,0:T(8,128)(2,1)}, u32[]{:S(2)}, u32[]{:S(2)}) collective-permute-start(bf16[320,1024]{1,0:T(8,128)(2,1)} %norm_back.2.refs_3_.refs_1_.refs_2_.refs_4_), channel_id=1, source_target_pairs={{0,4},{4,0},{8,12},{12,8},{1,5},{5,1},{9,13},{13,9},{2,6},{6,2},{1... | collective-permute-start | bytes 1966088 | tf_op jit(solution)/shard_map/ppermute | solution.py:38
  333.2 101.8 %reduce-scatter.9.cloned.1.call-start = ((), (), s32[]{:S(2)}) async-start(), calls=%async_computation.6 | async-start | bytes 1638400 | tf_op jit(solution)/shard_map/reduce_scatter | solution.py:1319
  340.2 47.4 %collective-permute-start.49 = (bf16[320,1024]{1,0:T(8,128)(2,1)}, bf16[320,1024]{1,0:T(8,128)(2,1)}, u32[]{:S(2)}, u32[]{:S(2)}) collective-permute-start(bf16[320,1024]{1,0:T(8,128)(2,1)} %bitcast.57.refs_6_), channel_id=1, source_target_pairs={{0,16},{16,0},{1,17},{17,1},{2,18},{18,2},{3,19},{19,3},{4,20},{20... | collective-permute-start | bytes 1966088 | tf_op jit(solution)/shard_map/ppermute | solution.py:38
  341.9 6.6 %collective-permute-start.42 = (bf16[320,1024]{1,0:T(8,128)(2,1)}, bf16[320,1024]{1,0:T(8,128)(2,1)}, u32[]{:S(2)}, u32[]{:S(2)}) collective-permute-start(bf16[320,1024]{1,0:T(8,128)(2,1)} %collective-permute-done.41.refs_3_.refs_4_), channel_id=1, source_target_pairs={{0,4},{4,0},{8,12},{12,8},{1,5},{5,1},{9,13},{13,9},{2,6},{6,2},{1... | collective-permute-start | bytes 1966088 | tf_op jit(solution)/shard_map/ppermute | solution.py:38
  345.2 24.1 %collective-permute-start.45 = (bf16[320,1024]{1,0:T(8,128)(2,1)}, bf16[320,1024]{1,0:T(8,128)(2,1)}, u32[]{:S(2)}, u32[]{:S(2)}) collective-permute-start(bf16[320,1024]{1,0:T(8,128)(2,1)} %norm_back.3.refs_0_.refs_6_.refs_1_.refs_4_), channel_id=1, source_target_pairs={{0,8},{4,12},{8,0},{12,4},{1,9},{5,13},{9,1},{13,5},{2,10},{6,14},... | collective-permute-start | bytes 1966088 | tf_op jit(solution)/shard_map/ppermute | solution.py:38
  370.9 16.7 %collective-permute-start.48 = (bf16[640,256]{1,0:T(8,128)(2,1)}, bf16[640,256]{1,0:T(8,128)(2,1)}, u32[]{:S(2)}, u32[]{:S(2)}) collective-permute-start(bf16[640,256]{1,0:T(8,128)(2,1)} %bitcast.52.refs_1_.refs_2_), channel_id=1, source_target_pairs={{0,16},{16,0},{1,17},{17,1},{2,18},{18,2},{3,19},{19,3},{4,20},{20... | collective-permute-start | bytes 983048 | tf_op jit(solution)/shard_map/ppermute | solution.py:38
  371.7 9.7 %collective-permute-start.47 = (bf16[2,320,1024]{2,1,0:T(8,128)(2,1)}, bf16[2,320,1024]{2,1,0:T(8,128)(2,1)S(1)}, u32[]{:S(2)}, u32[]{:S(2)}) collective-permute-start(bf16[2,320,1024]{2,1,0:T(8,128)(2,1)} %get-tuple-element.191), channel_id=1, source_target_pairs={{0,4},{4,0},{8,12},{12,8},{1,5},{5,1},{9,13},{13,9},{2,6},{6,2},{1... | collective-permute-start | bytes 3932168 | tf_op jit(solution)/shard_map/ppermute | solution.py:38
  381.4 86.2 %reduce-scatter.11.cloned.1.call-start = ((), (), s32[]{:S(2)}) async-start(), calls=%async_computation.7 | async-start | bytes 2334720 | tf_op jit(solution)/shard_map/reduce_scatter | solution.py:1319
  385.4 46.5 %collective-permute-start.53 = (bf16[1,320,1024]{2,1,0:T(8,128)(2,1)}, bf16[1,320,1024]{2,1,0:T(8,128)(2,1)}, u32[]{:S(2)}, u32[]{:S(2)}) collective-permute-start(bf16[1,320,1024]{2,1,0:T(8,128)(2,1)} %picked_sum.28.refs_7_), channel_id=1, source_target_pairs={{0,8},{4,12},{8,0},{12,4},{1,9},{5,13},{9,1},{13,5},{2,10},{6,14},... | collective-permute-start | bytes 1966088 | tf_op jit(solution)/shard_map/ppermute | solution.py:38
  386.9 26.6 %collective-permute-start.51 = (bf16[912,256]{1,0:T(8,128)(2,1)}, bf16[912,256]{1,0:T(8,128)(2,1)}, u32[]{:S(2)}, u32[]{:S(2)}) collective-permute-start(bf16[912,256]{1,0:T(8,128)(2,1)} %bitcast.169), channel_id=1, source_target_pairs={{0,16},{16,0},{1,17},{17,1},{2,18},{18,2},{3,19},{19,3},{4,20},{20... | collective-permute-start | bytes 1400840 | tf_op jit(solution)/shard_map/ppermute | solution.py:38
  409.5 17.8 %collective-permute-start.50 = (bf16[2,320,1024]{2,1,0:T(8,128)(2,1)}, bf16[2,320,1024]{2,1,0:T(8,128)(2,1)}, u32[]{:S(2)}, u32[]{:S(2)}) collective-permute-start(bf16[2,320,1024]{2,1,0:T(8,128)(2,1)} %get-tuple-element.196), channel_id=1, source_target_pairs={{0,4},{4,0},{8,12},{12,8},{1,5},{5,1},{9,13},{13,9},{2,6},{6,2},{1... | collective-permute-start | bytes 3932168 | tf_op jit(solution)/shard_map/ppermute | solution.py:38
  431.0 17.5 %collective-permute-start.52 = (bf16[1,320,1024]{2,1,0:T(8,128)(2,1)}, bf16[1,320,1024]{2,1,0:T(8,128)(2,1)}, u32[]{:S(2)}, u32[]{:S(2)}) collective-permute-start(bf16[1,320,1024]{2,1,0:T(8,128)(2,1)} %picked_sum.29.refs_4_), channel_id=1, source_target_pairs={{0,8},{4,12},{8,0},{12,4},{1,9},{5,13},{9,1},{13,5},{2,10},{6,14},... | collective-permute-start | bytes 1966088 | tf_op jit(solution)/shard_map/ppermute | solution.py:38
  433.7 18.8 %collective-permute-start.55 = (bf16[320,1024]{1,0:T(8,128)(2,1)S(1)}, bf16[320,1024]{1,0:T(8,128)(2,1)S(1)}, u32[]{:S(2)}, u32[]{:S(2)}) collective-permute-start(bf16[320,1024]{1,0:T(8,128)(2,1)S(1)} %bitcast.189), channel_id=1, source_target_pairs={{0,16},{16,0},{1,17},{17,1},{2,18},{18,2},{3,19},{19,3},{4,20},{20... | collective-permute-start | bytes 1966088 | tf_op jit(solution)/shard_map/ppermute | solution.py:38
  434.9 23.5 %collective-permute-start.56 = (bf16[640,256]{1,0:T(8,128)(2,1)}, bf16[640,256]{1,0:T(8,128)(2,1)}, u32[]{:S(2)}, u32[]{:S(2)}) collective-permute-start(bf16[640,256]{1,0:T(8,128)(2,1)} %bitcast.195), channel_id=1, source_target_pairs={{0,16},{16,0},{1,17},{17,1},{2,18},{18,2},{3,19},{19,3},{4,20},{20... | collective-permute-start | bytes 983048 | tf_op jit(solution)/shard_map/ppermute | solution.py:38
  451.1 23.5 %collective-permute-start.54 = (bf16[320,1024]{1,0:T(8,128)(2,1)}, bf16[320,1024]{1,0:T(8,128)(2,1)}, u32[]{:S(2)}, u32[]{:S(2)}) collective-permute-start(bf16[320,1024]{1,0:T(8,128)(2,1)} %bitcast.63.refs_2_), channel_id=1, source_target_pairs={{0,16},{16,0},{1,17},{17,1},{2,18},{18,2},{3,19},{19,3},{4,20},{20... | collective-permute-start | bytes 1966088 | tf_op jit(solution)/shard_map/ppermute | solution.py:38
  470.3 15.8 %collective-permute-start.61 = (bf16[912,256]{1,0:T(8,128)(2,1)}, bf16[912,256]{1,0:T(8,128)(2,1)S(1)}, u32[]{:S(2)}, u32[]{:S(2)}) collective-permute-start(bf16[912,256]{1,0:T(8,128)(2,1)} %bitcast.172), channel_id=1, source_target_pairs={{0,16},{16,0},{1,17},{17,1},{2,18},{18,2},{3,19},{19,3},{4,20},{20... | collective-permute-start | bytes 1400840 | tf_op jit(solution)/shard_map/ppermute | solution.py:38
  473.0 10.5 %collective-permute-start.60 = (f32[832]{0:T(1024)S(1)}, f32[832]{0:T(1024)S(1)}, u32[]{:S(2)}, u32[]{:S(2)}) collective-permute-start(f32[832]{0:T(1024)S(1)} %get-tuple-element.249), channel_id=1, source_target_pairs={{0,16},{16,0},{1,17},{17,1},{2,18},{18,2},{3,19},{19,3},{4,20},{20... | collective-permute-start | bytes 9992 | tf_op jit(solution)/shard_map/ppermute | solution.py:38
  (146 other events, 1374.5 us)
Sparse Core Ops, SparseCore 0:
  37.9 65.5 all-gather.4
  105.6 62.6 all-gather.6
  309.6 30.5 reduce-scatter.4
  343.0 38.7 reduce-scatter.6
  383.9 30.3 reduce-scatter.8
  427.4 40.0 reduce-scatter.10

commit v4 on v3

--- a/solution.py
+++ b/solution.py
@@ -308,15 +308,43 @@
         leaving.reached(at.stop)
 
 
-def do_enter(w, c_all, low, slope_ref, grad_context, pre_ref, sum_ref):
+def do_enter(w, products, slope_ref, grad_context, pre_ref, sum_ref):
     total = jnp.zeros(sum_ref.shape, F32)
     for at in chunks():
-        both = dot(c_all[at], low[...], 1, 1)
+        both = products(at)
         grad_context[at] = both[:, :w].astype(BF)
         grad_pre = (both[:, w:] * slope_ref[at].astype(F32)).astype(BF)
         pre_ref[at] = grad_pre
         total = total + jnp.sum(grad_pre.astype(F32), axis=0, keepdims=True)
     sum_ref[...] = total
+
+
+def cotangent_kernel(blocks, row, *refs):
+    index_ref = refs[0]
+    c_refs = refs[1 : 1 + blocks]
+    low_ref, out_ref, c_all, low, c_sems, low_sems = refs[1 + blocks :]
+    loads = loads_of_weights(low_ref, row, low, low_sems)
+    loads += copies_of_blocks(index_ref[0], c_refs, c_all, c_sems)
+    start_all(loads)
+    wait_all(loads)
+    for at in chunks():
+        out_ref[at] = dot(c_all[at], low[...], 1, 1)
+
+
+def cotangent(order, index, c_blocks, weights):
+    w, ff = weights["w"], weights["ff"]
+    low, row = weights["low"]
+    blocks = len(c_blocks)
+    return order.call(
+        functools.partial(cotangent_kernel, blocks, row),
+        "cotangent",
+        24,
+        [SMEM] + [ANY] * (blocks + 1),
+        [VMEM],
+        [shape((TOK_MB, w + ff), F32)],
+        held(D) + [pltpu.VMEM((w + ff, D), BF)] + dma(blocks, low.shape[0]),
+        [index, *c_blocks, low],
+    )[0]
 
 
 def do_backward(
@@ -496,7 +524,9 @@
     loads += copies_of_blocks(index_ref[0], c_refs, c_all, c_sems)
     start_all(loads)
     wait_all(loads)
-    do_enter(w, c_all, low, slope_ref, context_ref, pre_ref, sum_ref)
+    do_enter(
+        w, lambda at: dot(c_all[at], low[...], 1, 1), slope_ref, context_ref, pre_ref, sum_ref
+    )
 
 
 def enter(order, index, c_blocks, kept, weights):
@@ -571,25 +601,34 @@
     )
 
 
-def whole_backward_kernel(blocks, heads, w, main_row, low_row, *refs):
+def products_of(ready, index, source_refs, low_ref, low_row, c_all, low, c_sems, low_sems):
+    if ready:
+        loads = [pltpu.make_async_copy(source_refs[0], c_all, c_sems.at[0])]
+        return loads, lambda at: c_all[at]
+    loads = loads_of_weights(low_ref, low_row, low, low_sems)
+    loads += copies_of_blocks(index, source_refs, c_all, c_sems)
+    return loads, lambda at: dot(c_all[at], low[...], 1, 1)
+
+
+def whole_backward_kernel(blocks, given, heads, w, main_row, low_row, *refs):
     index_ref = refs[0]
-    c_refs = refs[1 : 1 + blocks]
-    x_refs = refs[1 + blocks : 1 + 2 * blocks]
-    starts_ref, q_ref, k_ref, v_ref, context_ref, logs_ref, slope_ref = refs[
-        1 + 2 * blocks : 8 + 2 * blocks
-    ]
-    main_ref, low_ref, norms_ref, table_ref = refs[8 + 2 * blocks : 12 + 2 * blocks]
-    keep_ref, send_ref, pre_ref, pre_sum_ref, *outs = refs[12 + 2 * blocks : 19 + 2 * blocks]
-    c_all, x_all, main, low, partial, grad_context, *scratch = refs[19 + 2 * blocks : 29 + 2 * blocks]
-    c_sems, x_sems, main_sems, low_sems, out_sems = refs[29 + 2 * blocks :]
-    loads = loads_of_weights(low_ref, low_row, low, low_sems)
-    loads += copies_of_blocks(index_ref[0], c_refs, c_all, c_sems)
+    c_refs = refs[1 : 1 + given]
+    refs = refs[1 + given :]
+    x_refs = refs[:blocks]
+    starts_ref, q_ref, k_ref, v_ref, context_ref, logs_ref, slope_ref = refs[blocks : 7 + blocks]
+    main_ref, low_ref, norms_ref, table_ref = refs[7 + blocks : 11 + blocks]
+    keep_ref, send_ref, pre_ref, pre_sum_ref, *outs = refs[11 + blocks : 18 + blocks]
+    c_all, x_all, main, low, partial, grad_context, *scratch = refs[18 + blocks : 28 + blocks]
+    c_sems, x_sems, main_sems, low_sems, out_sems = refs[28 + blocks :]
+    loads, products = products_of(
+        given < blocks, index_ref[0], c_refs, low_ref, low_row, c_all, low, c_sems, low_sems
+    )
     later = copies_of_blocks(index_ref[0], x_refs, x_all, x_sems)
     later += loads_of_weights(main_ref, main_row, main, main_sems)
     start_all(loads + later)
     leaving = Leaving(index_ref[0], partial, keep_ref, send_ref, out_sems)
     wait_all(loads)
-    do_enter(w, c_all, low, slope_ref, grad_context, pre_ref, pre_sum_ref)
+    do_enter(w, products, slope_ref, grad_context, pre_ref, pre_sum_ref)
     do_backward(
         heads,
         w,
@@ -614,6 +653,12 @@
     leaving.wait()
 
 
+def held_cotangent(c_blocks, blocks):
+    if len(c_blocks) < blocks:
+        return [pltpu.VMEM(c_blocks[0].shape, F32)]
+    return held(D)
+
+
 def whole_backward(order, index, c_blocks, x_blocks, kept, weights, angles):
     queries, keys, values, _, slope, context, logs = kept
     blocks = len(x_blocks)
@@ -622,17 +667,20 @@
     low, low_row = weights["low"]
     dp = main.shape[0]
     return order.call(
-        functools.partial(whole_backward_kernel, blocks, heads, w, main_row, low_row),
+        functools.partial(
+            whole_backward_kernel, blocks, len(c_blocks), heads, w, main_row, low_row
+        ),
         "whole_backward",
         60,
-        [SMEM] + [ANY] * (2 * blocks) + [VMEM] * 7 + [ANY] * 2 + [VMEM] * 2,
+        [SMEM] + [ANY] * (len(c_blocks) + blocks) + [VMEM] * 7 + [ANY] * 2 + [VMEM] * 2,
         [ANY, ANY] + [VMEM] * 5,
         halves_of(blocks)
         + rows_of(ff)
         + [shape((1, ff), F32)]
         + rows_of(3 * w)
         + [shape((8, D), F32), shape((1, 3 * w), F32)],
-        held(D, D)
+        held_cotangent(c_blocks, blocks)
+        + held(D)
         + [pltpu.VMEM((3 * w + ff, D), BF), pltpu.VMEM((w + ff, D), BF)]
         + held(D, w)
         + scratch_of_backward(w)
@@ -658,24 +706,23 @@
 
 def layer_kernel(blocks, heads, w, main_row, low_row, *refs):
     index_ref = refs[0]
-    c_refs = refs[1 : 1 + blocks]
-    x_refs = refs[1 + blocks : 1 + 2 * blocks]
-    starts_ref, main_ref, low_ref, norms_ref, bias_ref, table_ref = refs[
-        1 + 2 * blocks : 7 + 2 * blocks
-    ]
+    c_ref = refs[1]
+    refs = refs[2:]
+    x_refs = refs[:blocks]
+    starts_ref, main_ref, low_ref, norms_ref, bias_ref, table_ref = refs[blocks : 6 + blocks]
     (y_keep, y_send, u_keep, u_send, hidden_ref, context_ref, pre_ref, pre_sum_ref, *outs) = refs[
-        7 + 2 * blocks : 18 + 2 * blocks
+        6 + blocks : 17 + blocks
     ]
     (c_all, x_all, main, low, y_all, u_all, q_ref, k_ref, v_ref, slope_ref, grad_context) = refs[
-        18 + 2 * blocks : 29 + 2 * blocks
+        17 + blocks : 28 + blocks
     ]
-    logs_ref, v_turned, *scratch = refs[29 + 2 * blocks : 35 + 2 * blocks]
-    c_sems, x_sems, main_sems, low_sems, y_sems, u_sems = refs[35 + 2 * blocks :]
+    logs_ref, v_turned, *scratch = refs[28 + blocks : 34 + blocks]
+    c_sems, x_sems, main_sems, low_sems, y_sems, u_sems = refs[34 + blocks :]
     index = index_ref[0]
     loads = copies_of_blocks(index, x_refs, x_all, x_sems)
     loads += loads_of_weights(main_ref, main_row, main, main_sems)
     low_loads = loads_of_weights(low_ref, low_row, low, low_sems)
-    c_loads = copies_of_blocks(index, c_refs, c_all, c_sems)
+    c_loads = [pltpu.make_async_copy(c_ref, c_all, c_sems.at[0])]
     start_all(loads + low_loads + c_loads)
     y_leaving = Leaving(index, y_all, y_keep, y_send, y_sems)
     u_leaving = Leaving(index, u_all, u_keep, u_send, u_sems)
@@ -700,7 +747,7 @@
         y_leaving,
     )
     wait_all(c_loads)
-    do_enter(w, c_all, low, slope_ref, grad_context, pre_ref, pre_sum_ref)
+    do_enter(w, lambda at: c_all[at], slope_ref, grad_context, pre_ref, pre_sum_ref)
     do_backward(
         heads,
         w,
@@ -726,7 +773,7 @@
     u_leaving.wait()
 
 
-def whole_layer(order, index, c_blocks, x_blocks, weights, angles):
+def whole_layer(order, index, products, x_blocks, weights, angles):
     blocks = len(x_blocks)
     w, heads, ff = weights["w"], weights["heads"], weights["ff"]
     main, main_row = weights["main"]
@@ -736,7 +783,7 @@
         functools.partial(layer_kernel, blocks, heads, w, main_row, low_row),
         "whole_layer",
         60,
-        [SMEM] + [ANY] * (2 * blocks) + [VMEM] + [ANY] * 2 + [VMEM] * 3,
+        [SMEM] + [ANY] * (1 + blocks) + [VMEM] + [ANY] * 2 + [VMEM] * 3,
         [ANY] * 4 + [VMEM] * 7,
         halves_of(blocks)
         + halves_of(blocks)
@@ -744,15 +791,16 @@
         + [shape((1, ff), F32)]
         + rows_of(3 * w)
         + [shape((8, D), F32), shape((1, 3 * w), F32)],
-        held(D, D)
+        [pltpu.VMEM(products.shape, F32)]
+        + held(D)
         + [pltpu.VMEM((3 * w + ff, D), BF), pltpu.VMEM((w + ff, D), BF)]
         + held(D, D, w, w, w, ff, w)
         + [pltpu.VMEM((8, TOK_MB), F32), pltpu.VMEM((w, TOK_MB), BF)]
         + scratch_of_backward(w)
-        + dma(blocks, blocks, dp, dp, blocks, blocks),
+        + dma(1, blocks, dp, dp, blocks, blocks),
         [
             index,
-            *c_blocks,
+            products,
             *x_blocks,
             angles[0],
             main,
@@ -764,6 +812,29 @@
     )
 
 
+def put_vectors(out_ref, begin, stage_ref, vec_a, vec_b, raw_a, raw_b, pre_a, pre_b, own_ref, order_ref, raw_order, pre_order):
+    dp, _, share = out_ref.shape
+    half = dp // 2
+    rows = [vec_a[:4] + vec_b[:4], own_ref[...], jnp.zeros((3, vec_a.shape[1]), F32)]
+    norms = dot(jnp.concatenate(rows, axis=0).astype(BF), order_ref[...], 1, 0)
+
+    def moved(first, second, order):
+        value = (first[...] + second[...]).astype(BF)
+        return dot(jnp.broadcast_to(value, (8, value.shape[1])), order[...], 1, 0)[:1]
+
+    raw, pre = moved(raw_a, raw_b, raw_order), moved(pre_a, pre_b, pre_order)
+    for j in range(dp):
+        mine = jnp.where(stage_ref[0] == j // half, 1.0, 0.0)
+        cols = slice(j % half * share, (j % half + 1) * share)
+        block = [
+            norms[:5, j * share : (j + 1) * share],
+            raw[:, cols] * mine,
+            pre[:, cols] * mine,
+            jnp.zeros((SMALL - 7, share), F32),
+        ]
+        out_ref[j, begin : begin + SMALL] = jnp.concatenate(block, axis=0).astype(BF)
+
+
 def grads_kernel(blocks, plan, extra, *refs):
     index_ref, norms_ref = refs[:2]
     with_cot = None in plan
@@ -772,7 +843,7 @@
     row_refs = refs[2 : 2 + count]
     lefts = refs[2 + count : 2 + count + MB * len(plan)]
     rest = refs[2 + count + MB * len(plan) :]
-    extra_ref, rest = (rest[0], rest[1:]) if extra else (None, rest)
+    extras, rest = rest[:extra], rest[extra:]
     out_ref, total, *scratch = rest
     side_sems, sems = scratch.pop(), scratch.pop()
     sides, scratch = scratch[: MB * len(plan)], scratch[MB * len(plan) :]
@@ -812,7 +883,7 @@
                     out_ref[j, rows] = part[:, j * share : (j + 1) * share].astype(BF)
             begin = rows.stop
     if extra:
-        out_ref[:, begin:] = extra_ref[...]
+        put_vectors(out_ref, begin, *extras)
 
 
 def weight_grads(order, index, c_blocks, x_blocks, pieces, norms, dp, extra=()):
@@ -820,13 +891,13 @@
     blocks = len(x_blocks[0])
     rows = [block for unit in (c_blocks if None in plan else x_blocks) for block in unit]
     lefts = [left for part, _ in pieces for left in part]
-    size = sum(part[0].shape[1] for part, _ in pieces) + sum(value.shape[1] for value in extra)
+    size = sum(part[0].shape[1] for part, _ in pieces) + (SMALL if extra else 0)
     buffers = len(set(plan))
     return order.call(
-        functools.partial(grads_kernel, blocks, plan, bool(extra)),
+        functools.partial(grads_kernel, blocks, plan, len(extra)),
         "weight_grads",
         60,
-        [SMEM, VMEM] + [ANY] * (len(rows) + len(lefts)) + [VMEM] * len(extra),
+        [SMEM, VMEM] + [ANY] * (len(rows) + len(lefts)) + [SMEM, *[VMEM] * (len(extra) - 1)][: len(extra)],
         [VMEM],
         [shape((dp, size, D // dp), BF)],
         [pltpu.VMEM((size, D), F32)]
@@ -1249,20 +1320,27 @@
     entered = [[None] * MB, [None] * MB]
     back = [[None] * MB, [None] * MB]
 
+    def picks(sources, count):
+        return (jnp.arange(count)[:, None] == sources[None, :]).astype(BF)
+
+    column = jnp.arange(D)
+    order_norms = picks(
+        column % share // piece * (D // tensor) + column // share * piece + column % piece, D
+    )
+    column = jnp.arange(dp // 2 * share)
+    group, place = column // share, column % share
+    order_raw = picks(
+        jnp.where(place < 3 * piece, place // piece * w + group * piece + place % piece, -1), 3 * w
+    )
+    up_piece = 2 * ff // dp
+    order_pre = picks(jnp.where(place < up_piece, group * up_piece + place, -1), ff)
+
     def vector_rows(layer, cots):
         own = sum(jnp.sum(rows.astype(F32), axis=0) for rows in cots)
         own = own * jnp.where(at_first, 1.0, 0.0)
-        rows = sum(back[layer][unit][1] for unit in units)[:4]
-        rows = jnp.concatenate([rows, own[None]]).reshape(5, tensor, dp, piece)
-        rows = rows.transpose(2, 0, 1, 3).reshape(dp, 5, share)
-        raw = sum(back[layer][unit][2] for unit in units).reshape(3, w)[:, :width]
-        raw = raw.reshape(3, dp // 2, piece).transpose(1, 0, 2).reshape(dp // 2, 3 * piece)
-        pre = sum(entered[layer][unit][2] for unit in units).reshape(dp // 2, -1)
-        pads = [jnp.pad(item, ((0, 0), (0, share - item.shape[1]))) for item in (raw, pre)]
-        held = lax.dynamic_update_slice(
-            jnp.zeros((dp, 2, share), F32), jnp.stack(pads, axis=1), (stage * (dp // 2), 0, 0)
-        )
-        return [jnp.pad(jnp.concatenate([rows, held], axis=1), ((0, 0), (0, SMALL - 7), (0, 0))).astype(BF)]
+        sources = ((back, 1), (back, 2), (entered, 2))
+        parts = [source[layer][unit][at] for source, at in sources for unit in units]
+        return [stage_word, *parts, own[None], order_norms, order_raw, order_pre]
 
     def vectors_from(rows_0, rows_1):
         both = jnp.stack([rows_0, rows_1]).astype(F32)
@@ -1299,7 +1377,7 @@
 
     def run_layer(unit, blocks):
         y_keep, y_send, u_keep, u_send, hidden, context, pre, pre_sum, *rest = whole_layer(
-            order, index, c_blocks[unit], blocks, layers[1], angles[unit]
+            order, index, products[unit], blocks, layers[1], angles[unit]
         )
         kept[1][unit] = [None, None, None, hidden, None, context, None]
         entered[1][unit] = [None, pre, pre_sum]
@@ -1329,12 +1407,12 @@
     middle_a = add_rows(order, x_rows[0], sum_a, layers[0])
     far_a = gather_far(middle_a)
     sum_b.cross(order)
-    order.pause()
+    layers[1].update(vectors_of(after(stack_1, order.last[0]), row))
+    products = [cotangent(order, index, c_blocks[unit], layers[1]) for unit in units]
     blocks_a = gather_near(order, far_a)
     order.hold(stack_1)
     middle_b = add_rows(order, x_rows[1], sum_b, layers[0])
     far_b = gather_far(middle_b)
-    layers[1].update(vectors_of(after(stack_1, middle_b), row))
 
     y_a, sum_a = run_layer(0, blocks_a)
     order.pause()
@@ -1348,7 +1426,7 @@
     order.hold(y_b.terms[1])
     y_a.send(order)
     y_b.send(order)
-    sum_b = run_backward(1, 1, c_blocks[1], blocks_b)
+    sum_b = run_backward(1, 1, [products[1]], blocks_b)
     cot_a = norm_back(order, middle_a, sum_a, cot_rows[0])
     sum_b.send(order)
     y_a.cross(order)
@@ -1370,12 +1448,9 @@
     outer_0 = reduced(0, ("out", "down"), cot_blocks, x_blocks)
     sum_a.send(order)
     order.hold(from_outer_1, inner_1, y_b.other)
-    entered[0][1] = enter(order, index, cot_blocks[1], kept[0][1], layers[0])
+    order.pause()
     from_inner_1 = swap(inner_1, "pipe", 0)
-    keep, send, *back[0][1] = backward(
-        order, index, x_blocks[1], kept[0][1], entered[0][1], layers[0], angles[1]
-    )
-    sum_b = Sum(index, keep, send)
+    sum_b = run_backward(0, 1, cot_blocks[1], x_blocks[1])
     order.hold(from_inner_1)
     inner_0 = reduced(0, ("up", "qkv"), cot_blocks, x_blocks, vector_rows(0, (cot_a, cot_b)))
     from_outer_0 = swap(after(outer_0, order.last[0]), "pipe", 0)

time: 501 us -> 493 us (0.984)
  waiting for transfers between devices: 126 us -> 110 us
    ppermute x59, waiting for transfers between devices: 118 us -> 101 us  [swap(): return lax.ppermute(value, axis, [(i, i ^ 1 << bit) for i in range(count)])]
    unnamed x265 -> x293, local copies, waits for them, and re-layouts: 33.8 us -> 38.2 us
    pallas_call x66 -> x67, Pallas kernels: 249 us -> 253 us  [call(): pl.pallas_call(outer, in_specs=in_specs + [ANY] * len(deps), out_specs=ou...]
  transfers between devices with their start and end apart: 68 -> 68, of which waited for: 28 -> 28; matrix products, arithmetic and copies ran while one was open for 5% -> 5% of each run, Pallas kernels for 49% -> 51%
where the time goes in v4:
time: 493 us; the launch traced here: 487 us
  Pallas kernels  253 us (51%)
  waiting for transfers between devices  110 us (22%)
  starting transfers between devices  46.3 us (9%)
  local copies, waits for them, and re-layouts  45.8 us (9%)
  between operations  16.3 us (3%)
  other arithmetic  16.1 us (3%)
    pallas_call x67, Pallas kernels, call(): pl.pallas_call(outer, in_specs=in_specs + [ANY] * len(deps), out_specs=ou...  253 us
    ppermute x59, waiting for transfers between devices, swap(): return lax.ppermute(value, axis, [(i, i ^ 1 << bit) for i in range(count)])  101 us
    ppermute x59, starting transfers between devices, swap(): return lax.ppermute(value, axis, [(i, i ^ 1 << bit) for i in range(count)])  43.6 us
    unnamed x293, local copies, waits for them, and re-layouts  38.2 us
  transfers between devices with their start and end apart: 68, of which 28 were waited for; matrix products, arithmetic and copies ran while one was open for 5% of the time, Pallas kernels for 51%

profile of v4, /device:TPU:0, one launch (start us, length us, event | category | flops | bytes accessed | tf_op | source)
XLA Modules:
  0.0 487.3 jit_solution(9195505742435701346)
XLA Ops:
  7.9 3.0 collective-permute-start.1
  10.9 3.0 pack.1
  20.8 2.2 fusion.refs_22_
  25.6 7.8 %collective-permute-done.3.refs_4_ = bf16[16,256]{1,0:T(8,128)(2,1)} collective-permute-done((bf16[16,256]{1,0:T(8,128)(2,1)}, bf16[16,256]{1,0:T(8,128)(2,1)}, u32[]{:S(2)}, u32[]{:S(2)}) %collective-permute-start.3) | collective-permute-done | bytes 8224 | tf_op jit(solution)/shard_map/ppermute | solution.py:38
  33.4 2.4 by_stage.5
  40.0 15.3 %collective-permute-done.5.refs_1_ = bf16[320,1024]{1,0:T(8,128)(2,1)} collective-permute-done((bf16[320,1024]{1,0:T(8,128)(2,1)}, bf16[320,1024]{1,0:T(8,128)(2,1)}, u32[]{:S(2)}, u32[]{:S(2)}) %collective-permute-start.5) | collective-permute-done | bytes 655392 | tf_op jit(solution)/shard_map/ppermute | solution.py:38
  57.5 9.2 %collective-permute-done.12.refs_1_ = bf16[320,1024]{1,0:T(8,128)(2,1)} collective-permute-done((bf16[320,1024]{1,0:T(8,128)(2,1)}, bf16[320,1024]{1,0:T(8,128)(2,1)}, u32[]{:S(2)}, u32[]{:S(2)}) %collective-permute-start.12) | collective-permute-done | bytes 655392 | tf_op jit(solution)/shard_map/ppermute | solution.py:38
  67.9 13.9 %collective-permute-done.6.refs_2_ = bf16[320,1024]{1,0:T(8,128)(2,1)S(1)} collective-permute-done((bf16[320,1024]{1,0:T(8,128)(2,1)}, bf16[320,1024]{1,0:T(8,128)(2,1)S(1)}, u32[]{:S(2)}, u32[]{:S(2)}) %collective-permute-start.6) | collective-permute-done | bytes 655392 | tf_op jit(solution)/shard_map/ppermute | solution.py:38
  105.8 1.9 copy-done.23
  109.9 6.1 %project.3 = (bf16[1280,128]{1,0:T(8,128)(2,1)S(1)}, bf16[1280,128]{1,0:T(8,128)(2,1)S(1)}, bf16[1280,128]{1,0:T(8,128)(2,1)S(1)}, bf16[1280,512]{1,0:T(8,128)(2,1)S(1)}, bf16[1280,512]{1,0:T(8,128)(2,1)S(1)}) custom-call(s32[1]{0:T(128)} %bitcast.26.refs_0_, bf16[320,1024]{1,0:T(8,128)(2,1)S(1)} %get-tuple-element.117.refs_3_.refs_1_.refs_0_.refs_5_.refs_2_, ...), custom_call_target="tpu_custom_call" | custom-call | flops 99999997952 | bytes 1024 | tf_op jit(solution)/shard_map/project/pallas_call | solution.py:190
  117.1 9.9 %attend.3 = (bf16[2,320,1024]{2,1,0:T(8,128)(2,1)S(1)}, bf16[2,320,1024]{2,1,0:T(8,128)(2,1)S(1)}, bf16[1280,128]{1,0:T(8,128)(2,1)S(1)}, f32[8,1280]{1,0:T(8,128)S(1)}) custom-call(s32[1]{0:T(128)} %bitcast.26.refs_0_, s32[1,1280]{1,0:T(1,128)S(1)} %copy-done.19, bf16[1280,128]{1,0:T(8,128)(2,1)S(1)} %get-tuple-element.131.refs_2_.refs_7_.refs_10_, ...), custom_call_target="tpu_custom_call" | custom-call | flops 99999997952 | bytes 1024 | tf_op jit(solution)/shard_map/attend/pallas_call | solution.py:190
  127.7 2.4 collective-permute-done.18
  133.2 6.1 %project.4 = (bf16[1280,128]{1,0:T(8,128)(2,1)S(1)}, bf16[1280,128]{1,0:T(8,128)(2,1)S(1)}, bf16[1280,128]{1,0:T(8,128)(2,1)S(1)}, bf16[1280,512]{1,0:T(8,128)(2,1)S(1)}, bf16[1280,512]{1,0:T(8,128)(2,1)S(1)}) custom-call(s32[1]{0:T(128)} %bitcast.26.refs_0_, bf16[320,1024]{1,0:T(8,128)(2,1)S(1)} %copy-done.46, bf16[320,1024]{1,0:T(8,128)(2,1)S(1)} %copy-done.62, ...), custom_call_target="tpu_custom_call" | custom-call | flops 99999997952 | bytes 1024 | tf_op jit(solution)/shard_map/project/pallas_call | solution.py:190
  140.4 10.1 %attend.4 = (bf16[2,320,1024]{2,1,0:T(8,128)(2,1)S(1)}, bf16[2,320,1024]{2,1,0:T(8,128)(2,1)S(1)}, bf16[1280,128]{1,0:T(8,128)(2,1)S(1)}, f32[8,1280]{1,0:T(8,128)S(1)}) custom-call(s32[1]{0:T(128)} %bitcast.26.refs_0_, s32[1,1280]{1,0:T(1,128)S(1)} %copy-done.16, bf16[1280,128]{1,0:T(8,128)(2,1)S(1)} %get-tuple-element.138.refs_2_.refs_7_.refs_10_, ...), custom_call_target="tpu_custom_call" | custom-call | flops 99999997952 | bytes 1024 | tf_op jit(solution)/shard_map/attend/pallas_call | solution.py:190
  155.6 14.1 %collective-permute-done.22.refs_2_ = bf16[320,1024]{1,0:T(8,128)(2,1)S(1)} collective-permute-done((bf16[320,1024]{1,0:T(8,128)(2,1)S(1)}, bf16[320,1024]{1,0:T(8,128)(2,1)S(1)}, u32[]{:S(2)}, u32[]{:S(2)}) %collective-permute-start.22) | collective-permute-done | bytes 655392 | tf_op jit(solution)/shard_map/ppermute | solution.py:38
  176.3 1.9 copy-done.26
  179.3 3.3 cotangent.2.refs_6_.refs_1_
  182.7 3.5 cotangent.3.refs_4_.refs_1_
  191.1 1.9 copy-done.28
  193.0 1.9 copy-done.97
  194.9 2.2 add_rows.3.refs_12_.refs_1_.refs_2_.refs_6_.refs_0_.refs_5_
  199.3 30.6 %whole_layer.1 = (bf16[2,320,1024]{2,1,0:T(8,128)(2,1)}, bf16[2,320,1024]{2,1,0:T(8,128)(2,1)}, bf16[2,320,1024]{2,1,0:T(8,128)(2,1)}, bf16[2,320,1024]{2,1,0:T(...) custom-call(s32[1]{0:T(128)} %bitcast.26.refs_0_, ...), custom_call_target="tpu_custom_call" | custom-call | flops 99999997952 | bytes 1024 | tf_op jit(solution)/shard_map/whole_layer/pallas_call | solution.py:190
  237.7 6.5 %project.5 = (bf16[1280,128]{1,0:T(8,128)(2,1)S(1)}, bf16[1280,128]{1,0:T(8,128)(2,1)S(1)}, bf16[1280,128]{1,0:T(8,128)(2,1)S(1)}, bf16[1280,512]{1,0:T(8,128)(2,1)S(1)}, bf16[1280,512]{1,0:T(8,128)(2,1)S(1)}) custom-call(s32[1]{0:T(128)} %bitcast.26.refs_0_, bf16[320,1024]{1,0:T(8,128)(2,1)} %add_rows.3.refs_12_.refs_1_.refs_2_.refs_6_.refs_0_.refs_5_, ...), custom_call_target="tpu_custom_call" | custom-call | flops 99999997952 | bytes 1024 | tf_op jit(solution)/shard_map/project/pallas_call | solution.py:190
  245.3 9.8 %attend.5 = (bf16[2,320,1024]{2,1,0:T(8,128)(2,1)S(1)}, bf16[2,320,1024]{2,1,0:T(8,128)(2,1)S(1)}, bf16[1280,128]{1,0:T(8,128)(2,1)S(1)}, f32[8,1280]{1,0:T(8,128)S(1)}) custom-call(s32[1]{0:T(128)} %bitcast.26.refs_0_, s32[1,1280]{1,0:T(1,128)S(1)} %copy-done.17, bf16[1280,128]{1,0:T(8,128)(2,1)S(1)} %get-tuple-element.156.refs_2_.refs_7_, ...), custom_call_target="tpu_custom_call" | custom-call | flops 99999997952 | bytes 1024 | tf_op jit(solution)/shard_map/attend/pallas_call | solution.py:190
  255.4 3.2 picked_sum.21.refs_3_
  265.7 18.6 %whole_backward.3 = (bf16[2,320,1024]{2,1,0:T(8,128)(2,1)}, bf16[2,320,1024]{2,1,0:T(8,128)(2,1)}, bf16[1280,512]{1,0:T(8,128)(2,1)}, f32[1,512]{1,0:T(1,128)}, ...) custom-call(s32[1]{0:T(128)} %bitcast.26.refs_0_, f32[1280,640]{1,0:T(8,128)} %copy-done.96, ...), custom_call_target="tpu_custom_call" | custom-call | flops 99999997952 | bytes 1024 | tf_op jit(solution)/shard_map/whole_backward/pallas_call | solution.py:190
  285.0 3.5 norm_back.2.refs_3_.refs_1_.refs_2_.refs_4_
  293.1 2.6 picked_sum.25.refs_14_
  295.7 8.2 %weight_grads.4.refs_4_ = bf16[4,640,256]{2,1,0:T(8,128)(2,1)} custom-call(s32[1]{0:T(128)} %bitcast.26.refs_0_, f32[6,1024]{1,0:T(8,128)} %reshape.402.refs_9_.refs_6_.refs_15_.refs_1_.refs_8_, bf16[320,1024]{1,0:T(8,128)(2,1)} %copy-done.9, bf16[320,1024]{1,0:T(8,128)(2,1)} %copy-done.67, bf16[320,1024]{1,0:T(8,128)(2,1)} %copy-done.63, ...), custom_call_target="tpu_custom_call" | custom-call | flops 99999997952 | bytes 1024 | tf_op jit(solution)/shard_map/weight_grads/pallas_call | solution.py:190
  304.5 4.8 collective-permute-done.36.refs_3_
  310.6 2.6 picked_sum.26.refs_25_
  315.0 14.0 %weight_grads.5.refs_4_ = bf16[4,912,256]{2,1,0:T(8,128)(2,1)} custom-call(s32[1]{0:T(128)} %bitcast.26.refs_0_, f32[6,1024]{1,0:T(8,128)} %reshape.402.refs_9_.refs_6_.refs_15_.refs_1_.refs_8_, bf16[320,1024]{1,0:T(8,128)(2,1)} %add_rows.2.refs_4_.refs_2_.refs_0_.refs_5_, bf16[320,1024]{1,0:T(8,128)(2,1)} %copy-done.136, ...), custom_call_target="tpu_custom_call" | custom-call | flops 99999997952 | bytes 1024 | tf_op jit(solution)/shard_map/weight_grads/pallas_call | solution.py:190
  330.7 2.7 picked_sum.27.refs_4_
  335.6 3.3 norm_back.3.refs_0_.refs_6_.refs_1_.refs_4_
  342.2 20.7 %whole_backward.4 = (bf16[2,320,1024]{2,1,0:T(8,128)(2,1)}, bf16[2,320,1024]{2,1,0:T(8,128)(2,1)}, bf16[1280,512]{1,0:T(8,128)(2,1)}, f32[1,512]{1,0:T(1,128)}, ...) custom-call(s32[1]{0:T(128)} %bitcast.26.refs_0_, ...), custom_call_target="tpu_custom_call" | custom-call | flops 99999997952 | bytes 1024 | tf_op jit(solution)/shard_map/whole_backward/pallas_call | solution.py:190
  367.0 8.1 %weight_grads.6.refs_3_ = bf16[4,640,256]{2,1,0:T(8,128)(2,1)} custom-call(s32[1]{0:T(128)} %bitcast.26.refs_0_, f32[6,1024]{1,0:T(8,128)} %copy-done.14, bf16[320,1024]{1,0:T(8,128)(2,1)} %norm_back.2.refs_3_.refs_1_.refs_2_.refs_4_, bf16[320,1024]{1,0:T(8,128)(2,1)} %collective-permute-done.40.refs_2_.refs_3_, ...), custom_call_target="tpu_custom_call" | custom-call | flops 99999997952 | bytes 1024 | tf_op jit(solution)/shard_map/weight_grads/pallas_call | solution.py:190
  382.9 20.7 %whole_backward.5 = (bf16[2,320,1024]{2,1,0:T(8,128)(2,1)}, bf16[2,320,1024]{2,1,0:T(8,128)(2,1)}, bf16[1280,512]{1,0:T(8,128)(2,1)}, f32[1,512]{1,0:T(1,128)}, ...) custom-call(s32[1]{0:T(128)} %bitcast.26.refs_0_, ...), custom_call_target="tpu_custom_call" | custom-call | flops 99999997952 | bytes 1024 | tf_op jit(solution)/shard_map/whole_backward/pallas_call | solution.py:190
  404.9 13.6 %weight_grads.7.refs_0_ = bf16[4,912,256]{2,1,0:T(8,128)(2,1)} custom-call(s32[1]{0:T(128)} %bitcast.26.refs_0_, f32[6,1024]{1,0:T(8,128)} %copy-done.14, bf16[320,1024]{1,0:T(8,128)(2,1)} %copy-done.49, bf16[320,1024]{1,0:T(8,128)(2,1)} %copy-done.55, bf16[320,1024]{1,0:T(8,128)(2,1)} %copy-done.51, bf16[320,1024]{1,0:T(8,128)(2,1)} %copy-done.53, ...), custom_call_target="tpu_custom_call" | custom-call | flops 99999997952 | bytes 1024 | tf_op jit(solution)/shard_map/weight_grads/pallas_call | solution.py:190
  421.4 2.4 picked_sum.29.refs_4_
  428.6 12.7 %collective-permute-done.52.refs_3_ = bf16[1,320,1024]{2,1,0:T(8,128)(2,1)} collective-permute-done((bf16[1,320,1024]{2,1,0:T(8,128)(2,1)}, bf16[1,320,1024]{2,1,0:T(8,128)(2,1)}, u32[]{:S(2)}, u32[]{:S(2)}) %collective-permute-start.52) | collective-permute-done | bytes 655392 | tf_op jit(solution)/shard_map/ppermute | solution.py:38
  441.3 2.6 picked_sum.31.refs_9_
  445.3 3.7 ends.2
  449.0 2.2 collective-permute-done.56.refs_3_.refs_6_
  451.2 2.3 unpack.2
  453.6 5.5 %reduce-scatter.11.cloned.1.call-done = bf16[1,912,256]{2,1,0:T(8,128)(2,1)} async-done(((bf16[4,912,256]{2,1,0:T(8,128)(2,1)}), bf16[1,912,256]{2,1,0:T(8,128)(2,1)}) %reduce-scatter.11.cloned.1.call-update) | async-done | bytes 466960 | tf_op jit(solution)/shard_map/reduce_scatter | solution.py:1397
  468.3 4.1 ends.3
  472.4 2.7 collective-permute-done.60
  477.8 2.5 unpack.3
  (545 shorter events, 135.2 us)
Async XLA Ops:
  7.2 97.3 %all-gather.5.cloned.1.call-start = ((), (), s32[]{:S(2)}) async-start(), calls=%async_computation.8 | async-start | bytes 3973120 | tf_op jit(solution)/shard_map/all_gather | solution.py:1273
  7.9 15.2 %collective-permute-start.1 = (bf16[1,6,64]{2,1,0:T(8,128)(2,1)S(1)}, bf16[1,6,64]{2,1,0:T(8,128)(2,1)S(1)}, u32[]{:S(2)}, u32[]{:S(2)}) collective-permute-start(bf16[1,6,64]{2,1,0:T(8,128)(2,1)S(1)} %maximum_bitcast_fusion.1), channel_id=1, source_target_pairs={{0,8},{4,12},{8,0},{12,4},{1,9},{5,13},{9,1},{13,5},{2,10},{6,14},... | collective-permute-start | bytes 2312 | tf_op jit(solution)/shard_map/ppermute | solution.py:38
  13.9 19.6 %collective-permute-start = (bf16[1536,256]{1,0:T(8,128)(2,1)}, bf16[1536,256]{1,0:T(8,128)(2,1)}, u32[]{:S(2)}, u32[]{:S(2)}) collective-permute-start(bf16[1536,256]{1,0:T(8,128)(2,1)} %get-tuple-element.111), channel_id=1, source_target_pairs={{0,16},{16,0},{1,17},{17,1},{2,18},{18,2},{3,19},{19,3},{4,20},{20... | collective-permute-start | bytes 2359304 | tf_op jit(solution)/shard_map/ppermute | solution.py:38
  25.1 8.3 %collective-permute-start.3 = (bf16[16,256]{1,0:T(8,128)(2,1)}, bf16[16,256]{1,0:T(8,128)(2,1)}, u32[]{:S(2)}, u32[]{:S(2)}) collective-permute-start(bf16[16,256]{1,0:T(8,128)(2,1)} %pad_maximum_fusion.1.refs_1_.refs_3_), channel_id=1, source_target_pairs={{0,16},{16,0},{1,17},{17,1},{2,18},{18,2},{3,19},{19,3},{4,20},{20... | collective-permute-start | bytes 24584 | tf_op jit(solution)/shard_map/ppermute | solution.py:38
  35.8 20.0 %collective-permute-start.7 = (bf16[320,1024]{1,0:T(8,128)(2,1)}, bf16[320,1024]{1,0:T(8,128)(2,1)}, u32[]{:S(2)}, u32[]{:S(2)}) collective-permute-start(bf16[320,1024]{1,0:T(8,128)(2,1)} %get-tuple-element.114.refs_1_), channel_id=1, source_target_pairs={{0,16},{16,0},{1,17},{17,1},{2,18},{18,2},{3,19},{19,3},{4,20},{20... | collective-permute-start | bytes 1966088 | tf_op jit(solution)/shard_map/ppermute | solution.py:38
  37.4 18.0 %collective-permute-start.5 = (bf16[320,1024]{1,0:T(8,128)(2,1)}, bf16[320,1024]{1,0:T(8,128)(2,1)}, u32[]{:S(2)}, u32[]{:S(2)}) collective-permute-start(bf16[320,1024]{1,0:T(8,128)(2,1)} %get-tuple-element.114.refs_1_), channel_id=1, source_target_pairs={{0,8},{4,12},{8,0},{12,4},{1,9},{5,13},{9,1},{13,5},{2,10},{6,14},... | collective-permute-start | bytes 1966088 | tf_op jit(solution)/shard_map/ppermute | solution.py:38
  37.9 53.0 %collective-permute-start.4 = (bf16[320,1024]{1,0:T(8,128)(2,1)}, bf16[320,1024]{1,0:T(8,128)(2,1)}, u32[]{:S(2)}, u32[]{:S(2)}) collective-permute-start(bf16[320,1024]{1,0:T(8,128)(2,1)} %get-tuple-element.113.refs_1_), channel_id=1, source_target_pairs={{0,16},{16,0},{1,17},{17,1},{2,18},{18,2},{3,19},{19,3},{4,20},{20... | collective-permute-start | bytes 1966088 | tf_op jit(solution)/shard_map/ppermute | solution.py:38
  38.2 28.5 %collective-permute-start.12 = (bf16[320,1024]{1,0:T(8,128)(2,1)}, bf16[320,1024]{1,0:T(8,128)(2,1)}, u32[]{:S(2)}, u32[]{:S(2)}) collective-permute-start(bf16[320,1024]{1,0:T(8,128)(2,1)} %get-tuple-element.113.refs_1_), channel_id=1, source_target_pairs={{0,8},{4,12},{8,0},{12,4},{1,9},{5,13},{9,1},{13,5},{2,10},{6,14},... | collective-permute-start | bytes 1966088 | tf_op jit(solution)/shard_map/ppermute | solution.py:38
  39.9 133.5 %all-gather.7.cloned.1.call-start = ((), (), s32[]{:S(2)}) async-start(), calls=%async_computation.9 | async-start | bytes 3973120 | tf_op jit(solution)/shard_map/all_gather | solution.py:1308
  55.3 26.5 %collective-permute-start.6 = (bf16[320,1024]{1,0:T(8,128)(2,1)}, bf16[320,1024]{1,0:T(8,128)(2,1)S(1)}, u32[]{:S(2)}, u32[]{:S(2)}) collective-permute-start(bf16[320,1024]{1,0:T(8,128)(2,1)} %collective-permute-done.5.refs_1_), channel_id=1, source_target_pairs={{0,16},{16,0},{1,17},{17,1},{2,18},{18,2},{3,19},{19,3},{4,20},{20... | collective-permute-start | bytes 1966088 | tf_op jit(solution)/shard_map/ppermute | solution.py:38
  57.3 284.3 %reduce-scatter.5.cloned.1.call-start = ((), (), s32[]{:S(2)}) async-start(), calls=%async_computation.4 | async-start | bytes 1638400 | tf_op jit(solution)/shard_map/reduce_scatter | solution.py:1397
  66.7 26.8 %collective-permute-start.13 = (bf16[320,1024]{1,0:T(8,128)(2,1)}, bf16[320,1024]{1,0:T(8,128)(2,1)}, u32[]{:S(2)}, u32[]{:S(2)}) collective-permute-start(bf16[320,1024]{1,0:T(8,128)(2,1)} %collective-permute-done.12.refs_1_), channel_id=1, source_target_pairs={{0,16},{16,0},{1,17},{17,1},{2,18},{18,2},{3,19},{19,3},{4,20},{20... | collective-permute-start | bytes 1966088 | tf_op jit(solution)/shard_map/ppermute | solution.py:38
  131.6 19.0 %collective-permute-start.20 = (bf16[1,320,1024]{2,1,0:T(8,128)(2,1)}, bf16[1,320,1024]{2,1,0:T(8,128)(2,1)}, u32[]{:S(2)}, u32[]{:S(2)}) collective-permute-start(bf16[1,320,1024]{2,1,0:T(8,128)(2,1)} %picked_sum.16.refs_9_), channel_id=1, source_target_pairs={{0,8},{4,12},{8,0},{12,4},{1,9},{5,13},{9,1},{13,5},{2,10},{6,14},... | collective-permute-start | bytes 1966088 | tf_op jit(solution)/shard_map/ppermute | solution.py:38
  152.4 17.2 %collective-permute-start.22 = (bf16[320,1024]{1,0:T(8,128)(2,1)S(1)}, bf16[320,1024]{1,0:T(8,128)(2,1)S(1)}, u32[]{:S(2)}, u32[]{:S(2)}) collective-permute-start(bf16[320,1024]{1,0:T(8,128)(2,1)S(1)} %bitcast.181), channel_id=1, source_target_pairs={{0,16},{16,0},{1,17},{17,1},{2,18},{18,2},{3,19},{19,3},{4,20},{20... | collective-permute-start | bytes 1966088 | tf_op jit(solution)/shard_map/ppermute | solution.py:38
  154.6 17.1 %collective-permute-start.21 = (bf16[1,320,1024]{2,1,0:T(8,128)(2,1)S(1)}, bf16[1,320,1024]{2,1,0:T(8,128)(2,1)S(1)}, u32[]{:S(2)}, u32[]{:S(2)}) collective-permute-start(bf16[1,320,1024]{2,1,0:T(8,128)(2,1)S(1)} %picked_sum.18.refs_4_), channel_id=1, source_target_pairs={{0,8},{4,12},{8,0},{12,4},{1,9},{5,13},{9,1},{13,5},{2,10},{6,14},... | collective-permute-start | bytes 1966088 | tf_op jit(solution)/shard_map/ppermute | solution.py:38
  170.8 18.9 %collective-permute-start.25 = (bf16[320,1024]{1,0:T(8,128)(2,1)}, bf16[320,1024]{1,0:T(8,128)(2,1)}, u32[]{:S(2)}, u32[]{:S(2)}) collective-permute-start(bf16[320,1024]{1,0:T(8,128)(2,1)} %add_rows.2.refs_4_.refs_2_.refs_0_.refs_5_), channel_id=1, source_target_pairs={{0,8},{4,12},{8,0},{12,4},{1,9},{5,13},{9,1},{13,5},{2,10},{6,14},... | collective-permute-start | bytes 1966088 | tf_op jit(solution)/shard_map/ppermute | solution.py:38
  174.8 16.3 %collective-permute-start.23 = (bf16[320,1024]{1,0:T(8,128)(2,1)}, bf16[320,1024]{1,0:T(8,128)(2,1)}, u32[]{:S(2)}, u32[]{:S(2)}) collective-permute-start(bf16[320,1024]{1,0:T(8,128)(2,1)} %bitcast.177), channel_id=1, source_target_pairs={{0,16},{16,0},{1,17},{17,1},{2,18},{18,2},{3,19},{19,3},{4,20},{20... | collective-permute-start | bytes 1966088 | tf_op jit(solution)/shard_map/ppermute | solution.py:38
  189.1 9.3 %collective-permute-start.24 = (bf16[320,1024]{1,0:T(8,128)(2,1)}, bf16[320,1024]{1,0:T(8,128)(2,1)S(1)}, u32[]{:S(2)}, u32[]{:S(2)}) collective-permute-start(bf16[320,1024]{1,0:T(8,128)(2,1)} %add_rows.2.refs_4_.refs_2_.refs_0_.refs_5_), channel_id=1, source_target_pairs={{0,4},{4,0},{8,12},{12,8},{1,5},{5,1},{9,13},{13,9},{2,6},{6,2},{1... | collective-permute-start | bytes 1966088 | tf_op jit(solution)/shard_map/ppermute | solution.py:38
  189.7 8.7 %collective-permute-start.26 = (bf16[320,1024]{1,0:T(8,128)(2,1)}, bf16[320,1024]{1,0:T(8,128)(2,1)}, u32[]{:S(2)}, u32[]{:S(2)}) collective-permute-start(bf16[320,1024]{1,0:T(8,128)(2,1)} %collective-permute-done.25.refs_4_), channel_id=1, source_target_pairs={{0,4},{4,0},{8,12},{12,8},{1,5},{5,1},{9,13},{13,9},{2,6},{6,2},{1... | collective-permute-start | bytes 1966088 | tf_op jit(solution)/shard_map/ppermute | solution.py:38
  197.2 34.0 %collective-permute-start.28 = (bf16[320,1024]{1,0:T(8,128)(2,1)}, bf16[320,1024]{1,0:T(8,128)(2,1)}, u32[]{:S(2)}, u32[]{:S(2)}) collective-permute-start(bf16[320,1024]{1,0:T(8,128)(2,1)} %add_rows.3.refs_12_.refs_1_.refs_2_.refs_6_.refs_0_.refs_5_), channel_id=1, source_target_pairs={{0,8},{4,12},{8,0},{12,4},{1,9},{5,13},{9,1},{13,5},{2,10},{6,14},... | collective-permute-start | bytes 1966088 | tf_op jit(solution)/shard_map/ppermute | solution.py:38
  231.1 6.2 %collective-permute-start.27 = (bf16[320,1024]{1,0:T(8,128)(2,1)}, bf16[320,1024]{1,0:T(8,128)(2,1)S(1)}, u32[]{:S(2)}, u32[]{:S(2)}) collective-permute-start(bf16[320,1024]{1,0:T(8,128)(2,1)} %add_rows.3.refs_12_.refs_1_.refs_2_.refs_6_.refs_0_.refs_5_), channel_id=1, source_target_pairs={{0,4},{4,0},{8,12},{12,8},{1,5},{5,1},{9,13},{13,9},{2,6},{6,2},{1... | collective-permute-start | bytes 1966088 | tf_op jit(solution)/shard_map/ppermute | solution.py:38
  231.2 6.2 %collective-permute-start.29 = (bf16[320,1024]{1,0:T(8,128)(2,1)}, bf16[320,1024]{1,0:T(8,128)(2,1)S(1)}, u32[]{:S(2)}, u32[]{:S(2)}) collective-permute-start(bf16[320,1024]{1,0:T(8,128)(2,1)} %collective-permute-done.28.refs_3_.refs_4_.refs_8_), channel_id=1, source_target_pairs={{0,4},{4,0},{8,12},{12,8},{1,5},{5,1},{9,13},{13,9},{2,6},{6,2},{1... | collective-permute-start | bytes 1966088 | tf_op jit(solution)/shard_map/ppermute | solution.py:38
  236.5 18.9 %collective-permute-start.33 = (bf16[1,320,1024]{2,1,0:T(8,128)(2,1)}, bf16[1,320,1024]{2,1,0:T(8,128)(2,1)}, u32[]{:S(2)}, u32[]{:S(2)}) collective-permute-start(bf16[1,320,1024]{2,1,0:T(8,128)(2,1)} %picked_sum.20.refs_9_), channel_id=1, source_target_pairs={{0,8},{4,12},{8,0},{12,4},{1,9},{5,13},{9,1},{13,5},{2,10},{6,14},... | collective-permute-start | bytes 1966088 | tf_op jit(solution)/shard_map/ppermute | solution.py:38
  258.6 25.7 %collective-permute-start.35 = (bf16[320,1024]{1,0:T(8,128)(2,1)}, bf16[320,1024]{1,0:T(8,128)(2,1)}, u32[]{:S(2)}, u32[]{:S(2)}) collective-permute-start(bf16[320,1024]{1,0:T(8,128)(2,1)} %bitcast.47.refs_1_), channel_id=1, source_target_pairs={{0,16},{16,0},{1,17},{17,1},{2,18},{18,2},{3,19},{19,3},{4,20},{20... | collective-permute-start | bytes 1966088 | tf_op jit(solution)/shard_map/ppermute | solution.py:38
  261.6 31.4 %collective-permute-start.37 = (bf16[1,320,1024]{2,1,0:T(8,128)(2,1)}, bf16[1,320,1024]{2,1,0:T(8,128)(2,1)}, u32[]{:S(2)}, u32[]{:S(2)}) collective-permute-start(bf16[1,320,1024]{2,1,0:T(8,128)(2,1)} %picked_sum.22.refs_3_), channel_id=1, source_target_pairs={{0,8},{4,12},{8,0},{12,4},{1,9},{5,13},{9,1},{13,5},{2,10},{6,14},... | collective-permute-start | bytes 1966088 | tf_op jit(solution)/shard_map/ppermute | solution.py:38
  264.7 64.4 %collective-permute-start.39 = (bf16[1,320,1024]{2,1,0:T(8,128)(2,1)}, bf16[1,320,1024]{2,1,0:T(8,128)(2,1)}, u32[]{:S(2)}, u32[]{:S(2)}) collective-permute-start(bf16[1,320,1024]{2,1,0:T(8,128)(2,1)} %picked_sum.23.refs_17_), channel_id=1, source_target_pairs={{0,8},{4,12},{8,0},{12,4},{1,9},{5,13},{9,1},{13,5},{2,10},{6,14},... | collective-permute-start | bytes 1966088 | tf_op jit(solution)/shard_map/ppermute | solution.py:38
  291.8 17.5 %collective-permute-start.36 = (bf16[1,320,1024]{2,1,0:T(8,128)(2,1)}, bf16[1,320,1024]{2,1,0:T(8,128)(2,1)}, u32[]{:S(2)}, u32[]{:S(2)}) collective-permute-start(bf16[1,320,1024]{2,1,0:T(8,128)(2,1)} %picked_sum.24.refs_4_), channel_id=1, source_target_pairs={{0,8},{4,12},{8,0},{12,4},{1,9},{5,13},{9,1},{13,5},{2,10},{6,14},... | collective-permute-start | bytes 1966088 | tf_op jit(solution)/shard_map/ppermute | solution.py:38
  303.9 76.6 %reduce-scatter.7.cloned.1.call-start = ((), (), s32[]{:S(2)}) async-start(), calls=%async_computation.5 | async-start | bytes 2334720 | tf_op jit(solution)/shard_map/reduce_scatter | solution.py:1397
  303.9 37.7 %collective-permute-start.43 = (bf16[320,1024]{1,0:T(8,128)(2,1)}, bf16[320,1024]{1,0:T(8,128)(2,1)}, u32[]{:S(2)}, u32[]{:S(2)}) collective-permute-start(bf16[320,1024]{1,0:T(8,128)(2,1)} %bitcast.51.refs_6_), channel_id=1, source_target_pairs={{0,16},{16,0},{1,17},{17,1},{2,18},{18,2},{3,19},{19,3},{4,20},{20... | collective-permute-start | bytes 1966088 | tf_op jit(solution)/shard_map/ppermute | solution.py:38
  313.2 22.4 %collective-permute-start.38 = (bf16[320,1024]{1,0:T(8,128)(2,1)}, bf16[320,1024]{1,0:T(8,128)(2,1)}, u32[]{:S(2)}, u32[]{:S(2)}) collective-permute-start(bf16[320,1024]{1,0:T(8,128)(2,1)} %bitcast.48.refs_1_), channel_id=1, source_target_pairs={{0,16},{16,0},{1,17},{17,1},{2,18},{18,2},{3,19},{19,3},{4,20},{20... | collective-permute-start | bytes 1966088 | tf_op jit(solution)/shard_map/ppermute | solution.py:38
  313.9 21.5 %collective-permute-start.41 = (bf16[320,1024]{1,0:T(8,128)(2,1)}, bf16[320,1024]{1,0:T(8,128)(2,1)}, u32[]{:S(2)}, u32[]{:S(2)}) collective-permute-start(bf16[320,1024]{1,0:T(8,128)(2,1)} %norm_back.2.refs_3_.refs_1_.refs_2_.refs_4_), channel_id=1, source_target_pairs={{0,8},{4,12},{8,0},{12,4},{1,9},{5,13},{9,1},{13,5},{2,10},{6,14},... | collective-permute-start | bytes 1966088 | tf_op jit(solution)/shard_map/ppermute | solution.py:38
  329.0 13.2 %collective-permute-start.40 = (bf16[320,1024]{1,0:T(8,128)(2,1)}, bf16[320,1024]{1,0:T(8,128)(2,1)}, u32[]{:S(2)}, u32[]{:S(2)}) collective-permute-start(bf16[320,1024]{1,0:T(8,128)(2,1)} %norm_back.2.refs_3_.refs_1_.refs_2_.refs_4_), channel_id=1, source_target_pairs={{0,4},{4,0},{8,12},{12,8},{1,5},{5,1},{9,13},{13,9},{2,6},{6,2},{1... | collective-permute-start | bytes 1966088 | tf_op jit(solution)/shard_map/ppermute | solution.py:38
  333.3 47.9 %collective-permute-start.49 = (bf16[320,1024]{1,0:T(8,128)(2,1)}, bf16[320,1024]{1,0:T(8,128)(2,1)}, u32[]{:S(2)}, u32[]{:S(2)}) collective-permute-start(bf16[320,1024]{1,0:T(8,128)(2,1)} %bitcast.55.refs_6_), channel_id=1, source_target_pairs={{0,16},{16,0},{1,17},{17,1},{2,18},{18,2},{3,19},{19,3},{4,20},{20... | collective-permute-start | bytes 1966088 | tf_op jit(solution)/shard_map/ppermute | solution.py:38
  334.9 93.0 %reduce-scatter.9.cloned.1.call-start = ((), (), s32[]{:S(2)}) async-start(), calls=%async_computation.6 | async-start | bytes 1638400 | tf_op jit(solution)/shard_map/reduce_scatter | solution.py:1397
  335.4 6.8 %collective-permute-start.42 = (bf16[320,1024]{1,0:T(8,128)(2,1)}, bf16[320,1024]{1,0:T(8,128)(2,1)}, u32[]{:S(2)}, u32[]{:S(2)}) collective-permute-start(bf16[320,1024]{1,0:T(8,128)(2,1)} %collective-permute-done.41.refs_3_.refs_4_), channel_id=1, source_target_pairs={{0,4},{4,0},{8,12},{12,8},{1,5},{5,1},{9,13},{13,9},{2,6},{6,2},{1... | collective-permute-start | bytes 1966088 | tf_op jit(solution)/shard_map/ppermute | solution.py:38
  338.9 24.0 %collective-permute-start.45 = (bf16[320,1024]{1,0:T(8,128)(2,1)}, bf16[320,1024]{1,0:T(8,128)(2,1)}, u32[]{:S(2)}, u32[]{:S(2)}) collective-permute-start(bf16[320,1024]{1,0:T(8,128)(2,1)} %norm_back.3.refs_0_.refs_6_.refs_1_.refs_4_), channel_id=1, source_target_pairs={{0,8},{4,12},{8,0},{12,4},{1,9},{5,13},{9,1},{13,5},{2,10},{6,14},... | collective-permute-start | bytes 1966088 | tf_op jit(solution)/shard_map/ppermute | solution.py:38
  364.7 16.5 %collective-permute-start.48 = (bf16[640,256]{1,0:T(8,128)(2,1)}, bf16[640,256]{1,0:T(8,128)(2,1)}, u32[]{:S(2)}, u32[]{:S(2)}) collective-permute-start(bf16[640,256]{1,0:T(8,128)(2,1)} %bitcast.50.refs_1_.refs_2_), channel_id=1, source_target_pairs={{0,16},{16,0},{1,17},{17,1},{2,18},{18,2},{3,19},{19,3},{4,20},{20... | collective-permute-start | bytes 983048 | tf_op jit(solution)/shard_map/ppermute | solution.py:38
  365.3 9.9 %collective-permute-start.47 = (bf16[2,320,1024]{2,1,0:T(8,128)(2,1)}, bf16[2,320,1024]{2,1,0:T(8,128)(2,1)S(1)}, u32[]{:S(2)}, u32[]{:S(2)}) collective-permute-start(bf16[2,320,1024]{2,1,0:T(8,128)(2,1)} %get-tuple-element.190), channel_id=1, source_target_pairs={{0,4},{4,0},{8,12},{12,8},{1,5},{5,1},{9,13},{13,9},{2,6},{6,2},{1... | collective-permute-start | bytes 3932168 | tf_op jit(solution)/shard_map/ppermute | solution.py:38
  375.1 83.9 %reduce-scatter.11.cloned.1.call-start = ((), (), s32[]{:S(2)}) async-start(), calls=%async_computation.7 | async-start | bytes 2334720 | tf_op jit(solution)/shard_map/reduce_scatter | solution.py:1397
  379.2 45.5 %collective-permute-start.53 = (bf16[1,320,1024]{2,1,0:T(8,128)(2,1)}, bf16[1,320,1024]{2,1,0:T(8,128)(2,1)}, u32[]{:S(2)}, u32[]{:S(2)}) collective-permute-start(bf16[1,320,1024]{2,1,0:T(8,128)(2,1)} %picked_sum.28.refs_0_), channel_id=1, source_target_pairs={{0,8},{4,12},{8,0},{12,4},{1,9},{5,13},{9,1},{13,5},{2,10},{6,14},... | collective-permute-start | bytes 1966088 | tf_op jit(solution)/shard_map/ppermute | solution.py:38
  380.5 24.5 %collective-permute-start.51 = (bf16[912,256]{1,0:T(8,128)(2,1)}, bf16[912,256]{1,0:T(8,128)(2,1)}, u32[]{:S(2)}, u32[]{:S(2)}) collective-permute-start(bf16[912,256]{1,0:T(8,128)(2,1)} %bitcast.157), channel_id=1, source_target_pairs={{0,16},{16,0},{1,17},{17,1},{2,18},{18,2},{3,19},{19,3},{4,20},{20... | collective-permute-start | bytes 1400840 | tf_op jit(solution)/shard_map/ppermute | solution.py:38
  403.6 16.5 %collective-permute-start.50 = (bf16[2,320,1024]{2,1,0:T(8,128)(2,1)}, bf16[2,320,1024]{2,1,0:T(8,128)(2,1)}, u32[]{:S(2)}, u32[]{:S(2)}) collective-permute-start(bf16[2,320,1024]{2,1,0:T(8,128)(2,1)} %get-tuple-element.192), channel_id=1, source_target_pairs={{0,4},{4,0},{8,12},{12,8},{1,5},{5,1},{9,13},{13,9},{2,6},{6,2},{1... | collective-permute-start | bytes 3932168 | tf_op jit(solution)/shard_map/ppermute | solution.py:38
  423.8 17.5 %collective-permute-start.52 = (bf16[1,320,1024]{2,1,0:T(8,128)(2,1)}, bf16[1,320,1024]{2,1,0:T(8,128)(2,1)}, u32[]{:S(2)}, u32[]{:S(2)}) collective-permute-start(bf16[1,320,1024]{2,1,0:T(8,128)(2,1)} %picked_sum.29.refs_4_), channel_id=1, source_target_pairs={{0,8},{4,12},{8,0},{12,4},{1,9},{5,13},{9,1},{13,5},{2,10},{6,14},... | collective-permute-start | bytes 1966088 | tf_op jit(solution)/shard_map/ppermute | solution.py:38
  426.5 18.9 %collective-permute-start.55 = (bf16[320,1024]{1,0:T(8,128)(2,1)S(1)}, bf16[320,1024]{1,0:T(8,128)(2,1)S(1)}, u32[]{:S(2)}, u32[]{:S(2)}) collective-permute-start(bf16[320,1024]{1,0:T(8,128)(2,1)S(1)} %bitcast.179), channel_id=1, source_target_pairs={{0,16},{16,0},{1,17},{17,1},{2,18},{18,2},{3,19},{19,3},{4,20},{20... | collective-permute-start | bytes 1966088 | tf_op jit(solution)/shard_map/ppermute | solution.py:38
  427.9 23.3 %collective-permute-start.56 = (bf16[640,256]{1,0:T(8,128)(2,1)}, bf16[640,256]{1,0:T(8,128)(2,1)}, u32[]{:S(2)}, u32[]{:S(2)}) collective-permute-start(bf16[640,256]{1,0:T(8,128)(2,1)} %bitcast.183), channel_id=1, source_target_pairs={{0,16},{16,0},{1,17},{17,1},{2,18},{18,2},{3,19},{19,3},{4,20},{20... | collective-permute-start | bytes 983048 | tf_op jit(solution)/shard_map/ppermute | solution.py:38
  443.9 22.4 %collective-permute-start.54 = (bf16[320,1024]{1,0:T(8,128)(2,1)}, bf16[320,1024]{1,0:T(8,128)(2,1)}, u32[]{:S(2)}, u32[]{:S(2)}) collective-permute-start(bf16[320,1024]{1,0:T(8,128)(2,1)} %bitcast.59.refs_2_), channel_id=1, source_target_pairs={{0,16},{16,0},{1,17},{17,1},{2,18},{18,2},{3,19},{19,3},{4,20},{20... | collective-permute-start | bytes 1966088 | tf_op jit(solution)/shard_map/ppermute | solution.py:38
  461.9 15.9 %collective-permute-start.61 = (bf16[912,256]{1,0:T(8,128)(2,1)}, bf16[912,256]{1,0:T(8,128)(2,1)S(1)}, u32[]{:S(2)}, u32[]{:S(2)}) collective-permute-start(bf16[912,256]{1,0:T(8,128)(2,1)} %bitcast.160), channel_id=1, source_target_pairs={{0,16},{16,0},{1,17},{17,1},{2,18},{18,2},{3,19},{19,3},{4,20},{20... | collective-permute-start | bytes 1400840 | tf_op jit(solution)/shard_map/ppermute | solution.py:38
  464.8 10.3 %collective-permute-start.60 = (f32[832]{0:T(1024)S(1)}, f32[832]{0:T(1024)S(1)}, u32[]{:S(2)}, u32[]{:S(2)}) collective-permute-start(f32[832]{0:T(1024)S(1)} %get-tuple-element.247), channel_id=1, source_target_pairs={{0,16},{16,0},{1,17},{17,1},{2,18},{18,2},{3,19},{19,3},{4,20},{20... | collective-permute-start | bytes 9992 | tf_op jit(solution)/shard_map/ppermute | solution.py:38
  (161 other events, 1284.2 us)
Sparse Core Ops, SparseCore 0:
  40.0 64.3 all-gather.4
  106.6 62.6 all-gather.6
  304.0 29.0 reduce-scatter.4
  335.2 38.6 reduce-scatter.6
  376.1 30.3 reduce-scatter.8
  420.2 38.8 reduce-scatter.10

commit v5 on v4

--- a/solution.py
+++ b/solution.py
@@ -1476,7 +1476,7 @@
     )
     last = 3 * w + ff
     from_inner_0 = swap(inner_0, "pipe", 0)
-    vectors = vectors_from(inner_0[last:], inner_1[last:])
+    vectors = vectors_from(inner_0[last:], after(inner_1, order.last[0])[last:])
     order.hold(from_inner_0)
     grad_up, grad_qkv = unpack(
         functools.partial(unpack_inner_kernel, width, w, ff),

time: 493 us -> 503 us (1.020)
  waiting for transfers between devices: 110 us -> 123 us
    ppermute x59, waiting for transfers between devices: 101 us -> 118 us  [swap(): return lax.ppermute(value, axis, [(i, i ^ 1 << bit) for i in range(count)])]
    reduce_scatter x4, waiting for transfers between devices: 5.51 us -> 0.01 us  [reduced(): return lax.psum_scatter(value, 'dp', scatter_dimension=0)]
    unnamed x293 -> x291, local copies, waits for them, and re-layouts: 38.2 us -> 38.2 us
  transfers between devices with their start and end apart: 68 -> 68, of which waited for: 28 -> 29; matrix products, arithmetic and copies ran while one was open for 5% -> 4% of each run, Pallas kernels for 51% -> 49%
where the time goes in v5:
time: 503 us; the launch traced here: 497 us
  Pallas kernels  253 us (50%)
  waiting for transfers between devices  123 us (24%)
  starting transfers between devices  45.4 us (9%)
  local copies, waits for them, and re-layouts  43.8 us (9%)
  between operations  16.3 us (3%)
  other arithmetic  16.1 us (3%)
    pallas_call x67, Pallas kernels, call(): pl.pallas_call(outer, in_specs=in_specs + [ANY] * len(deps), out_specs=ou...  253 us
    ppermute x59, waiting for transfers between devices, swap(): return lax.ppermute(value, axis, [(i, i ^ 1 << bit) for i in range(count)])  118 us
    ppermute x59, starting transfers between devices, swap(): return lax.ppermute(value, axis, [(i, i ^ 1 << bit) for i in range(count)])  42.6 us
    unnamed x291, local copies, waits for them, and re-layouts  38.2 us
  transfers between devices with their start and end apart: 68, of which 29 were waited for; matrix products, arithmetic and copies ran while one was open for 4% of the time, Pallas kernels for 49%

profile of v5, /device:TPU:0, one launch (start us, length us, event | category | flops | bytes accessed | tf_op | source)
XLA Modules:
  0.0 497.0 jit_solution(7775509792974400385)
XLA Ops:
  7.9 3.0 collective-permute-start.1
  10.9 3.0 pack.1
  20.8 2.2 fusion.refs_22_
  25.6 7.8 %collective-permute-done.3.refs_4_ = bf16[16,256]{1,0:T(8,128)(2,1)} collective-permute-done((bf16[16,256]{1,0:T(8,128)(2,1)}, bf16[16,256]{1,0:T(8,128)(2,1)}, u32[]{:S(2)}, u32[]{:S(2)}) %collective-permute-start.3) | collective-permute-done | bytes 8224 | tf_op jit(solution)/shard_map/ppermute | solution.py:38
  33.4 2.4 by_stage.5
  40.0 15.3 %collective-permute-done.5.refs_1_ = bf16[320,1024]{1,0:T(8,128)(2,1)} collective-permute-done((bf16[320,1024]{1,0:T(8,128)(2,1)}, bf16[320,1024]{1,0:T(8,128)(2,1)}, u32[]{:S(2)}, u32[]{:S(2)}) %collective-permute-start.5) | collective-permute-done | bytes 655392 | tf_op jit(solution)/shard_map/ppermute | solution.py:38
  57.5 9.2 %collective-permute-done.12.refs_1_ = bf16[320,1024]{1,0:T(8,128)(2,1)} collective-permute-done((bf16[320,1024]{1,0:T(8,128)(2,1)}, bf16[320,1024]{1,0:T(8,128)(2,1)}, u32[]{:S(2)}, u32[]{:S(2)}) %collective-permute-start.12) | collective-permute-done | bytes 655392 | tf_op jit(solution)/shard_map/ppermute | solution.py:38
  67.9 13.9 %collective-permute-done.6.refs_2_ = bf16[320,1024]{1,0:T(8,128)(2,1)S(1)} collective-permute-done((bf16[320,1024]{1,0:T(8,128)(2,1)}, bf16[320,1024]{1,0:T(8,128)(2,1)S(1)}, u32[]{:S(2)}, u32[]{:S(2)}) %collective-permute-start.6) | collective-permute-done | bytes 655392 | tf_op jit(solution)/shard_map/ppermute | solution.py:38
  105.8 1.9 copy-done.23
  109.9 6.1 %project.3 = (bf16[1280,128]{1,0:T(8,128)(2,1)S(1)}, bf16[1280,128]{1,0:T(8,128)(2,1)S(1)}, bf16[1280,128]{1,0:T(8,128)(2,1)S(1)}, bf16[1280,512]{1,0:T(8,128)(2,1)S(1)}, bf16[1280,512]{1,0:T(8,128)(2,1)S(1)}) custom-call(s32[1]{0:T(128)} %bitcast.26.refs_0_, bf16[320,1024]{1,0:T(8,128)(2,1)S(1)} %get-tuple-element.118.refs_3_.refs_1_.refs_0_.refs_5_.refs_2_, ...), custom_call_target="tpu_custom_call" | custom-call | flops 99999997952 | bytes 1024 | tf_op jit(solution)/shard_map/project/pallas_call | solution.py:190
  117.1 9.9 %attend.3 = (bf16[2,320,1024]{2,1,0:T(8,128)(2,1)S(1)}, bf16[2,320,1024]{2,1,0:T(8,128)(2,1)S(1)}, bf16[1280,128]{1,0:T(8,128)(2,1)S(1)}, f32[8,1280]{1,0:T(8,128)S(1)}) custom-call(s32[1]{0:T(128)} %bitcast.26.refs_0_, s32[1,1280]{1,0:T(1,128)S(1)} %copy-done.19, bf16[1280,128]{1,0:T(8,128)(2,1)S(1)} %get-tuple-element.132.refs_2_.refs_7_.refs_10_, ...), custom_call_target="tpu_custom_call" | custom-call | flops 99999997952 | bytes 1024 | tf_op jit(solution)/shard_map/attend/pallas_call | solution.py:190
  127.7 2.4 collective-permute-done.18
  133.2 6.1 %project.4 = (bf16[1280,128]{1,0:T(8,128)(2,1)S(1)}, bf16[1280,128]{1,0:T(8,128)(2,1)S(1)}, bf16[1280,128]{1,0:T(8,128)(2,1)S(1)}, bf16[1280,512]{1,0:T(8,128)(2,1)S(1)}, bf16[1280,512]{1,0:T(8,128)(2,1)S(1)}) custom-call(s32[1]{0:T(128)} %bitcast.26.refs_0_, bf16[320,1024]{1,0:T(8,128)(2,1)S(1)} %copy-done.48, bf16[320,1024]{1,0:T(8,128)(2,1)S(1)} %copy-done.62, ...), custom_call_target="tpu_custom_call" | custom-call | flops 99999997952 | bytes 1024 | tf_op jit(solution)/shard_map/project/pallas_call | solution.py:190
  140.4 10.1 %attend.4 = (bf16[2,320,1024]{2,1,0:T(8,128)(2,1)S(1)}, bf16[2,320,1024]{2,1,0:T(8,128)(2,1)S(1)}, bf16[1280,128]{1,0:T(8,128)(2,1)S(1)}, f32[8,1280]{1,0:T(8,128)S(1)}) custom-call(s32[1]{0:T(128)} %bitcast.26.refs_0_, s32[1,1280]{1,0:T(1,128)S(1)} %copy-done.16, bf16[1280,128]{1,0:T(8,128)(2,1)S(1)} %get-tuple-element.139.refs_2_.refs_7_.refs_10_, ...), custom_call_target="tpu_custom_call" | custom-call | flops 99999997952 | bytes 1024 | tf_op jit(solution)/shard_map/attend/pallas_call | solution.py:190
  155.5 14.1 %collective-permute-done.22.refs_2_ = bf16[320,1024]{1,0:T(8,128)(2,1)S(1)} collective-permute-done((bf16[320,1024]{1,0:T(8,128)(2,1)S(1)}, bf16[320,1024]{1,0:T(8,128)(2,1)S(1)}, u32[]{:S(2)}, u32[]{:S(2)}) %collective-permute-start.22) | collective-permute-done | bytes 655392 | tf_op jit(solution)/shard_map/ppermute | solution.py:38
  176.3 1.9 copy-done.26
  179.2 3.3 cotangent.2.refs_6_.refs_1_
  182.7 3.5 cotangent.3.refs_4_.refs_1_
  191.1 1.9 copy-done.28
  193.0 1.9 copy-done.97
  194.9 2.2 add_rows.3.refs_12_.refs_1_.refs_2_.refs_6_.refs_0_.refs_5_
  199.3 30.6 %whole_layer.1 = (bf16[2,320,1024]{2,1,0:T(8,128)(2,1)}, bf16[2,320,1024]{2,1,0:T(8,128)(2,1)}, bf16[2,320,1024]{2,1,0:T(8,128)(2,1)}, bf16[2,320,1024]{2,1,0:T(...) custom-call(s32[1]{0:T(128)} %bitcast.26.refs_0_, ...), custom_call_target="tpu_custom_call" | custom-call | flops 99999997952 | bytes 1024 | tf_op jit(solution)/shard_map/whole_layer/pallas_call | solution.py:190
  237.7 6.5 %project.5 = (bf16[1280,128]{1,0:T(8,128)(2,1)S(1)}, bf16[1280,128]{1,0:T(8,128)(2,1)S(1)}, bf16[1280,128]{1,0:T(8,128)(2,1)S(1)}, bf16[1280,512]{1,0:T(8,128)(2,1)S(1)}, bf16[1280,512]{1,0:T(8,128)(2,1)S(1)}) custom-call(s32[1]{0:T(128)} %bitcast.26.refs_0_, bf16[320,1024]{1,0:T(8,128)(2,1)} %add_rows.3.refs_12_.refs_1_.refs_2_.refs_6_.refs_0_.refs_5_, ...), custom_call_target="tpu_custom_call" | custom-call | flops 99999997952 | bytes 1024 | tf_op jit(solution)/shard_map/project/pallas_call | solution.py:190
  245.3 9.7 %attend.5 = (bf16[2,320,1024]{2,1,0:T(8,128)(2,1)S(1)}, bf16[2,320,1024]{2,1,0:T(8,128)(2,1)S(1)}, bf16[1280,128]{1,0:T(8,128)(2,1)S(1)}, f32[8,1280]{1,0:T(8,128)S(1)}) custom-call(s32[1]{0:T(128)} %bitcast.26.refs_0_, s32[1,1280]{1,0:T(1,128)S(1)} %copy-done.17, bf16[1280,128]{1,0:T(8,128)(2,1)S(1)} %get-tuple-element.157.refs_2_.refs_7_, ...), custom_call_target="tpu_custom_call" | custom-call | flops 99999997952 | bytes 1024 | tf_op jit(solution)/shard_map/attend/pallas_call | solution.py:190
  255.4 3.2 picked_sum.21.refs_3_
  265.6 18.6 %whole_backward.3 = (bf16[2,320,1024]{2,1,0:T(8,128)(2,1)}, bf16[2,320,1024]{2,1,0:T(8,128)(2,1)}, bf16[1280,512]{1,0:T(8,128)(2,1)}, f32[1,512]{1,0:T(1,128)}, ...) custom-call(s32[1]{0:T(128)} %bitcast.26.refs_0_, f32[1280,640]{1,0:T(8,128)} %copy-done.96, ...), custom_call_target="tpu_custom_call" | custom-call | flops 99999997952 | bytes 1024 | tf_op jit(solution)/shard_map/whole_backward/pallas_call | solution.py:190
  285.0 3.5 norm_back.2.refs_3_.refs_1_.refs_2_.refs_4_
  293.1 2.6 picked_sum.25.refs_14_
  295.7 8.2 %weight_grads.4.refs_4_ = bf16[4,640,256]{2,1,0:T(8,128)(2,1)} custom-call(s32[1]{0:T(128)} %bitcast.26.refs_0_, f32[6,1024]{1,0:T(8,128)} %reshape.400.refs_9_.refs_6_.refs_15_.refs_1_.refs_8_, bf16[320,1024]{1,0:T(8,128)(2,1)} %copy-done.9, bf16[320,1024]{1,0:T(8,128)(2,1)} %copy-done.67, bf16[320,1024]{1,0:T(8,128)(2,1)} %copy-done.63, ...), custom_call_target="tpu_custom_call" | custom-call | flops 99999997952 | bytes 1024 | tf_op jit(solution)/shard_map/weight_grads/pallas_call | solution.py:190
  304.5 4.7 collective-permute-done.36.refs_3_
  310.6 2.6 picked_sum.26.refs_25_
  315.0 14.0 %weight_grads.5.refs_4_ = bf16[4,912,256]{2,1,0:T(8,128)(2,1)} custom-call(s32[1]{0:T(128)} %bitcast.26.refs_0_, f32[6,1024]{1,0:T(8,128)} %reshape.400.refs_9_.refs_6_.refs_15_.refs_1_.refs_8_, bf16[320,1024]{1,0:T(8,128)(2,1)} %add_rows.2.refs_4_.refs_2_.refs_0_.refs_5_, bf16[320,1024]{1,0:T(8,128)(2,1)} %copy-done.135, ...), custom_call_target="tpu_custom_call" | custom-call | flops 99999997952 | bytes 1024 | tf_op jit(solution)/shard_map/weight_grads/pallas_call | solution.py:190
  330.7 2.6 picked_sum.27.refs_4_
  335.6 3.3 norm_back.3.refs_0_.refs_6_.refs_1_.refs_4_
  342.2 20.7 %whole_backward.4 = (bf16[2,320,1024]{2,1,0:T(8,128)(2,1)}, bf16[2,320,1024]{2,1,0:T(8,128)(2,1)}, bf16[1280,512]{1,0:T(8,128)(2,1)}, f32[1,512]{1,0:T(1,128)}, ...) custom-call(s32[1]{0:T(128)} %bitcast.26.refs_0_, ...), custom_call_target="tpu_custom_call" | custom-call | flops 99999997952 | bytes 1024 | tf_op jit(solution)/shard_map/whole_backward/pallas_call | solution.py:190
  367.0 8.0 %weight_grads.6.refs_3_ = bf16[4,640,256]{2,1,0:T(8,128)(2,1)} custom-call(s32[1]{0:T(128)} %bitcast.26.refs_0_, f32[6,1024]{1,0:T(8,128)} %copy-done.12, bf16[320,1024]{1,0:T(8,128)(2,1)} %norm_back.2.refs_3_.refs_1_.refs_2_.refs_4_, bf16[320,1024]{1,0:T(8,128)(2,1)} %collective-permute-done.40.refs_2_.refs_3_, ...), custom_call_target="tpu_custom_call" | custom-call | flops 99999997952 | bytes 1024 | tf_op jit(solution)/shard_map/weight_grads/pallas_call | solution.py:190
  382.8 20.7 %whole_backward.5 = (bf16[2,320,1024]{2,1,0:T(8,128)(2,1)}, bf16[2,320,1024]{2,1,0:T(8,128)(2,1)}, bf16[1280,512]{1,0:T(8,128)(2,1)}, f32[1,512]{1,0:T(1,128)}, ...) custom-call(s32[1]{0:T(128)} %bitcast.26.refs_0_, ...), custom_call_target="tpu_custom_call" | custom-call | flops 99999997952 | bytes 1024 | tf_op jit(solution)/shard_map/whole_backward/pallas_call | solution.py:190
  403.5 13.7 %weight_grads.7.refs_0_ = bf16[4,912,256]{2,1,0:T(8,128)(2,1)} custom-call(s32[1]{0:T(128)} %bitcast.26.refs_0_, f32[6,1024]{1,0:T(8,128)} %copy-done.12, bf16[320,1024]{1,0:T(8,128)(2,1)} %copy-done.45, bf16[320,1024]{1,0:T(8,128)(2,1)} %copy-done.55, bf16[320,1024]{1,0:T(8,128)(2,1)} %copy-done.51, bf16[320,1024]{1,0:T(8,128)(2,1)} %copy-done.53, ...), custom_call_target="tpu_custom_call" | custom-call | flops 99999997952 | bytes 1024 | tf_op jit(solution)/shard_map/weight_grads/pallas_call | solution.py:190
  420.1 2.4 picked_sum.29.refs_4_
  427.3 12.7 %collective-permute-done.52.refs_3_ = bf16[1,320,1024]{2,1,0:T(8,128)(2,1)} collective-permute-done((bf16[1,320,1024]{2,1,0:T(8,128)(2,1)}, bf16[1,320,1024]{2,1,0:T(8,128)(2,1)}, u32[]{:S(2)}, u32[]{:S(2)}) %collective-permute-start.52) | collective-permute-done | bytes 655392 | tf_op jit(solution)/shard_map/ppermute | solution.py:38
  439.9 2.6 picked_sum.31.refs_9_
  443.9 3.7 ends.2
  447.6 2.3 collective-permute-done.56.refs_3_.refs_6_
  449.9 2.3 unpack.2
  452.2 11.0 %collective-permute-done.54.refs_3_ = bf16[320,1024]{1,0:T(8,128)(2,1)} collective-permute-done((bf16[320,1024]{1,0:T(8,128)(2,1)}, bf16[320,1024]{1,0:T(8,128)(2,1)}, u32[]{:S(2)}, u32[]{:S(2)}) %collective-permute-start.54) | collective-permute-done | bytes 655392 | tf_op jit(solution)/shard_map/ppermute | solution.py:38
  465.2 4.1 ends.3
  480.6 6.9 %collective-permute-done.61.refs_3_.refs_6_ = bf16[912,256]{1,0:T(8,128)(2,1)S(1)} collective-permute-done((bf16[912,256]{1,0:T(8,128)(2,1)S(1)}, bf16[912,256]{1,0:T(8,128)(2,1)S(1)}, u32[]{:S(2)}, u32[]{:S(2)}) %collective-permute-start.61) | collective-permute-done | bytes 466976 | tf_op jit(solution)/shard_map/ppermute | solution.py:38
  487.4 2.5 unpack.3
  (543 shorter events, 135.1 us)
Async XLA Ops:
  7.2 97.3 %all-gather.5.cloned.1.call-start = ((), (), s32[]{:S(2)}) async-start(), calls=%async_computation.8 | async-start | bytes 3973120 | tf_op jit(solution)/shard_map/all_gather | solution.py:1273
  7.9 15.2 %collective-permute-start.1 = (bf16[1,6,64]{2,1,0:T(8,128)(2,1)S(1)}, bf16[1,6,64]{2,1,0:T(8,128)(2,1)S(1)}, u32[]{:S(2)}, u32[]{:S(2)}) collective-permute-start(bf16[1,6,64]{2,1,0:T(8,128)(2,1)S(1)} %maximum_bitcast_fusion.1), channel_id=1, source_target_pairs={{0,8},{4,12},{8,0},{12,4},{1,9},{5,13},{9,1},{13,5},{2,10},{6,14},... | collective-permute-start | bytes 2312 | tf_op jit(solution)/shard_map/ppermute | solution.py:38
  13.9 19.6 %collective-permute-start = (bf16[1536,256]{1,0:T(8,128)(2,1)}, bf16[1536,256]{1,0:T(8,128)(2,1)}, u32[]{:S(2)}, u32[]{:S(2)}) collective-permute-start(bf16[1536,256]{1,0:T(8,128)(2,1)} %get-tuple-element.112), channel_id=1, source_target_pairs={{0,16},{16,0},{1,17},{17,1},{2,18},{18,2},{3,19},{19,3},{4,20},{20... | collective-permute-start | bytes 2359304 | tf_op jit(solution)/shard_map/ppermute | solution.py:38
  25.1 8.3 %collective-permute-start.3 = (bf16[16,256]{1,0:T(8,128)(2,1)}, bf16[16,256]{1,0:T(8,128)(2,1)}, u32[]{:S(2)}, u32[]{:S(2)}) collective-permute-start(bf16[16,256]{1,0:T(8,128)(2,1)} %pad_maximum_fusion.1.refs_1_.refs_3_), channel_id=1, source_target_pairs={{0,16},{16,0},{1,17},{17,1},{2,18},{18,2},{3,19},{19,3},{4,20},{20... | collective-permute-start | bytes 24584 | tf_op jit(solution)/shard_map/ppermute | solution.py:38
  35.8 20.0 %collective-permute-start.7 = (bf16[320,1024]{1,0:T(8,128)(2,1)}, bf16[320,1024]{1,0:T(8,128)(2,1)}, u32[]{:S(2)}, u32[]{:S(2)}) collective-permute-start(bf16[320,1024]{1,0:T(8,128)(2,1)} %get-tuple-element.115.refs_1_), channel_id=1, source_target_pairs={{0,16},{16,0},{1,17},{17,1},{2,18},{18,2},{3,19},{19,3},{4,20},{20... | collective-permute-start | bytes 1966088 | tf_op jit(solution)/shard_map/ppermute | solution.py:38
  37.4 18.0 %collective-permute-start.5 = (bf16[320,1024]{1,0:T(8,128)(2,1)}, bf16[320,1024]{1,0:T(8,128)(2,1)}, u32[]{:S(2)}, u32[]{:S(2)}) collective-permute-start(bf16[320,1024]{1,0:T(8,128)(2,1)} %get-tuple-element.115.refs_1_), channel_id=1, source_target_pairs={{0,8},{4,12},{8,0},{12,4},{1,9},{5,13},{9,1},{13,5},{2,10},{6,14},... | collective-permute-start | bytes 1966088 | tf_op jit(solution)/shard_map/ppermute | solution.py:38
  37.9 53.0 %collective-permute-start.4 = (bf16[320,1024]{1,0:T(8,128)(2,1)}, bf16[320,1024]{1,0:T(8,128)(2,1)}, u32[]{:S(2)}, u32[]{:S(2)}) collective-permute-start(bf16[320,1024]{1,0:T(8,128)(2,1)} %get-tuple-element.114.refs_1_), channel_id=1, source_target_pairs={{0,16},{16,0},{1,17},{17,1},{2,18},{18,2},{3,19},{19,3},{4,20},{20... | collective-permute-start | bytes 1966088 | tf_op jit(solution)/shard_map/ppermute | solution.py:38
  38.2 28.5 %collective-permute-start.12 = (bf16[320,1024]{1,0:T(8,128)(2,1)}, bf16[320,1024]{1,0:T(8,128)(2,1)}, u32[]{:S(2)}, u32[]{:S(2)}) collective-permute-start(bf16[320,1024]{1,0:T(8,128)(2,1)} %get-tuple-element.114.refs_1_), channel_id=1, source_target_pairs={{0,8},{4,12},{8,0},{12,4},{1,9},{5,13},{9,1},{13,5},{2,10},{6,14},... | collective-permute-start | bytes 1966088 | tf_op jit(solution)/shard_map/ppermute | solution.py:38
  39.9 133.4 %all-gather.7.cloned.1.call-start = ((), (), s32[]{:S(2)}) async-start(), calls=%async_computation.9 | async-start | bytes 3973120 | tf_op jit(solution)/shard_map/all_gather | solution.py:1308
  55.3 26.5 %collective-permute-start.6 = (bf16[320,1024]{1,0:T(8,128)(2,1)}, bf16[320,1024]{1,0:T(8,128)(2,1)S(1)}, u32[]{:S(2)}, u32[]{:S(2)}) collective-permute-start(bf16[320,1024]{1,0:T(8,128)(2,1)} %collective-permute-done.5.refs_1_), channel_id=1, source_target_pairs={{0,16},{16,0},{1,17},{17,1},{2,18},{18,2},{3,19},{19,3},{4,20},{20... | collective-permute-start | bytes 1966088 | tf_op jit(solution)/shard_map/ppermute | solution.py:38
  57.3 284.3 %reduce-scatter.5.cloned.1.call-start = ((), (), s32[]{:S(2)}) async-start(), calls=%async_computation.4 | async-start | bytes 1638400 | tf_op jit(solution)/shard_map/reduce_scatter | solution.py:1397
  66.7 26.8 %collective-permute-start.13 = (bf16[320,1024]{1,0:T(8,128)(2,1)}, bf16[320,1024]{1,0:T(8,128)(2,1)}, u32[]{:S(2)}, u32[]{:S(2)}) collective-permute-start(bf16[320,1024]{1,0:T(8,128)(2,1)} %collective-permute-done.12.refs_1_), channel_id=1, source_target_pairs={{0,16},{16,0},{1,17},{17,1},{2,18},{18,2},{3,19},{19,3},{4,20},{20... | collective-permute-start | bytes 1966088 | tf_op jit(solution)/shard_map/ppermute | solution.py:38
  131.6 19.0 %collective-permute-start.20 = (bf16[1,320,1024]{2,1,0:T(8,128)(2,1)}, bf16[1,320,1024]{2,1,0:T(8,128)(2,1)}, u32[]{:S(2)}, u32[]{:S(2)}) collective-permute-start(bf16[1,320,1024]{2,1,0:T(8,128)(2,1)} %picked_sum.16.refs_9_), channel_id=1, source_target_pairs={{0,8},{4,12},{8,0},{12,4},{1,9},{5,13},{9,1},{13,5},{2,10},{6,14},... | collective-permute-start | bytes 1966088 | tf_op jit(solution)/shard_map/ppermute | solution.py:38
  152.4 17.2 %collective-permute-start.22 = (bf16[320,1024]{1,0:T(8,128)(2,1)S(1)}, bf16[320,1024]{1,0:T(8,128)(2,1)S(1)}, u32[]{:S(2)}, u32[]{:S(2)}) collective-permute-start(bf16[320,1024]{1,0:T(8,128)(2,1)S(1)} %bitcast.184), channel_id=1, source_target_pairs={{0,16},{16,0},{1,17},{17,1},{2,18},{18,2},{3,19},{19,3},{4,20},{20... | collective-permute-start | bytes 1966088 | tf_op jit(solution)/shard_map/ppermute | solution.py:38
  154.5 17.1 %collective-permute-start.21 = (bf16[1,320,1024]{2,1,0:T(8,128)(2,1)S(1)}, bf16[1,320,1024]{2,1,0:T(8,128)(2,1)S(1)}, u32[]{:S(2)}, u32[]{:S(2)}) collective-permute-start(bf16[1,320,1024]{2,1,0:T(8,128)(2,1)S(1)} %picked_sum.18.refs_4_), channel_id=1, source_target_pairs={{0,8},{4,12},{8,0},{12,4},{1,9},{5,13},{9,1},{13,5},{2,10},{6,14},... | collective-permute-start | bytes 1966088 | tf_op jit(solution)/shard_map/ppermute | solution.py:38
  170.8 18.9 %collective-permute-start.25 = (bf16[320,1024]{1,0:T(8,128)(2,1)}, bf16[320,1024]{1,0:T(8,128)(2,1)}, u32[]{:S(2)}, u32[]{:S(2)}) collective-permute-start(bf16[320,1024]{1,0:T(8,128)(2,1)} %add_rows.2.refs_4_.refs_2_.refs_0_.refs_5_), channel_id=1, source_target_pairs={{0,8},{4,12},{8,0},{12,4},{1,9},{5,13},{9,1},{13,5},{2,10},{6,14},... | collective-permute-start | bytes 1966088 | tf_op jit(solution)/shard_map/ppermute | solution.py:38
  174.8 16.3 %collective-permute-start.23 = (bf16[320,1024]{1,0:T(8,128)(2,1)}, bf16[320,1024]{1,0:T(8,128)(2,1)}, u32[]{:S(2)}, u32[]{:S(2)}) collective-permute-start(bf16[320,1024]{1,0:T(8,128)(2,1)} %bitcast.180), channel_id=1, source_target_pairs={{0,16},{16,0},{1,17},{17,1},{2,18},{18,2},{3,19},{19,3},{4,20},{20... | collective-permute-start | bytes 1966088 | tf_op jit(solution)/shard_map/ppermute | solution.py:38
  189.1 9.3 %collective-permute-start.24 = (bf16[320,1024]{1,0:T(8,128)(2,1)}, bf16[320,1024]{1,0:T(8,128)(2,1)S(1)}, u32[]{:S(2)}, u32[]{:S(2)}) collective-permute-start(bf16[320,1024]{1,0:T(8,128)(2,1)} %add_rows.2.refs_4_.refs_2_.refs_0_.refs_5_), channel_id=1, source_target_pairs={{0,4},{4,0},{8,12},{12,8},{1,5},{5,1},{9,13},{13,9},{2,6},{6,2},{1... | collective-permute-start | bytes 1966088 | tf_op jit(solution)/shard_map/ppermute | solution.py:38
  189.7 8.7 %collective-permute-start.26 = (bf16[320,1024]{1,0:T(8,128)(2,1)}, bf16[320,1024]{1,0:T(8,128)(2,1)}, u32[]{:S(2)}, u32[]{:S(2)}) collective-permute-start(bf16[320,1024]{1,0:T(8,128)(2,1)} %collective-permute-done.25.refs_4_), channel_id=1, source_target_pairs={{0,4},{4,0},{8,12},{12,8},{1,5},{5,1},{9,13},{13,9},{2,6},{6,2},{1... | collective-permute-start | bytes 1966088 | tf_op jit(solution)/shard_map/ppermute | solution.py:38
  197.1 34.0 %collective-permute-start.28 = (bf16[320,1024]{1,0:T(8,128)(2,1)}, bf16[320,1024]{1,0:T(8,128)(2,1)}, u32[]{:S(2)}, u32[]{:S(2)}) collective-permute-start(bf16[320,1024]{1,0:T(8,128)(2,1)} %add_rows.3.refs_12_.refs_1_.refs_2_.refs_6_.refs_0_.refs_5_), channel_id=1, source_target_pairs={{0,8},{4,12},{8,0},{12,4},{1,9},{5,13},{9,1},{13,5},{2,10},{6,14},... | collective-permute-start | bytes 1966088 | tf_op jit(solution)/shard_map/ppermute | solution.py:38
  231.1 6.3 %collective-permute-start.27 = (bf16[320,1024]{1,0:T(8,128)(2,1)}, bf16[320,1024]{1,0:T(8,128)(2,1)S(1)}, u32[]{:S(2)}, u32[]{:S(2)}) collective-permute-start(bf16[320,1024]{1,0:T(8,128)(2,1)} %add_rows.3.refs_12_.refs_1_.refs_2_.refs_6_.refs_0_.refs_5_), channel_id=1, source_target_pairs={{0,4},{4,0},{8,12},{12,8},{1,5},{5,1},{9,13},{13,9},{2,6},{6,2},{1... | collective-permute-start | bytes 1966088 | tf_op jit(solution)/shard_map/ppermute | solution.py:38
  231.2 6.2 %collective-permute-start.29 = (bf16[320,1024]{1,0:T(8,128)(2,1)}, bf16[320,1024]{1,0:T(8,128)(2,1)S(1)}, u32[]{:S(2)}, u32[]{:S(2)}) collective-permute-start(bf16[320,1024]{1,0:T(8,128)(2,1)} %collective-permute-done.28.refs_3_.refs_4_.refs_8_), channel_id=1, source_target_pairs={{0,4},{4,0},{8,12},{12,8},{1,5},{5,1},{9,13},{13,9},{2,6},{6,2},{1... | collective-permute-start | bytes 1966088 | tf_op jit(solution)/shard_map/ppermute | solution.py:38
  236.5 18.8 %collective-permute-start.33 = (bf16[1,320,1024]{2,1,0:T(8,128)(2,1)}, bf16[1,320,1024]{2,1,0:T(8,128)(2,1)}, u32[]{:S(2)}, u32[]{:S(2)}) collective-permute-start(bf16[1,320,1024]{2,1,0:T(8,128)(2,1)} %picked_sum.20.refs_9_), channel_id=1, source_target_pairs={{0,8},{4,12},{8,0},{12,4},{1,9},{5,13},{9,1},{13,5},{2,10},{6,14},... | collective-permute-start | bytes 1966088 | tf_op jit(solution)/shard_map/ppermute | solution.py:38
  258.6 25.7 %collective-permute-start.35 = (bf16[320,1024]{1,0:T(8,128)(2,1)}, bf16[320,1024]{1,0:T(8,128)(2,1)}, u32[]{:S(2)}, u32[]{:S(2)}) collective-permute-start(bf16[320,1024]{1,0:T(8,128)(2,1)} %bitcast.47.refs_1_), channel_id=1, source_target_pairs={{0,16},{16,0},{1,17},{17,1},{2,18},{18,2},{3,19},{19,3},{4,20},{20... | collective-permute-start | bytes 1966088 | tf_op jit(solution)/shard_map/ppermute | solution.py:38
  261.6 31.4 %collective-permute-start.37 = (bf16[1,320,1024]{2,1,0:T(8,128)(2,1)}, bf16[1,320,1024]{2,1,0:T(8,128)(2,1)}, u32[]{:S(2)}, u32[]{:S(2)}) collective-permute-start(bf16[1,320,1024]{2,1,0:T(8,128)(2,1)} %picked_sum.22.refs_3_), channel_id=1, source_target_pairs={{0,8},{4,12},{8,0},{12,4},{1,9},{5,13},{9,1},{13,5},{2,10},{6,14},... | collective-permute-start | bytes 1966088 | tf_op jit(solution)/shard_map/ppermute | solution.py:38
  264.7 64.4 %collective-permute-start.39 = (bf16[1,320,1024]{2,1,0:T(8,128)(2,1)}, bf16[1,320,1024]{2,1,0:T(8,128)(2,1)}, u32[]{:S(2)}, u32[]{:S(2)}) collective-permute-start(bf16[1,320,1024]{2,1,0:T(8,128)(2,1)} %picked_sum.23.refs_17_), channel_id=1, source_target_pairs={{0,8},{4,12},{8,0},{12,4},{1,9},{5,13},{9,1},{13,5},{2,10},{6,14},... | collective-permute-start | bytes 1966088 | tf_op jit(solution)/shard_map/ppermute | solution.py:38
  284.2 6.1 %collective-permute-start.34 = (bf16[2,320,1024]{2,1,0:T(8,128)(2,1)}, bf16[2,320,1024]{2,1,0:T(8,128)(2,1)S(1)}, u32[]{:S(2)}, u32[]{:S(2)}) collective-permute-start(bf16[2,320,1024]{2,1,0:T(8,128)(2,1)} %get-tuple-element.168), channel_id=1, source_target_pairs={{0,4},{4,0},{8,12},{12,8},{1,5},{5,1},{9,13},{13,9},{2,6},{6,2},{1... | collective-permute-start | bytes 3932168 | tf_op jit(solution)/shard_map/ppermute | solution.py:38
  291.8 17.5 %collective-permute-start.36 = (bf16[1,320,1024]{2,1,0:T(8,128)(2,1)}, bf16[1,320,1024]{2,1,0:T(8,128)(2,1)}, u32[]{:S(2)}, u32[]{:S(2)}) collective-permute-start(bf16[1,320,1024]{2,1,0:T(8,128)(2,1)} %picked_sum.24.refs_4_), channel_id=1, source_target_pairs={{0,8},{4,12},{8,0},{12,4},{1,9},{5,13},{9,1},{13,5},{2,10},{6,14},... | collective-permute-start | bytes 1966088 | tf_op jit(solution)/shard_map/ppermute | solution.py:38
  303.9 76.5 %reduce-scatter.7.cloned.1.call-start = ((), (), s32[]{:S(2)}) async-start(), calls=%async_computation.5 | async-start | bytes 2334720 | tf_op jit(solution)/shard_map/reduce_scatter | solution.py:1397
  303.9 37.7 %collective-permute-start.43 = (bf16[320,1024]{1,0:T(8,128)(2,1)}, bf16[320,1024]{1,0:T(8,128)(2,1)}, u32[]{:S(2)}, u32[]{:S(2)}) collective-permute-start(bf16[320,1024]{1,0:T(8,128)(2,1)} %bitcast.51.refs_6_), channel_id=1, source_target_pairs={{0,16},{16,0},{1,17},{17,1},{2,18},{18,2},{3,19},{19,3},{4,20},{20... | collective-permute-start | bytes 1966088 | tf_op jit(solution)/shard_map/ppermute | solution.py:38
  313.2 22.4 %collective-permute-start.38 = (bf16[320,1024]{1,0:T(8,128)(2,1)}, bf16[320,1024]{1,0:T(8,128)(2,1)}, u32[]{:S(2)}, u32[]{:S(2)}) collective-permute-start(bf16[320,1024]{1,0:T(8,128)(2,1)} %bitcast.48.refs_1_), channel_id=1, source_target_pairs={{0,16},{16,0},{1,17},{17,1},{2,18},{18,2},{3,19},{19,3},{4,20},{20... | collective-permute-start | bytes 1966088 | tf_op jit(solution)/shard_map/ppermute | solution.py:38
  313.8 21.5 %collective-permute-start.41 = (bf16[320,1024]{1,0:T(8,128)(2,1)}, bf16[320,1024]{1,0:T(8,128)(2,1)}, u32[]{:S(2)}, u32[]{:S(2)}) collective-permute-start(bf16[320,1024]{1,0:T(8,128)(2,1)} %norm_back.2.refs_3_.refs_1_.refs_2_.refs_4_), channel_id=1, source_target_pairs={{0,8},{4,12},{8,0},{12,4},{1,9},{5,13},{9,1},{13,5},{2,10},{6,14},... | collective-permute-start | bytes 1966088 | tf_op jit(solution)/shard_map/ppermute | solution.py:38
  329.0 13.2 %collective-permute-start.40 = (bf16[320,1024]{1,0:T(8,128)(2,1)}, bf16[320,1024]{1,0:T(8,128)(2,1)}, u32[]{:S(2)}, u32[]{:S(2)}) collective-permute-start(bf16[320,1024]{1,0:T(8,128)(2,1)} %norm_back.2.refs_3_.refs_1_.refs_2_.refs_4_), channel_id=1, source_target_pairs={{0,4},{4,0},{8,12},{12,8},{1,5},{5,1},{9,13},{13,9},{2,6},{6,2},{1... | collective-permute-start | bytes 1966088 | tf_op jit(solution)/shard_map/ppermute | solution.py:38
  333.3 47.8 %collective-permute-start.49 = (bf16[320,1024]{1,0:T(8,128)(2,1)}, bf16[320,1024]{1,0:T(8,128)(2,1)}, u32[]{:S(2)}, u32[]{:S(2)}) collective-permute-start(bf16[320,1024]{1,0:T(8,128)(2,1)} %bitcast.55.refs_6_), channel_id=1, source_target_pairs={{0,16},{16,0},{1,17},{17,1},{2,18},{18,2},{3,19},{19,3},{4,20},{20... | collective-permute-start | bytes 1966088 | tf_op jit(solution)/shard_map/ppermute | solution.py:38
  334.9 91.7 %reduce-scatter.9.cloned.1.call-start = ((), (), s32[]{:S(2)}) async-start(), calls=%async_computation.6 | async-start | bytes 1638400 | tf_op jit(solution)/shard_map/reduce_scatter | solution.py:1397
  335.4 6.8 %collective-permute-start.42 = (bf16[320,1024]{1,0:T(8,128)(2,1)}, bf16[320,1024]{1,0:T(8,128)(2,1)}, u32[]{:S(2)}, u32[]{:S(2)}) collective-permute-start(bf16[320,1024]{1,0:T(8,128)(2,1)} %collective-permute-done.41.refs_3_.refs_4_), channel_id=1, source_target_pairs={{0,4},{4,0},{8,12},{12,8},{1,5},{5,1},{9,13},{13,9},{2,6},{6,2},{1... | collective-permute-start | bytes 1966088 | tf_op jit(solution)/shard_map/ppermute | solution.py:38
  338.9 24.0 %collective-permute-start.45 = (bf16[320,1024]{1,0:T(8,128)(2,1)}, bf16[320,1024]{1,0:T(8,128)(2,1)}, u32[]{:S(2)}, u32[]{:S(2)}) collective-permute-start(bf16[320,1024]{1,0:T(8,128)(2,1)} %norm_back.3.refs_0_.refs_6_.refs_1_.refs_4_), channel_id=1, source_target_pairs={{0,8},{4,12},{8,0},{12,4},{1,9},{5,13},{9,1},{13,5},{2,10},{6,14},... | collective-permute-start | bytes 1966088 | tf_op jit(solution)/shard_map/ppermute | solution.py:38
  364.7 16.4 %collective-permute-start.48 = (bf16[640,256]{1,0:T(8,128)(2,1)}, bf16[640,256]{1,0:T(8,128)(2,1)}, u32[]{:S(2)}, u32[]{:S(2)}) collective-permute-start(bf16[640,256]{1,0:T(8,128)(2,1)} %bitcast.50.refs_1_.refs_2_), channel_id=1, source_target_pairs={{0,16},{16,0},{1,17},{17,1},{2,18},{18,2},{3,19},{19,3},{4,20},{20... | collective-permute-start | bytes 983048 | tf_op jit(solution)/shard_map/ppermute | solution.py:38
  365.2 9.9 %collective-permute-start.47 = (bf16[2,320,1024]{2,1,0:T(8,128)(2,1)}, bf16[2,320,1024]{2,1,0:T(8,128)(2,1)S(1)}, u32[]{:S(2)}, u32[]{:S(2)}) collective-permute-start(bf16[2,320,1024]{2,1,0:T(8,128)(2,1)} %get-tuple-element.191), channel_id=1, source_target_pairs={{0,4},{4,0},{8,12},{12,8},{1,5},{5,1},{9,13},{13,9},{2,6},{6,2},{1... | collective-permute-start | bytes 3932168 | tf_op jit(solution)/shard_map/ppermute | solution.py:38
  375.1 88.1 %reduce-scatter.11.cloned.1.call-start = ((), (), s32[]{:S(2)}) async-start(), calls=%async_computation.7 | async-start | bytes 2334720 | tf_op jit(solution)/shard_map/reduce_scatter | solution.py:1397
  379.1 44.2 %collective-permute-start.53 = (bf16[1,320,1024]{2,1,0:T(8,128)(2,1)}, bf16[1,320,1024]{2,1,0:T(8,128)(2,1)}, u32[]{:S(2)}, u32[]{:S(2)}) collective-permute-start(bf16[1,320,1024]{2,1,0:T(8,128)(2,1)} %picked_sum.28.refs_0_), channel_id=1, source_target_pairs={{0,8},{4,12},{8,0},{12,4},{1,9},{5,13},{9,1},{13,5},{2,10},{6,14},... | collective-permute-start | bytes 1966088 | tf_op jit(solution)/shard_map/ppermute | solution.py:38
  380.4 23.2 %collective-permute-start.51 = (bf16[912,256]{1,0:T(8,128)(2,1)}, bf16[912,256]{1,0:T(8,128)(2,1)}, u32[]{:S(2)}, u32[]{:S(2)}) collective-permute-start(bf16[912,256]{1,0:T(8,128)(2,1)} %bitcast.159), channel_id=1, source_target_pairs={{0,16},{16,0},{1,17},{17,1},{2,18},{18,2},{3,19},{19,3},{4,20},{20... | collective-permute-start | bytes 1400840 | tf_op jit(solution)/shard_map/ppermute | solution.py:38
  403.5 15.3 %collective-permute-start.50 = (bf16[2,320,1024]{2,1,0:T(8,128)(2,1)}, bf16[2,320,1024]{2,1,0:T(8,128)(2,1)}, u32[]{:S(2)}, u32[]{:S(2)}) collective-permute-start(bf16[2,320,1024]{2,1,0:T(8,128)(2,1)} %get-tuple-element.193), channel_id=1, source_target_pairs={{0,4},{4,0},{8,12},{12,8},{1,5},{5,1},{9,13},{13,9},{2,6},{6,2},{1... | collective-permute-start | bytes 3932168 | tf_op jit(solution)/shard_map/ppermute | solution.py:38
  422.4 17.5 %collective-permute-start.52 = (bf16[1,320,1024]{2,1,0:T(8,128)(2,1)}, bf16[1,320,1024]{2,1,0:T(8,128)(2,1)}, u32[]{:S(2)}, u32[]{:S(2)}) collective-permute-start(bf16[1,320,1024]{2,1,0:T(8,128)(2,1)} %picked_sum.29.refs_4_), channel_id=1, source_target_pairs={{0,8},{4,12},{8,0},{12,4},{1,9},{5,13},{9,1},{13,5},{2,10},{6,14},... | collective-permute-start | bytes 1966088 | tf_op jit(solution)/shard_map/ppermute | solution.py:38
  425.2 18.8 %collective-permute-start.55 = (bf16[320,1024]{1,0:T(8,128)(2,1)S(1)}, bf16[320,1024]{1,0:T(8,128)(2,1)S(1)}, u32[]{:S(2)}, u32[]{:S(2)}) collective-permute-start(bf16[320,1024]{1,0:T(8,128)(2,1)S(1)} %bitcast.182), channel_id=1, source_target_pairs={{0,16},{16,0},{1,17},{17,1},{2,18},{18,2},{3,19},{19,3},{4,20},{20... | collective-permute-start | bytes 1966088 | tf_op jit(solution)/shard_map/ppermute | solution.py:38
  426.6 23.3 %collective-permute-start.56 = (bf16[640,256]{1,0:T(8,128)(2,1)}, bf16[640,256]{1,0:T(8,128)(2,1)}, u32[]{:S(2)}, u32[]{:S(2)}) collective-permute-start(bf16[640,256]{1,0:T(8,128)(2,1)} %bitcast.186), channel_id=1, source_target_pairs={{0,16},{16,0},{1,17},{17,1},{2,18},{18,2},{3,19},{19,3},{4,20},{20... | collective-permute-start | bytes 983048 | tf_op jit(solution)/shard_map/ppermute | solution.py:38
  442.5 20.7 %collective-permute-start.54 = (bf16[320,1024]{1,0:T(8,128)(2,1)}, bf16[320,1024]{1,0:T(8,128)(2,1)}, u32[]{:S(2)}, u32[]{:S(2)}) collective-permute-start(bf16[320,1024]{1,0:T(8,128)(2,1)} %bitcast.59.refs_2_), channel_id=1, source_target_pairs={{0,16},{16,0},{1,17},{17,1},{2,18},{18,2},{3,19},{19,3},{4,20},{20... | collective-permute-start | bytes 1966088 | tf_op jit(solution)/shard_map/ppermute | solution.py:38
  474.9 12.5 %collective-permute-start.61 = (bf16[912,256]{1,0:T(8,128)(2,1)S(1)}, bf16[912,256]{1,0:T(8,128)(2,1)S(1)}, u32[]{:S(2)}, u32[]{:S(2)}) collective-permute-start(bf16[912,256]{1,0:T(8,128)(2,1)S(1)} %bitcast.164), channel_id=1, source_target_pairs={{0,16},{16,0},{1,17},{17,1},{2,18},{18,2},{3,19},{19,3},{4,20},{20... | collective-permute-start | bytes 1400840 | tf_op jit(solution)/shard_map/ppermute | solution.py:38
  (160 other events, 1264.9 us)
Sparse Core Ops, SparseCore 0:
  40.0 64.3 all-gather.4
  106.6 62.6 all-gather.6
  304.0 29.0 reduce-scatter.4
  335.3 38.6 reduce-scatter.6
  376.1 30.3 reduce-scatter.8
  418.9 38.8 reduce-scatter.10
